TPU v7x, 128 devices: a whole 4x4x4 slice. The times are simulated.
128 devices in a mesh: aux: 4 (over y_lo, core), blk: 32 (over y_hi, z, x).
Axes of the slice: x: 4, y: 4 (y_hi: 2, y_lo: 2; y = y_hi * 2 + y_lo), z: 4, core: 2. Of those that a mesh axis runs over, the one named last changes fastest.
Arguments:
- b_factors: bfloat16 [8192, 64, 128], P('blk', 'aux'), may hold values from -0.3125 to 0.3125
Outputs:
- exchange: float32 [8192, 8192], P('blk', 'aux')
All inputs are finite; a program needn't handle non-finite values.
Results may differ from a plain program's by a relative error of at most 0.0003.
Values may be sent and summed in bfloat16 or wider, within the bound.
No kernel may reach another device: no remote copies, remote signals or barrier semaphores. Data moves between devices by JAX's collectives and lax.ppermute only.
A program may use at most 128 MiB of HBM per device.

v0:
```python
import jax
import jax.numpy as jnp
from jax import lax
from jax.sharding import PartitionSpec as P


def local(b_factors):
    rows = b_factors.shape[0]
    flat = b_factors.reshape(rows, -1)
    piece = lax.all_gather(b_factors, "blk", axis=0, tiled=True)
    other = piece.reshape(piece.shape[0], -1)
    partial_value = jnp.dot(flat, other.T, preferred_element_type=jnp.float32)
    return lax.psum_scatter(partial_value, "aux", scatter_dimension=1, tiled=True)


def solution(mesh):
    placed = (P("blk", "aux", None),)
    return jax.shard_map(
        local, mesh=mesh, in_specs=placed, out_specs=P("blk", "aux"), check_vma=False
    )
```

profile of v0, /device:TPU:9, one launch (start us, length us, event | category | flops | bytes accessed | tf_op | source)
XLA Modules:
  0.0 372.6 jit_solution(16575337114786662386)
XLA Ops:
  6.5 0.0 all-gather.2.cloned.1.call-start
  6.5 2.5 copy.3
  9.0 0.0 all-gather.2.cloned.1.call-update
  9.0 0.0 reduce-scatter.2.cloned.1.call-start
  9.1 261.0 %all-gather.2.cloned.1.call-done = bf16[8192,16,128]{2,0,1:T(8,128)(2,1)} async-done(((bf16[256,16,128]{2,0,1:T(8,128)(2,1)}), bf16[8192,16,128]{2,0,1:T(8,128)(2,1)}) %all-gather.2.cloned.1.call-update) | async-done | bytes 33554448 | tf_op jit(solution)/shard_map/all_gather | solution.py:10
  270.1 18.5 %convolution_bitcast_fusion = f32[256,8192]{1,0:T(8,128)} fusion(bf16[8192,16,128]{2,0,1:T(8,128)(2,1)} %all-gather.2.cloned.1.call-done, bf16[256,16,128]{2,1,0:T(8,128)(2,1)} %param.1), kind=kOutput, calls=%fused_computation | convolution fusion | flops 8589934592 | bytes 42991616 | tf_op jit(solution)/shard_map/dot_general | solution.py:12
  288.5 0.0 reduce-scatter.2.cloned.1.call-update
  288.6 77.2 %reduce-scatter.2.cloned.1.call-done = f32[256,2048]{1,0:T(8,128)} async-done(((f32[256,8192]{1,0:T(8,128)}), f32[256,2048]{1,0:T(8,128)}) %reduce-scatter.2.cloned.1.call-update) | async-done | bytes 2097168 | tf_op jit(solution)/shard_map/reduce_scatter | solution.py:13
Async XLA Ops:
  6.5 263.5 %all-gather.2.cloned.1.call-start = ((), (), s32[]{:S(2)}) async-start(), calls=%async_computation.1 | async-start | bytes 34603008 | tf_op jit(solution)/shard_map/all_gather | solution.py:10
  9.0 356.8 %reduce-scatter.2.cloned.1.call-start = ((), (), s32[]{:S(2)}) async-start(), calls=%async_computation.2 | async-start | bytes 10485760 | tf_op jit(solution)/shard_map/reduce_scatter | solution.py:13
Sparse Core Ops, SparseCore 0:
  10.4 259.6 all-gather.1
  288.7 77.0 reduce-scatter.1
where the time goes:
time: 375 us; the launch traced here: 373 us
  waiting for transfers between devices  338 us (90%)
  matrix products  18.5 us (5%)
  between operations  13.4 us (4%)
    all_gather x1, waiting for transfers between devices, local(): piece = lax.all_gather(b_factors, 'blk', axis=0, tiled=True)  261 us
    reduce_scatter x1, waiting for transfers between devices, local(): lax.psum_scatter(partial_value, 'aux', scatter_dimension=1, tiled=True)  77.2 us
    dot_general x1, matrix products, local(): partial_value = jnp.dot(flat, other.T, preferred_element_type=jnp.float32)  18.5 us
  transfers between devices with their start and end apart: 2, of which 2 were waited for; matrix products, arithmetic and copies ran while one was open for 0% of the time, Pallas kernels for 0%

commit v1 on v0

v1 whole, which is shorter than its diff:
```python
import functools
import math

import jax
import jax.numpy as jnp
from jax import lax
from jax.experimental import pallas as pl
from jax.experimental.pallas import tpu as pltpu
from jax.sharding import PartitionSpec as P

ORDER = 32
TOP = 2.0**3.9
FLOOR = 2.0**-3.9
VMEM = 48 << 20

DEVICES = [
    (x, z, yh, yl, c)
    for yl in range(2)
    for c in range(2)
    for yh in range(2)
    for z in range(4)
    for x in range(4)
]


def move(value, where):
    index = {d: i for i, d in enumerate(DEVICES)}
    pairs = [(index[d], index[where(*d)]) for d in DEVICES]
    return lax.ppermute(value, ("aux", "blk"), pairs)


def to_own_layer(x, z, yh, yl, c):
    return x, z, c, yl, yh


def to_core(x, z, yh, yl, c):
    return x, z, yh, yl, 1 - c


def to_position(dx, dz, swap=False):
    def where(x, z, yh, yl, c):
        x, z = (x + dx) % 4, (z + dz) % 4
        return (x, z, yl, yh, c) if swap else (x, z, yh, yl, c)

    return where


def to_owner(m1, m2):
    def where(x, z, yh, yl, c):
        return x, z, c, yl ^ m1, yh ^ m2

    return where


MATCHINGS = ((0, 0), (0, 1), (1, 0), (1, 1))


def product(a, b):
    return lax.dot_general(a, b, (((1,), (1,)), ((), ())), preferred_element_type=jnp.float32)


def encode(value, bound):
    v = jnp.abs(value) * (TOP / bound) + FLOOR
    for _ in range(int(math.log2(ORDER))):
        v = v * v
    return jnp.where(value < 0, -v, v).astype(jnp.bfloat16)


def decode(code, bound):
    y = code.astype(jnp.float32)
    v = jnp.exp(jnp.log(jnp.abs(y)) * (1.0 / ORDER)) - FLOOR
    return jnp.where(y < 0, -v, v) * (bound * (1.0 / TOP))


def tiles_kernel(classes, n_in, place, *refs):
    ins, outs, acc = refs[:n_in], refs[n_in : n_in + 4], refs[n_in + 4]
    yh, yl, c = place[0], place[1], place[2]
    half = acc.shape[1] // 2
    width = acc.shape[2]
    count = len(classes)
    row = lax.broadcasted_iota(jnp.int32, (16, width), 0)
    bounds = jnp.zeros((16, width), jnp.float32)
    for k, (rows, own, other) in enumerate(classes):
        for slot, columns in ((c, own), (1 - c, other)):
            r0 = 0
            for r in rows:
                c0 = 0
                for q in columns:
                    h, w = ins[r].shape[0], ins[q].shape[0]
                    acc[slot, r0 : r0 + h, c0 : c0 + w] = product(ins[r][...], ins[q][...])
                    c0 += w
                r0 += h
        top = jnp.maximum(jnp.max(jnp.abs(acc[...])), 1e-30) * 1.008
        coded = jnp.full((16, width), top, jnp.float32).astype(jnp.bfloat16).astype(jnp.float32)
        bounds = jnp.where(row == k, coded, bounds)
        bound = coded[0:1, :]
        for (m1, m2), out in zip(MATCHINGS, outs):
            part = acc[yl ^ m1, pl.ds(pl.multiple_of((yh ^ m2) * half, half), half), :]
            out[k * half : (k + 1) * half, :] = encode(part, bound)
    for out in outs:
        out[count * half :, :] = bounds.astype(jnp.bfloat16)


def partial_tiles(place, blocks, classes, rows):
    names, arrays, ids = list(blocks), [], {}
    for name in names:
        ids[name] = tuple(range(len(arrays), len(arrays) + len(blocks[name])))
        arrays += blocks[name]
    listed = tuple((ids[r], ids[o], ids[t]) for r, o, t in classes)
    out = jax.ShapeDtypeStruct((len(classes) * (rows // 2) + 16, rows), jnp.bfloat16)
    flops = len(classes) * 4 * rows * rows * arrays[0].shape[1]
    return pl.pallas_call(
        functools.partial(tiles_kernel, listed, len(arrays)),
        out_shape=[out] * 4,
        in_specs=[pl.BlockSpec(memory_space=pltpu.SMEM)]
        + [pl.BlockSpec(memory_space=pltpu.VMEM)] * len(arrays),
        out_specs=[pl.BlockSpec(memory_space=pltpu.VMEM)] * 4,
        scratch_shapes=[pltpu.VMEM((2, rows, rows), jnp.float32)],
        compiler_params=pltpu.CompilerParams(vmem_limit_bytes=VMEM),
        cost_estimate=pl.CostEstimate(flops=flops, bytes_accessed=1 << 23, transcendentals=0),
    )(place, *arrays)


def sum_kernel(groups, *refs):
    ins, outs = refs[:4], refs[4:]
    half, width = outs[0].shape[1], outs[0].shape[2]
    count = (ins[0].shape[0] - 16) // half
    for k in range(count):
        total = None
        for r in ins:
            bound = r[count * half :, :].astype(jnp.float32)[k : k + 1, :]
            term = decode(r[k * half : (k + 1) * half, :], bound)
            total = term if total is None else total + term
        for out, members in zip(outs, groups):
            for i, member in enumerate(members):
                if member == k:
                    out[i, :, :] = total


def summed(coded, groups, rows):
    return pl.pallas_call(
        functools.partial(sum_kernel, groups),
        out_shape=[jax.ShapeDtypeStruct((len(g), rows // 2, rows), jnp.float32) for g in groups],
        in_specs=[pl.BlockSpec(memory_space=pltpu.VMEM)] * 4,
        out_specs=[pl.BlockSpec(memory_space=pltpu.VMEM)] * len(groups),
        compiler_params=pltpu.CompilerParams(vmem_limit_bytes=VMEM),
        cost_estimate=pl.CostEstimate(flops=1 << 24, bytes_accessed=1 << 22, transcendentals=1 << 21),
    )(*coded)


def place_kernel(tiles, n, place, *refs):
    own, other, out = refs[:n], refs[n : 2 * n], refs[2 * n]
    c, z, x = place[2], place[3], place[4]
    rows = out.shape[0]
    half = rows // 2
    for array, i, (dx, dz), turned in tiles:
        zz = (z + dz) % 4
        xx = (x + dx) % 4

        @pl.when(zz // 2 == c)
        def _():
            start = pl.multiple_of(((zz % 2) * 4 + xx) * rows, rows)
            first = pl.multiple_of(c * half, half)
            second = pl.multiple_of((1 - c) * half, half)
            if turned:
                out[:, pl.ds(pl.multiple_of(start + first, half), half)] = own[array][i, :, :].T
                out[:, pl.ds(pl.multiple_of(start + second, half), half)] = other[array][i, :, :].T
            else:
                out[pl.ds(first, half), pl.ds(start, rows)] = own[array][i, :, :]
                out[pl.ds(second, half), pl.ds(start, rows)] = other[array][i, :, :]


def placed(place, own, other, tiles, rows):
    n = len(own)
    return pl.pallas_call(
        functools.partial(place_kernel, tiles, n),
        out_shape=jax.ShapeDtypeStruct((rows, 8 * rows), jnp.float32),
        in_specs=[pl.BlockSpec(memory_space=pltpu.SMEM)]
        + [pl.BlockSpec(memory_space=pltpu.VMEM)] * (2 * n),
        out_specs=pl.BlockSpec(memory_space=pltpu.VMEM),
        compiler_params=pltpu.CompilerParams(vmem_limit_bytes=VMEM),
        cost_estimate=pl.CostEstimate(flops=0, bytes_accessed=6 << 20, transcendentals=0),
    )(place, *own, *other)


O, PX, MX, PZ, MZ, PE, ME = (0, 0), (1, 0), (3, 0), (0, 1), (0, 3), (1, 1), (3, 3)
EARLY = ((O, O), (O, PX), (O, PZ), (MX, PX), (MZ, PZ), (MZ, PX), (PZ, PX))
LATE = ((MX, PE), (MZ, PE), (ME, PE))
EARLY_SENDS = (
    (O, False, (0, 1, 2)),
    (MX, False, (3,)),
    (MZ, False, (4, 5)),
    (PZ, False, (6,)),
    (PX, True, (1, 5, 6)),
    (PZ, True, (2,)),
)
LATE_SENDS = (
    (MX, False, (0,)),
    (MZ, False, (1,)),
    (ME, False, (2,)),
    (PE, True, (0, 1)),
)


def minus(a, b):
    return (a[0] - b[0]) % 4, (a[1] - b[1]) % 4


def deliver(groups, sends):
    return [
        g if to == O else move(g, to_position(*to, swap=turned))
        for g, (to, turned, _) in zip(groups, sends)
    ]


def local(b_factors):
    rows = b_factors.shape[0]
    half = rows // 2
    flat = b_factors.reshape(rows, -1)
    aux, blk = lax.axis_index("aux"), lax.axis_index("blk")
    place = jnp.stack(
        [blk // 16, aux // 2, aux % 2, (blk // 4) % 4, blk % 4]
    ).astype(jnp.int32)

    own = {O: (move(flat, to_own_layer),)}
    base = own[O][0]
    for o in (PX, MX, PZ, MZ):
        own[o] = (move(base, to_position(-o[0], -o[1])),)
    other = {o: (move(own[o][0], to_core),) for o in (O, PX, PZ)}
    own[PE] = (
        move(own[PZ][0][:half], to_position(-1, 0)),
        move(own[PX][0][half:], to_position(0, -1)),
    )
    own[ME] = (
        move(own[MZ][0][:half], to_position(1, 0)),
        move(own[MX][0][half:], to_position(0, 1)),
    )
    other[PE] = tuple(move(v, to_core) for v in own[PE])

    own_parts, other_parts, tiles = [], [], []
    for classes, sends in ((EARLY, EARLY_SENDS), (LATE, LATE_SENDS)):
        needed = {r for r, _ in classes} | {q for _, q in classes}
        blocks = {("own", o): own[o] for o in own if o in needed}
        blocks |= {("other", q): other[q] for q in other if q in {b for _, b in classes}}
        coded = partial_tiles(
            place, blocks, [(("own", r), ("own", q), ("other", q)) for r, q in classes], rows
        )
        arrived = [move(v, to_owner(*m)) for v, m in zip(coded, MATCHINGS)]
        groups = summed(arrived, [members for _, _, members in sends], rows)
        parts = deliver(groups, sends)
        for (to, turned, members) in sends:
            for i, k in enumerate(members):
                r, q = classes[k]
                d = minus(r, q) if turned else minus(q, r)
                tiles.append((len(own_parts), i, d, turned))
            own_parts.append(parts.pop(0))
            other_parts.append(move(own_parts[-1], to_core))
    return placed(place, own_parts, other_parts, tuple(tiles), rows)


def solution(mesh):
    return jax.shard_map(
        local, mesh=mesh, in_specs=(P("blk", "aux", None),), out_specs=P("blk", "aux"), check_vma=False
    )
```

time: 375 us -> 154 us (0.41)
  waiting for transfers between devices: 338 us -> 75.9 us
  starting transfers between devices: 0.04 us -> 50.4 us
  Pallas kernels: 0 us -> 19.5 us
  matrix products: 18.5 us -> 0 us
  between operations: 13.4 us -> 0.24 us
  local copies, waits for them, and re-layouts: 2.47 us -> 6.75 us
    all_gather x1 -> x0, waiting for transfers between devices: 261 us -> none  [local(): piece = lax.all_gather(b_factors, 'blk', axis=0, tiled=True)]
    reduce_scatter x1 -> x0, waiting for transfers between devices: 77.2 us -> none  [local(): lax.psum_scatter(partial_value, 'aux', scatter_dimension=1, tiled=True)]
    ppermute x0 -> x41, waiting for transfers between devices: none -> 75.9 us  [move(): return lax.ppermute(value, ('aux', 'blk'), pairs)]
    ppermute x0 -> x41, starting transfers between devices: none -> 50.4 us  [move(): return lax.ppermute(value, ('aux', 'blk'), pairs)]
    pallas_call x0 -> x5, Pallas kernels: none -> 19.5 us  [the longest x2 14.8 us: partial_tiles(): pl.pallas_call(functools.partial(tiles_kernel, listed, len(arrays)), out_...]
    dot_general x1 -> x0, matrix products: 18.5 us -> none  [local(): partial_value = jnp.dot(flat, other.T, preferred_element_type=jnp.float32)]
    unnamed x1 -> x17, local copies, waits for them, and re-layouts: 2.47 us -> 6.51 us
  transfers between devices with their start and end apart: 2 -> 41, of which waited for: 2 -> 16; matrix products, arithmetic and copies ran while one was open for 0% -> 0% of each run, Pallas kernels for 0% -> 11%
where the time goes in v1:
time: 154 us; the launch traced here: 153 us
  waiting for transfers between devices  75.9 us (49%)
  starting transfers between devices  50.4 us (33%)
  Pallas kernels  19.5 us (13%)
  local copies, waits for them, and re-layouts  6.75 us (4%)
    ppermute x41, waiting for transfers between devices, move(): return lax.ppermute(value, ('aux', 'blk'), pairs)  75.9 us
    ppermute x41, starting transfers between devices, move(): return lax.ppermute(value, ('aux', 'blk'), pairs)  50.4 us
    pallas_call x2, Pallas kernels, partial_tiles(): pl.pallas_call(functools.partial(tiles_kernel, listed, len(arrays)), out_...  14.8 us
    unnamed x17, local copies, waits for them, and re-layouts  6.51 us
  transfers between devices with their start and end apart: 41, of which 16 were waited for; matrix products, arithmetic and copies ran while one was open for 0% of the time, Pallas kernels for 11%

profile of v1, /device:TPU:9, one launch (start us, length us, event | category | flops | bytes accessed | tf_op | source)
XLA Modules:
  0.0 152.7 jit_solution(16533204045885417522)
XLA Ops:
  0.0 1.5 copy.4
  1.5 4.5 %collective-permute-start = (bf16[256,2048]{1,0:T(8,128)(2,1)S(1)}, bf16[256,2048]{1,0:T(8,128)(2,1)}, u32[]{:S(2)}, u32[]{:S(2)}) collective-permute-start(bf16[256,2048]{1,0:T(8,128)(2,1)S(1)} %bitcast.10), channel_id=1, source_target_pairs={{0,0},{1,1},{2,2},{3,3},{4,4},{5,5},{6,6},{7,7},{8,8},{9,9},{10,10... | collective-permute-start | bytes 3145736 | tf_op jit(solution)/shard_map/ppermute | solution.py:29
  6.0 13.4 %collective-permute-done.refs_0_ = bf16[256,2048]{1,0:T(8,128)(2,1)} collective-permute-done((bf16[256,2048]{1,0:T(8,128)(2,1)S(1)}, bf16[256,2048]{1,0:T(8,128)(2,1)}, u32[]{:S(2)}, u32[]{:S(2)}) %collective-permute-start) | collective-permute-done | bytes 1048608 | tf_op jit(solution)/shard_map/ppermute | solution.py:29
  19.4 3.8 %collective-permute-start.3 = (bf16[256,2048]{1,0:T(8,128)(2,1)}, bf16[256,2048]{1,0:T(8,128)(2,1)S(1)}, u32[]{:S(2)}, u32[]{:S(2)}) collective-permute-start(bf16[256,2048]{1,0:T(8,128)(2,1)} %collective-permute-done.refs_0_), channel_id=1, source_target_pairs={{0,12},{1,13},{2,14},{3,15},{4,0},{5,1},{6,2},{7,3},{8,4},{9,5},{1... | collective-permute-start | bytes 3145736 | tf_op jit(solution)/shard_map/ppermute | solution.py:29
  23.2 2.5 %collective-permute-start.1 = (bf16[256,2048]{1,0:T(8,128)(2,1)}, bf16[256,2048]{1,0:T(8,128)(2,1)S(1)}, u32[]{:S(2)}, u32[]{:S(2)}) collective-permute-start(bf16[256,2048]{1,0:T(8,128)(2,1)} %collective-permute-done.refs_0_), channel_id=1, source_target_pairs={{0,3},{1,0},{2,1},{3,2},{4,7},{5,4},{6,5},{7,6},{8,11},{9,8},{10,9... | collective-permute-start | bytes 3145736 | tf_op jit(solution)/shard_map/ppermute | solution.py:29
  25.7 15.2 %collective-permute-done.3.refs_3_ = bf16[256,2048]{1,0:T(8,128)(2,1)S(1)} collective-permute-done((bf16[256,2048]{1,0:T(8,128)(2,1)}, bf16[256,2048]{1,0:T(8,128)(2,1)S(1)}, u32[]{:S(2)}, u32[]{:S(2)}) %collective-permute-start.3) | collective-permute-done | bytes 1048608 | tf_op jit(solution)/shard_map/ppermute | solution.py:29
  40.9 2.5 %collective-permute-start.17 = (bf16[128,2048]{1,0:T(8,128)(2,1)S(1)}, bf16[128,2048]{1,0:T(8,128)(2,1)}, u32[]{:S(2)}, u32[]{:S(2)}) collective-permute-start(bf16[128,2048]{1,0:T(8,128)(2,1)S(1)} %slice.16), channel_id=1, source_target_pairs={{0,3},{1,0},{2,1},{3,2},{4,7},{5,4},{6,5},{7,6},{8,11},{9,8},{10,9... | collective-permute-start | bytes 1572872 | tf_op jit(solution)/shard_map/ppermute | solution.py:29
  43.5 3.1 %collective-permute-start.18 = (bf16[128,2048]{1,0:T(8,128)(2,1)S(1)}, bf16[128,2048]{1,0:T(8,128)(2,1)}, u32[]{:S(2)}, u32[]{:S(2)}) collective-permute-start(bf16[128,2048]{1,0:T(8,128)(2,1)S(1)} %slice.17), channel_id=1, source_target_pairs={{0,12},{1,13},{2,14},{3,15},{4,0},{5,1},{6,2},{7,3},{8,4},{9,5},{1... | collective-permute-start | bytes 1572872 | tf_op jit(solution)/shard_map/ppermute | solution.py:29
  47.0 2.6 %collective-permute-done.17.refs_2_ = bf16[128,2048]{1,0:T(8,128)(2,1)} collective-permute-done((bf16[128,2048]{1,0:T(8,128)(2,1)S(1)}, bf16[128,2048]{1,0:T(8,128)(2,1)}, u32[]{:S(2)}, u32[]{:S(2)}) %collective-permute-start.17) | collective-permute-done | bytes 524320 | tf_op jit(solution)/shard_map/ppermute | solution.py:29
  49.6 3.1 %collective-permute-done.18.refs_3_ = bf16[128,2048]{1,0:T(8,128)(2,1)} collective-permute-done((bf16[128,2048]{1,0:T(8,128)(2,1)S(1)}, bf16[128,2048]{1,0:T(8,128)(2,1)}, u32[]{:S(2)}, u32[]{:S(2)}) %collective-permute-start.18) | collective-permute-done | bytes 524320 | tf_op jit(solution)/shard_map/ppermute | solution.py:29
  52.7 3.2 %collective-permute-done.19.refs_4_ = bf16[128,2048]{1,0:T(8,128)(2,1)S(1)} collective-permute-done((bf16[128,2048]{1,0:T(8,128)(2,1)S(1)}, bf16[128,2048]{1,0:T(8,128)(2,1)S(1)}, u32[]{:S(2)}, u32[]{:S(2)}) %collective-permute-start.19) | collective-permute-done | bytes 524320 | tf_op jit(solution)/shard_map/ppermute | solution.py:29
  55.9 0.8 copy-done.4
  56.8 0.9 copy-done.6
  57.6 0.5 collective-permute-start.22
  58.2 0.8 collective-permute-done.21.refs_6_
  59.0 1.0 collective-permute-done.22.refs_7_
  60.0 1.2 copy-done.2
  61.3 1.0 copy-done.5
  62.3 1.0 copy-done.7
  63.3 6.0 %shard_map.19 = (bf16[400,256]{1,0:T(8,128)(2,1)S(1)}, bf16[400,256]{1,0:T(8,128)(2,1)S(1)}, bf16[400,256]{1,0:T(8,128)(2,1)S(1)}, bf16[400,256]{1,0:T(8,128)(2,1)S(1)}) custom-call(s32[5]{0:T(128)S(1)} %stack.23.place, bf16[256,2048]{1,0:T(8,128)(2,1)S(1)} %copy-done.2, bf16[256,2048]{1,0:T(8,128)(2,1)S(1)} %collective-permute-done.4.refs_4_.refs_1_, ...), custom_call_target="tpu_custom_call" | custom-call | flops 1610612736 | bytes 8388608 | tf_op jit(solution)/shard_map/pallas_call | solution.py:112
  69.4 6.0 %collective-permute-start.23 = (bf16[400,256]{1,0:T(8,128)(2,1)S(1)}, bf16[400,256]{1,0:T(8,128)(2,1)S(1)}, u32[]{:S(2)}, u32[]{:S(2)}) collective-permute-start(bf16[400,256]{1,0:T(8,128)(2,1)S(1)} %get-tuple-element.33), channel_id=1, source_target_pairs={{0,0},{1,1},{2,2},{3,3},{4,4},{5,5},{6,6},{7,7},{8,8},{9,9},{10,10... | collective-permute-start | bytes 614408 | tf_op jit(solution)/shard_map/ppermute | solution.py:29
  75.7 8.7 %shard_map.17 = (bf16[912,256]{1,0:T(8,128)(2,1)S(1)}, bf16[912,256]{1,0:T(8,128)(2,1)S(1)}, bf16[912,256]{1,0:T(8,128)(2,1)S(1)}, bf16[912,256]{1,0:T(8,128)(2,1)S(1)}) custom-call(s32[5]{0:T(128)S(1)} %stack.23.place, bf16[256,2048]{1,0:T(8,128)(2,1)} %collective-permute-done.refs_0_, bf16[256,2048]{1,0:T(8,128)(2,1)S(1)} %collective-permute-done.1.refs_1_, ...), custom_call_target="tpu_custom_call" | custom-call | flops 3758096384 | bytes 8388608 | tf_op jit(solution)/shard_map/pallas_call | solution.py:112
  84.4 1.9 %collective-permute-start.8 = (bf16[912,256]{1,0:T(8,128)(2,1)S(1)}, bf16[912,256]{1,0:T(8,128)(2,1)S(1)}, u32[]{:S(2)}, u32[]{:S(2)}) collective-permute-start(bf16[912,256]{1,0:T(8,128)(2,1)S(1)} %get-tuple-element.23), channel_id=1, source_target_pairs={{0,0},{1,1},{2,2},{3,3},{4,4},{5,5},{6,6},{7,7},{8,8},{9,9},{10,10... | collective-permute-start | bytes 1400840 | tf_op jit(solution)/shard_map/ppermute | solution.py:29
  86.4 2.4 %collective-permute-start.10 = (bf16[912,256]{1,0:T(8,128)(2,1)S(1)}, bf16[912,256]{1,0:T(8,128)(2,1)S(1)}, u32[]{:S(2)}, u32[]{:S(2)}) collective-permute-start(bf16[912,256]{1,0:T(8,128)(2,1)S(1)} %get-tuple-element.25), channel_id=1, source_target_pairs={{0,64},{1,65},{2,66},{3,67},{4,68},{5,69},{6,70},{7,71},{8,72},{9,... | collective-permute-start | bytes 1400840 | tf_op jit(solution)/shard_map/ppermute | solution.py:29
  88.9 1.2 collective-permute-start.11
  90.1 22.3 %collective-permute-done.25.refs_2_ = bf16[400,256]{1,0:T(8,128)(2,1)S(1)} collective-permute-done((bf16[400,256]{1,0:T(8,128)(2,1)S(1)}, bf16[400,256]{1,0:T(8,128)(2,1)S(1)}, u32[]{:S(2)}, u32[]{:S(2)}) %collective-permute-start.25) | collective-permute-done | bytes 204832 | tf_op jit(solution)/shard_map/ppermute | solution.py:29
  112.3 1.0 collective-permute-start.26
  113.3 4.2 %collective-permute-done.26.refs_3_ = bf16[400,256]{1,0:T(8,128)(2,1)S(1)} collective-permute-done((bf16[400,256]{1,0:T(8,128)(2,1)S(1)}, bf16[400,256]{1,0:T(8,128)(2,1)S(1)}, u32[]{:S(2)}, u32[]{:S(2)}) %collective-permute-start.26) | collective-permute-done | bytes 204832 | tf_op jit(solution)/shard_map/ppermute | solution.py:29
  117.5 0.7 shard_map.20
  118.2 2.2 %collective-permute-start.27 = (f32[1,128,256]{2,1,0:T(8,128)S(1)}, f32[1,128,256]{2,1,0:T(8,128)S(1)}, u32[]{:S(2)}, u32[]{:S(2)}) collective-permute-start(f32[1,128,256]{2,1,0:T(8,128)S(1)} %get-tuple-element.37), channel_id=1, source_target_pairs={{0,3},{1,0},{2,1},{3,2},{4,7},{5,4},{6,5},{7,6},{8,11},{9,8},{10,9... | collective-permute-start | bytes 393224 | tf_op jit(solution)/shard_map/ppermute | solution.py:29
  120.4 0.7 collective-permute-start.30
  121.0 1.5 %shard_map.18 = (f32[3,128,256]{2,1,0:T(8,128)S(1)}, f32[1,128,256]{2,1,0:T(8,128)S(1)}, f32[2,128,256]{2,1,0:T(8,128)S(1)}, f32[1,128,256]{2,1,0:T(8,128)S(1)},...) custom-call(bf16[912,256]{1,0:T(8,128)(2,1)S(1)} %collective-permute-done.8.refs_0_, ...), custom_call_target="tpu_custom_call" | custom-call | flops 16777216 | bytes 4194304 | tf_op jit(solution)/shard_map/pallas_call | solution.py:141
  122.6 1.4 collective-permute-start.15
  123.9 3.2 %collective-permute-start.29 = (f32[1,128,256]{2,1,0:T(8,128)S(1)}, f32[1,128,256]{2,1,0:T(8,128)S(1)}, u32[]{:S(2)}, u32[]{:S(2)}) collective-permute-start(f32[1,128,256]{2,1,0:T(8,128)S(1)} %get-tuple-element.39), channel_id=1, source_target_pairs={{0,15},{1,12},{2,13},{3,14},{4,3},{5,0},{6,1},{7,2},{8,7},{9,4},{1... | collective-permute-start | bytes 393224 | tf_op jit(solution)/shard_map/ppermute | solution.py:29
  127.2 1.5 collective-permute-start.37
  129.1 2.0 %collective-permute-start.39 = (f32[1,128,256]{2,1,0:T(8,128)S(1)}, f32[1,128,256]{2,1,0:T(8,128)S(1)}, u32[]{:S(2)}, u32[]{:S(2)}) collective-permute-start(f32[1,128,256]{2,1,0:T(8,128)S(1)} %collective-permute-done.29.refs_8_), channel_id=1, source_target_pairs={{0,32},{1,33},{2,34},{3,35},{4,36},{5,37},{6,38},{7,39},{8,40},{9,... | collective-permute-start | bytes 393224 | tf_op jit(solution)/shard_map/ppermute | solution.py:29
  131.2 1.0 collective-permute-done.30.refs_9_
  132.2 2.2 %collective-permute-start.12 = (f32[1,128,256]{2,1,0:T(8,128)S(1)}, f32[1,128,256]{2,1,0:T(8,128)S(1)}, u32[]{:S(2)}, u32[]{:S(2)}) collective-permute-start(f32[1,128,256]{2,1,0:T(8,128)S(1)} %get-tuple-element.28), channel_id=1, source_target_pairs={{0,3},{1,0},{2,1},{3,2},{4,7},{5,4},{6,5},{7,6},{8,11},{9,8},{10,9... | collective-permute-start | bytes 393224 | tf_op jit(solution)/shard_map/ppermute | solution.py:29
  134.4 2.5 %collective-permute-start.13 = (f32[2,128,256]{2,1,0:T(8,128)S(1)}, f32[2,128,256]{2,1,0:T(8,128)S(1)}, u32[]{:S(2)}, u32[]{:S(2)}) collective-permute-start(f32[2,128,256]{2,1,0:T(8,128)S(1)} %get-tuple-element.29), channel_id=1, source_target_pairs={{0,12},{1,13},{2,14},{3,15},{4,0},{5,1},{6,2},{7,3},{8,4},{9,5},{1... | collective-permute-start | bytes 786440 | tf_op jit(solution)/shard_map/ppermute | solution.py:29
  137.3 1.8 %collective-permute-start.31 = (f32[3,128,256]{2,1,0:T(8,128)S(1)}, f32[3,128,256]{2,1,0:T(8,128)S(1)}, u32[]{:S(2)}, u32[]{:S(2)}) collective-permute-start(f32[3,128,256]{2,1,0:T(8,128)S(1)} %get-tuple-element.27.refs_0_), channel_id=1, source_target_pairs={{0,32},{1,33},{2,34},{3,35},{4,36},{5,37},{6,38},{7,39},{8,40},{9,... | collective-permute-start | bytes 1179656 | tf_op jit(solution)/shard_map/ppermute | solution.py:29
  139.1 6.3 %collective-permute-done.14.refs_3_ = f32[1,128,256]{2,1,0:T(8,128)S(1)} collective-permute-done((f32[1,128,256]{2,1,0:T(8,128)S(1)}, f32[1,128,256]{2,1,0:T(8,128)S(1)}, u32[]{:S(2)}, u32[]{:S(2)}) %collective-permute-start.14) | collective-permute-done | bytes 131104 | tf_op jit(solution)/shard_map/ppermute | solution.py:29
  145.5 1.4 collective-permute-start.32
  146.9 0.5 collective-permute-start.34
  147.5 0.4 collective-permute-done.32.refs_11_
  147.9 0.4 collective-permute-start.33
  148.2 0.6 collective-permute-done.34.refs_13_
  149.0 1.2 collective-permute-done.36.refs_15_
  150.2 2.6 %shard_map.21 = f32[256,2048]{1,0:T(8,128)} custom-call(s32[5]{0:T(128)S(1)} %stack.23.place, f32[3,128,256]{2,1,0:T(8,128)S(1)} %get-tuple-element.27.refs_0_, f32[1,128,256]{2,1,0:T(8,128)S(1)} %collective-permute-done.12.refs_1_, f32[2,128,256]{2,1,0:T(8,128)S(1)} %collective-permute-done.13.refs_2_, f32[1,128,256]{2,1,0:T(8,128)S(1)} %collective-permute-done.14.refs_3_, ...), custom_call_target="tpu_custom_call" | custom-call | bytes 6291456 | tf_op jit(solution)/shard_map/pallas_call | solution.py:175
  (61 shorter events, 2.0 us)
Async XLA Ops:
  1.5 17.9 %collective-permute-start = (bf16[256,2048]{1,0:T(8,128)(2,1)S(1)}, bf16[256,2048]{1,0:T(8,128)(2,1)}, u32[]{:S(2)}, u32[]{:S(2)}) collective-permute-start(bf16[256,2048]{1,0:T(8,128)(2,1)S(1)} %bitcast.10), channel_id=1, source_target_pairs={{0,0},{1,1},{2,2},{3,3},{4,4},{5,5},{6,6},{7,7},{8,8},{9,9},{10,10... | collective-permute-start | bytes 3145736 | tf_op jit(solution)/shard_map/ppermute | solution.py:29
  19.4 21.4 %collective-permute-start.3 = (bf16[256,2048]{1,0:T(8,128)(2,1)}, bf16[256,2048]{1,0:T(8,128)(2,1)S(1)}, u32[]{:S(2)}, u32[]{:S(2)}) collective-permute-start(bf16[256,2048]{1,0:T(8,128)(2,1)} %collective-permute-done.refs_0_), channel_id=1, source_target_pairs={{0,12},{1,13},{2,14},{3,15},{4,0},{5,1},{6,2},{7,3},{8,4},{9,5},{1... | collective-permute-start | bytes 3145736 | tf_op jit(solution)/shard_map/ppermute | solution.py:29
  23.2 20.3 %collective-permute-start.1 = (bf16[256,2048]{1,0:T(8,128)(2,1)}, bf16[256,2048]{1,0:T(8,128)(2,1)S(1)}, u32[]{:S(2)}, u32[]{:S(2)}) collective-permute-start(bf16[256,2048]{1,0:T(8,128)(2,1)} %collective-permute-done.refs_0_), channel_id=1, source_target_pairs={{0,3},{1,0},{2,1},{3,2},{4,7},{5,4},{6,5},{7,6},{8,11},{9,8},{10,9... | collective-permute-start | bytes 3145736 | tf_op jit(solution)/shard_map/ppermute | solution.py:29
  25.7 20.9 %collective-permute-start.4 = (bf16[256,2048]{1,0:T(8,128)(2,1)}, bf16[256,2048]{1,0:T(8,128)(2,1)S(1)}, u32[]{:S(2)}, u32[]{:S(2)}) collective-permute-start(bf16[256,2048]{1,0:T(8,128)(2,1)} %collective-permute-done.refs_0_), channel_id=1, source_target_pairs={{0,4},{1,5},{2,6},{3,7},{4,8},{5,9},{6,10},{7,11},{8,12},{9,13},{1... | collective-permute-start | bytes 3145736 | tf_op jit(solution)/shard_map/ppermute | solution.py:29
  25.7 21.1 %collective-permute-start.2 = (bf16[256,2048]{1,0:T(8,128)(2,1)}, bf16[256,2048]{1,0:T(8,128)(2,1)S(1)}, u32[]{:S(2)}, u32[]{:S(2)}) collective-permute-start(bf16[256,2048]{1,0:T(8,128)(2,1)} %collective-permute-done.refs_0_), channel_id=1, source_target_pairs={{0,1},{1,2},{2,3},{3,0},{4,5},{5,6},{6,7},{7,4},{8,9},{9,10},{10,1... | collective-permute-start | bytes 3145736 | tf_op jit(solution)/shard_map/ppermute | solution.py:29
  40.9 8.7 %collective-permute-start.17 = (bf16[128,2048]{1,0:T(8,128)(2,1)S(1)}, bf16[128,2048]{1,0:T(8,128)(2,1)}, u32[]{:S(2)}, u32[]{:S(2)}) collective-permute-start(bf16[128,2048]{1,0:T(8,128)(2,1)S(1)} %slice.16), channel_id=1, source_target_pairs={{0,3},{1,0},{2,1},{3,2},{4,7},{5,4},{6,5},{7,6},{8,11},{9,8},{10,9... | collective-permute-start | bytes 1572872 | tf_op jit(solution)/shard_map/ppermute | solution.py:29
  43.5 9.2 %collective-permute-start.18 = (bf16[128,2048]{1,0:T(8,128)(2,1)S(1)}, bf16[128,2048]{1,0:T(8,128)(2,1)}, u32[]{:S(2)}, u32[]{:S(2)}) collective-permute-start(bf16[128,2048]{1,0:T(8,128)(2,1)S(1)} %slice.17), channel_id=1, source_target_pairs={{0,12},{1,13},{2,14},{3,15},{4,0},{5,1},{6,2},{7,3},{8,4},{9,5},{1... | collective-permute-start | bytes 1572872 | tf_op jit(solution)/shard_map/ppermute | solution.py:29
  46.6 22.8 %copy-start = (bf16[256,2048]{1,0:T(8,128)(2,1)}, bf16[256,2048]{1,0:T(8,128)(2,1)S(1)}, u32[]{:S(2)}) copy-start(bf16[256,2048]{1,0:T(8,128)(2,1)S(1)} %collective-permute-done.4.refs_4_.refs_1_) | copy-start | bytes 3145732
  46.6 9.3 %collective-permute-start.19 = (bf16[128,2048]{1,0:T(8,128)(2,1)S(1)}, bf16[128,2048]{1,0:T(8,128)(2,1)S(1)}, u32[]{:S(2)}, u32[]{:S(2)}) collective-permute-start(bf16[128,2048]{1,0:T(8,128)(2,1)S(1)} %slice.18), channel_id=1, source_target_pairs={{0,1},{1,2},{2,3},{3,0},{4,5},{5,6},{6,7},{7,4},{8,9},{9,10},{10,1... | collective-permute-start | bytes 1572872 | tf_op jit(solution)/shard_map/ppermute | solution.py:29
  46.7 2.9 %copy-start.1 = (bf16[256,2048]{1,0:T(8,128)(2,1)}, bf16[256,2048]{1,0:T(8,128)(2,1)S(1)}, u32[]{:S(2)}) copy-start(bf16[256,2048]{1,0:T(8,128)(2,1)S(1)} %collective-permute-done.2.refs_2_.refs_0_) | copy-start | bytes 3145732
  46.8 10.0 %collective-permute-start.20 = (bf16[128,2048]{1,0:T(8,128)(2,1)S(1)}, bf16[128,2048]{1,0:T(8,128)(2,1)S(1)}, u32[]{:S(2)}, u32[]{:S(2)}) collective-permute-start(bf16[128,2048]{1,0:T(8,128)(2,1)S(1)} %slice.19), channel_id=1, source_target_pairs={{0,4},{1,5},{2,6},{3,7},{4,8},{5,9},{6,10},{7,11},{8,12},{9,13},{1... | collective-permute-start | bytes 1572872 | tf_op jit(solution)/shard_map/ppermute | solution.py:29
  46.9 28.8 %collective-permute-start.5 = (bf16[256,2048]{1,0:T(8,128)(2,1)}, bf16[256,2048]{1,0:T(8,128)(2,1)}, u32[]{:S(2)}, u32[]{:S(2)}) collective-permute-start(bf16[256,2048]{1,0:T(8,128)(2,1)} %collective-permute-done.refs_0_), channel_id=1, source_target_pairs={{0,32},{1,33},{2,34},{3,35},{4,36},{5,37},{6,38},{7,39},{8,40},{9,... | collective-permute-start | bytes 3145736 | tf_op jit(solution)/shard_map/ppermute | solution.py:29
  49.6 26.1 %collective-permute-start.6 = (bf16[256,2048]{1,0:T(8,128)(2,1)S(1)}, bf16[256,2048]{1,0:T(8,128)(2,1)}, u32[]{:S(2)}, u32[]{:S(2)}) collective-permute-start(bf16[256,2048]{1,0:T(8,128)(2,1)S(1)} %collective-permute-done.1.refs_1_), channel_id=1, source_target_pairs={{0,32},{1,33},{2,34},{3,35},{4,36},{5,37},{6,38},{7,39},{8,40},{9,... | collective-permute-start | bytes 3145736 | tf_op jit(solution)/shard_map/ppermute | solution.py:29
  52.7 23.0 %collective-permute-start.7 = (bf16[256,2048]{1,0:T(8,128)(2,1)S(1)}, bf16[256,2048]{1,0:T(8,128)(2,1)}, u32[]{:S(2)}, u32[]{:S(2)}) collective-permute-start(bf16[256,2048]{1,0:T(8,128)(2,1)S(1)} %collective-permute-done.3.refs_3_), channel_id=1, source_target_pairs={{0,32},{1,33},{2,34},{3,35},{4,36},{5,37},{6,38},{7,39},{8,40},{9,... | collective-permute-start | bytes 3145736 | tf_op jit(solution)/shard_map/ppermute | solution.py:29
  56.8 2.3 %collective-permute-start.21 = (bf16[128,2048]{1,0:T(8,128)(2,1)}, bf16[128,2048]{1,0:T(8,128)(2,1)}, u32[]{:S(2)}, u32[]{:S(2)}) collective-permute-start(bf16[128,2048]{1,0:T(8,128)(2,1)} %collective-permute-done.17.refs_2_), channel_id=1, source_target_pairs={{0,32},{1,33},{2,34},{3,35},{4,36},{5,37},{6,38},{7,39},{8,40},{9,... | collective-permute-start | bytes 1572872 | tf_op jit(solution)/shard_map/ppermute | solution.py:29
  56.8 0.9 copy-start.6
  57.6 2.4 %collective-permute-start.22 = (bf16[128,2048]{1,0:T(8,128)(2,1)}, bf16[128,2048]{1,0:T(8,128)(2,1)}, u32[]{:S(2)}, u32[]{:S(2)}) collective-permute-start(bf16[128,2048]{1,0:T(8,128)(2,1)} %collective-permute-done.18.refs_3_), channel_id=1, source_target_pairs={{0,32},{1,33},{2,34},{3,35},{4,36},{5,37},{6,38},{7,39},{8,40},{9,... | collective-permute-start | bytes 1572872 | tf_op jit(solution)/shard_map/ppermute | solution.py:29
  60.0 1.2 copy-start.2
  61.3 1.0 copy-start.5
  62.3 1.0 copy-start.7
  63.3 12.3 %copy-start.3 = (bf16[256,2048]{1,0:T(8,128)(2,1)S(1)}, bf16[256,2048]{1,0:T(8,128)(2,1)}, u32[]{:S(2)}) copy-start(bf16[256,2048]{1,0:T(8,128)(2,1)} %copy-done.1) | copy-start | bytes 3145732
  69.4 19.5 %collective-permute-start.23 = (bf16[400,256]{1,0:T(8,128)(2,1)S(1)}, bf16[400,256]{1,0:T(8,128)(2,1)S(1)}, u32[]{:S(2)}, u32[]{:S(2)}) collective-permute-start(bf16[400,256]{1,0:T(8,128)(2,1)S(1)} %get-tuple-element.33), channel_id=1, source_target_pairs={{0,0},{1,1},{2,2},{3,3},{4,4},{5,5},{6,6},{7,7},{8,8},{9,9},{10,10... | collective-permute-start | bytes 614408 | tf_op jit(solution)/shard_map/ppermute | solution.py:29
  75.4 14.7 %collective-permute-start.24 = (bf16[400,256]{1,0:T(8,128)(2,1)S(1)}, bf16[400,256]{1,0:T(8,128)(2,1)S(1)}, u32[]{:S(2)}, u32[]{:S(2)}) collective-permute-start(bf16[400,256]{1,0:T(8,128)(2,1)S(1)} %get-tuple-element.34), channel_id=1, source_target_pairs={{0,32},{1,33},{2,34},{3,35},{4,36},{5,37},{6,38},{7,39},{8,40},{9,... | collective-permute-start | bytes 614408 | tf_op jit(solution)/shard_map/ppermute | solution.py:29
  84.4 35.9 %collective-permute-start.8 = (bf16[912,256]{1,0:T(8,128)(2,1)S(1)}, bf16[912,256]{1,0:T(8,128)(2,1)S(1)}, u32[]{:S(2)}, u32[]{:S(2)}) collective-permute-start(bf16[912,256]{1,0:T(8,128)(2,1)S(1)} %get-tuple-element.23), channel_id=1, source_target_pairs={{0,0},{1,1},{2,2},{3,3},{4,4},{5,5},{6,6},{7,7},{8,8},{9,9},{10,10... | collective-permute-start | bytes 1400840 | tf_op jit(solution)/shard_map/ppermute | solution.py:29
  86.4 34.0 %collective-permute-start.9 = (bf16[912,256]{1,0:T(8,128)(2,1)S(1)}, bf16[912,256]{1,0:T(8,128)(2,1)S(1)}, u32[]{:S(2)}, u32[]{:S(2)}) collective-permute-start(bf16[912,256]{1,0:T(8,128)(2,1)S(1)} %get-tuple-element.24), channel_id=1, source_target_pairs={{0,32},{1,33},{2,34},{3,35},{4,36},{5,37},{6,38},{7,39},{8,40},{9,... | collective-permute-start | bytes 1400840 | tf_op jit(solution)/shard_map/ppermute | solution.py:29
  86.4 34.6 %collective-permute-start.10 = (bf16[912,256]{1,0:T(8,128)(2,1)S(1)}, bf16[912,256]{1,0:T(8,128)(2,1)S(1)}, u32[]{:S(2)}, u32[]{:S(2)}) collective-permute-start(bf16[912,256]{1,0:T(8,128)(2,1)S(1)} %get-tuple-element.25), channel_id=1, source_target_pairs={{0,64},{1,65},{2,66},{3,67},{4,68},{5,69},{6,70},{7,71},{8,72},{9,... | collective-permute-start | bytes 1400840 | tf_op jit(solution)/shard_map/ppermute | solution.py:29
  88.9 32.1 %collective-permute-start.11 = (bf16[912,256]{1,0:T(8,128)(2,1)S(1)}, bf16[912,256]{1,0:T(8,128)(2,1)S(1)}, u32[]{:S(2)}, u32[]{:S(2)}) collective-permute-start(bf16[912,256]{1,0:T(8,128)(2,1)S(1)} %get-tuple-element.26), channel_id=1, source_target_pairs={{0,96},{1,97},{2,98},{3,99},{4,100},{5,101},{6,102},{7,103},{8,104... | collective-permute-start | bytes 1400840 | tf_op jit(solution)/shard_map/ppermute | solution.py:29
  90.1 22.3 %collective-permute-start.25 = (bf16[400,256]{1,0:T(8,128)(2,1)S(1)}, bf16[400,256]{1,0:T(8,128)(2,1)S(1)}, u32[]{:S(2)}, u32[]{:S(2)}) collective-permute-start(bf16[400,256]{1,0:T(8,128)(2,1)S(1)} %get-tuple-element.35), channel_id=1, source_target_pairs={{0,64},{1,65},{2,66},{3,67},{4,68},{5,69},{6,70},{7,71},{8,72},{9,... | collective-permute-start | bytes 614408 | tf_op jit(solution)/shard_map/ppermute | solution.py:29
  112.3 5.2 %collective-permute-start.26 = (bf16[400,256]{1,0:T(8,128)(2,1)S(1)}, bf16[400,256]{1,0:T(8,128)(2,1)S(1)}, u32[]{:S(2)}, u32[]{:S(2)}) collective-permute-start(bf16[400,256]{1,0:T(8,128)(2,1)S(1)} %get-tuple-element.36), channel_id=1, source_target_pairs={{0,96},{1,97},{2,98},{3,99},{4,100},{5,101},{6,102},{7,103},{8,104... | collective-permute-start | bytes 614408 | tf_op jit(solution)/shard_map/ppermute | solution.py:29
  118.2 9.0 %collective-permute-start.27 = (f32[1,128,256]{2,1,0:T(8,128)S(1)}, f32[1,128,256]{2,1,0:T(8,128)S(1)}, u32[]{:S(2)}, u32[]{:S(2)}) collective-permute-start(f32[1,128,256]{2,1,0:T(8,128)S(1)} %get-tuple-element.37), channel_id=1, source_target_pairs={{0,3},{1,0},{2,1},{3,2},{4,7},{5,4},{6,5},{7,6},{8,11},{9,8},{10,9... | collective-permute-start | bytes 393224 | tf_op jit(solution)/shard_map/ppermute | solution.py:29
  120.4 8.3 %collective-permute-start.28 = (f32[1,128,256]{2,1,0:T(8,128)S(1)}, f32[1,128,256]{2,1,0:T(8,128)S(1)}, u32[]{:S(2)}, u32[]{:S(2)}) collective-permute-start(f32[1,128,256]{2,1,0:T(8,128)S(1)} %get-tuple-element.38), channel_id=1, source_target_pairs={{0,12},{1,13},{2,14},{3,15},{4,0},{5,1},{6,2},{7,3},{8,4},{9,5},{1... | collective-permute-start | bytes 393224 | tf_op jit(solution)/shard_map/ppermute | solution.py:29
  120.4 11.8 %collective-permute-start.30 = (f32[2,128,256]{2,1,0:T(8,128)S(1)}, f32[2,128,256]{2,1,0:T(8,128)S(1)}, u32[]{:S(2)}, u32[]{:S(2)}) collective-permute-start(f32[2,128,256]{2,1,0:T(8,128)S(1)} %get-tuple-element.40), channel_id=1, source_target_pairs={{0,5},{1,6},{2,7},{3,4},{4,9},{5,10},{6,11},{7,8},{8,13},{9,14},{1... | collective-permute-start | bytes 786440 | tf_op jit(solution)/shard_map/ppermute | solution.py:29
  122.6 24.3 %collective-permute-start.15 = (f32[3,128,256]{2,1,0:T(8,128)S(1)}, f32[3,128,256]{2,1,0:T(8,128)S(1)}, u32[]{:S(2)}, u32[]{:S(2)}) collective-permute-start(f32[3,128,256]{2,1,0:T(8,128)S(1)} %get-tuple-element.31), channel_id=1, source_target_pairs={{0,1},{1,2},{2,3},{3,0},{4,5},{5,6},{6,7},{7,4},{8,9},{9,10},{10,1... | collective-permute-start | bytes 1179656 | tf_op jit(solution)/shard_map/ppermute | solution.py:29
  123.9 5.2 %collective-permute-start.29 = (f32[1,128,256]{2,1,0:T(8,128)S(1)}, f32[1,128,256]{2,1,0:T(8,128)S(1)}, u32[]{:S(2)}, u32[]{:S(2)}) collective-permute-start(f32[1,128,256]{2,1,0:T(8,128)S(1)} %get-tuple-element.39), channel_id=1, source_target_pairs={{0,15},{1,12},{2,13},{3,14},{4,3},{5,0},{6,1},{7,2},{8,7},{9,4},{1... | collective-permute-start | bytes 393224 | tf_op jit(solution)/shard_map/ppermute | solution.py:29
  127.2 7.2 %collective-permute-start.37 = (f32[1,128,256]{2,1,0:T(8,128)S(1)}, f32[1,128,256]{2,1,0:T(8,128)S(1)}, u32[]{:S(2)}, u32[]{:S(2)}) collective-permute-start(f32[1,128,256]{2,1,0:T(8,128)S(1)} %collective-permute-done.27.refs_6_), channel_id=1, source_target_pairs={{0,32},{1,33},{2,34},{3,35},{4,36},{5,37},{6,38},{7,39},{8,40},{9,... | collective-permute-start | bytes 393224 | tf_op jit(solution)/shard_map/ppermute | solution.py:29
  128.6 8.3 %collective-permute-start.38 = (f32[1,128,256]{2,1,0:T(8,128)S(1)}, f32[1,128,256]{2,1,0:T(8,128)S(1)}, u32[]{:S(2)}, u32[]{:S(2)}) collective-permute-start(f32[1,128,256]{2,1,0:T(8,128)S(1)} %collective-permute-done.28.refs_7_), channel_id=1, source_target_pairs={{0,32},{1,33},{2,34},{3,35},{4,36},{5,37},{6,38},{7,39},{8,40},{9,... | collective-permute-start | bytes 393224 | tf_op jit(solution)/shard_map/ppermute | solution.py:29
  129.1 7.8 %collective-permute-start.39 = (f32[1,128,256]{2,1,0:T(8,128)S(1)}, f32[1,128,256]{2,1,0:T(8,128)S(1)}, u32[]{:S(2)}, u32[]{:S(2)}) collective-permute-start(f32[1,128,256]{2,1,0:T(8,128)S(1)} %collective-permute-done.29.refs_8_), channel_id=1, source_target_pairs={{0,32},{1,33},{2,34},{3,35},{4,36},{5,37},{6,38},{7,39},{8,40},{9,... | collective-permute-start | bytes 393224 | tf_op jit(solution)/shard_map/ppermute | solution.py:29
  132.2 5.1 %collective-permute-start.12 = (f32[1,128,256]{2,1,0:T(8,128)S(1)}, f32[1,128,256]{2,1,0:T(8,128)S(1)}, u32[]{:S(2)}, u32[]{:S(2)}) collective-permute-start(f32[1,128,256]{2,1,0:T(8,128)S(1)} %get-tuple-element.28), channel_id=1, source_target_pairs={{0,3},{1,0},{2,1},{3,2},{4,7},{5,4},{6,5},{7,6},{8,11},{9,8},{10,9... | collective-permute-start | bytes 393224 | tf_op jit(solution)/shard_map/ppermute | solution.py:29
  134.4 13.0 %collective-permute-start.13 = (f32[2,128,256]{2,1,0:T(8,128)S(1)}, f32[2,128,256]{2,1,0:T(8,128)S(1)}, u32[]{:S(2)}, u32[]{:S(2)}) collective-permute-start(f32[2,128,256]{2,1,0:T(8,128)S(1)} %get-tuple-element.29), channel_id=1, source_target_pairs={{0,12},{1,13},{2,14},{3,15},{4,0},{5,1},{6,2},{7,3},{8,4},{9,5},{1... | collective-permute-start | bytes 786440 | tf_op jit(solution)/shard_map/ppermute | solution.py:29
  136.9 8.5 %collective-permute-start.14 = (f32[1,128,256]{2,1,0:T(8,128)S(1)}, f32[1,128,256]{2,1,0:T(8,128)S(1)}, u32[]{:S(2)}, u32[]{:S(2)}) collective-permute-start(f32[1,128,256]{2,1,0:T(8,128)S(1)} %get-tuple-element.30), channel_id=1, source_target_pairs={{0,4},{1,5},{2,6},{3,7},{4,8},{5,9},{6,10},{7,11},{8,12},{9,13},{1... | collective-permute-start | bytes 393224 | tf_op jit(solution)/shard_map/ppermute | solution.py:29
  136.9 9.9 %collective-permute-start.16 = (f32[1,128,256]{2,1,0:T(8,128)S(1)}, f32[1,128,256]{2,1,0:T(8,128)S(1)}, u32[]{:S(2)}, u32[]{:S(2)}) collective-permute-start(f32[1,128,256]{2,1,0:T(8,128)S(1)} %get-tuple-element.32), channel_id=1, source_target_pairs={{0,4},{1,5},{2,6},{3,7},{4,8},{5,9},{6,10},{7,11},{8,12},{9,13},{1... | collective-permute-start | bytes 393224 | tf_op jit(solution)/shard_map/ppermute | solution.py:29
  137.3 12.8 %collective-permute-start.31 = (f32[3,128,256]{2,1,0:T(8,128)S(1)}, f32[3,128,256]{2,1,0:T(8,128)S(1)}, u32[]{:S(2)}, u32[]{:S(2)}) collective-permute-start(f32[3,128,256]{2,1,0:T(8,128)S(1)} %get-tuple-element.27.refs_0_), channel_id=1, source_target_pairs={{0,32},{1,33},{2,34},{3,35},{4,36},{5,37},{6,38},{7,39},{8,40},{9,... | collective-permute-start | bytes 1179656 | tf_op jit(solution)/shard_map/ppermute | solution.py:29
  145.5 2.4 %collective-permute-start.32 = (f32[1,128,256]{2,1,0:T(8,128)S(1)}, f32[1,128,256]{2,1,0:T(8,128)S(1)}, u32[]{:S(2)}, u32[]{:S(2)}) collective-permute-start(f32[1,128,256]{2,1,0:T(8,128)S(1)} %collective-permute-done.12.refs_1_), channel_id=1, source_target_pairs={{0,32},{1,33},{2,34},{3,35},{4,36},{5,37},{6,38},{7,39},{8,40},{9,... | collective-permute-start | bytes 393224 | tf_op jit(solution)/shard_map/ppermute | solution.py:29
  146.9 3.3 %collective-permute-start.35 = (f32[3,128,256]{2,1,0:T(8,128)S(1)}, f32[3,128,256]{2,1,0:T(8,128)S(1)}, u32[]{:S(2)}, u32[]{:S(2)}) collective-permute-start(f32[3,128,256]{2,1,0:T(8,128)S(1)} %collective-permute-done.15.refs_4_), channel_id=1, source_target_pairs={{0,32},{1,33},{2,34},{3,35},{4,36},{5,37},{6,38},{7,39},{8,40},{9,... | collective-permute-start | bytes 1179656 | tf_op jit(solution)/shard_map/ppermute | solution.py:29
  146.9 1.9 %collective-permute-start.34 = (f32[1,128,256]{2,1,0:T(8,128)S(1)}, f32[1,128,256]{2,1,0:T(8,128)S(1)}, u32[]{:S(2)}, u32[]{:S(2)}) collective-permute-start(f32[1,128,256]{2,1,0:T(8,128)S(1)} %collective-permute-done.14.refs_3_), channel_id=1, source_target_pairs={{0,32},{1,33},{2,34},{3,35},{4,36},{5,37},{6,38},{7,39},{8,40},{9,... | collective-permute-start | bytes 393224 | tf_op jit(solution)/shard_map/ppermute | solution.py:29
  147.4 2.7 %collective-permute-start.40 = (f32[2,128,256]{2,1,0:T(8,128)S(1)}, f32[2,128,256]{2,1,0:T(8,128)S(1)}, u32[]{:S(2)}, u32[]{:S(2)}) collective-permute-start(f32[2,128,256]{2,1,0:T(8,128)S(1)} %collective-permute-done.30.refs_9_), channel_id=1, source_target_pairs={{0,32},{1,33},{2,34},{3,35},{4,36},{5,37},{6,38},{7,39},{8,40},{9,... | collective-permute-start | bytes 786440 | tf_op jit(solution)/shard_map/ppermute | solution.py:29
  147.9 2.3 %collective-permute-start.33 = (f32[2,128,256]{2,1,0:T(8,128)S(1)}, f32[2,128,256]{2,1,0:T(8,128)S(1)}, u32[]{:S(2)}, u32[]{:S(2)}) collective-permute-start(f32[2,128,256]{2,1,0:T(8,128)S(1)} %collective-permute-done.13.refs_2_), channel_id=1, source_target_pairs={{0,32},{1,33},{2,34},{3,35},{4,36},{5,37},{6,38},{7,39},{8,40},{9,... | collective-permute-start | bytes 786440 | tf_op jit(solution)/shard_map/ppermute | solution.py:29
  148.8 1.3 collective-permute-start.36
  (1 other events, 0.8 us)

commit v2 on v0

v2 whole, which is shorter than its diff:
```python
import functools
import math

import jax
import jax.numpy as jnp
from jax import lax
from jax.experimental import pallas as pl
from jax.experimental.pallas import tpu as pltpu
from jax.sharding import PartitionSpec as P

ORDER = 32
TOP = 2.0**3.9
FLOOR = 2.0**-3.9
VMEM = 20 << 20

DEVICES = [
    (x, z, yh, yl, c)
    for yl in range(2)
    for c in range(2)
    for yh in range(2)
    for z in range(4)
    for x in range(4)
]


def move(value, where):
    index = {d: i for i, d in enumerate(DEVICES)}
    pairs = [(index[d], index[where(*d)]) for d in DEVICES]
    return lax.ppermute(value, ("aux", "blk"), pairs)


def to_own_layer(x, z, yh, yl, c):
    return x, z, c, yl, yh


def to_core(x, z, yh, yl, c):
    return x, z, yh, yl, 1 - c


def to_position(dx, dz, swap=False):
    def where(x, z, yh, yl, c):
        x, z = (x + dx) % 4, (z + dz) % 4
        return (x, z, yl, yh, c) if swap else (x, z, yh, yl, c)

    return where


def to_owner(m1):
    def where(x, z, yh, yl, c):
        return x, z, c, yl ^ m1, yh

    return where


def product(a, b):
    return lax.dot_general(a, b, (((1,), (1,)), ((), ())), preferred_element_type=jnp.float32)


def encode(value, bound):
    v = jnp.abs(value) * (TOP / bound) + FLOOR
    for _ in range(int(math.log2(ORDER))):
        v = v * v
    return jnp.where(value < 0, -v, v).astype(jnp.bfloat16)


def decode(code, bound):
    y = code.astype(jnp.float32)
    v = jnp.exp(jnp.log(jnp.abs(y)) * (1.0 / ORDER)) - FLOOR
    return jnp.where(y < 0, -v, v) * (bound * (1.0 / TOP))


def bound_of(top, width):
    rows = jnp.full((16, width), jnp.maximum(top, 1e-30) * 1.008, jnp.float32)
    return rows.astype(jnp.bfloat16).astype(jnp.float32)


def coded_shape(count, rows):
    return jax.ShapeDtypeStruct((count * rows + 16, rows), jnp.bfloat16)


def tile_of(ref, k):
    rows = ref.shape[1]
    bound = ref[ref.shape[0] - 16 :, :].astype(jnp.float32)[k : k + 1, :]
    return decode(ref[k * rows : (k + 1) * rows, :], bound)


def call(kernel, args, out_shape, scratch=(), any_from=None, flops=0, moved=0, transcendentals=0):
    whole = pl.BlockSpec(memory_space=pltpu.VMEM)
    specs = []
    for i, a in enumerate(args):
        if a.dtype == jnp.int32:
            specs.append(pl.BlockSpec(memory_space=pltpu.SMEM))
        else:
            specs.append(pl.BlockSpec(memory_space=pl.ANY) if any_from is not None and i >= any_from else whole)
    many = isinstance(out_shape, (list, tuple))
    return pl.pallas_call(
        kernel,
        out_shape=out_shape,
        in_specs=specs,
        out_specs=[whole] * len(out_shape) if many else whole,
        scratch_shapes=scratch,
        compiler_params=pltpu.CompilerParams(vmem_limit_bytes=VMEM),
        cost_estimate=pl.CostEstimate(flops=flops, bytes_accessed=moved, transcendentals=transcendentals),
    )(*args)


def tiles_kernel(classes, n_in, n_extra, place, *refs):
    ins = refs[:n_in]
    outs, (held, acc, sems) = refs[n_in + n_extra : n_in + n_extra + 2], refs[n_in + n_extra + 2 :]
    yl, c = place[1], place[2]
    rows = acc.shape[1]
    copies = [pltpu.make_async_copy(r, held.at[i], sems.at[i]) for i, r in enumerate(ins)]
    for copy in copies:
        copy.start()
    ready = set()
    row = lax.broadcasted_iota(jnp.int32, (16, rows), 0)
    bounds = jnp.zeros((16, rows), jnp.float32)
    for k, (r, own, other) in enumerate(classes):
        for i in (r, own, other):
            if i not in ready:
                copies[i].wait()
                ready.add(i)
        acc[c] = product(held[r], held[own])
        acc[1 - c] = product(held[r], held[other])
        coded = bound_of(jnp.max(jnp.abs(acc[...])), rows)
        bounds = jnp.where(row == k, coded, bounds)
        for m1, out in enumerate(outs):
            out[k * rows : (k + 1) * rows, :] = encode(acc[yl ^ m1], coded[0:1, :])
    for out in outs:
        out[len(classes) * rows :, :] = bounds.astype(jnp.bfloat16)


def partial_tiles(place, blocks, classes, rows, after=()):
    names = list(blocks)
    listed = tuple(tuple(names.index(n) for n in k) for k in classes)
    arrays = list(blocks.values())
    depth = arrays[0].shape[1]
    return call(
        functools.partial(tiles_kernel, listed, len(arrays), len(after)),
        [place, *arrays, *after],
        [coded_shape(len(classes), rows)] * 2,
        scratch=[
            pltpu.VMEM((len(arrays), rows, depth), jnp.bfloat16),
            pltpu.VMEM((2, rows, rows), jnp.float32),
            pltpu.SemaphoreType.DMA((len(arrays),)),
        ],
        any_from=1,
        flops=len(classes) * 4 * rows * rows * depth,
        moved=len(arrays) * rows * depth * 2,
    )


def sum_kernel(a, b, out):
    for k in range(out.shape[0]):
        out[k, :, :] = tile_of(a, k) + tile_of(b, k)


def group_kernel(groups, coded, a, b, *outs):
    rows = a.shape[1]
    row = lax.broadcasted_iota(jnp.int32, (16, rows), 0)
    bounds = [jnp.zeros((16, rows), jnp.float32) for _ in groups]
    for k in range(a.shape[0]):
        total = a[k, :, :] + b[k, :, :]
        bound = bound_of(jnp.max(jnp.abs(total)), rows)
        code = encode(total, bound[0:1, :]) if any(k in g and s for g, s in zip(groups, coded)) else None
        for j, (out, members) in enumerate(zip(outs, groups)):
            for i, member in enumerate(members):
                if member == k and coded[j]:
                    out[i * rows : (i + 1) * rows, :] = code
                    bounds[j] = jnp.where(row == i, bound, bounds[j])
                elif member == k:
                    out[i, :, :] = total
    for out, send, rows_of in zip(outs, coded, bounds):
        if send:
            out[out.shape[0] - 16 :, :] = rows_of.astype(jnp.bfloat16)


def grouped(mine, others, sends, rows):
    groups = tuple(members for _, _, members in sends)
    coded = tuple(to != O for to, _, _ in sends)
    return call(
        functools.partial(group_kernel, groups, coded),
        [mine, others],
        [
            coded_shape(len(g), rows) if s else jax.ShapeDtypeStruct((len(g), rows, rows), jnp.float32)
            for g, s in zip(groups, coded)
        ],
        moved=4 << 20,
    )


def place_kernel(tiles, place, *refs):
    ins, out = refs[:-1], refs[-1]
    c, z, x = place[2], place[3], place[4]
    rows = out.shape[0]
    for array, i, (dx, dz), turned in tiles:
        zz = (z + dz) % 4
        xx = (x + dx) % 4
        ref = ins[array]

        @pl.when(zz // 2 == c)
        def _():
            tile = ref[i, :, :] if ref.dtype == jnp.float32 else tile_of(ref, i)
            start = pl.multiple_of(((zz % 2) * 4 + xx) * rows, rows)
            out[:, pl.ds(start, rows)] = tile.T if turned else tile


O, PX, MX, PZ, MZ, F = (0, 0), (1, 0), (3, 0), (0, 1), (0, 3), (2, 2)
EARLY = ((O, O), (O, PX), (O, PZ), (MX, PX), (MZ, PZ), (MZ, PX), (PZ, PX))
LATE = ((O, F), (PX, F), (PZ, F))
EARLY_SENDS = (
    (O, False, (0, 1, 2)),
    (PX, True, (1, 3, 5, 6)),
    (PZ, True, (2, 4)),
    (MZ, False, (5,)),
    (PZ, False, (6,)),
)
LATE_SENDS = (
    (O, False, (0,)),
    (F, True, (1, 2)),
    (PX, False, (1,)),
    (PZ, False, (2,)),
)


def minus(a, b):
    return (a[0] - b[0]) % 4, (a[1] - b[1]) % 4


def local(b_factors):
    rows = b_factors.shape[0]
    flat = b_factors.reshape(rows, -1)
    aux, blk = lax.axis_index("aux"), lax.axis_index("blk")
    place = jnp.stack([blk // 16, aux // 2, aux % 2, (blk // 4) % 4, blk % 4]).astype(jnp.int32)

    own = {O: move(flat, to_own_layer)}
    for o in (PX, MX, PZ, MZ, F):
        own[o] = move(own[O], to_position(-o[0], -o[1]))
    other = {o: move(own[o], to_core) for o in (O, PX, PZ, F)}

    parts, tiles, after = [], [], ()
    for classes, sends in ((EARLY, EARLY_SENDS), (LATE, LATE_SENDS)):
        blocks = {}
        for r, q in classes:
            blocks |= {("own", r): own[r], ("own", q): own[q], ("other", q): other[q]}
        listed = [(("own", r), ("own", q), ("other", q)) for r, q in classes]
        coded = partial_tiles(place, blocks, listed, rows, after)
        after = (coded[0],)
        arrived = [move(v, to_owner(m1)) for m1, v in enumerate(coded)]
        mine = call(
            sum_kernel,
            arrived,
            jax.ShapeDtypeStruct((len(classes), rows, rows), jnp.float32),
            moved=4 << 20,
            transcendentals=1 << 21,
        )
        groups = grouped(mine, move(mine, to_core), sends, rows)
        for g, (to, turned, members) in zip(groups, sends):
            for i, k in enumerate(members):
                r, q = classes[k]
                tiles.append((len(parts), i, minus(r, q) if turned else minus(q, r), turned))
            parts.append(g if to == O else move(g, to_position(*to, swap=turned)))
    return call(
        functools.partial(place_kernel, tuple(tiles)),
        [place, *parts],
        jax.ShapeDtypeStruct((rows, 8 * rows), jnp.float32),
        moved=6 << 20,
        transcendentals=1 << 20,
    )


def solution(mesh):
    return jax.shard_map(
        local, mesh=mesh, in_specs=(P("blk", "aux", None),), out_specs=P("blk", "aux"), check_vma=False
    )
```

time: 375 us -> 171 us (0.46)
  waiting for transfers between devices: 338 us -> 111 us
  starting transfers between devices: 0.04 us -> 35.3 us
  Pallas kernels: 0 us -> 20.4 us
  matrix products: 18.5 us -> 0 us
  between operations: 13.4 us -> 0.15 us
    all_gather x1 -> x0, waiting for transfers between devices: 261 us -> none  [local(): piece = lax.all_gather(b_factors, 'blk', axis=0, tiled=True)]
    ppermute x0 -> x23, waiting for transfers between devices: none -> 111 us  [move(): return lax.ppermute(value, ('aux', 'blk'), pairs)]
    reduce_scatter x1 -> x0, waiting for transfers between devices: 77.2 us -> none  [local(): lax.psum_scatter(partial_value, 'aux', scatter_dimension=1, tiled=True)]
    ppermute x0 -> x23, starting transfers between devices: none -> 35.3 us  [move(): return lax.ppermute(value, ('aux', 'blk'), pairs)]
    pallas_call x0 -> x7, Pallas kernels: none -> 20.4 us  [call(): pl.pallas_call(kernel, out_shape=out_shape, in_specs=specs, out_specs=[wh...]
    dot_general x1 -> x0, matrix products: 18.5 us -> none  [local(): partial_value = jnp.dot(flat, other.T, preferred_element_type=jnp.float32)]
  transfers between devices with their start and end apart: 2 -> 23, of which waited for: 2 -> 12; matrix products, arithmetic and copies ran while one was open for 0% -> 0% of each run, Pallas kernels for 0% -> 10%
where the time goes in v2:
time: 171 us; the launch traced here: 170 us
  waiting for transfers between devices  111 us (65%)
  starting transfers between devices  35.3 us (21%)
  Pallas kernels  20.4 us (12%)
  local copies, waits for them, and re-layouts  3.77 us (2%)
    ppermute x23, waiting for transfers between devices, move(): return lax.ppermute(value, ('aux', 'blk'), pairs)  111 us
    ppermute x23, starting transfers between devices, move(): return lax.ppermute(value, ('aux', 'blk'), pairs)  35.3 us
    pallas_call x7, Pallas kernels, call(): pl.pallas_call(kernel, out_shape=out_shape, in_specs=specs, out_specs=[wh...  20.4 us
    unnamed x5, local copies, waits for them, and re-layouts  3.69 us
  transfers between devices with their start and end apart: 23, of which 12 were waited for; matrix products, arithmetic and copies ran while one was open for 0% of the time, Pallas kernels for 10%

profile of v2, /device:TPU:9, one launch (start us, length us, event | category | flops | bytes accessed | tf_op | source)
XLA Modules:
  0.0 170.2 jit_solution(1252325894569361138)
XLA Ops:
  0.0 1.5 copy.4
  1.5 4.5 %collective-permute-start = (bf16[256,2048]{1,0:T(8,128)(2,1)S(1)}, bf16[256,2048]{1,0:T(8,128)(2,1)S(1)}, u32[]{:S(2)}, u32[]{:S(2)}) collective-permute-start(bf16[256,2048]{1,0:T(8,128)(2,1)S(1)} %bitcast.10), channel_id=1, source_target_pairs={{0,0},{1,1},{2,2},{3,3},{4,4},{5,5},{6,6},{7,7},{8,8},{9,9},{10,10... | collective-permute-start | bytes 3145736 | tf_op jit(solution)/shard_map/ppermute | solution.py:29
  6.0 13.1 %collective-permute-done.refs_0_ = bf16[256,2048]{1,0:T(8,128)(2,1)S(1)} collective-permute-done((bf16[256,2048]{1,0:T(8,128)(2,1)S(1)}, bf16[256,2048]{1,0:T(8,128)(2,1)S(1)}, u32[]{:S(2)}, u32[]{:S(2)}) %collective-permute-start) | collective-permute-done | bytes 1048608 | tf_op jit(solution)/shard_map/ppermute | solution.py:29
  19.1 2.5 %collective-permute-start.2 = (bf16[256,2048]{1,0:T(8,128)(2,1)S(1)}, bf16[256,2048]{1,0:T(8,128)(2,1)S(1)}, u32[]{:S(2)}, u32[]{:S(2)}) collective-permute-start(bf16[256,2048]{1,0:T(8,128)(2,1)S(1)} %collective-permute-done.refs_0_), channel_id=1, source_target_pairs={{0,3},{1,0},{2,1},{3,2},{4,7},{5,4},{6,5},{7,6},{8,11},{9,8},{10,9... | collective-permute-start | bytes 3145736 | tf_op jit(solution)/shard_map/ppermute | solution.py:29
  21.6 4.1 %collective-permute-start.4 = (bf16[256,2048]{1,0:T(8,128)(2,1)S(1)}, bf16[256,2048]{1,0:T(8,128)(2,1)S(1)}, u32[]{:S(2)}, u32[]{:S(2)}) collective-permute-start(bf16[256,2048]{1,0:T(8,128)(2,1)S(1)} %collective-permute-done.refs_0_), channel_id=1, source_target_pairs={{0,12},{1,13},{2,14},{3,15},{4,0},{5,1},{6,2},{7,3},{8,4},{9,5},{1... | collective-permute-start | bytes 3145736 | tf_op jit(solution)/shard_map/ppermute | solution.py:29
  25.7 0.0 collective-permute-start.6
  25.7 0.0 collective-permute-start.7
  25.7 7.7 %collective-permute-done.2.refs_2_.refs_3_ = bf16[256,2048]{1,0:T(8,128)(2,1)S(1)} collective-permute-done((bf16[256,2048]{1,0:T(8,128)(2,1)S(1)}, bf16[256,2048]{1,0:T(8,128)(2,1)S(1)}, u32[]{:S(2)}, u32[]{:S(2)}) %collective-permute-start.2) | collective-permute-done | bytes 1048608 | tf_op jit(solution)/shard_map/ppermute | solution.py:29
  33.3 4.0 %collective-permute-done.4.refs_4_ = bf16[256,2048]{1,0:T(8,128)(2,1)S(1)} collective-permute-done((bf16[256,2048]{1,0:T(8,128)(2,1)S(1)}, bf16[256,2048]{1,0:T(8,128)(2,1)S(1)}, u32[]{:S(2)}, u32[]{:S(2)}) %collective-permute-start.4) | collective-permute-done | bytes 1048608 | tf_op jit(solution)/shard_map/ppermute | solution.py:29
  37.4 0.0 collective-permute-start.5
  37.4 0.0 collective-permute-done.1.refs_1_
  37.4 1.0 copy-done
  38.4 2.3 %collective-permute-start.15 = (bf16[256,2048]{1,0:T(8,128)(2,1)S(1)}, bf16[256,2048]{1,0:T(8,128)(2,1)}, u32[]{:S(2)}, u32[]{:S(2)}) collective-permute-start(bf16[256,2048]{1,0:T(8,128)(2,1)S(1)} %collective-permute-done.refs_0_), channel_id=1, source_target_pairs={{0,10},{1,11},{2,8},{3,9},{4,14},{5,15},{6,12},{7,13},{8,2},{9,3},... | collective-permute-start | bytes 3145736 | tf_op jit(solution)/shard_map/ppermute | solution.py:29
  40.7 0.1 stack.23.place
  40.8 32.9 %collective-permute-done.6.refs_6_ = bf16[256,2048]{1,0:T(8,128)(2,1)} collective-permute-done((bf16[256,2048]{1,0:T(8,128)(2,1)S(1)}, bf16[256,2048]{1,0:T(8,128)(2,1)}, u32[]{:S(2)}, u32[]{:S(2)}) %collective-permute-start.6) | collective-permute-done | bytes 1048608 | tf_op jit(solution)/shard_map/ppermute | solution.py:29
  73.7 0.0 collective-permute-done.7.refs_7_
  73.7 0.0 collective-permute-done.3.refs_3_
  73.7 0.0 collective-permute-done.5.refs_5_
  73.7 0.0 copy-start.1
  73.7 1.2 copy-done.1
  74.9 8.4 %shard_map.17 = (bf16[1808,256]{1,0:T(8,128)(2,1)S(1)}, bf16[1808,256]{1,0:T(8,128)(2,1)S(1)}) custom-call(s32[5]{0:T(128)S(1)} %stack.23.place, bf16[256,2048]{1,0:T(8,128)(2,1)S(1)} %collective-permute-done.refs_0_, bf16[256,2048]{1,0:T(8,128)(2,1)S(1)} %copy-done.1, bf16[256,2048]{1,0:T(8,128)(2,1)S(1)} %collective-permute-done.2.refs_2_.refs_3_, ...), custom_call_target="tpu_custom_call" | custom-call | flops 3758096384 | bytes 8388608 | tf_op jit(solution)/shard_map/pallas_call | solution.py:96
  83.3 6.1 %collective-permute-start.8 = (bf16[1808,256]{1,0:T(8,128)(2,1)S(1)}, bf16[1808,256]{1,0:T(8,128)(2,1)S(1)}, u32[]{:S(2)}, u32[]{:S(2)}) collective-permute-start(bf16[1808,256]{1,0:T(8,128)(2,1)S(1)} %get-tuple-element.18.refs_5_), channel_id=1, source_target_pairs={{0,0},{1,1},{2,2},{3,3},{4,4},{5,5},{6,6},{7,7},{8,8},{9,9},{10,10... | collective-permute-start | bytes 2777096 | tf_op jit(solution)/shard_map/ppermute | solution.py:29
  89.4 0.1 collective-permute-start.9
  89.5 0.1 collective-permute-start.16
  89.6 19.4 %collective-permute-done.8.a = bf16[1808,256]{1,0:T(8,128)(2,1)S(1)} collective-permute-done((bf16[1808,256]{1,0:T(8,128)(2,1)S(1)}, bf16[1808,256]{1,0:T(8,128)(2,1)S(1)}, u32[]{:S(2)}, u32[]{:S(2)}) %collective-permute-start.8) | collective-permute-done | bytes 925728 | tf_op jit(solution)/shard_map/ppermute | solution.py:29
  109.0 2.4 %collective-permute-done.9.b = bf16[1808,256]{1,0:T(8,128)(2,1)S(1)} collective-permute-done((bf16[1808,256]{1,0:T(8,128)(2,1)S(1)}, bf16[1808,256]{1,0:T(8,128)(2,1)S(1)}, u32[]{:S(2)}, u32[]{:S(2)}) %collective-permute-start.9) | collective-permute-done | bytes 925728 | tf_op jit(solution)/shard_map/ppermute | solution.py:29
  111.4 1.5 shard_map.18.a
  113.0 0.3 collective-permute-start.10
  113.2 0.0 collective-permute-done.16.refs_2_
  113.2 5.4 %shard_map.20 = (bf16[784,256]{1,0:T(8,128)(2,1)S(1)}, bf16[784,256]{1,0:T(8,128)(2,1)S(1)}) custom-call(s32[5]{0:T(128)S(1)} %stack.23.place, bf16[256,2048]{1,0:T(8,128)(2,1)S(1)} %collective-permute-done.refs_0_, bf16[256,2048]{1,0:T(8,128)(2,1)} %collective-permute-done.15.refs_1_, bf16[256,2048]{1,0:T(8,128)(2,1)S(1)} %collective-permute-done.16.refs_2_, ...), custom_call_target="tpu_custom_call" | custom-call | flops 1610612736 | bytes 5242880 | tf_op jit(solution)/shard_map/pallas_call | solution.py:96
  118.6 4.2 %collective-permute-start.17 = (bf16[784,256]{1,0:T(8,128)(2,1)S(1)}, bf16[784,256]{1,0:T(8,128)(2,1)S(1)}, u32[]{:S(2)}, u32[]{:S(2)}) collective-permute-start(bf16[784,256]{1,0:T(8,128)(2,1)S(1)} %get-tuple-element.25), channel_id=1, source_target_pairs={{0,0},{1,1},{2,2},{3,3},{4,4},{5,5},{6,6},{7,7},{8,8},{9,9},{10,10... | collective-permute-start | bytes 1204232 | tf_op jit(solution)/shard_map/ppermute | solution.py:29
  122.8 0.9 collective-permute-start.18
  123.7 7.7 %collective-permute-done.17.a = bf16[784,256]{1,0:T(8,128)(2,1)S(1)} collective-permute-done((bf16[784,256]{1,0:T(8,128)(2,1)S(1)}, bf16[784,256]{1,0:T(8,128)(2,1)S(1)}, u32[]{:S(2)}, u32[]{:S(2)}) %collective-permute-start.17) | collective-permute-done | bytes 401440 | tf_op jit(solution)/shard_map/ppermute | solution.py:29
  131.4 2.6 %collective-permute-done.18.b = bf16[784,256]{1,0:T(8,128)(2,1)S(1)} collective-permute-done((bf16[784,256]{1,0:T(8,128)(2,1)S(1)}, bf16[784,256]{1,0:T(8,128)(2,1)S(1)}, u32[]{:S(2)}, u32[]{:S(2)}) %collective-permute-start.18) | collective-permute-done | bytes 401440 | tf_op jit(solution)/shard_map/ppermute | solution.py:29
  134.1 0.6 shard_map.21.a
  134.7 0.1 collective-permute-start.19
  134.8 1.0 shard_map.19
  135.9 0.9 collective-permute-start.11
  136.8 0.3 collective-permute-done.19.b
  137.1 0.4 shard_map.22
  137.5 1.0 collective-permute-start.21
  138.5 3.7 %collective-permute-start.20 = (bf16[528,256]{1,0:T(8,128)(2,1)S(1)}, bf16[528,256]{1,0:T(8,128)(2,1)S(1)}, u32[]{:S(2)}, u32[]{:S(2)}) collective-permute-start(bf16[528,256]{1,0:T(8,128)(2,1)S(1)} %get-tuple-element.28), channel_id=1, source_target_pairs={{0,10},{1,11},{2,8},{3,9},{4,14},{5,15},{6,12},{7,13},{8,2},{9,3},... | collective-permute-start | bytes 811016 | tf_op jit(solution)/shard_map/ppermute | solution.py:29
  142.2 3.1 %collective-permute-start.12 = (bf16[528,256]{1,0:T(8,128)(2,1)S(1)}, bf16[528,256]{1,0:T(8,128)(2,1)S(1)}, u32[]{:S(2)}, u32[]{:S(2)}) collective-permute-start(bf16[528,256]{1,0:T(8,128)(2,1)S(1)} %get-tuple-element.22), channel_id=1, source_target_pairs={{0,4},{1,5},{2,6},{3,7},{4,8},{5,9},{6,10},{7,11},{8,12},{9,13},{1... | collective-permute-start | bytes 811016 | tf_op jit(solution)/shard_map/ppermute | solution.py:29
  145.3 11.4 %collective-permute-done.21.refs_7_ = bf16[272,256]{1,0:T(8,128)(2,1)S(1)} collective-permute-done((bf16[272,256]{1,0:T(8,128)(2,1)S(1)}, bf16[272,256]{1,0:T(8,128)(2,1)S(1)}, u32[]{:S(2)}, u32[]{:S(2)}) %collective-permute-start.21) | collective-permute-done | bytes 139296 | tf_op jit(solution)/shard_map/ppermute | solution.py:29
  156.7 1.5 collective-permute-start.14
  158.2 4.6 %collective-permute-done.20.refs_6_ = bf16[528,256]{1,0:T(8,128)(2,1)S(1)} collective-permute-done((bf16[528,256]{1,0:T(8,128)(2,1)S(1)}, bf16[528,256]{1,0:T(8,128)(2,1)S(1)}, u32[]{:S(2)}, u32[]{:S(2)}) %collective-permute-start.20) | collective-permute-done | bytes 270368 | tf_op jit(solution)/shard_map/ppermute | solution.py:29
  162.7 4.4 %collective-permute-done.13.refs_3_ = bf16[272,256]{1,0:T(8,128)(2,1)S(1)} collective-permute-done((bf16[272,256]{1,0:T(8,128)(2,1)S(1)}, bf16[272,256]{1,0:T(8,128)(2,1)S(1)}, u32[]{:S(2)}, u32[]{:S(2)}) %collective-permute-start.13) | collective-permute-done | bytes 139296 | tf_op jit(solution)/shard_map/ppermute | solution.py:29
  167.2 3.1 %shard_map.23 = f32[256,2048]{1,0:T(8,128)} custom-call(s32[5]{0:T(128)S(1)} %stack.23.place, f32[3,256,256]{2,1,0:T(8,128)S(1)} %get-tuple-element.20.refs_0_, bf16[1040,256]{1,0:T(8,128)(2,1)S(1)} %collective-permute-done.11.refs_1_, bf16[528,256]{1,0:T(8,128)(2,1)S(1)} %collective-permute-done.12.refs_2_, ...), custom_call_target="tpu_custom_call" | custom-call | bytes 6291456 | tf_op jit(solution)/shard_map/pallas_call | solution.py:96
  (11 shorter events, 0.0 us)
Async XLA Ops:
  1.5 17.6 %collective-permute-start = (bf16[256,2048]{1,0:T(8,128)(2,1)S(1)}, bf16[256,2048]{1,0:T(8,128)(2,1)S(1)}, u32[]{:S(2)}, u32[]{:S(2)}) collective-permute-start(bf16[256,2048]{1,0:T(8,128)(2,1)S(1)} %bitcast.10), channel_id=1, source_target_pairs={{0,0},{1,1},{2,2},{3,3},{4,4},{5,5},{6,6},{7,7},{8,8},{9,9},{10,10... | collective-permute-start | bytes 3145736 | tf_op jit(solution)/shard_map/ppermute | solution.py:29
  19.1 14.2 %collective-permute-start.2 = (bf16[256,2048]{1,0:T(8,128)(2,1)S(1)}, bf16[256,2048]{1,0:T(8,128)(2,1)S(1)}, u32[]{:S(2)}, u32[]{:S(2)}) collective-permute-start(bf16[256,2048]{1,0:T(8,128)(2,1)S(1)} %collective-permute-done.refs_0_), channel_id=1, source_target_pairs={{0,3},{1,0},{2,1},{3,2},{4,7},{5,4},{6,5},{7,6},{8,11},{9,8},{10,9... | collective-permute-start | bytes 3145736 | tf_op jit(solution)/shard_map/ppermute | solution.py:29
  21.6 15.8 %collective-permute-start.4 = (bf16[256,2048]{1,0:T(8,128)(2,1)S(1)}, bf16[256,2048]{1,0:T(8,128)(2,1)S(1)}, u32[]{:S(2)}, u32[]{:S(2)}) collective-permute-start(bf16[256,2048]{1,0:T(8,128)(2,1)S(1)} %collective-permute-done.refs_0_), channel_id=1, source_target_pairs={{0,12},{1,13},{2,14},{3,15},{4,0},{5,1},{6,2},{7,3},{8,4},{9,5},{1... | collective-permute-start | bytes 3145736 | tf_op jit(solution)/shard_map/ppermute | solution.py:29
  25.7 11.8 %collective-permute-start.1 = (bf16[256,2048]{1,0:T(8,128)(2,1)S(1)}, bf16[256,2048]{1,0:T(8,128)(2,1)S(1)}, u32[]{:S(2)}, u32[]{:S(2)}) collective-permute-start(bf16[256,2048]{1,0:T(8,128)(2,1)S(1)} %collective-permute-done.refs_0_), channel_id=1, source_target_pairs={{0,32},{1,33},{2,34},{3,35},{4,36},{5,37},{6,38},{7,39},{8,40},{9,... | collective-permute-start | bytes 3145736 | tf_op jit(solution)/shard_map/ppermute | solution.py:29
  25.7 48.0 %collective-permute-start.6 = (bf16[256,2048]{1,0:T(8,128)(2,1)S(1)}, bf16[256,2048]{1,0:T(8,128)(2,1)}, u32[]{:S(2)}, u32[]{:S(2)}) collective-permute-start(bf16[256,2048]{1,0:T(8,128)(2,1)S(1)} %collective-permute-done.refs_0_), channel_id=1, source_target_pairs={{0,1},{1,2},{2,3},{3,0},{4,5},{5,6},{6,7},{7,4},{8,9},{9,10},{10,1... | collective-permute-start | bytes 3145736 | tf_op jit(solution)/shard_map/ppermute | solution.py:29
  25.7 48.0 %collective-permute-start.7 = (bf16[256,2048]{1,0:T(8,128)(2,1)S(1)}, bf16[256,2048]{1,0:T(8,128)(2,1)}, u32[]{:S(2)}, u32[]{:S(2)}) collective-permute-start(bf16[256,2048]{1,0:T(8,128)(2,1)S(1)} %collective-permute-done.refs_0_), channel_id=1, source_target_pairs={{0,4},{1,5},{2,6},{3,7},{4,8},{5,9},{6,10},{7,11},{8,12},{9,13},{1... | collective-permute-start | bytes 3145736 | tf_op jit(solution)/shard_map/ppermute | solution.py:29
  33.3 40.3 %collective-permute-start.3 = (bf16[256,2048]{1,0:T(8,128)(2,1)S(1)}, bf16[256,2048]{1,0:T(8,128)(2,1)}, u32[]{:S(2)}, u32[]{:S(2)}) collective-permute-start(bf16[256,2048]{1,0:T(8,128)(2,1)S(1)} %collective-permute-done.2.refs_2_.refs_3_), channel_id=1, source_target_pairs={{0,32},{1,33},{2,34},{3,35},{4,36},{5,37},{6,38},{7,39},{8,40},{9,... | collective-permute-start | bytes 3145736 | tf_op jit(solution)/shard_map/ppermute | solution.py:29
  37.4 36.3 %collective-permute-start.5 = (bf16[256,2048]{1,0:T(8,128)(2,1)S(1)}, bf16[256,2048]{1,0:T(8,128)(2,1)}, u32[]{:S(2)}, u32[]{:S(2)}) collective-permute-start(bf16[256,2048]{1,0:T(8,128)(2,1)S(1)} %collective-permute-done.4.refs_4_), channel_id=1, source_target_pairs={{0,32},{1,33},{2,34},{3,35},{4,36},{5,37},{6,38},{7,39},{8,40},{9,... | collective-permute-start | bytes 3145736 | tf_op jit(solution)/shard_map/ppermute | solution.py:29
  37.4 1.0 copy-start
  38.4 51.1 %collective-permute-start.15 = (bf16[256,2048]{1,0:T(8,128)(2,1)S(1)}, bf16[256,2048]{1,0:T(8,128)(2,1)}, u32[]{:S(2)}, u32[]{:S(2)}) collective-permute-start(bf16[256,2048]{1,0:T(8,128)(2,1)S(1)} %collective-permute-done.refs_0_), channel_id=1, source_target_pairs={{0,10},{1,11},{2,8},{3,9},{4,14},{5,15},{6,12},{7,13},{8,2},{9,3},... | collective-permute-start | bytes 3145736 | tf_op jit(solution)/shard_map/ppermute | solution.py:29
  73.7 1.2 copy-start.1
  83.3 25.7 %collective-permute-start.8 = (bf16[1808,256]{1,0:T(8,128)(2,1)S(1)}, bf16[1808,256]{1,0:T(8,128)(2,1)S(1)}, u32[]{:S(2)}, u32[]{:S(2)}) collective-permute-start(bf16[1808,256]{1,0:T(8,128)(2,1)S(1)} %get-tuple-element.18.refs_5_), channel_id=1, source_target_pairs={{0,0},{1,1},{2,2},{3,3},{4,4},{5,5},{6,6},{7,7},{8,8},{9,9},{10,10... | collective-permute-start | bytes 2777096 | tf_op jit(solution)/shard_map/ppermute | solution.py:29
  89.4 22.0 %collective-permute-start.9 = (bf16[1808,256]{1,0:T(8,128)(2,1)S(1)}, bf16[1808,256]{1,0:T(8,128)(2,1)S(1)}, u32[]{:S(2)}, u32[]{:S(2)}) collective-permute-start(bf16[1808,256]{1,0:T(8,128)(2,1)S(1)} %get-tuple-element.19), channel_id=1, source_target_pairs={{0,64},{1,65},{2,66},{3,67},{4,68},{5,69},{6,70},{7,71},{8,72},{9,... | collective-permute-start | bytes 2777096 | tf_op jit(solution)/shard_map/ppermute | solution.py:29
  89.5 23.7 %collective-permute-start.16 = (bf16[256,2048]{1,0:T(8,128)(2,1)}, bf16[256,2048]{1,0:T(8,128)(2,1)S(1)}, u32[]{:S(2)}, u32[]{:S(2)}) collective-permute-start(bf16[256,2048]{1,0:T(8,128)(2,1)} %collective-permute-done.15.refs_1_), channel_id=1, source_target_pairs={{0,32},{1,33},{2,34},{3,35},{4,36},{5,37},{6,38},{7,39},{8,40},{9,... | collective-permute-start | bytes 3145736 | tf_op jit(solution)/shard_map/ppermute | solution.py:29
  113.0 21.9 %collective-permute-start.10 = (f32[7,256,256]{2,1,0:T(8,128)S(1)}, f32[7,256,256]{2,1,0:T(8,128)S(1)}, u32[]{:S(2)}, u32[]{:S(2)}) collective-permute-start(f32[7,256,256]{2,1,0:T(8,128)S(1)} %shard_map.18.a), channel_id=1, source_target_pairs={{0,32},{1,33},{2,34},{3,35},{4,36},{5,37},{6,38},{7,39},{8,40},{9,... | collective-permute-start | bytes 5505032 | tf_op jit(solution)/shard_map/ppermute | solution.py:29
  118.6 12.8 %collective-permute-start.17 = (bf16[784,256]{1,0:T(8,128)(2,1)S(1)}, bf16[784,256]{1,0:T(8,128)(2,1)S(1)}, u32[]{:S(2)}, u32[]{:S(2)}) collective-permute-start(bf16[784,256]{1,0:T(8,128)(2,1)S(1)} %get-tuple-element.25), channel_id=1, source_target_pairs={{0,0},{1,1},{2,2},{3,3},{4,4},{5,5},{6,6},{7,7},{8,8},{9,9},{10,10... | collective-permute-start | bytes 1204232 | tf_op jit(solution)/shard_map/ppermute | solution.py:29
  122.8 11.3 %collective-permute-start.18 = (bf16[784,256]{1,0:T(8,128)(2,1)S(1)}, bf16[784,256]{1,0:T(8,128)(2,1)S(1)}, u32[]{:S(2)}, u32[]{:S(2)}) collective-permute-start(bf16[784,256]{1,0:T(8,128)(2,1)S(1)} %get-tuple-element.26), channel_id=1, source_target_pairs={{0,64},{1,65},{2,66},{3,67},{4,68},{5,69},{6,70},{7,71},{8,72},{9,... | collective-permute-start | bytes 1204232 | tf_op jit(solution)/shard_map/ppermute | solution.py:29
  134.7 2.4 %collective-permute-start.19 = (f32[3,256,256]{2,1,0:T(8,128)S(1)}, f32[3,256,256]{2,1,0:T(8,128)S(1)}, u32[]{:S(2)}, u32[]{:S(2)}) collective-permute-start(f32[3,256,256]{2,1,0:T(8,128)S(1)} %shard_map.21.a), channel_id=1, source_target_pairs={{0,32},{1,33},{2,34},{3,35},{4,36},{5,37},{6,38},{7,39},{8,40},{9,... | collective-permute-start | bytes 2359304 | tf_op jit(solution)/shard_map/ppermute | solution.py:29
  135.9 31.3 %collective-permute-start.11 = (bf16[1040,256]{1,0:T(8,128)(2,1)S(1)}, bf16[1040,256]{1,0:T(8,128)(2,1)S(1)}, u32[]{:S(2)}, u32[]{:S(2)}) collective-permute-start(bf16[1040,256]{1,0:T(8,128)(2,1)S(1)} %get-tuple-element.21), channel_id=1, source_target_pairs={{0,1},{1,2},{2,3},{3,0},{4,5},{5,6},{6,7},{7,4},{8,9},{9,10},{10,1... | collective-permute-start | bytes 1597448 | tf_op jit(solution)/shard_map/ppermute | solution.py:29
  137.5 19.2 %collective-permute-start.21 = (bf16[272,256]{1,0:T(8,128)(2,1)S(1)}, bf16[272,256]{1,0:T(8,128)(2,1)S(1)}, u32[]{:S(2)}, u32[]{:S(2)}) collective-permute-start(bf16[272,256]{1,0:T(8,128)(2,1)S(1)} %get-tuple-element.29), channel_id=1, source_target_pairs={{0,1},{1,2},{2,3},{3,0},{4,5},{5,6},{6,7},{7,4},{8,9},{9,10},{10,1... | collective-permute-start | bytes 417800 | tf_op jit(solution)/shard_map/ppermute | solution.py:29
  138.5 18.2 %collective-permute-start.22 = (bf16[272,256]{1,0:T(8,128)(2,1)S(1)}, bf16[272,256]{1,0:T(8,128)(2,1)S(1)}, u32[]{:S(2)}, u32[]{:S(2)}) collective-permute-start(bf16[272,256]{1,0:T(8,128)(2,1)S(1)} %get-tuple-element.30), channel_id=1, source_target_pairs={{0,4},{1,5},{2,6},{3,7},{4,8},{5,9},{6,10},{7,11},{8,12},{9,13},{1... | collective-permute-start | bytes 417800 | tf_op jit(solution)/shard_map/ppermute | solution.py:29
  138.5 24.2 %collective-permute-start.20 = (bf16[528,256]{1,0:T(8,128)(2,1)S(1)}, bf16[528,256]{1,0:T(8,128)(2,1)S(1)}, u32[]{:S(2)}, u32[]{:S(2)}) collective-permute-start(bf16[528,256]{1,0:T(8,128)(2,1)S(1)} %get-tuple-element.28), channel_id=1, source_target_pairs={{0,10},{1,11},{2,8},{3,9},{4,14},{5,15},{6,12},{7,13},{8,2},{9,3},... | collective-permute-start | bytes 811016 | tf_op jit(solution)/shard_map/ppermute | solution.py:29
  142.2 24.9 %collective-permute-start.12 = (bf16[528,256]{1,0:T(8,128)(2,1)S(1)}, bf16[528,256]{1,0:T(8,128)(2,1)S(1)}, u32[]{:S(2)}, u32[]{:S(2)}) collective-permute-start(bf16[528,256]{1,0:T(8,128)(2,1)S(1)} %get-tuple-element.22), channel_id=1, source_target_pairs={{0,4},{1,5},{2,6},{3,7},{4,8},{5,9},{6,10},{7,11},{8,12},{9,13},{1... | collective-permute-start | bytes 811016 | tf_op jit(solution)/shard_map/ppermute | solution.py:29
  156.7 10.4 %collective-permute-start.13 = (bf16[272,256]{1,0:T(8,128)(2,1)S(1)}, bf16[272,256]{1,0:T(8,128)(2,1)S(1)}, u32[]{:S(2)}, u32[]{:S(2)}) collective-permute-start(bf16[272,256]{1,0:T(8,128)(2,1)S(1)} %get-tuple-element.23), channel_id=1, source_target_pairs={{0,12},{1,13},{2,14},{3,15},{4,0},{5,1},{6,2},{7,3},{8,4},{9,5},{1... | collective-permute-start | bytes 417800 | tf_op jit(solution)/shard_map/ppermute | solution.py:29
  156.7 10.4 %collective-permute-start.14 = (bf16[272,256]{1,0:T(8,128)(2,1)S(1)}, bf16[272,256]{1,0:T(8,128)(2,1)S(1)}, u32[]{:S(2)}, u32[]{:S(2)}) collective-permute-start(bf16[272,256]{1,0:T(8,128)(2,1)S(1)} %get-tuple-element.24), channel_id=1, source_target_pairs={{0,4},{1,5},{2,6},{3,7},{4,8},{5,9},{6,10},{7,11},{8,12},{9,13},{1... | collective-permute-start | bytes 417800 | tf_op jit(solution)/shard_map/ppermute | solution.py:29

commit v3 on v2

v3 whole, which is shorter than its diff:
```python
import functools
import math

import jax
import jax.numpy as jnp
from jax import lax
from jax.experimental import pallas as pl
from jax.experimental.pallas import tpu as pltpu
from jax.sharding import PartitionSpec as P

ORDER = 32
TOP = 2.0**3.9
FLOOR = 2.0**-3.9
VMEM = 20 << 20

DEVICES = [
    (x, z, yh, yl, c)
    for yl in range(2)
    for c in range(2)
    for yh in range(2)
    for z in range(4)
    for x in range(4)
]


def move(value, where):
    index = {d: i for i, d in enumerate(DEVICES)}
    pairs = [(index[d], index[where(*d)]) for d in DEVICES]
    return lax.ppermute(value, ("aux", "blk"), pairs)


def to_own_layer(x, z, yh, yl, c):
    return x, z, c, yl, yh


def to_core(x, z, yh, yl, c):
    return x, z, yh, yl, 1 - c


def to_position(dx, dz, swap=False):
    def where(x, z, yh, yl, c):
        x, z = (x + dx) % 4, (z + dz) % 4
        return (x, z, yl, yh, c) if swap else (x, z, yh, yl, c)

    return where


def to_owner(m1):
    def where(x, z, yh, yl, c):
        return x, z, c, yl ^ m1, yh

    return where


def by_core(first, second):
    def where(x, z, yh, yl, c):
        return (second if c else first)(x, z, yh, yl, c)

    return where


def product(a, b):
    return lax.dot_general(a, b, (((1,), (1,)), ((), ())), preferred_element_type=jnp.float32)


def encode(value, bound):
    v = jnp.abs(value) * (TOP / bound) + FLOOR
    for _ in range(int(math.log2(ORDER))):
        v = v * v
    return jnp.where(value < 0, -v, v).astype(jnp.bfloat16)


def decode(code, bound):
    y = code.astype(jnp.float32)
    v = jnp.exp(jnp.log(jnp.abs(y)) * (1.0 / ORDER)) - FLOOR
    return jnp.where(y < 0, -v, v) * (bound * (1.0 / TOP))


def bound_of(top, width):
    rows = jnp.full((16, width), jnp.maximum(top, 1e-30) * 1.008, jnp.float32)
    return rows.astype(jnp.bfloat16).astype(jnp.float32)


def coded_shape(count, rows):
    return jax.ShapeDtypeStruct((count * rows + 16, rows), jnp.bfloat16)


def tile_of(ref, k):
    rows = ref.shape[1]
    bound = ref[ref.shape[0] - 16 :, :].astype(jnp.float32)[k : k + 1, :]
    return decode(ref[k * rows : (k + 1) * rows, :], bound)


def call(kernel, args, out_shape, scratch=(), any_from=None, flops=0, moved=0, transcendentals=0):
    whole = pl.BlockSpec(memory_space=pltpu.VMEM)
    specs = []
    for i, a in enumerate(args):
        if a.dtype == jnp.int32:
            specs.append(pl.BlockSpec(memory_space=pltpu.SMEM))
        else:
            specs.append(pl.BlockSpec(memory_space=pl.ANY) if any_from is not None and i >= any_from else whole)
    many = isinstance(out_shape, (list, tuple))
    return pl.pallas_call(
        kernel,
        out_shape=out_shape,
        in_specs=specs,
        out_specs=[whole] * len(out_shape) if many else whole,
        scratch_shapes=scratch,
        compiler_params=pltpu.CompilerParams(vmem_limit_bytes=VMEM),
        cost_estimate=pl.CostEstimate(flops=flops, bytes_accessed=moved, transcendentals=transcendentals),
    )(*args)


def tiles_kernel(classes, n_in, n_extra, place, *refs):
    ins = refs[:n_in]
    outs, (held, *accs, sems) = refs[n_in + n_extra : n_in + n_extra + 2], refs[n_in + n_extra + 2 :]
    yl, c = place[1], place[2]
    rows = outs[0].shape[1]
    copies = [pltpu.make_async_copy(r, held.at[i], sems.at[i]) for i, r in enumerate(ins)]
    for copy in copies:
        copy.start()
    ready = set()
    row = lax.broadcasted_iota(jnp.int32, (16, rows), 0)
    bounds = jnp.zeros((16, rows), jnp.float32)
    for k, names in enumerate(classes):
        for i in (i for pair in names for i in pair):
            if i not in ready:
                copies[i].wait()
                ready.add(i)
        acc = accs[k % 2]
        r, own, other = (i if i == j else jnp.where(c == 0, i, j) for i, j in names)
        acc[0] = product(held[r], held[own])
        acc[1] = product(held[r], held[other])
        coded = bound_of(jnp.max(jnp.abs(acc[...])), rows)
        bounds = jnp.where(row == k, coded, bounds)
        for m1, out in enumerate(outs):
            part = acc[jnp.where(yl ^ m1 == c, 0, 1)]
            out[k * rows : (k + 1) * rows, :] = encode(part, coded[0:1, :])
    for out in outs:
        out[len(classes) * rows :, :] = bounds.astype(jnp.bfloat16)


def partial_tiles(place, arrays, classes, rows, after=()):
    names = list(arrays)
    listed = tuple(tuple((names.index(i), names.index(j)) for i, j in k) for k in classes)
    depth = arrays[names[0]].shape[1]
    return call(
        functools.partial(tiles_kernel, listed, len(names), len(after)),
        [place, *arrays.values(), *after],
        [coded_shape(len(classes), rows)] * 2,
        scratch=[
            pltpu.VMEM((len(names), rows, depth), jnp.bfloat16),
            pltpu.VMEM((2, rows, rows), jnp.float32),
            pltpu.VMEM((2, rows, rows), jnp.float32),
            pltpu.SemaphoreType.DMA((len(names),)),
        ],
        any_from=1,
        flops=len(classes) * 4 * rows * rows * depth,
        moved=len(names) * rows * depth * 2,
    )


def sum_kernel(a, b, _, out):
    for k in range(out.shape[0]):
        out[k, :, :] = tile_of(a, k) + tile_of(b, k)


def group_kernel(counts, groups, *refs):
    n = 2 * len(counts)
    ins, outs = refs[:n], refs[n:]
    rows = ins[0].shape[2]
    row = lax.broadcasted_iota(jnp.int32, (16, rows), 0)
    bounds = [jnp.zeros((16, rows), jnp.float32) for _ in groups]
    first = 0
    for stage, count in enumerate(counts):
        for k in range(count):
            total = ins[2 * stage][k, :, :] + ins[2 * stage + 1][k, :, :]
            code = None
            for j, (out, (send, members)) in enumerate(zip(outs, groups)):
                for i, member in enumerate(members):
                    if member != first + k:
                        continue
                    if send:
                        if code is None:
                            bound = bound_of(jnp.max(jnp.abs(total)), rows)
                            code = encode(total, bound[0:1, :])
                        out[i * rows : (i + 1) * rows, :] = code
                        bounds[j] = jnp.where(row == i, bound, bounds[j])
                    else:
                        out[i, :, :] = total
        first += count
    for out, (send, _), rows_of in zip(outs, groups, bounds):
        if send:
            out[out.shape[0] - 16 :, :] = rows_of.astype(jnp.bfloat16)


def place_kernel(tiles, place, *refs):
    ins, out = refs[:-1], refs[-1]
    c, z, x = place[2], place[3], place[4]
    rows = out.shape[0]
    for array, i, (dx, dz), turned in tiles:
        zz = (z + dz) % 4
        xx = (x + dx) % 4
        ref = ins[array]

        @pl.when(zz // 2 == c)
        def _():
            tile = ref[i, :, :] if ref.dtype == jnp.float32 else tile_of(ref, i)
            start = pl.multiple_of(((zz % 2) * 4 + xx) * rows, rows)
            out[:, pl.ds(start, rows)] = tile.T if turned else tile


O, PX, MX, PZ, MZ, PE, ME = (0, 0), (1, 0), (3, 0), (0, 1), (0, 3), (1, 1), (3, 3)
EARLY = ((O, O), (O, PX), (O, PZ), (MX, PX), (MZ, PZ), (MZ, PX), (PZ, PX))
LATE = ((ME, PX), (ME, PZ), (ME, PE))
SENDS = (
    (O, False, (0, 1, 2)),
    (PX, True, (1, 3, 5, 6, 7)),
    (PZ, True, (2, 4, 8)),
    (ME, False, (7, 8, 9)),
    (MZ, False, (5,)),
    (PZ, False, (6,)),
)
OWN = {
    O: ("o", "o"),
    PX: ("q2", "q1"),
    PZ: ("q1", "q2"),
    MX: ("q4", "q3"),
    MZ: ("q3", "q4"),
    PE: ("pe", "pe"),
    ME: ("me", "me"),
}
OTHER = {O: ("so", "so"), PX: ("s1", "s2"), PZ: ("s2", "s1"), PE: ("spe", "spe")}


def minus(a, b):
    return (a[0] - b[0]) % 4, (a[1] - b[1]) % 4


def fetch(value, first, second):
    ways = (to_position(*minus(O, p)) for p in (first, second))
    return move(value, by_core(*ways))


def local(b_factors):
    rows = b_factors.shape[0]
    flat = b_factors.reshape(rows, -1)
    aux, blk = lax.axis_index("aux"), lax.axis_index("blk")
    place = jnp.stack([blk // 16, aux // 2, aux % 2, (blk // 4) % 4, blk % 4]).astype(jnp.int32)

    held = {"o": move(flat, to_own_layer)}
    held["q1"] = fetch(held["o"], PZ, PX)
    held["q2"] = fetch(held["o"], PX, PZ)
    held["q3"] = fetch(held["o"], MZ, MX)
    held["q4"] = fetch(held["o"], MX, MZ)
    held["pe"] = fetch(held["q1"], PX, PZ)
    held["me"] = fetch(held["q3"], MX, MZ)
    for name, source in (("so", "o"), ("s1", "q1"), ("s2", "q2")):
        held[name] = move(held[source], to_core)

    coded, after = [], ()
    for classes in (EARLY, LATE):
        if after:
            first, _ = lax.optimization_barrier((held["pe"], after[0]))
            held["spe"] = move(first, to_core)
        listed = [(OWN[r], OWN[q], OTHER[q]) for r, q in classes]
        used = {i for k in listed for pair in k for i in pair}
        arrays = {name: v for name, v in held.items() if name in used}
        coded.append(partial_tiles(place, arrays, listed, rows, after))
        after = (coded[-1][0],)

    sums = []
    for classes, stage in zip((EARLY, LATE), coded):
        mine = call(
            sum_kernel,
            [*(move(v, to_owner(m1)) for m1, v in enumerate(stage)), *after],
            jax.ShapeDtypeStruct((len(classes), rows, rows), jnp.float32),
            any_from=2,
            moved=4 << 20,
            transcendentals=1 << 21,
        )
        sums += [mine, move(mine, to_core)]

    groups = tuple((to != O, members) for to, _, members in SENDS)
    parts = call(
        functools.partial(group_kernel, (len(EARLY), len(LATE)), groups),
        sums,
        [
            coded_shape(len(g), rows) if s else jax.ShapeDtypeStruct((len(g), rows, rows), jnp.float32)
            for s, g in groups
        ],
        moved=4 << 20,
    )
    arrived, tiles = [], []
    for j, (part, (to, turned, members)) in enumerate(zip(parts, SENDS)):
        for i, k in enumerate(members):
            r, q = (EARLY + LATE)[k]
            tiles.append((j, i, minus(r, q) if turned else minus(q, r), turned))
        arrived.append(part if to == O else move(part, to_position(*to, swap=turned)))
    return call(
        functools.partial(place_kernel, tuple(tiles)),
        [place, *arrived],
        jax.ShapeDtypeStruct((rows, 8 * rows), jnp.float32),
        moved=6 << 20,
        transcendentals=1 << 20,
    )


def solution(mesh):
    return jax.shard_map(
        local, mesh=mesh, in_specs=(P("blk", "aux", None),), out_specs=P("blk", "aux"), check_vma=False
    )
```

time: 171 us -> 135 us (0.79)
  waiting for transfers between devices: 111 us -> 80.2 us
  starting transfers between devices: 35.3 us -> 32.1 us
  local copies, waits for them, and re-layouts: 3.77 us -> 1.58 us
    ppermute x23 -> x22, waiting for transfers between devices: 111 us -> 80.2 us  [move(): return lax.ppermute(value, ('aux', 'blk'), pairs)]
    ppermute x23 -> x22, starting transfers between devices: 35.3 us -> 32.1 us  [move(): return lax.ppermute(value, ('aux', 'blk'), pairs)]
    unnamed x5 -> x1, local copies, waits for them, and re-layouts: 3.69 us -> 1.5 us
    pallas_call x7 -> x6, Pallas kernels: 20.4 us -> 21.1 us  [call(): pl.pallas_call(kernel, out_shape=out_shape, in_specs=specs, out_specs=[wh...]
  transfers between devices with their start and end apart: 23 -> 22, of which waited for: 12 -> 12; matrix products, arithmetic and copies ran while one was open for 0% -> 0% of each run, Pallas kernels for 10% -> 11%
where the time goes in v3:
time: 135 us
  waiting for transfers between devices  80.2 us (59%)
  starting transfers between devices  32.1 us (24%)
  Pallas kernels  21.1 us (16%)
  local copies, waits for them, and re-layouts  1.58 us (1%)
    ppermute x22, waiting for transfers between devices, move(): return lax.ppermute(value, ('aux', 'blk'), pairs)  80.2 us
    ppermute x22, starting transfers between devices, move(): return lax.ppermute(value, ('aux', 'blk'), pairs)  32.1 us
    pallas_call x6, Pallas kernels, call(): pl.pallas_call(kernel, out_shape=out_shape, in_specs=specs, out_specs=[wh...  21.1 us
  transfers between devices with their start and end apart: 22, of which 12 were waited for; matrix products, arithmetic and copies ran while one was open for 0% of the time, Pallas kernels for 11%

profile of v3, /device:TPU:9, one launch (start us, length us, event | category | flops | bytes accessed | tf_op | source)
XLA Modules:
  0.0 135.2 jit_solution(14511618905811937098)
XLA Ops:
  0.0 1.5 %copy.4 = bf16[32,8,16,128]{3,1,2,0:T(8,128)(2,1)S(1)} copy(bf16[32,8,16,128]{3,2,1,0:T(8,128)(2,1)} %bitcast.9) | data formatting | bytes 2097152
  1.5 4.5 %collective-permute-start = (bf16[256,2048]{1,0:T(8,128)(2,1)S(1)}, bf16[256,2048]{1,0:T(8,128)(2,1)}, u32[]{:S(2)}, u32[]{:S(2)}) collective-permute-start(bf16[256,2048]{1,0:T(8,128)(2,1)S(1)} %bitcast.10), channel_id=1, source_target_pairs={{0,0},{1,1},{2,2},{3,3},{4,4},{5,5},{6,6},{7,7},{8,8},{9,9},{10,10... | collective-permute-start | bytes 3145736 | tf_op jit(solution)/shard_map/ppermute | solution.py:29
  6.0 13.5 %collective-permute-done.refs_0_ = bf16[256,2048]{1,0:T(8,128)(2,1)} collective-permute-done((bf16[256,2048]{1,0:T(8,128)(2,1)S(1)}, bf16[256,2048]{1,0:T(8,128)(2,1)}, u32[]{:S(2)}, u32[]{:S(2)}) %collective-permute-start) | collective-permute-done | bytes 1048608 | tf_op jit(solution)/shard_map/ppermute | solution.py:29
  19.5 2.5 %collective-permute-start.1 = (bf16[256,2048]{1,0:T(8,128)(2,1)}, bf16[256,2048]{1,0:T(8,128)(2,1)S(1)}, u32[]{:S(2)}, u32[]{:S(2)}) collective-permute-start(bf16[256,2048]{1,0:T(8,128)(2,1)} %collective-permute-done.refs_0_), channel_id=1, source_target_pairs={{0,12},{1,13},{2,14},{3,15},{4,0},{5,1},{6,2},{7,3},{8,4},{9,5},{1... | collective-permute-start | bytes 3145736 | tf_op jit(solution)/shard_map/ppermute | solution.py:29
  22.0 3.7 %collective-permute-start.2 = (bf16[256,2048]{1,0:T(8,128)(2,1)}, bf16[256,2048]{1,0:T(8,128)(2,1)S(1)}, u32[]{:S(2)}, u32[]{:S(2)}) collective-permute-start(bf16[256,2048]{1,0:T(8,128)(2,1)} %collective-permute-done.refs_0_), channel_id=1, source_target_pairs={{0,3},{1,0},{2,1},{3,2},{4,7},{5,4},{6,5},{7,6},{8,11},{9,8},{10,9... | collective-permute-start | bytes 3145736 | tf_op jit(solution)/shard_map/ppermute | solution.py:29
  25.7 0.0 collective-permute-start.3
  25.7 0.0 collective-permute-start.4
  25.7 0.0 collective-permute-start.5
  25.7 8.4 %collective-permute-done.1.refs_1_.refs_0_ = bf16[256,2048]{1,0:T(8,128)(2,1)S(1)} collective-permute-done((bf16[256,2048]{1,0:T(8,128)(2,1)}, bf16[256,2048]{1,0:T(8,128)(2,1)S(1)}, u32[]{:S(2)}, u32[]{:S(2)}) %collective-permute-start.1) | collective-permute-done | bytes 1048608 | tf_op jit(solution)/shard_map/ppermute | solution.py:29
  34.1 0.0 collective-permute-start.6
  34.1 3.6 %collective-permute-done.2.refs_2_.refs_1_ = bf16[256,2048]{1,0:T(8,128)(2,1)S(1)} collective-permute-done((bf16[256,2048]{1,0:T(8,128)(2,1)}, bf16[256,2048]{1,0:T(8,128)(2,1)S(1)}, u32[]{:S(2)}, u32[]{:S(2)}) %collective-permute-start.2) | collective-permute-done | bytes 1048608 | tf_op jit(solution)/shard_map/ppermute | solution.py:29
  37.7 0.0 collective-permute-start.7
  37.7 3.1 %collective-permute-done.3.refs_3_ = bf16[256,2048]{1,0:T(8,128)(2,1)} collective-permute-done((bf16[256,2048]{1,0:T(8,128)(2,1)}, bf16[256,2048]{1,0:T(8,128)(2,1)}, u32[]{:S(2)}, u32[]{:S(2)}) %collective-permute-start.3) | collective-permute-done | bytes 1048608 | tf_op jit(solution)/shard_map/ppermute | solution.py:29
  40.8 0.1 collective-permute-start.10
  41.0 0.1 stack.23.place
  41.0 1.3 collective-permute-start.11
  42.4 0.0 collective-permute-done.5.refs_5_
  42.4 0.0 collective-permute-done.6.refs_6_.refs_4_
  42.4 9.0 %shard_map.17 = (bf16[1808,256]{1,0:T(8,128)(2,1)S(1)}, bf16[1808,256]{1,0:T(8,128)(2,1)S(1)}) custom-call(s32[5]{0:T(128)S(1)} %stack.23.place, bf16[256,2048]{1,0:T(8,128)(2,1)} %collective-permute-done.refs_0_, bf16[256,2048]{1,0:T(8,128)(2,1)S(1)} %collective-permute-done.1.refs_1_.refs_0_, bf16[256,2048]{1,0:T(8,128)(2,1)S(1)} %collective-permute-done.2.refs_2_.refs_1_, ...), custom_call_target="tpu_custom_call" | custom-call | flops 3758096384 | bytes 8388608 | tf_op jit(solution)/shard_map/pallas_call | solution.py:103
  51.4 3.3 %collective-permute-done.10.refs_2_ = bf16[256,2048]{1,0:T(8,128)(2,1)} collective-permute-done((bf16[256,2048]{1,0:T(8,128)(2,1)S(1)}, bf16[256,2048]{1,0:T(8,128)(2,1)}, u32[]{:S(2)}, u32[]{:S(2)}) %collective-permute-start.10) | collective-permute-done | bytes 1048608 | tf_op jit(solution)/shard_map/ppermute | solution.py:29
  54.8 0.0 collective-permute-start.12
  54.8 7.0 %collective-permute-start.8 = (bf16[1808,256]{1,0:T(8,128)(2,1)S(1)}, bf16[1808,256]{1,0:T(8,128)(2,1)S(1)}, u32[]{:S(2)}, u32[]{:S(2)}) collective-permute-start(bf16[1808,256]{1,0:T(8,128)(2,1)S(1)} %get-tuple-element.16.refs_7_), channel_id=1, source_target_pairs={{0,0},{1,1},{2,2},{3,3},{4,4},{5,5},{6,6},{7,7},{8,8},{9,9},{10,10... | collective-permute-start | bytes 2777096 | tf_op jit(solution)/shard_map/ppermute | solution.py:29
  61.7 0.3 collective-permute-start.9
  62.0 0.0 collective-permute-done.11.refs_3_
  62.0 0.0 collective-permute-done.12.refs_6_
  62.0 5.4 %shard_map.18 = (bf16[784,256]{1,0:T(8,128)(2,1)S(1)}, bf16[784,256]{1,0:T(8,128)(2,1)S(1)}) custom-call(s32[5]{0:T(128)S(1)} %stack.23.place, bf16[256,2048]{1,0:T(8,128)(2,1)S(1)} %collective-permute-done.1.refs_1_.refs_0_, bf16[256,2048]{1,0:T(8,128)(2,1)S(1)} %collective-permute-done.2.refs_2_.refs_1_, ...), custom_call_target="tpu_custom_call" | custom-call | flops 1610612736 | bytes 7340032 | tf_op jit(solution)/shard_map/pallas_call | solution.py:103
  67.4 14.8 %collective-permute-done.8.a = bf16[1808,256]{1,0:T(8,128)(2,1)S(1)} collective-permute-done((bf16[1808,256]{1,0:T(8,128)(2,1)S(1)}, bf16[1808,256]{1,0:T(8,128)(2,1)S(1)}, u32[]{:S(2)}, u32[]{:S(2)}) %collective-permute-start.8) | collective-permute-done | bytes 925728 | tf_op jit(solution)/shard_map/ppermute | solution.py:29
  82.3 1.5 %collective-permute-done.9.b = bf16[1808,256]{1,0:T(8,128)(2,1)S(1)} collective-permute-done((bf16[1808,256]{1,0:T(8,128)(2,1)S(1)}, bf16[1808,256]{1,0:T(8,128)(2,1)S(1)}, u32[]{:S(2)}, u32[]{:S(2)}) %collective-permute-start.9) | collective-permute-done | bytes 925728 | tf_op jit(solution)/shard_map/ppermute | solution.py:29
  83.8 1.5 %shard_map.19.refs_0_ = f32[7,256,256]{2,1,0:T(8,128)S(1)} custom-call(bf16[1808,256]{1,0:T(8,128)(2,1)S(1)} %collective-permute-done.8.a, bf16[1808,256]{1,0:T(8,128)(2,1)S(1)} %collective-permute-done.9.b, bf16[784,256]{1,0:T(8,128)(2,1)S(1)} %get-tuple-element.19._), custom_call_target="tpu_custom_call" | custom-call | bytes 4194304 | tf_op jit(solution)/shard_map/pallas_call | solution.py:103
  85.3 0.1 collective-permute-start.13
  85.4 4.3 %collective-permute-start.14 = (bf16[784,256]{1,0:T(8,128)(2,1)S(1)}, bf16[784,256]{1,0:T(8,128)(2,1)S(1)}, u32[]{:S(2)}, u32[]{:S(2)}) collective-permute-start(bf16[784,256]{1,0:T(8,128)(2,1)S(1)} %get-tuple-element.19._), channel_id=1, source_target_pairs={{0,0},{1,1},{2,2},{3,3},{4,4},{5,5},{6,6},{7,7},{8,8},{9,9},{10,10... | collective-permute-start | bytes 1204232 | tf_op jit(solution)/shard_map/ppermute | solution.py:29
  89.7 0.9 collective-permute-start.15
  90.5 7.7 %collective-permute-done.14.a = bf16[784,256]{1,0:T(8,128)(2,1)S(1)} collective-permute-done((bf16[784,256]{1,0:T(8,128)(2,1)S(1)}, bf16[784,256]{1,0:T(8,128)(2,1)S(1)}, u32[]{:S(2)}, u32[]{:S(2)}) %collective-permute-start.14) | collective-permute-done | bytes 401440 | tf_op jit(solution)/shard_map/ppermute | solution.py:29
  98.3 2.6 %collective-permute-done.15.b = bf16[784,256]{1,0:T(8,128)(2,1)S(1)} collective-permute-done((bf16[784,256]{1,0:T(8,128)(2,1)S(1)}, bf16[784,256]{1,0:T(8,128)(2,1)S(1)}, u32[]{:S(2)}, u32[]{:S(2)}) %collective-permute-start.15) | collective-permute-done | bytes 401440 | tf_op jit(solution)/shard_map/ppermute | solution.py:29
  100.9 0.6 shard_map.20.refs_2_
  101.5 0.1 collective-permute-start.16
  101.6 2.3 %collective-permute-done.16.refs_3_ = f32[3,256,256]{2,1,0:T(8,128)S(1)} collective-permute-done((f32[3,256,256]{2,1,0:T(8,128)S(1)}, f32[3,256,256]{2,1,0:T(8,128)S(1)}, u32[]{:S(2)}, u32[]{:S(2)}) %collective-permute-start.16) | collective-permute-done | bytes 786464 | tf_op jit(solution)/shard_map/ppermute | solution.py:29
  103.9 0.0 collective-permute-done.13.refs_1_
  103.9 1.5 %shard_map.21 = (f32[3,256,256]{2,1,0:T(8,128)S(1)}, bf16[1296,256]{1,0:T(8,128)(2,1)S(1)}, bf16[784,256]{1,0:T(8,128)(2,1)S(1)}, bf16[784,256]{1,0:T(8,128)(2,1...) custom-call(f32[7,256,256]{2,1,0:T(8,128)S(1)} %shard_map.19.refs_0_, ...), custom_call_target="tpu_custom_call" | custom-call | bytes 4194304 | tf_op jit(solution)/shard_map/pallas_call | solution.py:103
  105.5 0.1 collective-permute-start.17
  105.5 0.1 collective-permute-start.18
  105.6 5.9 %collective-permute-start.19 = (bf16[784,256]{1,0:T(8,128)(2,1)S(1)}, bf16[784,256]{1,0:T(8,128)(2,1)S(1)}, u32[]{:S(2)}, u32[]{:S(2)}) collective-permute-start(bf16[784,256]{1,0:T(8,128)(2,1)S(1)} %get-tuple-element.24), channel_id=1, source_target_pairs={{0,15},{1,12},{2,13},{3,14},{4,3},{5,0},{6,1},{7,2},{8,7},{9,4},{1... | collective-permute-start | bytes 1204232 | tf_op jit(solution)/shard_map/ppermute | solution.py:29
  111.5 0.0 collective-permute-start.20
  111.5 1.5 %collective-permute-start.21 = (bf16[272,256]{1,0:T(8,128)(2,1)S(1)}, bf16[272,256]{1,0:T(8,128)(2,1)S(1)}, u32[]{:S(2)}, u32[]{:S(2)}) collective-permute-start(bf16[272,256]{1,0:T(8,128)(2,1)S(1)} %get-tuple-element.26), channel_id=1, source_target_pairs={{0,4},{1,5},{2,6},{3,7},{4,8},{5,9},{6,10},{7,11},{8,12},{9,13},{1... | collective-permute-start | bytes 417800 | tf_op jit(solution)/shard_map/ppermute | solution.py:29
  113.0 8.6 %collective-permute-done.20.refs_4_ = bf16[272,256]{1,0:T(8,128)(2,1)S(1)} collective-permute-done((bf16[272,256]{1,0:T(8,128)(2,1)S(1)}, bf16[272,256]{1,0:T(8,128)(2,1)S(1)}, u32[]{:S(2)}, u32[]{:S(2)}) %collective-permute-start.20) | collective-permute-done | bytes 139296 | tf_op jit(solution)/shard_map/ppermute | solution.py:29
  121.5 0.0 collective-permute-done.21.refs_5_
  121.6 10.6 %collective-permute-done.18.refs_2_ = bf16[784,256]{1,0:T(8,128)(2,1)S(1)} collective-permute-done((bf16[784,256]{1,0:T(8,128)(2,1)S(1)}, bf16[784,256]{1,0:T(8,128)(2,1)S(1)}, u32[]{:S(2)}, u32[]{:S(2)}) %collective-permute-start.18) | collective-permute-done | bytes 401440 | tf_op jit(solution)/shard_map/ppermute | solution.py:29
  132.2 3.0 %shard_map.22 = f32[256,2048]{1,0:T(8,128)} custom-call(s32[5]{0:T(128)S(1)} %stack.23.place, f32[3,256,256]{2,1,0:T(8,128)S(1)} %get-tuple-element.21.refs_0_, bf16[1296,256]{1,0:T(8,128)(2,1)S(1)} %collective-permute-done.17.refs_1_, bf16[784,256]{1,0:T(8,128)(2,1)S(1)} %collective-permute-done.18.refs_2_, ...), custom_call_target="tpu_custom_call" | custom-call | bytes 6291456 | tf_op jit(solution)/shard_map/pallas_call | solution.py:103
  (4 shorter events, 0.0 us)
Async XLA Ops:
  1.5 18.0 %collective-permute-start = (bf16[256,2048]{1,0:T(8,128)(2,1)S(1)}, bf16[256,2048]{1,0:T(8,128)(2,1)}, u32[]{:S(2)}, u32[]{:S(2)}) collective-permute-start(bf16[256,2048]{1,0:T(8,128)(2,1)S(1)} %bitcast.10), channel_id=1, source_target_pairs={{0,0},{1,1},{2,2},{3,3},{4,4},{5,5},{6,6},{7,7},{8,8},{9,9},{10,10... | collective-permute-start | bytes 3145736 | tf_op jit(solution)/shard_map/ppermute | solution.py:29
  19.5 14.6 %collective-permute-start.1 = (bf16[256,2048]{1,0:T(8,128)(2,1)}, bf16[256,2048]{1,0:T(8,128)(2,1)S(1)}, u32[]{:S(2)}, u32[]{:S(2)}) collective-permute-start(bf16[256,2048]{1,0:T(8,128)(2,1)} %collective-permute-done.refs_0_), channel_id=1, source_target_pairs={{0,12},{1,13},{2,14},{3,15},{4,0},{5,1},{6,2},{7,3},{8,4},{9,5},{1... | collective-permute-start | bytes 3145736 | tf_op jit(solution)/shard_map/ppermute | solution.py:29
  22.0 15.7 %collective-permute-start.2 = (bf16[256,2048]{1,0:T(8,128)(2,1)}, bf16[256,2048]{1,0:T(8,128)(2,1)S(1)}, u32[]{:S(2)}, u32[]{:S(2)}) collective-permute-start(bf16[256,2048]{1,0:T(8,128)(2,1)} %collective-permute-done.refs_0_), channel_id=1, source_target_pairs={{0,3},{1,0},{2,1},{3,2},{4,7},{5,4},{6,5},{7,6},{8,11},{9,8},{10,9... | collective-permute-start | bytes 3145736 | tf_op jit(solution)/shard_map/ppermute | solution.py:29
  25.7 15.2 %collective-permute-start.3 = (bf16[256,2048]{1,0:T(8,128)(2,1)}, bf16[256,2048]{1,0:T(8,128)(2,1)}, u32[]{:S(2)}, u32[]{:S(2)}) collective-permute-start(bf16[256,2048]{1,0:T(8,128)(2,1)} %collective-permute-done.refs_0_), channel_id=1, source_target_pairs={{0,4},{1,5},{2,6},{3,7},{4,8},{5,9},{6,10},{7,11},{8,12},{9,13},{1... | collective-permute-start | bytes 3145736 | tf_op jit(solution)/shard_map/ppermute | solution.py:29
  25.7 15.4 %collective-permute-start.4 = (bf16[256,2048]{1,0:T(8,128)(2,1)}, bf16[256,2048]{1,0:T(8,128)(2,1)}, u32[]{:S(2)}, u32[]{:S(2)}) collective-permute-start(bf16[256,2048]{1,0:T(8,128)(2,1)} %collective-permute-done.refs_0_), channel_id=1, source_target_pairs={{0,1},{1,2},{2,3},{3,0},{4,5},{5,6},{6,7},{7,4},{8,9},{9,10},{10,1... | collective-permute-start | bytes 3145736 | tf_op jit(solution)/shard_map/ppermute | solution.py:29
  25.7 16.7 %collective-permute-start.5 = (bf16[256,2048]{1,0:T(8,128)(2,1)}, bf16[256,2048]{1,0:T(8,128)(2,1)}, u32[]{:S(2)}, u32[]{:S(2)}) collective-permute-start(bf16[256,2048]{1,0:T(8,128)(2,1)} %collective-permute-done.refs_0_), channel_id=1, source_target_pairs={{0,32},{1,33},{2,34},{3,35},{4,36},{5,37},{6,38},{7,39},{8,40},{9,... | collective-permute-start | bytes 3145736 | tf_op jit(solution)/shard_map/ppermute | solution.py:29
  34.1 8.3 %collective-permute-start.6 = (bf16[256,2048]{1,0:T(8,128)(2,1)S(1)}, bf16[256,2048]{1,0:T(8,128)(2,1)S(1)}, u32[]{:S(2)}, u32[]{:S(2)}) collective-permute-start(bf16[256,2048]{1,0:T(8,128)(2,1)S(1)} %collective-permute-done.1.refs_1_.refs_0_), channel_id=1, source_target_pairs={{0,32},{1,33},{2,34},{3,35},{4,36},{5,37},{6,38},{7,39},{8,40},{9,... | collective-permute-start | bytes 3145736 | tf_op jit(solution)/shard_map/ppermute | solution.py:29
  37.7 4.7 %collective-permute-start.7 = (bf16[256,2048]{1,0:T(8,128)(2,1)S(1)}, bf16[256,2048]{1,0:T(8,128)(2,1)}, u32[]{:S(2)}, u32[]{:S(2)}) collective-permute-start(bf16[256,2048]{1,0:T(8,128)(2,1)S(1)} %collective-permute-done.2.refs_2_.refs_1_), channel_id=1, source_target_pairs={{0,32},{1,33},{2,34},{3,35},{4,36},{5,37},{6,38},{7,39},{8,40},{9,... | collective-permute-start | bytes 3145736 | tf_op jit(solution)/shard_map/ppermute | solution.py:29
  40.8 13.9 %collective-permute-start.10 = (bf16[256,2048]{1,0:T(8,128)(2,1)S(1)}, bf16[256,2048]{1,0:T(8,128)(2,1)}, u32[]{:S(2)}, u32[]{:S(2)}) collective-permute-start(bf16[256,2048]{1,0:T(8,128)(2,1)S(1)} %collective-permute-done.1.refs_1_.refs_0_), channel_id=1, source_target_pairs={{0,3},{1,0},{2,1},{3,2},{4,7},{5,4},{6,5},{7,6},{8,11},{9,8},{10,9... | collective-permute-start | bytes 3145736 | tf_op jit(solution)/shard_map/ppermute | solution.py:29
  41.0 21.0 %collective-permute-start.11 = (bf16[256,2048]{1,0:T(8,128)(2,1)}, bf16[256,2048]{1,0:T(8,128)(2,1)S(1)}, u32[]{:S(2)}, u32[]{:S(2)}) collective-permute-start(bf16[256,2048]{1,0:T(8,128)(2,1)} %collective-permute-done.3.refs_3_), channel_id=1, source_target_pairs={{0,1},{1,2},{2,3},{3,0},{4,5},{5,6},{6,7},{7,4},{8,9},{9,10},{10,1... | collective-permute-start | bytes 3145736 | tf_op jit(solution)/shard_map/ppermute | solution.py:29
  54.8 7.3 %collective-permute-start.12 = (bf16[256,2048]{1,0:T(8,128)(2,1)}, bf16[256,2048]{1,0:T(8,128)(2,1)S(1)}, u32[]{:S(2)}, u32[]{:S(2)}) collective-permute-start(bf16[256,2048]{1,0:T(8,128)(2,1)} %collective-permute-done.10.refs_2_), channel_id=1, source_target_pairs={{0,32},{1,33},{2,34},{3,35},{4,36},{5,37},{6,38},{7,39},{8,40},{9,... | collective-permute-start | bytes 3145736 | tf_op jit(solution)/shard_map/ppermute | solution.py:29
  54.8 27.5 %collective-permute-start.8 = (bf16[1808,256]{1,0:T(8,128)(2,1)S(1)}, bf16[1808,256]{1,0:T(8,128)(2,1)S(1)}, u32[]{:S(2)}, u32[]{:S(2)}) collective-permute-start(bf16[1808,256]{1,0:T(8,128)(2,1)S(1)} %get-tuple-element.16.refs_7_), channel_id=1, source_target_pairs={{0,0},{1,1},{2,2},{3,3},{4,4},{5,5},{6,6},{7,7},{8,8},{9,9},{10,10... | collective-permute-start | bytes 2777096 | tf_op jit(solution)/shard_map/ppermute | solution.py:29
  61.7 22.1 %collective-permute-start.9 = (bf16[1808,256]{1,0:T(8,128)(2,1)S(1)}, bf16[1808,256]{1,0:T(8,128)(2,1)S(1)}, u32[]{:S(2)}, u32[]{:S(2)}) collective-permute-start(bf16[1808,256]{1,0:T(8,128)(2,1)S(1)} %get-tuple-element.17), channel_id=1, source_target_pairs={{0,64},{1,65},{2,66},{3,67},{4,68},{5,69},{6,70},{7,71},{8,72},{9,... | collective-permute-start | bytes 2777096 | tf_op jit(solution)/shard_map/ppermute | solution.py:29
  85.3 18.6 %collective-permute-start.13 = (f32[7,256,256]{2,1,0:T(8,128)S(1)}, f32[7,256,256]{2,1,0:T(8,128)S(1)}, u32[]{:S(2)}, u32[]{:S(2)}) collective-permute-start(f32[7,256,256]{2,1,0:T(8,128)S(1)} %shard_map.19.refs_0_), channel_id=1, source_target_pairs={{0,32},{1,33},{2,34},{3,35},{4,36},{5,37},{6,38},{7,39},{8,40},{9,... | collective-permute-start | bytes 5505032 | tf_op jit(solution)/shard_map/ppermute | solution.py:29
  85.4 12.9 %collective-permute-start.14 = (bf16[784,256]{1,0:T(8,128)(2,1)S(1)}, bf16[784,256]{1,0:T(8,128)(2,1)S(1)}, u32[]{:S(2)}, u32[]{:S(2)}) collective-permute-start(bf16[784,256]{1,0:T(8,128)(2,1)S(1)} %get-tuple-element.19._), channel_id=1, source_target_pairs={{0,0},{1,1},{2,2},{3,3},{4,4},{5,5},{6,6},{7,7},{8,8},{9,9},{10,10... | collective-permute-start | bytes 1204232 | tf_op jit(solution)/shard_map/ppermute | solution.py:29
  89.7 11.2 %collective-permute-start.15 = (bf16[784,256]{1,0:T(8,128)(2,1)S(1)}, bf16[784,256]{1,0:T(8,128)(2,1)S(1)}, u32[]{:S(2)}, u32[]{:S(2)}) collective-permute-start(bf16[784,256]{1,0:T(8,128)(2,1)S(1)} %get-tuple-element.20), channel_id=1, source_target_pairs={{0,64},{1,65},{2,66},{3,67},{4,68},{5,69},{6,70},{7,71},{8,72},{9,... | collective-permute-start | bytes 1204232 | tf_op jit(solution)/shard_map/ppermute | solution.py:29
  101.5 2.4 %collective-permute-start.16 = (f32[3,256,256]{2,1,0:T(8,128)S(1)}, f32[3,256,256]{2,1,0:T(8,128)S(1)}, u32[]{:S(2)}, u32[]{:S(2)}) collective-permute-start(f32[3,256,256]{2,1,0:T(8,128)S(1)} %shard_map.20.refs_2_), channel_id=1, source_target_pairs={{0,32},{1,33},{2,34},{3,35},{4,36},{5,37},{6,38},{7,39},{8,40},{9,... | collective-permute-start | bytes 2359304 | tf_op jit(solution)/shard_map/ppermute | solution.py:29
  105.5 26.7 %collective-permute-start.17 = (bf16[1296,256]{1,0:T(8,128)(2,1)S(1)}, bf16[1296,256]{1,0:T(8,128)(2,1)S(1)}, u32[]{:S(2)}, u32[]{:S(2)}) collective-permute-start(bf16[1296,256]{1,0:T(8,128)(2,1)S(1)} %get-tuple-element.22), channel_id=1, source_target_pairs={{0,1},{1,2},{2,3},{3,0},{4,5},{5,6},{6,7},{7,4},{8,9},{9,10},{10,1... | collective-permute-start | bytes 1990664 | tf_op jit(solution)/shard_map/ppermute | solution.py:29
  105.5 26.7 %collective-permute-start.18 = (bf16[784,256]{1,0:T(8,128)(2,1)S(1)}, bf16[784,256]{1,0:T(8,128)(2,1)S(1)}, u32[]{:S(2)}, u32[]{:S(2)}) collective-permute-start(bf16[784,256]{1,0:T(8,128)(2,1)S(1)} %get-tuple-element.23), channel_id=1, source_target_pairs={{0,4},{1,5},{2,6},{3,7},{4,8},{5,9},{6,10},{7,11},{8,12},{9,13},{1... | collective-permute-start | bytes 1204232 | tf_op jit(solution)/shard_map/ppermute | solution.py:29
  105.6 26.6 %collective-permute-start.19 = (bf16[784,256]{1,0:T(8,128)(2,1)S(1)}, bf16[784,256]{1,0:T(8,128)(2,1)S(1)}, u32[]{:S(2)}, u32[]{:S(2)}) collective-permute-start(bf16[784,256]{1,0:T(8,128)(2,1)S(1)} %get-tuple-element.24), channel_id=1, source_target_pairs={{0,15},{1,12},{2,13},{3,14},{4,3},{5,0},{6,1},{7,2},{8,7},{9,4},{1... | collective-permute-start | bytes 1204232 | tf_op jit(solution)/shard_map/ppermute | solution.py:29
  111.5 10.1 %collective-permute-start.20 = (bf16[272,256]{1,0:T(8,128)(2,1)S(1)}, bf16[272,256]{1,0:T(8,128)(2,1)S(1)}, u32[]{:S(2)}, u32[]{:S(2)}) collective-permute-start(bf16[272,256]{1,0:T(8,128)(2,1)S(1)} %get-tuple-element.25), channel_id=1, source_target_pairs={{0,12},{1,13},{2,14},{3,15},{4,0},{5,1},{6,2},{7,3},{8,4},{9,5},{1... | collective-permute-start | bytes 417800 | tf_op jit(solution)/shard_map/ppermute | solution.py:29
  111.5 10.1 %collective-permute-start.21 = (bf16[272,256]{1,0:T(8,128)(2,1)S(1)}, bf16[272,256]{1,0:T(8,128)(2,1)S(1)}, u32[]{:S(2)}, u32[]{:S(2)}) collective-permute-start(bf16[272,256]{1,0:T(8,128)(2,1)S(1)} %get-tuple-element.26), channel_id=1, source_target_pairs={{0,4},{1,5},{2,6},{3,7},{4,8},{5,9},{6,10},{7,11},{8,12},{9,13},{1... | collective-permute-start | bytes 417800 | tf_op jit(solution)/shard_map/ppermute | solution.py:29

commit v4 on v3

--- a/solution.py
+++ b/solution.py
@@ -81,14 +81,14 @@
     return rows.astype(jnp.bfloat16).astype(jnp.float32)
 
 
-def coded_shape(count, rows):
-    return jax.ShapeDtypeStruct((count * rows + 16, rows), jnp.bfloat16)
-
-
-def tile_of(ref, k):
-    rows = ref.shape[1]
+def coded_shape(count, size, width):
+    return jax.ShapeDtypeStruct((count * size + 16, width), jnp.bfloat16)
+
+
+def part_of(ref, k, size, start=0):
     bound = ref[ref.shape[0] - 16 :, :].astype(jnp.float32)[k : k + 1, :]
-    return decode(ref[k * rows : (k + 1) * rows, :], bound)
+    count = size if isinstance(start, int) and start == 0 else size // 2
+    return decode(ref[pl.ds(k * size + start, count), :], bound)
 
 
 def call(kernel, args, out_shape, scratch=(), any_from=None, flops=0, moved=0, transcendentals=0):
@@ -147,7 +147,7 @@
     return call(
         functools.partial(tiles_kernel, listed, len(names), len(after)),
         [place, *arrays.values(), *after],
-        [coded_shape(len(classes), rows)] * 2,
+        [coded_shape(len(classes), rows, rows)] * 2,
         scratch=[
             pltpu.VMEM((len(names), rows, depth), jnp.bfloat16),
             pltpu.VMEM((2, rows, rows), jnp.float32),
@@ -160,65 +160,87 @@
     )
 
 
-def sum_kernel(a, b, _, out):
-    for k in range(out.shape[0]):
-        out[k, :, :] = tile_of(a, k) + tile_of(b, k)
-
-
-def group_kernel(counts, groups, *refs):
-    n = 2 * len(counts)
-    ins, outs = refs[:n], refs[n:]
-    rows = ins[0].shape[2]
-    row = lax.broadcasted_iota(jnp.int32, (16, rows), 0)
-    bounds = [jnp.zeros((16, rows), jnp.float32) for _ in groups]
-    first = 0
-    for stage, count in enumerate(counts):
-        for k in range(count):
-            total = ins[2 * stage][k, :, :] + ins[2 * stage + 1][k, :, :]
-            code = None
-            for j, (out, (send, members)) in enumerate(zip(outs, groups)):
-                for i, member in enumerate(members):
-                    if member != first + k:
-                        continue
-                    if send:
-                        if code is None:
-                            bound = bound_of(jnp.max(jnp.abs(total)), rows)
-                            code = encode(total, bound[0:1, :])
-                        out[i * rows : (i + 1) * rows, :] = code
-                        bounds[j] = jnp.where(row == i, bound, bounds[j])
-                    else:
-                        out[i, :, :] = total
-        first += count
-    for out, (send, _), rows_of in zip(outs, groups, bounds):
-        if send:
-            out[out.shape[0] - 16 :, :] = rows_of.astype(jnp.bfloat16)
-
-
-def place_kernel(tiles, place, *refs):
-    ins, out = refs[:-1], refs[-1]
+def sum_kernel(whole, place, a, b, _, *outs):
+    c = place[2]
+    rows = a.shape[1]
+    half = rows // 2
+    kept, given = outs[-2], outs[-1]
+    count = (a.shape[0] - 16) // rows
+    for k in range(count):
+        if k < whole:
+            outs[0][k, :, :] = part_of(a, k, rows) + part_of(b, k, rows)
+        else:
+            for out, h in ((kept, c), (given, 1 - c)):
+                start = pl.multiple_of(h * half, half)
+                out[k - whole, :, :] = part_of(a, k, rows, start) + part_of(b, k, rows, start)
+
+
+def group_kernel(classes, groups, place, *refs):
+    ins, outs = refs[: len(refs) - len(groups)], refs[len(refs) - len(groups) :]
+    width = outs[0].shape[1]
+    half = width // 2
+    start = pl.multiple_of(place[2] * half, half)
+    row = lax.broadcasted_iota(jnp.int32, (16, width), 0)
+    bounds = [jnp.zeros((16, width), jnp.float32) for _ in groups]
+    for k, (pair, i) in classes.items():
+        rows = pl.ds(start, half) if ins[2 * pair].shape[1] == width else pl.ds(0, half)
+        total = ins[2 * pair][i, rows, :] + ins[2 * pair + 1][i, rows, :]
+        bound = bound_of(jnp.max(jnp.abs(total)), width)
+        code = encode(total, bound[0:1, :])
+        for j, (out, members) in enumerate(zip(outs, groups)):
+            for i, member in enumerate(members):
+                if member == k:
+                    out[i * half : (i + 1) * half, :] = code
+                    bounds[j] = jnp.where(row == i, bound, bounds[j])
+    for out, rows_of in zip(outs, bounds):
+        out[out.shape[0] - 16 :, :] = rows_of.astype(jnp.bfloat16)
+
+
+def place_kernel(stay, tiles, n, place, *refs):
+    sums, own, other, out = refs[:2], refs[2 : 2 + n], refs[2 + n : 2 + 2 * n], refs[2 + 2 * n]
     c, z, x = place[2], place[3], place[4]
     rows = out.shape[0]
-    for array, i, (dx, dz), turned in tiles:
+    half = rows // 2
+    first = pl.multiple_of(c * half, half)
+    second = pl.multiple_of((1 - c) * half, half)
+
+    def at(d, write):
+        dx, dz = d
         zz = (z + dz) % 4
         xx = (x + dx) % 4
-        ref = ins[array]
 
         @pl.when(zz // 2 == c)
         def _():
-            tile = ref[i, :, :] if ref.dtype == jnp.float32 else tile_of(ref, i)
-            start = pl.multiple_of(((zz % 2) * 4 + xx) * rows, rows)
-            out[:, pl.ds(start, rows)] = tile.T if turned else tile
+            write(pl.multiple_of(((zz % 2) * 4 + xx) * rows, rows))
+
+    for i, d in stay:
+
+        def write(start, i=i):
+            out[:, pl.ds(start, rows)] = sums[0][i, :, :] + sums[1][i, :, :]
+
+        at(d, write)
+    for array, i, d, turned in tiles:
+
+        def write(start, array=array, i=i, turned=turned):
+            for ref, offset in ((own[array], first), (other[array], second)):
+                tile = part_of(ref, i, half)
+                if turned:
+                    out[:, pl.ds(pl.multiple_of(start + offset, half), half)] = tile.T
+                else:
+                    out[pl.ds(offset, half), pl.ds(start, rows)] = tile
+
+        at(d, write)
 
 
 O, PX, MX, PZ, MZ, PE, ME = (0, 0), (1, 0), (3, 0), (0, 1), (0, 3), (1, 1), (3, 3)
 EARLY = ((O, O), (O, PX), (O, PZ), (MX, PX), (MZ, PZ), (MZ, PX), (PZ, PX))
 LATE = ((ME, PX), (ME, PZ), (ME, PE))
+STAY = 3
 SENDS = (
-    (O, False, (0, 1, 2)),
     (PX, True, (1, 3, 5, 6, 7)),
-    (PZ, True, (2, 4, 8)),
+    (PZ, True, (2, 8)),
     (ME, False, (7, 8, 9)),
-    (MZ, False, (5,)),
+    (MZ, False, (4, 5)),
     (PZ, False, (6,)),
 )
 OWN = {
@@ -270,36 +292,42 @@
         after = (coded[-1][0],)
 
     sums = []
-    for classes, stage in zip((EARLY, LATE), coded):
-        mine = call(
-            sum_kernel,
-            [*(move(v, to_owner(m1)) for m1, v in enumerate(stage)), *after],
-            jax.ShapeDtypeStruct((len(classes), rows, rows), jnp.float32),
-            any_from=2,
-            moved=4 << 20,
-            transcendentals=1 << 21,
+    for classes, stage, whole, weight in zip((EARLY, LATE), coded, (STAY, 0), (1, 10**11)):
+        halves = jax.ShapeDtypeStruct((len(classes) - whole, rows // 2, rows), jnp.float32)
+        full = [jax.ShapeDtypeStruct((whole, rows, rows), jnp.float32)] * (whole > 0)
+        *full, kept, given = call(
+            functools.partial(sum_kernel, whole),
+            [place, *(move(v, to_owner(m1)) for m1, v in enumerate(stage)), *after],
+            [*full, halves, halves],
+            any_from=3,
+            flops=weight,
+            moved=weight,
+            transcendentals=weight,
         )
-        sums += [mine, move(mine, to_core)]
-
-    groups = tuple((to != O, members) for to, _, members in SENDS)
+        sums += [v for f in full for v in (f, move(f, to_core))] + [kept, move(given, to_core)]
+
+    where = {k: (0, k) for k in range(1, STAY)}
+    where |= {k: (1, k - STAY) for k in range(STAY, len(EARLY))}
+    where |= {len(EARLY) + k: (2, k) for k in range(len(LATE))}
+    groups = tuple(members for _, _, members in SENDS)
     parts = call(
-        functools.partial(group_kernel, (len(EARLY), len(LATE)), groups),
-        sums,
-        [
-            coded_shape(len(g), rows) if s else jax.ShapeDtypeStruct((len(g), rows, rows), jnp.float32)
-            for s, g in groups
-        ],
+        functools.partial(group_kernel, where, groups),
+        [place, *sums],
+        [coded_shape(len(g), rows // 2, rows) for g in groups],
         moved=4 << 20,
     )
-    arrived, tiles = [], []
+    own, tiles = [], []
     for j, (part, (to, turned, members)) in enumerate(zip(parts, SENDS)):
         for i, k in enumerate(members):
             r, q = (EARLY + LATE)[k]
             tiles.append((j, i, minus(r, q) if turned else minus(q, r), turned))
-        arrived.append(part if to == O else move(part, to_position(*to, swap=turned)))
+        own.append(move(part, to_position(*to, swap=turned)))
+    own = lax.optimization_barrier(own)
+    other = [move(v, to_core) for v in own]
+    stay = tuple((k, minus(q, r)) for k, (r, q) in enumerate(EARLY[:STAY]))
     return call(
-        functools.partial(place_kernel, tuple(tiles)),
-        [place, *arrived],
+        functools.partial(place_kernel, stay, tuple(tiles), len(own)),
+        [place, *sums[:2], *own, *other],
         jax.ShapeDtypeStruct((rows, 8 * rows), jnp.float32),
         moved=6 << 20,
         transcendentals=1 << 20,

time: 135 us -> 119 us (0.88)
  waiting for transfers between devices: 80.2 us -> 59.1 us
  Pallas kernels: 21.1 us -> 24.6 us
    ppermute x22 -> x28, waiting for transfers between devices: 80.2 us -> 59.1 us  [move(): return lax.ppermute(value, ('aux', 'blk'), pairs)]
    pallas_call x6, Pallas kernels: 21.1 us -> 24.6 us  [call(): pl.pallas_call(kernel, out_shape=out_shape, in_specs=specs, out_specs=[wh...]
    ppermute x22 -> x28, starting transfers between devices: 32.1 us -> 33.4 us  [move(): return lax.ppermute(value, ('aux', 'blk'), pairs)]
  transfers between devices with their start and end apart: 22 -> 28, of which waited for: 12 -> 13; matrix products, arithmetic and copies ran while one was open for 0% -> 0% of each run, Pallas kernels for 11% -> 16%
where the time goes in v4:
time: 119 us
  waiting for transfers between devices  59.1 us (50%)
  starting transfers between devices  33.4 us (28%)
  Pallas kernels  24.6 us (21%)
  local copies, waits for them, and re-layouts  1.58 us (1%)
    ppermute x28, waiting for transfers between devices, move(): return lax.ppermute(value, ('aux', 'blk'), pairs)  59.1 us
    ppermute x28, starting transfers between devices, move(): return lax.ppermute(value, ('aux', 'blk'), pairs)  33.4 us
    pallas_call x6, Pallas kernels, call(): pl.pallas_call(kernel, out_shape=out_shape, in_specs=specs, out_specs=[wh...  24.6 us
  transfers between devices with their start and end apart: 28, of which 13 were waited for; matrix products, arithmetic and copies ran while one was open for 0% of the time, Pallas kernels for 16%

profile of v4, /device:TPU:9, one launch (start us, length us, event | category | flops | bytes accessed | tf_op | source)
XLA Modules:
  0.0 118.9 jit_solution(6019390088870939605)
XLA Ops:
  0.0 1.5 %copy.4 = bf16[32,8,16,128]{3,1,2,0:T(8,128)(2,1)S(1)} copy(bf16[32,8,16,128]{3,2,1,0:T(8,128)(2,1)} %bitcast.9) | data formatting | bytes 2097152
  1.5 4.5 %collective-permute-start = (bf16[256,2048]{1,0:T(8,128)(2,1)S(1)}, bf16[256,2048]{1,0:T(8,128)(2,1)}, u32[]{:S(2)}, u32[]{:S(2)}) collective-permute-start(bf16[256,2048]{1,0:T(8,128)(2,1)S(1)} %bitcast.10), channel_id=1, source_target_pairs={{0,0},{1,1},{2,2},{3,3},{4,4},{5,5},{6,6},{7,7},{8,8},{9,9},{10,10... | collective-permute-start | bytes 3145736 | tf_op jit(solution)/shard_map/ppermute | solution.py:29
  6.0 13.5 %collective-permute-done.refs_0_ = bf16[256,2048]{1,0:T(8,128)(2,1)} collective-permute-done((bf16[256,2048]{1,0:T(8,128)(2,1)S(1)}, bf16[256,2048]{1,0:T(8,128)(2,1)}, u32[]{:S(2)}, u32[]{:S(2)}) %collective-permute-start) | collective-permute-done | bytes 1048608 | tf_op jit(solution)/shard_map/ppermute | solution.py:29
  19.5 2.5 %collective-permute-start.1 = (bf16[256,2048]{1,0:T(8,128)(2,1)}, bf16[256,2048]{1,0:T(8,128)(2,1)S(1)}, u32[]{:S(2)}, u32[]{:S(2)}) collective-permute-start(bf16[256,2048]{1,0:T(8,128)(2,1)} %collective-permute-done.refs_0_), channel_id=1, source_target_pairs={{0,12},{1,13},{2,14},{3,15},{4,0},{5,1},{6,2},{7,3},{8,4},{9,5},{1... | collective-permute-start | bytes 3145736 | tf_op jit(solution)/shard_map/ppermute | solution.py:29
  22.0 3.7 %collective-permute-start.2 = (bf16[256,2048]{1,0:T(8,128)(2,1)}, bf16[256,2048]{1,0:T(8,128)(2,1)S(1)}, u32[]{:S(2)}, u32[]{:S(2)}) collective-permute-start(bf16[256,2048]{1,0:T(8,128)(2,1)} %collective-permute-done.refs_0_), channel_id=1, source_target_pairs={{0,3},{1,0},{2,1},{3,2},{4,7},{5,4},{6,5},{7,6},{8,11},{9,8},{10,9... | collective-permute-start | bytes 3145736 | tf_op jit(solution)/shard_map/ppermute | solution.py:29
  25.7 0.0 collective-permute-start.5
  25.7 8.4 %collective-permute-done.1.refs_1_.refs_0_ = bf16[256,2048]{1,0:T(8,128)(2,1)S(1)} collective-permute-done((bf16[256,2048]{1,0:T(8,128)(2,1)}, bf16[256,2048]{1,0:T(8,128)(2,1)S(1)}, u32[]{:S(2)}, u32[]{:S(2)}) %collective-permute-start.1) | collective-permute-done | bytes 1048608 | tf_op jit(solution)/shard_map/ppermute | solution.py:29
  34.1 0.0 collective-permute-start.6
  34.1 3.6 %collective-permute-done.2.refs_2_.refs_1_ = bf16[256,2048]{1,0:T(8,128)(2,1)S(1)} collective-permute-done((bf16[256,2048]{1,0:T(8,128)(2,1)}, bf16[256,2048]{1,0:T(8,128)(2,1)S(1)}, u32[]{:S(2)}, u32[]{:S(2)}) %collective-permute-start.2) | collective-permute-done | bytes 1048608 | tf_op jit(solution)/shard_map/ppermute | solution.py:29
  37.7 3.1 %collective-permute-done.3.refs_3_ = bf16[256,2048]{1,0:T(8,128)(2,1)} collective-permute-done((bf16[256,2048]{1,0:T(8,128)(2,1)}, bf16[256,2048]{1,0:T(8,128)(2,1)}, u32[]{:S(2)}, u32[]{:S(2)}) %collective-permute-start.3) | collective-permute-done | bytes 1048608 | tf_op jit(solution)/shard_map/ppermute | solution.py:29
  40.8 0.1 collective-permute-start.10
  41.0 0.1 stack.23.place
  41.0 1.3 %collective-permute-start.11 = (bf16[256,2048]{1,0:T(8,128)(2,1)}, bf16[256,2048]{1,0:T(8,128)(2,1)S(1)}, u32[]{:S(2)}, u32[]{:S(2)}) collective-permute-start(bf16[256,2048]{1,0:T(8,128)(2,1)} %collective-permute-done.3.refs_3_), channel_id=1, source_target_pairs={{0,1},{1,2},{2,3},{3,0},{4,5},{5,6},{6,7},{7,4},{8,9},{9,10},{10,1... | collective-permute-start | bytes 3145736 | tf_op jit(solution)/shard_map/ppermute | solution.py:29
  42.4 0.0 collective-permute-done.5.refs_5_
  42.4 0.0 collective-permute-done.6.refs_6_.refs_4_
  42.4 9.0 %shard_map.17 = (bf16[1808,256]{1,0:T(8,128)(2,1)S(1)}, bf16[1808,256]{1,0:T(8,128)(2,1)S(1)}) custom-call(s32[5]{0:T(128)S(1)} %stack.23.place, bf16[256,2048]{1,0:T(8,128)(2,1)} %collective-permute-done.refs_0_, bf16[256,2048]{1,0:T(8,128)(2,1)S(1)} %collective-permute-done.1.refs_1_.refs_0_, bf16[256,2048]{1,0:T(8,128)(2,1)S(1)} %collective-permute-done.2.refs_2_.refs_1_, ...), custom_call_target="tpu_custom_call" | custom-call | flops 3758096384 | bytes 8388608 | tf_op jit(solution)/shard_map/pallas_call | solution.py:103
  51.4 3.3 %collective-permute-done.10.refs_2_ = bf16[256,2048]{1,0:T(8,128)(2,1)} collective-permute-done((bf16[256,2048]{1,0:T(8,128)(2,1)S(1)}, bf16[256,2048]{1,0:T(8,128)(2,1)}, u32[]{:S(2)}, u32[]{:S(2)}) %collective-permute-start.10) | collective-permute-done | bytes 1048608 | tf_op jit(solution)/shard_map/ppermute | solution.py:29
  54.8 0.0 collective-permute-start.12
  54.8 7.0 %collective-permute-start.8 = (bf16[1808,256]{1,0:T(8,128)(2,1)S(1)}, bf16[1808,256]{1,0:T(8,128)(2,1)S(1)}, u32[]{:S(2)}, u32[]{:S(2)}) collective-permute-start(bf16[1808,256]{1,0:T(8,128)(2,1)S(1)} %get-tuple-element.25.refs_7_), channel_id=1, source_target_pairs={{0,0},{1,1},{2,2},{3,3},{4,4},{5,5},{6,6},{7,7},{8,8},{9,9},{10,10... | collective-permute-start | bytes 2777096 | tf_op jit(solution)/shard_map/ppermute | solution.py:29
  61.7 0.3 collective-permute-start.9
  62.0 0.0 collective-permute-done.11.refs_3_
  62.0 5.4 %shard_map.18 = (bf16[784,256]{1,0:T(8,128)(2,1)S(1)}, bf16[784,256]{1,0:T(8,128)(2,1)S(1)}) custom-call(s32[5]{0:T(128)S(1)} %stack.23.place, bf16[256,2048]{1,0:T(8,128)(2,1)S(1)} %collective-permute-done.1.refs_1_.refs_0_, bf16[256,2048]{1,0:T(8,128)(2,1)S(1)} %collective-permute-done.2.refs_2_.refs_1_, ...), custom_call_target="tpu_custom_call" | custom-call | flops 1610612736 | bytes 7340032 | tf_op jit(solution)/shard_map/pallas_call | solution.py:103
  67.4 5.0 %collective-permute-start.15 = (bf16[784,256]{1,0:T(8,128)(2,1)S(1)}, bf16[784,256]{1,0:T(8,128)(2,1)S(1)}, u32[]{:S(2)}, u32[]{:S(2)}) collective-permute-start(bf16[784,256]{1,0:T(8,128)(2,1)S(1)} %get-tuple-element.28._), channel_id=1, source_target_pairs={{0,0},{1,1},{2,2},{3,3},{4,4},{5,5},{6,6},{7,7},{8,8},{9,9},{10,10... | collective-permute-start | bytes 1204232 | tf_op jit(solution)/shard_map/ppermute | solution.py:29
  72.5 0.1 collective-permute-start.16
  72.6 10.2 %collective-permute-done.8.a = bf16[1808,256]{1,0:T(8,128)(2,1)S(1)} collective-permute-done((bf16[1808,256]{1,0:T(8,128)(2,1)S(1)}, bf16[1808,256]{1,0:T(8,128)(2,1)S(1)}, u32[]{:S(2)}, u32[]{:S(2)}) %collective-permute-start.8) | collective-permute-done | bytes 925728 | tf_op jit(solution)/shard_map/ppermute | solution.py:29
  82.8 2.1 %collective-permute-done.9.b = bf16[1808,256]{1,0:T(8,128)(2,1)S(1)} collective-permute-done((bf16[1808,256]{1,0:T(8,128)(2,1)S(1)}, bf16[1808,256]{1,0:T(8,128)(2,1)S(1)}, u32[]{:S(2)}, u32[]{:S(2)}) %collective-permute-start.9) | collective-permute-done | bytes 925728 | tf_op jit(solution)/shard_map/ppermute | solution.py:29
  84.8 2.9 %shard_map.19 = (f32[3,256,256]{2,1,0:T(8,128)}, f32[4,128,256]{2,1,0:T(8,128)S(1)}, f32[4,128,256]{2,1,0:T(8,128)}) custom-call(s32[5]{0:T(128)S(1)} %stack.23.place, bf16[1808,256]{1,0:T(8,128)(2,1)S(1)} %collective-permute-done.8.a, bf16[1808,256]{1,0:T(8,128)(2,1)S(1)} %collective-permute-done.9.b, bf16[784,256]{1,0:T(8,128)(2,1)S(1)} %get-tuple-element.28._), custom_call_target="tpu_custom_call" | custom-call | flops 1 | bytes 1 | tf_op jit(solution)/shard_map/pallas_call | solution.py:103
  87.7 0.5 collective-permute-start.14
  88.2 2.7 %collective-permute-done.15.a = bf16[784,256]{1,0:T(8,128)(2,1)S(1)} collective-permute-done((bf16[784,256]{1,0:T(8,128)(2,1)S(1)}, bf16[784,256]{1,0:T(8,128)(2,1)S(1)}, u32[]{:S(2)}, u32[]{:S(2)}) %collective-permute-start.15) | collective-permute-done | bytes 401440 | tf_op jit(solution)/shard_map/ppermute | solution.py:29
  90.9 1.5 %collective-permute-done.16.b = bf16[784,256]{1,0:T(8,128)(2,1)S(1)} collective-permute-done((bf16[784,256]{1,0:T(8,128)(2,1)S(1)}, bf16[784,256]{1,0:T(8,128)(2,1)S(1)}, u32[]{:S(2)}, u32[]{:S(2)}) %collective-permute-start.16) | collective-permute-done | bytes 401440 | tf_op jit(solution)/shard_map/ppermute | solution.py:29
  92.4 1.2 %shard_map.20 = (f32[3,128,256]{2,1,0:T(8,128)S(1)}, f32[3,128,256]{2,1,0:T(8,128)S(1)}) custom-call(s32[5]{0:T(128)S(1)} %stack.23.place, bf16[784,256]{1,0:T(8,128)(2,1)S(1)} %collective-permute-done.15.a, bf16[784,256]{1,0:T(8,128)(2,1)S(1)} %collective-permute-done.16.b, bf16[784,256]{1,0:T(8,128)(2,1)S(1)} %get-tuple-element.28._), custom_call_target="tpu_custom_call" | custom-call | flops 99999997952 | bytes 99999997952 | tf_op jit(solution)/shard_map/pallas_call | solution.py:103
  93.6 0.1 collective-permute-start.17
  93.7 1.7 %collective-permute-done.17.refs_5_ = f32[3,128,256]{2,1,0:T(8,128)S(1)} collective-permute-done((f32[3,128,256]{2,1,0:T(8,128)S(1)}, f32[3,128,256]{2,1,0:T(8,128)S(1)}, u32[]{:S(2)}, u32[]{:S(2)}) %collective-permute-start.17) | collective-permute-done | bytes 393248 | tf_op jit(solution)/shard_map/ppermute | solution.py:29
  95.4 2.2 %shard_map.21 = (bf16[656,256]{1,0:T(8,128)(2,1)S(1)}, bf16[272,256]{1,0:T(8,128)(2,1)S(1)}, bf16[400,256]{1,0:T(8,128)(2,1)S(1)}, bf16[272,256]{1,0:T(8,128)(2,1)S(1)}, bf16[144,256]{1,0:T(8,128)(2,1)S(1)}) custom-call(s32[5]{0:T(128)S(1)} %stack.23.place, f32[3,256,256]{2,1,0:T(8,128)} %get-tuple-element.29.refs_0_, ...), custom_call_target="tpu_custom_call" | custom-call | bytes 4194304 | tf_op jit(solution)/shard_map/pallas_call | solution.py:103
  97.7 0.1 collective-permute-start.18
  97.7 2.1 %collective-permute-start.20 = (bf16[400,256]{1,0:T(8,128)(2,1)S(1)}, bf16[400,256]{1,0:T(8,128)(2,1)S(1)}, u32[]{:S(2)}, u32[]{:S(2)}) collective-permute-start(bf16[400,256]{1,0:T(8,128)(2,1)S(1)} %get-tuple-element.37), channel_id=1, source_target_pairs={{0,15},{1,12},{2,13},{3,14},{4,3},{5,0},{6,1},{7,2},{8,7},{9,4},{1... | collective-permute-start | bytes 614408 | tf_op jit(solution)/shard_map/ppermute | solution.py:29
  99.9 2.6 %collective-permute-start.19 = (bf16[272,256]{1,0:T(8,128)(2,1)S(1)}, bf16[272,256]{1,0:T(8,128)(2,1)S(1)}, u32[]{:S(2)}, u32[]{:S(2)}) collective-permute-start(bf16[272,256]{1,0:T(8,128)(2,1)S(1)} %get-tuple-element.36), channel_id=1, source_target_pairs={{0,4},{1,5},{2,6},{3,7},{4,8},{5,9},{6,10},{7,11},{8,12},{9,13},{1... | collective-permute-start | bytes 417800 | tf_op jit(solution)/shard_map/ppermute | solution.py:29
  102.5 0.6 collective-permute-start.21
  103.1 0.8 collective-permute-start.22
  103.9 3.9 %collective-permute-done.22.refs_6_ = bf16[144,256]{1,0:T(8,128)(2,1)S(1)} collective-permute-done((bf16[144,256]{1,0:T(8,128)(2,1)S(1)}, bf16[144,256]{1,0:T(8,128)(2,1)S(1)}, u32[]{:S(2)}, u32[]{:S(2)}) %collective-permute-start.22) | collective-permute-done | bytes 73760 | tf_op jit(solution)/shard_map/ppermute | solution.py:29
  107.8 4.0 %collective-permute-done.19.refs_3_ = bf16[272,256]{1,0:T(8,128)(2,1)S(1)} collective-permute-done((bf16[272,256]{1,0:T(8,128)(2,1)S(1)}, bf16[272,256]{1,0:T(8,128)(2,1)S(1)}, u32[]{:S(2)}, u32[]{:S(2)}) %collective-permute-start.19) | collective-permute-done | bytes 139296 | tf_op jit(solution)/shard_map/ppermute | solution.py:29
  111.8 1.1 collective-permute-start.23
  112.9 0.1 collective-permute-start.25
  113.0 0.4 collective-permute-start.24
  113.5 0.1 collective-permute-start.26
  113.5 0.4 collective-permute-start.27
  114.0 1.0 collective-permute-done.27.refs_11_
  115.0 3.9 %shard_map.22 = f32[256,2048]{1,0:T(8,128)} custom-call(s32[5]{0:T(128)S(1)} %stack.23.place, f32[3,256,256]{2,1,0:T(8,128)} %get-tuple-element.29.refs_0_, f32[3,256,256]{2,1,0:T(8,128)} %collective-permute-done.13.refs_1_, bf16[656,256]{1,0:T(8,128)(2,1)S(1)} %collective-permute-done.18.refs_2_, bf16[272,256]{1,0:T(8,128)(2,1)S(1)} %collective-permute-done.19.refs_3_, ...), custom_call_target="tpu_custom_call" | custom-call | bytes 6291456 | tf_op jit(solution)/shard_map/pallas_call | solution.py:103
  (16 shorter events, 0.0 us)
Async XLA Ops:
  1.5 18.0 %collective-permute-start = (bf16[256,2048]{1,0:T(8,128)(2,1)S(1)}, bf16[256,2048]{1,0:T(8,128)(2,1)}, u32[]{:S(2)}, u32[]{:S(2)}) collective-permute-start(bf16[256,2048]{1,0:T(8,128)(2,1)S(1)} %bitcast.10), channel_id=1, source_target_pairs={{0,0},{1,1},{2,2},{3,3},{4,4},{5,5},{6,6},{7,7},{8,8},{9,9},{10,10... | collective-permute-start | bytes 3145736 | tf_op jit(solution)/shard_map/ppermute | solution.py:29
  19.5 14.6 %collective-permute-start.1 = (bf16[256,2048]{1,0:T(8,128)(2,1)}, bf16[256,2048]{1,0:T(8,128)(2,1)S(1)}, u32[]{:S(2)}, u32[]{:S(2)}) collective-permute-start(bf16[256,2048]{1,0:T(8,128)(2,1)} %collective-permute-done.refs_0_), channel_id=1, source_target_pairs={{0,12},{1,13},{2,14},{3,15},{4,0},{5,1},{6,2},{7,3},{8,4},{9,5},{1... | collective-permute-start | bytes 3145736 | tf_op jit(solution)/shard_map/ppermute | solution.py:29
  22.0 15.7 %collective-permute-start.2 = (bf16[256,2048]{1,0:T(8,128)(2,1)}, bf16[256,2048]{1,0:T(8,128)(2,1)S(1)}, u32[]{:S(2)}, u32[]{:S(2)}) collective-permute-start(bf16[256,2048]{1,0:T(8,128)(2,1)} %collective-permute-done.refs_0_), channel_id=1, source_target_pairs={{0,3},{1,0},{2,1},{3,2},{4,7},{5,4},{6,5},{7,6},{8,11},{9,8},{10,9... | collective-permute-start | bytes 3145736 | tf_op jit(solution)/shard_map/ppermute | solution.py:29
  25.7 15.2 %collective-permute-start.3 = (bf16[256,2048]{1,0:T(8,128)(2,1)}, bf16[256,2048]{1,0:T(8,128)(2,1)}, u32[]{:S(2)}, u32[]{:S(2)}) collective-permute-start(bf16[256,2048]{1,0:T(8,128)(2,1)} %collective-permute-done.refs_0_), channel_id=1, source_target_pairs={{0,4},{1,5},{2,6},{3,7},{4,8},{5,9},{6,10},{7,11},{8,12},{9,13},{1... | collective-permute-start | bytes 3145736 | tf_op jit(solution)/shard_map/ppermute | solution.py:29
  25.7 15.4 %collective-permute-start.4 = (bf16[256,2048]{1,0:T(8,128)(2,1)}, bf16[256,2048]{1,0:T(8,128)(2,1)}, u32[]{:S(2)}, u32[]{:S(2)}) collective-permute-start(bf16[256,2048]{1,0:T(8,128)(2,1)} %collective-permute-done.refs_0_), channel_id=1, source_target_pairs={{0,1},{1,2},{2,3},{3,0},{4,5},{5,6},{6,7},{7,4},{8,9},{9,10},{10,1... | collective-permute-start | bytes 3145736 | tf_op jit(solution)/shard_map/ppermute | solution.py:29
  25.7 16.7 %collective-permute-start.5 = (bf16[256,2048]{1,0:T(8,128)(2,1)}, bf16[256,2048]{1,0:T(8,128)(2,1)}, u32[]{:S(2)}, u32[]{:S(2)}) collective-permute-start(bf16[256,2048]{1,0:T(8,128)(2,1)} %collective-permute-done.refs_0_), channel_id=1, source_target_pairs={{0,32},{1,33},{2,34},{3,35},{4,36},{5,37},{6,38},{7,39},{8,40},{9,... | collective-permute-start | bytes 3145736 | tf_op jit(solution)/shard_map/ppermute | solution.py:29
  34.1 8.3 %collective-permute-start.6 = (bf16[256,2048]{1,0:T(8,128)(2,1)S(1)}, bf16[256,2048]{1,0:T(8,128)(2,1)S(1)}, u32[]{:S(2)}, u32[]{:S(2)}) collective-permute-start(bf16[256,2048]{1,0:T(8,128)(2,1)S(1)} %collective-permute-done.1.refs_1_.refs_0_), channel_id=1, source_target_pairs={{0,32},{1,33},{2,34},{3,35},{4,36},{5,37},{6,38},{7,39},{8,40},{9,... | collective-permute-start | bytes 3145736 | tf_op jit(solution)/shard_map/ppermute | solution.py:29
  37.7 4.7 %collective-permute-start.7 = (bf16[256,2048]{1,0:T(8,128)(2,1)S(1)}, bf16[256,2048]{1,0:T(8,128)(2,1)}, u32[]{:S(2)}, u32[]{:S(2)}) collective-permute-start(bf16[256,2048]{1,0:T(8,128)(2,1)S(1)} %collective-permute-done.2.refs_2_.refs_1_), channel_id=1, source_target_pairs={{0,32},{1,33},{2,34},{3,35},{4,36},{5,37},{6,38},{7,39},{8,40},{9,... | collective-permute-start | bytes 3145736 | tf_op jit(solution)/shard_map/ppermute | solution.py:29
  40.8 13.9 %collective-permute-start.10 = (bf16[256,2048]{1,0:T(8,128)(2,1)S(1)}, bf16[256,2048]{1,0:T(8,128)(2,1)}, u32[]{:S(2)}, u32[]{:S(2)}) collective-permute-start(bf16[256,2048]{1,0:T(8,128)(2,1)S(1)} %collective-permute-done.1.refs_1_.refs_0_), channel_id=1, source_target_pairs={{0,3},{1,0},{2,1},{3,2},{4,7},{5,4},{6,5},{7,6},{8,11},{9,8},{10,9... | collective-permute-start | bytes 3145736 | tf_op jit(solution)/shard_map/ppermute | solution.py:29
  41.0 21.0 %collective-permute-start.11 = (bf16[256,2048]{1,0:T(8,128)(2,1)}, bf16[256,2048]{1,0:T(8,128)(2,1)S(1)}, u32[]{:S(2)}, u32[]{:S(2)}) collective-permute-start(bf16[256,2048]{1,0:T(8,128)(2,1)} %collective-permute-done.3.refs_3_), channel_id=1, source_target_pairs={{0,1},{1,2},{2,3},{3,0},{4,5},{5,6},{6,7},{7,4},{8,9},{9,10},{10,1... | collective-permute-start | bytes 3145736 | tf_op jit(solution)/shard_map/ppermute | solution.py:29
  54.8 7.3 %collective-permute-start.12 = (bf16[256,2048]{1,0:T(8,128)(2,1)}, bf16[256,2048]{1,0:T(8,128)(2,1)S(1)}, u32[]{:S(2)}, u32[]{:S(2)}) collective-permute-start(bf16[256,2048]{1,0:T(8,128)(2,1)} %collective-permute-done.10.refs_2_), channel_id=1, source_target_pairs={{0,32},{1,33},{2,34},{3,35},{4,36},{5,37},{6,38},{7,39},{8,40},{9,... | collective-permute-start | bytes 3145736 | tf_op jit(solution)/shard_map/ppermute | solution.py:29
  54.8 28.0 %collective-permute-start.8 = (bf16[1808,256]{1,0:T(8,128)(2,1)S(1)}, bf16[1808,256]{1,0:T(8,128)(2,1)S(1)}, u32[]{:S(2)}, u32[]{:S(2)}) collective-permute-start(bf16[1808,256]{1,0:T(8,128)(2,1)S(1)} %get-tuple-element.25.refs_7_), channel_id=1, source_target_pairs={{0,0},{1,1},{2,2},{3,3},{4,4},{5,5},{6,6},{7,7},{8,8},{9,9},{10,10... | collective-permute-start | bytes 2777096 | tf_op jit(solution)/shard_map/ppermute | solution.py:29
  61.7 23.1 %collective-permute-start.9 = (bf16[1808,256]{1,0:T(8,128)(2,1)S(1)}, bf16[1808,256]{1,0:T(8,128)(2,1)S(1)}, u32[]{:S(2)}, u32[]{:S(2)}) collective-permute-start(bf16[1808,256]{1,0:T(8,128)(2,1)S(1)} %get-tuple-element.26), channel_id=1, source_target_pairs={{0,64},{1,65},{2,66},{3,67},{4,68},{5,69},{6,70},{7,71},{8,72},{9,... | collective-permute-start | bytes 2777096 | tf_op jit(solution)/shard_map/ppermute | solution.py:29
  67.4 23.4 %collective-permute-start.15 = (bf16[784,256]{1,0:T(8,128)(2,1)S(1)}, bf16[784,256]{1,0:T(8,128)(2,1)S(1)}, u32[]{:S(2)}, u32[]{:S(2)}) collective-permute-start(bf16[784,256]{1,0:T(8,128)(2,1)S(1)} %get-tuple-element.28._), channel_id=1, source_target_pairs={{0,0},{1,1},{2,2},{3,3},{4,4},{5,5},{6,6},{7,7},{8,8},{9,9},{10,10... | collective-permute-start | bytes 1204232 | tf_op jit(solution)/shard_map/ppermute | solution.py:29
  72.5 19.9 %collective-permute-start.16 = (bf16[784,256]{1,0:T(8,128)(2,1)S(1)}, bf16[784,256]{1,0:T(8,128)(2,1)S(1)}, u32[]{:S(2)}, u32[]{:S(2)}) collective-permute-start(bf16[784,256]{1,0:T(8,128)(2,1)S(1)} %get-tuple-element.32), channel_id=1, source_target_pairs={{0,64},{1,65},{2,66},{3,67},{4,68},{5,69},{6,70},{7,71},{8,72},{9,... | collective-permute-start | bytes 1204232 | tf_op jit(solution)/shard_map/ppermute | solution.py:29
  87.7 6.0 %collective-permute-start.13 = (f32[3,256,256]{2,1,0:T(8,128)}, f32[3,256,256]{2,1,0:T(8,128)}, u32[]{:S(2)}, u32[]{:S(2)}) collective-permute-start(f32[3,256,256]{2,1,0:T(8,128)} %get-tuple-element.29.refs_0_), channel_id=1, source_target_pairs={{0,32},{1,33},{2,34},{3,35},{4,36},{5,37},{6,38},{7,39},{8,40},{9,... | collective-permute-start | bytes 2359304 | tf_op jit(solution)/shard_map/ppermute | solution.py:29
  87.7 6.0 %collective-permute-start.14 = (f32[4,128,256]{2,1,0:T(8,128)}, f32[4,128,256]{2,1,0:T(8,128)}, u32[]{:S(2)}, u32[]{:S(2)}) collective-permute-start(f32[4,128,256]{2,1,0:T(8,128)} %get-tuple-element.31), channel_id=1, source_target_pairs={{0,32},{1,33},{2,34},{3,35},{4,36},{5,37},{6,38},{7,39},{8,40},{9,... | collective-permute-start | bytes 1572872 | tf_op jit(solution)/shard_map/ppermute | solution.py:29
  93.6 1.8 %collective-permute-start.17 = (f32[3,128,256]{2,1,0:T(8,128)S(1)}, f32[3,128,256]{2,1,0:T(8,128)S(1)}, u32[]{:S(2)}, u32[]{:S(2)}) collective-permute-start(f32[3,128,256]{2,1,0:T(8,128)S(1)} %get-tuple-element.34), channel_id=1, source_target_pairs={{0,32},{1,33},{2,34},{3,35},{4,36},{5,37},{6,38},{7,39},{8,40},{9,... | collective-permute-start | bytes 1179656 | tf_op jit(solution)/shard_map/ppermute | solution.py:29
  97.7 14.2 %collective-permute-start.18 = (bf16[656,256]{1,0:T(8,128)(2,1)S(1)}, bf16[656,256]{1,0:T(8,128)(2,1)S(1)}, u32[]{:S(2)}, u32[]{:S(2)}) collective-permute-start(bf16[656,256]{1,0:T(8,128)(2,1)S(1)} %get-tuple-element.35), channel_id=1, source_target_pairs={{0,1},{1,2},{2,3},{3,0},{4,5},{5,6},{6,7},{7,4},{8,9},{9,10},{10,1... | collective-permute-start | bytes 1007624 | tf_op jit(solution)/shard_map/ppermute | solution.py:29
  97.7 14.1 %collective-permute-start.20 = (bf16[400,256]{1,0:T(8,128)(2,1)S(1)}, bf16[400,256]{1,0:T(8,128)(2,1)S(1)}, u32[]{:S(2)}, u32[]{:S(2)}) collective-permute-start(bf16[400,256]{1,0:T(8,128)(2,1)S(1)} %get-tuple-element.37), channel_id=1, source_target_pairs={{0,15},{1,12},{2,13},{3,14},{4,3},{5,0},{6,1},{7,2},{8,7},{9,4},{1... | collective-permute-start | bytes 614408 | tf_op jit(solution)/shard_map/ppermute | solution.py:29
  99.9 11.9 %collective-permute-start.19 = (bf16[272,256]{1,0:T(8,128)(2,1)S(1)}, bf16[272,256]{1,0:T(8,128)(2,1)S(1)}, u32[]{:S(2)}, u32[]{:S(2)}) collective-permute-start(bf16[272,256]{1,0:T(8,128)(2,1)S(1)} %get-tuple-element.36), channel_id=1, source_target_pairs={{0,4},{1,5},{2,6},{3,7},{4,8},{5,9},{6,10},{7,11},{8,12},{9,13},{1... | collective-permute-start | bytes 417800 | tf_op jit(solution)/shard_map/ppermute | solution.py:29
  102.5 9.3 %collective-permute-start.21 = (bf16[272,256]{1,0:T(8,128)(2,1)S(1)}, bf16[272,256]{1,0:T(8,128)(2,1)S(1)}, u32[]{:S(2)}, u32[]{:S(2)}) collective-permute-start(bf16[272,256]{1,0:T(8,128)(2,1)S(1)} %get-tuple-element.38), channel_id=1, source_target_pairs={{0,12},{1,13},{2,14},{3,15},{4,0},{5,1},{6,2},{7,3},{8,4},{9,5},{1... | collective-permute-start | bytes 417800 | tf_op jit(solution)/shard_map/ppermute | solution.py:29
  103.1 4.7 %collective-permute-start.22 = (bf16[144,256]{1,0:T(8,128)(2,1)S(1)}, bf16[144,256]{1,0:T(8,128)(2,1)S(1)}, u32[]{:S(2)}, u32[]{:S(2)}) collective-permute-start(bf16[144,256]{1,0:T(8,128)(2,1)S(1)} %get-tuple-element.39), channel_id=1, source_target_pairs={{0,4},{1,5},{2,6},{3,7},{4,8},{5,9},{6,10},{7,11},{8,12},{9,13},{1... | collective-permute-start | bytes 221192 | tf_op jit(solution)/shard_map/ppermute | solution.py:29
  111.8 3.2 %collective-permute-start.23 = (bf16[656,256]{1,0:T(8,128)(2,1)S(1)}, bf16[656,256]{1,0:T(8,128)(2,1)S(1)}, u32[]{:S(2)}, u32[]{:S(2)}) collective-permute-start(bf16[656,256]{1,0:T(8,128)(2,1)S(1)} %collective-permute-done.18.refs_2_), channel_id=1, source_target_pairs={{0,32},{1,33},{2,34},{3,35},{4,36},{5,37},{6,38},{7,39},{8,40},{9,... | collective-permute-start | bytes 1007624 | tf_op jit(solution)/shard_map/ppermute | solution.py:29
  112.9 2.1 %collective-permute-start.25 = (bf16[400,256]{1,0:T(8,128)(2,1)S(1)}, bf16[400,256]{1,0:T(8,128)(2,1)S(1)}, u32[]{:S(2)}, u32[]{:S(2)}) collective-permute-start(bf16[400,256]{1,0:T(8,128)(2,1)S(1)} %collective-permute-done.20.refs_4_), channel_id=1, source_target_pairs={{0,32},{1,33},{2,34},{3,35},{4,36},{5,37},{6,38},{7,39},{8,40},{9,... | collective-permute-start | bytes 614408 | tf_op jit(solution)/shard_map/ppermute | solution.py:29
  113.0 2.0 %collective-permute-start.24 = (bf16[272,256]{1,0:T(8,128)(2,1)S(1)}, bf16[272,256]{1,0:T(8,128)(2,1)S(1)}, u32[]{:S(2)}, u32[]{:S(2)}) collective-permute-start(bf16[272,256]{1,0:T(8,128)(2,1)S(1)} %collective-permute-done.19.refs_3_), channel_id=1, source_target_pairs={{0,32},{1,33},{2,34},{3,35},{4,36},{5,37},{6,38},{7,39},{8,40},{9,... | collective-permute-start | bytes 417800 | tf_op jit(solution)/shard_map/ppermute | solution.py:29
  113.5 1.6 %collective-permute-start.26 = (bf16[272,256]{1,0:T(8,128)(2,1)S(1)}, bf16[272,256]{1,0:T(8,128)(2,1)S(1)}, u32[]{:S(2)}, u32[]{:S(2)}) collective-permute-start(bf16[272,256]{1,0:T(8,128)(2,1)S(1)} %collective-permute-done.21.refs_5_), channel_id=1, source_target_pairs={{0,32},{1,33},{2,34},{3,35},{4,36},{5,37},{6,38},{7,39},{8,40},{9,... | collective-permute-start | bytes 417800 | tf_op jit(solution)/shard_map/ppermute | solution.py:29
  113.5 1.5 %collective-permute-start.27 = (bf16[144,256]{1,0:T(8,128)(2,1)S(1)}, bf16[144,256]{1,0:T(8,128)(2,1)S(1)}, u32[]{:S(2)}, u32[]{:S(2)}) collective-permute-start(bf16[144,256]{1,0:T(8,128)(2,1)S(1)} %collective-permute-done.22.refs_6_), channel_id=1, source_target_pairs={{0,32},{1,33},{2,34},{3,35},{4,36},{5,37},{6,38},{7,39},{8,40},{9,... | collective-permute-start | bytes 221192 | tf_op jit(solution)/shard_map/ppermute | solution.py:29

commit v5 on v4

--- a/solution.py
+++ b/solution.py
@@ -91,7 +91,7 @@
     return decode(ref[pl.ds(k * size + start, count), :], bound)
 
 
-def call(kernel, args, out_shape, scratch=(), any_from=None, flops=0, moved=0, transcendentals=0):
+def call(kernel, args, out_shape, scratch=(), any_from=None, flops=0, moved=0, transcendentals=0, vmem=VMEM, out_any=False):
     whole = pl.BlockSpec(memory_space=pltpu.VMEM)
     specs = []
     for i, a in enumerate(args):
@@ -104,9 +104,9 @@
         kernel,
         out_shape=out_shape,
         in_specs=specs,
-        out_specs=[whole] * len(out_shape) if many else whole,
+        out_specs=[whole] * len(out_shape) if many else pl.BlockSpec(memory_space=pl.ANY) if out_any else whole,
         scratch_shapes=scratch,
-        compiler_params=pltpu.CompilerParams(vmem_limit_bytes=VMEM),
+        compiler_params=pltpu.CompilerParams(vmem_limit_bytes=vmem),
         cost_estimate=pl.CostEstimate(flops=flops, bytes_accessed=moved, transcendentals=transcendentals),
     )(*args)
 
@@ -133,7 +133,7 @@
         acc[1] = product(held[r], held[other])
         coded = bound_of(jnp.max(jnp.abs(acc[...])), rows)
         bounds = jnp.where(row == k, coded, bounds)
-        for m1, out in enumerate(outs):
+        for m1, out in zip((1, 0), outs):
             part = acc[jnp.where(yl ^ m1 == c, 0, 1)]
             out[k * rows : (k + 1) * rows, :] = encode(part, coded[0:1, :])
     for out in outs:
@@ -164,11 +164,11 @@
     c = place[2]
     rows = a.shape[1]
     half = rows // 2
-    kept, given = outs[-2], outs[-1]
+    full, kept, given = outs
     count = (a.shape[0] - 16) // rows
     for k in range(count):
         if k < whole:
-            outs[0][k, :, :] = part_of(a, k, rows) + part_of(b, k, rows)
+            full[k, :, :] = part_of(a, k, rows) + part_of(b, k, rows)
         else:
             for out, h in ((kept, c), (given, 1 - c)):
                 start = pl.multiple_of(h * half, half)
@@ -197,12 +197,17 @@
 
 
 def place_kernel(stay, tiles, n, place, *refs):
-    sums, own, other, out = refs[:2], refs[2 : 2 + n], refs[2 + n : 2 + 2 * n], refs[2 + 2 * n]
+    own, other, sums = refs[:n], refs[n : 2 * n], refs[2 * n : 2 * n + 4]
+    out, result, early, late, in_sems, out_sem = refs[2 * n + 4 :]
+    held = (early, late)
     c, z, x = place[2], place[3], place[4]
-    rows = out.shape[0]
+    rows = result.shape[0]
     half = rows // 2
     first = pl.multiple_of(c * half, half)
     second = pl.multiple_of((1 - c) * half, half)
+    arriving = [pltpu.make_async_copy(v, held[i // 2].at[i % 2], in_sems.at[i]) for i, v in enumerate(sums)]
+    for copy in arriving:
+        copy.start()
 
     def at(d, write):
         dx, dz = d
@@ -211,37 +216,44 @@
 
         @pl.when(zz // 2 == c)
         def _():
-            write(pl.multiple_of(((zz % 2) * 4 + xx) * rows, rows))
-
-    for i, d in stay:
-
-        def write(start, i=i):
-            out[:, pl.ds(start, rows)] = sums[0][i, :, :] + sums[1][i, :, :]
-
-        at(d, write)
+            start = pl.multiple_of(((zz % 2) * 4 + xx) * rows, rows)
+            write(start)
+            columns = pl.ds(start, rows)
+            pltpu.make_async_copy(result.at[:, columns], out.at[:, columns], out_sem).start()
+
     for array, i, d, turned in tiles:
 
         def write(start, array=array, i=i, turned=turned):
             for ref, offset in ((own[array], first), (other[array], second)):
                 tile = part_of(ref, i, half)
                 if turned:
-                    out[:, pl.ds(pl.multiple_of(start + offset, half), half)] = tile.T
+                    result[:, pl.ds(pl.multiple_of(start + offset, half), half)] = tile.T
                 else:
-                    out[pl.ds(offset, half), pl.ds(start, rows)] = tile
+                    result[pl.ds(offset, half), pl.ds(start, rows)] = tile
 
         at(d, write)
+    for copy in arriving:
+        copy.wait()
+    for stage, i, d in stay:
+
+        def write(start, stage=stage, i=i):
+            result[:, pl.ds(start, rows)] = held[stage][0, i, :, :] + held[stage][1, i, :, :]
+
+        at(d, write)
+    pltpu.make_async_copy(result, out, out_sem).wait()
 
 
 O, PX, MX, PZ, MZ, PE, ME = (0, 0), (1, 0), (3, 0), (0, 1), (0, 3), (1, 1), (3, 3)
-EARLY = ((O, O), (O, PX), (O, PZ), (MX, PX), (MZ, PZ), (MZ, PX), (PZ, PX))
-LATE = ((ME, PX), (ME, PZ), (ME, PE))
-STAY = 3
+EARLY = ((O, PX), (O, PZ), (MX, PX), (MZ, PZ), (MZ, PX), (PZ, PX))
+LATE = ((O, O), (ME, PX), (ME, PZ), (ME, PE))
+CLASSES = EARLY + LATE
+STAY = (2, 1)
 SENDS = (
-    (PX, True, (1, 3, 5, 6, 7)),
-    (PZ, True, (2, 8)),
+    (PX, True, (0, 2, 4, 5, 7)),
+    (PZ, True, (1, 8)),
     (ME, False, (7, 8, 9)),
-    (MZ, False, (4, 5)),
-    (PZ, False, (6,)),
+    (MZ, False, (3, 4)),
+    (PZ, False, (5,)),
 )
 OWN = {
     O: ("o", "o"),
@@ -277,14 +289,15 @@
     held["q4"] = fetch(held["o"], MX, MZ)
     held["pe"] = fetch(held["q1"], PX, PZ)
     held["me"] = fetch(held["q3"], MX, MZ)
-    for name, source in (("so", "o"), ("s1", "q1"), ("s2", "q2")):
+    for name, source in (("s1", "q1"), ("s2", "q2")):
         held[name] = move(held[source], to_core)
 
     coded, after = [], ()
     for classes in (EARLY, LATE):
         if after:
-            first, _ = lax.optimization_barrier((held["pe"], after[0]))
-            held["spe"] = move(first, to_core)
+            first, second, _ = lax.optimization_barrier((held["o"], held["pe"], after[0]))
+            held["so"] = move(first, to_core)
+            held["spe"] = move(second, to_core)
         listed = [(OWN[r], OWN[q], OTHER[q]) for r, q in classes]
         used = {i for k in listed for pair in k for i in pair}
         arrays = {name: v for name, v in held.items() if name in used}
@@ -292,26 +305,29 @@
         after = (coded[-1][0],)
 
     sums = []
-    for classes, stage, whole, weight in zip((EARLY, LATE), coded, (STAY, 0), (1, 10**11)):
+    for classes, stage, whole, weight in zip((EARLY, LATE), coded, STAY, (1, 10**11)):
         halves = jax.ShapeDtypeStruct((len(classes) - whole, rows // 2, rows), jnp.float32)
-        full = [jax.ShapeDtypeStruct((whole, rows, rows), jnp.float32)] * (whole > 0)
-        *full, kept, given = call(
+        full = jax.ShapeDtypeStruct((whole, rows, rows), jnp.float32)
+        full, kept, given = call(
             functools.partial(sum_kernel, whole),
-            [place, *(move(v, to_owner(m1)) for m1, v in enumerate(stage)), *after],
-            [*full, halves, halves],
+            [place, *(move(v, to_owner(m1)) for m1, v in zip((1, 0), stage)), *after],
+            [full, halves, halves],
             any_from=3,
             flops=weight,
             moved=weight,
             transcendentals=weight,
         )
-        sums += [v for f in full for v in (f, move(f, to_core))] + [kept, move(given, to_core)]
-
-    where = {k: (0, k) for k in range(1, STAY)}
-    where |= {k: (1, k - STAY) for k in range(STAY, len(EARLY))}
-    where |= {len(EARLY) + k: (2, k) for k in range(len(LATE))}
+        sums += [full, move(full, to_core), kept, move(given, to_core)]
+
+    where = {}
+    for stage, (classes, whole) in enumerate(zip((EARLY, LATE), STAY)):
+        for k in range(len(classes)):
+            pair = (2 * stage, k) if k < whole else (2 * stage + 1, k - whole)
+            where[len(where)] = pair
+    sent = {k: where[k] for k in range(len(CLASSES)) if any(k in m for _, _, m in SENDS)}
     groups = tuple(members for _, _, members in SENDS)
     parts = call(
-        functools.partial(group_kernel, where, groups),
+        functools.partial(group_kernel, sent, groups),
         [place, *sums],
         [coded_shape(len(g), rows // 2, rows) for g in groups],
         moved=4 << 20,
@@ -319,18 +335,27 @@
     own, tiles = [], []
     for j, (part, (to, turned, members)) in enumerate(zip(parts, SENDS)):
         for i, k in enumerate(members):
-            r, q = (EARLY + LATE)[k]
+            r, q = CLASSES[k]
             tiles.append((j, i, minus(r, q) if turned else minus(q, r), turned))
         own.append(move(part, to_position(*to, swap=turned)))
     own = lax.optimization_barrier(own)
     other = [move(v, to_core) for v in own]
-    stay = tuple((k, minus(q, r)) for k, (r, q) in enumerate(EARLY[:STAY]))
+    stay = tuple(
+        (where[k][0] // 2, where[k][1], minus(q, r)) for k, (r, q) in enumerate(CLASSES) if where[k][0] % 2 == 0
+    )
     return call(
         functools.partial(place_kernel, stay, tuple(tiles), len(own)),
-        [place, *sums[:2], *own, *other],
+        [place, *own, *other, *sums[:2], *sums[4:6]],
         jax.ShapeDtypeStruct((rows, 8 * rows), jnp.float32),
+        scratch=[
+            pltpu.VMEM((rows, 8 * rows), jnp.float32),
+            *(pltpu.VMEM((2, n, rows, rows), jnp.float32) for n in STAY),
+            pltpu.SemaphoreType.DMA((4,)),
+            pltpu.SemaphoreType.DMA,
+        ],
+        any_from=1 + 2 * len(own),
+        out_any=True,
         moved=6 << 20,
-        transcendentals=1 << 20,
     )
 
 

time: 119 us -> 114 us (0.958)
  waiting for transfers between devices: 59.1 us -> 53.3 us
  starting transfers between devices: 33.4 us -> 36.3 us
  Pallas kernels: 24.6 us -> 22.5 us
    ppermute x28 -> x29, waiting for transfers between devices: 59.1 us -> 53.3 us  [move(): return lax.ppermute(value, ('aux', 'blk'), pairs)]
    ppermute x28 -> x29, starting transfers between devices: 33.4 us -> 36.3 us  [move(): return lax.ppermute(value, ('aux', 'blk'), pairs)]
    pallas_call x6, Pallas kernels: 24.6 us -> 22.5 us  [call(): pl.pallas_call(kernel, out_shape=out_shape, in_specs=specs, out_specs=[wh...]
  transfers between devices with their start and end apart: 28 -> 29, of which waited for: 13 -> 12; matrix products, arithmetic and copies ran while one was open for 0% -> 0% of each run, Pallas kernels for 16% -> 16%
where the time goes in v5:
time: 114 us
  waiting for transfers between devices  53.3 us (47%)
  starting transfers between devices  36.3 us (32%)
  Pallas kernels  22.5 us (20%)
  local copies, waits for them, and re-layouts  1.58 us (1%)
    ppermute x29, waiting for transfers between devices, move(): return lax.ppermute(value, ('aux', 'blk'), pairs)  53.3 us
    ppermute x29, starting transfers between devices, move(): return lax.ppermute(value, ('aux', 'blk'), pairs)  36.3 us
    pallas_call x6, Pallas kernels, call(): pl.pallas_call(kernel, out_shape=out_shape, in_specs=specs, out_specs=[wh...  22.5 us
  transfers between devices with their start and end apart: 29, of which 12 were waited for; matrix products, arithmetic and copies ran while one was open for 0% of the time, Pallas kernels for 16%

profile of v5, /device:TPU:9, one launch (start us, length us, event | category | flops | bytes accessed | tf_op | source)
XLA Modules:
  0.0 114.0 jit_solution(6876952939431234999)
XLA Ops:
  0.0 1.5 %copy.4 = bf16[32,8,16,128]{3,1,2,0:T(8,128)(2,1)S(1)} copy(bf16[32,8,16,128]{3,2,1,0:T(8,128)(2,1)} %bitcast.9) | data formatting | bytes 2097152
  1.5 4.5 %collective-permute-start = (bf16[256,2048]{1,0:T(8,128)(2,1)S(1)}, bf16[256,2048]{1,0:T(8,128)(2,1)S(1)}, u32[]{:S(2)}, u32[]{:S(2)}) collective-permute-start(bf16[256,2048]{1,0:T(8,128)(2,1)S(1)} %bitcast.10), channel_id=1, source_target_pairs={{0,0},{1,1},{2,2},{3,3},{4,4},{5,5},{6,6},{7,7},{8,8},{9,9},{10,10... | collective-permute-start | bytes 3145736 | tf_op jit(solution)/shard_map/ppermute | solution.py:29
  6.0 13.5 %collective-permute-done.refs_0_ = bf16[256,2048]{1,0:T(8,128)(2,1)S(1)} collective-permute-done((bf16[256,2048]{1,0:T(8,128)(2,1)S(1)}, bf16[256,2048]{1,0:T(8,128)(2,1)S(1)}, u32[]{:S(2)}, u32[]{:S(2)}) %collective-permute-start) | collective-permute-done | bytes 1048608 | tf_op jit(solution)/shard_map/ppermute | solution.py:29
  19.5 2.5 %collective-permute-start.1 = (bf16[256,2048]{1,0:T(8,128)(2,1)S(1)}, bf16[256,2048]{1,0:T(8,128)(2,1)S(1)}, u32[]{:S(2)}, u32[]{:S(2)}) collective-permute-start(bf16[256,2048]{1,0:T(8,128)(2,1)S(1)} %collective-permute-done.refs_0_), channel_id=1, source_target_pairs={{0,12},{1,13},{2,14},{3,15},{4,0},{5,1},{6,2},{7,3},{8,4},{9,5},{1... | collective-permute-start | bytes 3145736 | tf_op jit(solution)/shard_map/ppermute | solution.py:29
  22.0 3.4 %collective-permute-start.2 = (bf16[256,2048]{1,0:T(8,128)(2,1)S(1)}, bf16[256,2048]{1,0:T(8,128)(2,1)S(1)}, u32[]{:S(2)}, u32[]{:S(2)}) collective-permute-start(bf16[256,2048]{1,0:T(8,128)(2,1)S(1)} %collective-permute-done.refs_0_), channel_id=1, source_target_pairs={{0,3},{1,0},{2,1},{3,2},{4,7},{5,4},{6,5},{7,6},{8,11},{9,8},{10,9... | collective-permute-start | bytes 3145736 | tf_op jit(solution)/shard_map/ppermute | solution.py:29
  25.4 8.4 %collective-permute-done.1.refs_1_ = bf16[256,2048]{1,0:T(8,128)(2,1)S(1)} collective-permute-done((bf16[256,2048]{1,0:T(8,128)(2,1)S(1)}, bf16[256,2048]{1,0:T(8,128)(2,1)S(1)}, u32[]{:S(2)}, u32[]{:S(2)}) %collective-permute-start.1) | collective-permute-done | bytes 1048608 | tf_op jit(solution)/shard_map/ppermute | solution.py:29
  33.7 3.4 %collective-permute-done.2.refs_2_ = bf16[256,2048]{1,0:T(8,128)(2,1)S(1)} collective-permute-done((bf16[256,2048]{1,0:T(8,128)(2,1)S(1)}, bf16[256,2048]{1,0:T(8,128)(2,1)S(1)}, u32[]{:S(2)}, u32[]{:S(2)}) %collective-permute-start.2) | collective-permute-done | bytes 1048608 | tf_op jit(solution)/shard_map/ppermute | solution.py:29
  37.1 0.0 collective-permute-start.6
  37.1 3.1 %collective-permute-start.9 = (bf16[256,2048]{1,0:T(8,128)(2,1)S(1)}, bf16[256,2048]{1,0:T(8,128)(2,1)}, u32[]{:S(2)}, u32[]{:S(2)}) collective-permute-start(bf16[256,2048]{1,0:T(8,128)(2,1)S(1)} %collective-permute-done.1.refs_1_), channel_id=1, source_target_pairs={{0,3},{1,0},{2,1},{3,2},{4,7},{5,4},{6,5},{7,6},{8,11},{9,8},{10,9... | collective-permute-start | bytes 3145736 | tf_op jit(solution)/shard_map/ppermute | solution.py:29
  40.2 0.1 stack.23.place
  40.3 0.0 collective-permute-done.3.refs_3_
  40.3 0.0 collective-permute-start.10
  40.3 0.0 collective-permute-done.5.refs_5_
  40.4 0.0 collective-permute-done.6.refs_6_
  40.4 8.1 %shard_map.17 = (bf16[1552,256]{1,0:T(8,128)(2,1)S(1)}, bf16[1552,256]{1,0:T(8,128)(2,1)S(1)}) custom-call(s32[5]{0:T(128)S(1)} %stack.23.place, bf16[256,2048]{1,0:T(8,128)(2,1)S(1)} %collective-permute-done.refs_0_, bf16[256,2048]{1,0:T(8,128)(2,1)S(1)} %collective-permute-done.1.refs_1_, bf16[256,2048]{1,0:T(8,128)(2,1)S(1)} %collective-permute-done.2.refs_2_, ...), custom_call_target="tpu_custom_call" | custom-call | flops 3221225472 | bytes 7340032 | tf_op jit(solution)/shard_map/pallas_call | solution.py:103
  48.4 3.5 %collective-permute-done.9.refs_3_ = bf16[256,2048]{1,0:T(8,128)(2,1)} collective-permute-done((bf16[256,2048]{1,0:T(8,128)(2,1)S(1)}, bf16[256,2048]{1,0:T(8,128)(2,1)}, u32[]{:S(2)}, u32[]{:S(2)}) %collective-permute-start.9) | collective-permute-done | bytes 1048608 | tf_op jit(solution)/shard_map/ppermute | solution.py:29
  52.0 0.6 collective-permute-start.11
  52.5 0.0 collective-permute-start.12
  52.5 4.1 %collective-permute-start.7 = (bf16[1552,256]{1,0:T(8,128)(2,1)S(1)}, bf16[1552,256]{1,0:T(8,128)(2,1)S(1)}, u32[]{:S(2)}, u32[]{:S(2)}) collective-permute-start(bf16[1552,256]{1,0:T(8,128)(2,1)S(1)} %get-tuple-element.27.refs_9_), channel_id=1, source_target_pairs={{0,64},{1,65},{2,66},{3,67},{4,68},{5,69},{6,70},{7,71},{8,72},{9,... | collective-permute-start | bytes 2383880 | tf_op jit(solution)/shard_map/ppermute | solution.py:29
  56.6 2.8 %collective-permute-start.8 = (bf16[1552,256]{1,0:T(8,128)(2,1)S(1)}, bf16[1552,256]{1,0:T(8,128)(2,1)S(1)}, u32[]{:S(2)}, u32[]{:S(2)}) collective-permute-start(bf16[1552,256]{1,0:T(8,128)(2,1)S(1)} %get-tuple-element.28), channel_id=1, source_target_pairs={{0,0},{1,1},{2,2},{3,3},{4,4},{5,5},{6,6},{7,7},{8,8},{9,9},{10,10... | collective-permute-start | bytes 2383880 | tf_op jit(solution)/shard_map/ppermute | solution.py:29
  59.5 5.8 %shard_map.18 = (bf16[1040,256]{1,0:T(8,128)(2,1)S(1)}, bf16[1040,256]{1,0:T(8,128)(2,1)S(1)}) custom-call(s32[5]{0:T(128)S(1)} %stack.23.place, bf16[256,2048]{1,0:T(8,128)(2,1)S(1)} %collective-permute-done.refs_0_, bf16[256,2048]{1,0:T(8,128)(2,1)S(1)} %collective-permute-done.1.refs_1_, bf16[256,2048]{1,0:T(8,128)(2,1)S(1)} %collective-permute-done.2.refs_2_, ...), custom_call_target="tpu_custom_call" | custom-call | flops 2147483648 | bytes 9437184 | tf_op jit(solution)/shard_map/pallas_call | solution.py:103
  65.2 2.4 %collective-permute-start.15 = (bf16[1040,256]{1,0:T(8,128)(2,1)S(1)}, bf16[1040,256]{1,0:T(8,128)(2,1)S(1)}, u32[]{:S(2)}, u32[]{:S(2)}) collective-permute-start(bf16[1040,256]{1,0:T(8,128)(2,1)S(1)} %get-tuple-element.31._), channel_id=1, source_target_pairs={{0,64},{1,65},{2,66},{3,67},{4,68},{5,69},{6,70},{7,71},{8,72},{9,... | collective-permute-start | bytes 1597448 | tf_op jit(solution)/shard_map/ppermute | solution.py:29
  67.7 2.7 %collective-permute-start.16 = (bf16[1040,256]{1,0:T(8,128)(2,1)S(1)}, bf16[1040,256]{1,0:T(8,128)(2,1)S(1)}, u32[]{:S(2)}, u32[]{:S(2)}) collective-permute-start(bf16[1040,256]{1,0:T(8,128)(2,1)S(1)} %get-tuple-element.35), channel_id=1, source_target_pairs={{0,0},{1,1},{2,2},{3,3},{4,4},{5,5},{6,6},{7,7},{8,8},{9,9},{10,10... | collective-permute-start | bytes 1597448 | tf_op jit(solution)/shard_map/ppermute | solution.py:29
  70.4 0.2 collective-permute-done.7.a
  70.6 9.5 %collective-permute-done.8.b = bf16[1552,256]{1,0:T(8,128)(2,1)S(1)} collective-permute-done((bf16[1552,256]{1,0:T(8,128)(2,1)S(1)}, bf16[1552,256]{1,0:T(8,128)(2,1)S(1)}, u32[]{:S(2)}, u32[]{:S(2)}) %collective-permute-start.8) | collective-permute-done | bytes 794656 | tf_op jit(solution)/shard_map/ppermute | solution.py:29
  80.1 2.7 %shard_map.19 = (f32[2,256,256]{2,1,0:T(8,128)}, f32[4,128,256]{2,1,0:T(8,128)S(1)}, f32[4,128,256]{2,1,0:T(8,128)}) custom-call(s32[5]{0:T(128)S(1)} %stack.23.place, bf16[1552,256]{1,0:T(8,128)(2,1)S(1)} %collective-permute-done.7.a, bf16[1552,256]{1,0:T(8,128)(2,1)S(1)} %collective-permute-done.8.b, bf16[1040,256]{1,0:T(8,128)(2,1)S(1)} %get-tuple-element.31._), custom_call_target="tpu_custom_call" | custom-call | flops 1 | bytes 1 | tf_op jit(solution)/shard_map/pallas_call | solution.py:103
  82.8 0.5 collective-permute-start.14
  83.3 2.3 %collective-permute-done.15.a = bf16[1040,256]{1,0:T(8,128)(2,1)S(1)} collective-permute-done((bf16[1040,256]{1,0:T(8,128)(2,1)S(1)}, bf16[1040,256]{1,0:T(8,128)(2,1)S(1)}, u32[]{:S(2)}, u32[]{:S(2)}) %collective-permute-start.15) | collective-permute-done | bytes 532512 | tf_op jit(solution)/shard_map/ppermute | solution.py:29
  85.6 1.2 %collective-permute-done.16.b = bf16[1040,256]{1,0:T(8,128)(2,1)S(1)} collective-permute-done((bf16[1040,256]{1,0:T(8,128)(2,1)S(1)}, bf16[1040,256]{1,0:T(8,128)(2,1)S(1)}, u32[]{:S(2)}, u32[]{:S(2)}) %collective-permute-start.16) | collective-permute-done | bytes 532512 | tf_op jit(solution)/shard_map/ppermute | solution.py:29
  86.8 1.4 %shard_map.20 = (f32[1,256,256]{2,1,0:T(8,128)S(1)}, f32[3,128,256]{2,1,0:T(8,128)S(1)}, f32[3,128,256]{2,1,0:T(8,128)S(1)}) custom-call(s32[5]{0:T(128)S(1)} %stack.23.place, bf16[1040,256]{1,0:T(8,128)(2,1)S(1)} %collective-permute-done.15.a, bf16[1040,256]{1,0:T(8,128)(2,1)S(1)} %collective-permute-done.16.b, bf16[1040,256]{1,0:T(8,128)(2,1)S(1)} %get-tuple-element.31._), custom_call_target="tpu_custom_call" | custom-call | flops 99999997952 | bytes 99999997952 | tf_op jit(solution)/shard_map/pallas_call | solution.py:103
  88.2 0.1 collective-permute-start.18
  88.3 0.5 collective-permute-start.17
  88.8 1.6 %collective-permute-done.17.refs_5_.refs_13_ = f32[1,256,256]{2,1,0:T(8,128)S(1)} collective-permute-done((f32[1,256,256]{2,1,0:T(8,128)S(1)}, f32[1,256,256]{2,1,0:T(8,128)S(1)}, u32[]{:S(2)}, u32[]{:S(2)}) %collective-permute-start.17) | collective-permute-done | bytes 262176 | tf_op jit(solution)/shard_map/ppermute | solution.py:29
  90.4 2.1 %shard_map.21 = (bf16[656,256]{1,0:T(8,128)(2,1)S(1)}, bf16[272,256]{1,0:T(8,128)(2,1)S(1)}, bf16[400,256]{1,0:T(8,128)(2,1)S(1)}, bf16[272,256]{1,0:T(8,128)(2,1)S(1)}, bf16[144,256]{1,0:T(8,128)(2,1)S(1)}) custom-call(s32[5]{0:T(128)S(1)} %stack.23.place, f32[2,256,256]{2,1,0:T(8,128)} %get-tuple-element.32.refs_0_.refs_10_, ...), custom_call_target="tpu_custom_call" | custom-call | bytes 4194304 | tf_op jit(solution)/shard_map/pallas_call | solution.py:103
  92.5 0.6 collective-permute-start.19
  93.1 3.7 %collective-permute-start.21 = (bf16[400,256]{1,0:T(8,128)(2,1)S(1)}, bf16[400,256]{1,0:T(8,128)(2,1)S(1)}, u32[]{:S(2)}, u32[]{:S(2)}) collective-permute-start(bf16[400,256]{1,0:T(8,128)(2,1)S(1)} %get-tuple-element.41), channel_id=1, source_target_pairs={{0,15},{1,12},{2,13},{3,14},{4,3},{5,0},{6,1},{7,2},{8,7},{9,4},{1... | collective-permute-start | bytes 614408 | tf_op jit(solution)/shard_map/ppermute | solution.py:29
  96.8 1.2 %collective-permute-start.20 = (bf16[272,256]{1,0:T(8,128)(2,1)S(1)}, bf16[272,256]{1,0:T(8,128)(2,1)S(1)}, u32[]{:S(2)}, u32[]{:S(2)}) collective-permute-start(bf16[272,256]{1,0:T(8,128)(2,1)S(1)} %get-tuple-element.40), channel_id=1, source_target_pairs={{0,4},{1,5},{2,6},{3,7},{4,8},{5,9},{6,10},{7,11},{8,12},{9,13},{1... | collective-permute-start | bytes 417800 | tf_op jit(solution)/shard_map/ppermute | solution.py:29
  98.0 1.4 %collective-permute-start.22 = (bf16[272,256]{1,0:T(8,128)(2,1)S(1)}, bf16[272,256]{1,0:T(8,128)(2,1)S(1)}, u32[]{:S(2)}, u32[]{:S(2)}) collective-permute-start(bf16[272,256]{1,0:T(8,128)(2,1)S(1)} %get-tuple-element.42), channel_id=1, source_target_pairs={{0,12},{1,13},{2,14},{3,15},{4,0},{5,1},{6,2},{7,3},{8,4},{9,5},{1... | collective-permute-start | bytes 417800 | tf_op jit(solution)/shard_map/ppermute | solution.py:29
  99.5 0.0 collective-permute-start.23
  99.5 4.7 %collective-permute-done.23.refs_4_ = bf16[144,256]{1,0:T(8,128)(2,1)S(1)} collective-permute-done((bf16[144,256]{1,0:T(8,128)(2,1)S(1)}, bf16[144,256]{1,0:T(8,128)(2,1)S(1)}, u32[]{:S(2)}, u32[]{:S(2)}) %collective-permute-start.23) | collective-permute-done | bytes 73760 | tf_op jit(solution)/shard_map/ppermute | solution.py:29
  104.2 3.9 %collective-permute-done.20.refs_1_ = bf16[272,256]{1,0:T(8,128)(2,1)S(1)} collective-permute-done((bf16[272,256]{1,0:T(8,128)(2,1)S(1)}, bf16[272,256]{1,0:T(8,128)(2,1)S(1)}, u32[]{:S(2)}, u32[]{:S(2)}) %collective-permute-start.20) | collective-permute-done | bytes 139296 | tf_op jit(solution)/shard_map/ppermute | solution.py:29
  108.1 1.1 collective-permute-start.24
  109.3 0.1 collective-permute-start.26
  109.3 0.4 collective-permute-start.25
  109.8 0.1 collective-permute-start.27
  109.9 0.4 collective-permute-start.28
  110.3 1.0 collective-permute-done.28.refs_9_
  111.3 2.5 %shard_map.22 = f32[256,2048]{1,0:T(8,128)} custom-call(s32[5]{0:T(128)S(1)} %stack.23.place, bf16[656,256]{1,0:T(8,128)(2,1)S(1)} %collective-permute-done.19.refs_0_, bf16[272,256]{1,0:T(8,128)(2,1)S(1)} %collective-permute-done.20.refs_1_, bf16[400,256]{1,0:T(8,128)(2,1)S(1)} %collective-permute-done.21.refs_2_, ...), custom_call_target="tpu_custom_call" | custom-call | bytes 6291456 | tf_op jit(solution)/shard_map/pallas_call | solution.py:103
  (18 shorter events, 0.0 us)
Async XLA Ops:
  1.5 18.0 %collective-permute-start = (bf16[256,2048]{1,0:T(8,128)(2,1)S(1)}, bf16[256,2048]{1,0:T(8,128)(2,1)S(1)}, u32[]{:S(2)}, u32[]{:S(2)}) collective-permute-start(bf16[256,2048]{1,0:T(8,128)(2,1)S(1)} %bitcast.10), channel_id=1, source_target_pairs={{0,0},{1,1},{2,2},{3,3},{4,4},{5,5},{6,6},{7,7},{8,8},{9,9},{10,10... | collective-permute-start | bytes 3145736 | tf_op jit(solution)/shard_map/ppermute | solution.py:29
  19.5 14.2 %collective-permute-start.1 = (bf16[256,2048]{1,0:T(8,128)(2,1)S(1)}, bf16[256,2048]{1,0:T(8,128)(2,1)S(1)}, u32[]{:S(2)}, u32[]{:S(2)}) collective-permute-start(bf16[256,2048]{1,0:T(8,128)(2,1)S(1)} %collective-permute-done.refs_0_), channel_id=1, source_target_pairs={{0,12},{1,13},{2,14},{3,15},{4,0},{5,1},{6,2},{7,3},{8,4},{9,5},{1... | collective-permute-start | bytes 3145736 | tf_op jit(solution)/shard_map/ppermute | solution.py:29
  22.0 15.1 %collective-permute-start.2 = (bf16[256,2048]{1,0:T(8,128)(2,1)S(1)}, bf16[256,2048]{1,0:T(8,128)(2,1)S(1)}, u32[]{:S(2)}, u32[]{:S(2)}) collective-permute-start(bf16[256,2048]{1,0:T(8,128)(2,1)S(1)} %collective-permute-done.refs_0_), channel_id=1, source_target_pairs={{0,3},{1,0},{2,1},{3,2},{4,7},{5,4},{6,5},{7,6},{8,11},{9,8},{10,9... | collective-permute-start | bytes 3145736 | tf_op jit(solution)/shard_map/ppermute | solution.py:29
  25.4 15.0 %collective-permute-start.3 = (bf16[256,2048]{1,0:T(8,128)(2,1)S(1)}, bf16[256,2048]{1,0:T(8,128)(2,1)}, u32[]{:S(2)}, u32[]{:S(2)}) collective-permute-start(bf16[256,2048]{1,0:T(8,128)(2,1)S(1)} %collective-permute-done.refs_0_), channel_id=1, source_target_pairs={{0,4},{1,5},{2,6},{3,7},{4,8},{5,9},{6,10},{7,11},{8,12},{9,13},{1... | collective-permute-start | bytes 3145736 | tf_op jit(solution)/shard_map/ppermute | solution.py:29
  25.4 15.0 %collective-permute-start.4 = (bf16[256,2048]{1,0:T(8,128)(2,1)S(1)}, bf16[256,2048]{1,0:T(8,128)(2,1)}, u32[]{:S(2)}, u32[]{:S(2)}) collective-permute-start(bf16[256,2048]{1,0:T(8,128)(2,1)S(1)} %collective-permute-done.refs_0_), channel_id=1, source_target_pairs={{0,1},{1,2},{2,3},{3,0},{4,5},{5,6},{6,7},{7,4},{8,9},{9,10},{10,1... | collective-permute-start | bytes 3145736 | tf_op jit(solution)/shard_map/ppermute | solution.py:29
  33.7 6.6 %collective-permute-start.5 = (bf16[256,2048]{1,0:T(8,128)(2,1)S(1)}, bf16[256,2048]{1,0:T(8,128)(2,1)}, u32[]{:S(2)}, u32[]{:S(2)}) collective-permute-start(bf16[256,2048]{1,0:T(8,128)(2,1)S(1)} %collective-permute-done.1.refs_1_), channel_id=1, source_target_pairs={{0,32},{1,33},{2,34},{3,35},{4,36},{5,37},{6,38},{7,39},{8,40},{9,... | collective-permute-start | bytes 3145736 | tf_op jit(solution)/shard_map/ppermute | solution.py:29
  37.1 3.2 %collective-permute-start.6 = (bf16[256,2048]{1,0:T(8,128)(2,1)S(1)}, bf16[256,2048]{1,0:T(8,128)(2,1)}, u32[]{:S(2)}, u32[]{:S(2)}) collective-permute-start(bf16[256,2048]{1,0:T(8,128)(2,1)S(1)} %collective-permute-done.2.refs_2_), channel_id=1, source_target_pairs={{0,32},{1,33},{2,34},{3,35},{4,36},{5,37},{6,38},{7,39},{8,40},{9,... | collective-permute-start | bytes 3145736 | tf_op jit(solution)/shard_map/ppermute | solution.py:29
  37.1 14.9 %collective-permute-start.9 = (bf16[256,2048]{1,0:T(8,128)(2,1)S(1)}, bf16[256,2048]{1,0:T(8,128)(2,1)}, u32[]{:S(2)}, u32[]{:S(2)}) collective-permute-start(bf16[256,2048]{1,0:T(8,128)(2,1)S(1)} %collective-permute-done.1.refs_1_), channel_id=1, source_target_pairs={{0,3},{1,0},{2,1},{3,2},{4,7},{5,4},{6,5},{7,6},{8,11},{9,8},{10,9... | collective-permute-start | bytes 3145736 | tf_op jit(solution)/shard_map/ppermute | solution.py:29
  40.3 19.1 %collective-permute-start.10 = (bf16[256,2048]{1,0:T(8,128)(2,1)}, bf16[256,2048]{1,0:T(8,128)(2,1)S(1)}, u32[]{:S(2)}, u32[]{:S(2)}) collective-permute-start(bf16[256,2048]{1,0:T(8,128)(2,1)} %collective-permute-done.3.refs_3_), channel_id=1, source_target_pairs={{0,1},{1,2},{2,3},{3,0},{4,5},{5,6},{6,7},{7,4},{8,9},{9,10},{10,1... | collective-permute-start | bytes 3145736 | tf_op jit(solution)/shard_map/ppermute | solution.py:29
  52.0 7.5 %collective-permute-start.11 = (bf16[256,2048]{1,0:T(8,128)(2,1)S(1)}, bf16[256,2048]{1,0:T(8,128)(2,1)S(1)}, u32[]{:S(2)}, u32[]{:S(2)}) collective-permute-start(bf16[256,2048]{1,0:T(8,128)(2,1)S(1)} %collective-permute-done.refs_0_), channel_id=1, source_target_pairs={{0,32},{1,33},{2,34},{3,35},{4,36},{5,37},{6,38},{7,39},{8,40},{9,... | collective-permute-start | bytes 3145736 | tf_op jit(solution)/shard_map/ppermute | solution.py:29
  52.5 6.9 %collective-permute-start.12 = (bf16[256,2048]{1,0:T(8,128)(2,1)}, bf16[256,2048]{1,0:T(8,128)(2,1)S(1)}, u32[]{:S(2)}, u32[]{:S(2)}) collective-permute-start(bf16[256,2048]{1,0:T(8,128)(2,1)} %collective-permute-done.9.refs_3_), channel_id=1, source_target_pairs={{0,32},{1,33},{2,34},{3,35},{4,36},{5,37},{6,38},{7,39},{8,40},{9,... | collective-permute-start | bytes 3145736 | tf_op jit(solution)/shard_map/ppermute | solution.py:29
  52.5 18.0 %collective-permute-start.7 = (bf16[1552,256]{1,0:T(8,128)(2,1)S(1)}, bf16[1552,256]{1,0:T(8,128)(2,1)S(1)}, u32[]{:S(2)}, u32[]{:S(2)}) collective-permute-start(bf16[1552,256]{1,0:T(8,128)(2,1)S(1)} %get-tuple-element.27.refs_9_), channel_id=1, source_target_pairs={{0,64},{1,65},{2,66},{3,67},{4,68},{5,69},{6,70},{7,71},{8,72},{9,... | collective-permute-start | bytes 2383880 | tf_op jit(solution)/shard_map/ppermute | solution.py:29
  56.6 23.5 %collective-permute-start.8 = (bf16[1552,256]{1,0:T(8,128)(2,1)S(1)}, bf16[1552,256]{1,0:T(8,128)(2,1)S(1)}, u32[]{:S(2)}, u32[]{:S(2)}) collective-permute-start(bf16[1552,256]{1,0:T(8,128)(2,1)S(1)} %get-tuple-element.28), channel_id=1, source_target_pairs={{0,0},{1,1},{2,2},{3,3},{4,4},{5,5},{6,6},{7,7},{8,8},{9,9},{10,10... | collective-permute-start | bytes 2383880 | tf_op jit(solution)/shard_map/ppermute | solution.py:29
  65.2 20.3 %collective-permute-start.15 = (bf16[1040,256]{1,0:T(8,128)(2,1)S(1)}, bf16[1040,256]{1,0:T(8,128)(2,1)S(1)}, u32[]{:S(2)}, u32[]{:S(2)}) collective-permute-start(bf16[1040,256]{1,0:T(8,128)(2,1)S(1)} %get-tuple-element.31._), channel_id=1, source_target_pairs={{0,64},{1,65},{2,66},{3,67},{4,68},{5,69},{6,70},{7,71},{8,72},{9,... | collective-permute-start | bytes 1597448 | tf_op jit(solution)/shard_map/ppermute | solution.py:29
  67.7 19.1 %collective-permute-start.16 = (bf16[1040,256]{1,0:T(8,128)(2,1)S(1)}, bf16[1040,256]{1,0:T(8,128)(2,1)S(1)}, u32[]{:S(2)}, u32[]{:S(2)}) collective-permute-start(bf16[1040,256]{1,0:T(8,128)(2,1)S(1)} %get-tuple-element.35), channel_id=1, source_target_pairs={{0,0},{1,1},{2,2},{3,3},{4,4},{5,5},{6,6},{7,7},{8,8},{9,9},{10,10... | collective-permute-start | bytes 1597448 | tf_op jit(solution)/shard_map/ppermute | solution.py:29
  82.8 6.0 %collective-permute-start.13 = (f32[2,256,256]{2,1,0:T(8,128)}, f32[2,256,256]{2,1,0:T(8,128)}, u32[]{:S(2)}, u32[]{:S(2)}) collective-permute-start(f32[2,256,256]{2,1,0:T(8,128)} %get-tuple-element.32.refs_0_.refs_10_), channel_id=1, source_target_pairs={{0,32},{1,33},{2,34},{3,35},{4,36},{5,37},{6,38},{7,39},{8,40},{9,... | collective-permute-start | bytes 1572872 | tf_op jit(solution)/shard_map/ppermute | solution.py:29
  82.8 6.0 %collective-permute-start.14 = (f32[4,128,256]{2,1,0:T(8,128)}, f32[4,128,256]{2,1,0:T(8,128)}, u32[]{:S(2)}, u32[]{:S(2)}) collective-permute-start(f32[4,128,256]{2,1,0:T(8,128)} %get-tuple-element.34), channel_id=1, source_target_pairs={{0,32},{1,33},{2,34},{3,35},{4,36},{5,37},{6,38},{7,39},{8,40},{9,... | collective-permute-start | bytes 1572872 | tf_op jit(solution)/shard_map/ppermute | solution.py:29
  88.2 2.2 %collective-permute-start.18 = (f32[3,128,256]{2,1,0:T(8,128)S(1)}, f32[3,128,256]{2,1,0:T(8,128)S(1)}, u32[]{:S(2)}, u32[]{:S(2)}) collective-permute-start(f32[3,128,256]{2,1,0:T(8,128)S(1)} %get-tuple-element.38), channel_id=1, source_target_pairs={{0,32},{1,33},{2,34},{3,35},{4,36},{5,37},{6,38},{7,39},{8,40},{9,... | collective-permute-start | bytes 1179656 | tf_op jit(solution)/shard_map/ppermute | solution.py:29
  88.3 2.1 %collective-permute-start.17 = (f32[1,256,256]{2,1,0:T(8,128)S(1)}, f32[1,256,256]{2,1,0:T(8,128)S(1)}, u32[]{:S(2)}, u32[]{:S(2)}) collective-permute-start(f32[1,256,256]{2,1,0:T(8,128)S(1)} %get-tuple-element.36.refs_4_.refs_12_), channel_id=1, source_target_pairs={{0,32},{1,33},{2,34},{3,35},{4,36},{5,37},{6,38},{7,39},{8,40},{9,... | collective-permute-start | bytes 786440 | tf_op jit(solution)/shard_map/ppermute | solution.py:29
  92.5 15.6 %collective-permute-start.19 = (bf16[656,256]{1,0:T(8,128)(2,1)S(1)}, bf16[656,256]{1,0:T(8,128)(2,1)S(1)}, u32[]{:S(2)}, u32[]{:S(2)}) collective-permute-start(bf16[656,256]{1,0:T(8,128)(2,1)S(1)} %get-tuple-element.39), channel_id=1, source_target_pairs={{0,1},{1,2},{2,3},{3,0},{4,5},{5,6},{6,7},{7,4},{8,9},{9,10},{10,1... | collective-permute-start | bytes 1007624 | tf_op jit(solution)/shard_map/ppermute | solution.py:29
  93.1 15.0 %collective-permute-start.21 = (bf16[400,256]{1,0:T(8,128)(2,1)S(1)}, bf16[400,256]{1,0:T(8,128)(2,1)S(1)}, u32[]{:S(2)}, u32[]{:S(2)}) collective-permute-start(bf16[400,256]{1,0:T(8,128)(2,1)S(1)} %get-tuple-element.41), channel_id=1, source_target_pairs={{0,15},{1,12},{2,13},{3,14},{4,3},{5,0},{6,1},{7,2},{8,7},{9,4},{1... | collective-permute-start | bytes 614408 | tf_op jit(solution)/shard_map/ppermute | solution.py:29
  96.8 11.3 %collective-permute-start.20 = (bf16[272,256]{1,0:T(8,128)(2,1)S(1)}, bf16[272,256]{1,0:T(8,128)(2,1)S(1)}, u32[]{:S(2)}, u32[]{:S(2)}) collective-permute-start(bf16[272,256]{1,0:T(8,128)(2,1)S(1)} %get-tuple-element.40), channel_id=1, source_target_pairs={{0,4},{1,5},{2,6},{3,7},{4,8},{5,9},{6,10},{7,11},{8,12},{9,13},{1... | collective-permute-start | bytes 417800 | tf_op jit(solution)/shard_map/ppermute | solution.py:29
  98.0 10.1 %collective-permute-start.22 = (bf16[272,256]{1,0:T(8,128)(2,1)S(1)}, bf16[272,256]{1,0:T(8,128)(2,1)S(1)}, u32[]{:S(2)}, u32[]{:S(2)}) collective-permute-start(bf16[272,256]{1,0:T(8,128)(2,1)S(1)} %get-tuple-element.42), channel_id=1, source_target_pairs={{0,12},{1,13},{2,14},{3,15},{4,0},{5,1},{6,2},{7,3},{8,4},{9,5},{1... | collective-permute-start | bytes 417800 | tf_op jit(solution)/shard_map/ppermute | solution.py:29
  99.5 4.7 %collective-permute-start.23 = (bf16[144,256]{1,0:T(8,128)(2,1)S(1)}, bf16[144,256]{1,0:T(8,128)(2,1)S(1)}, u32[]{:S(2)}, u32[]{:S(2)}) collective-permute-start(bf16[144,256]{1,0:T(8,128)(2,1)S(1)} %get-tuple-element.43), channel_id=1, source_target_pairs={{0,4},{1,5},{2,6},{3,7},{4,8},{5,9},{6,10},{7,11},{8,12},{9,13},{1... | collective-permute-start | bytes 221192 | tf_op jit(solution)/shard_map/ppermute | solution.py:29
  108.1 3.2 %collective-permute-start.24 = (bf16[656,256]{1,0:T(8,128)(2,1)S(1)}, bf16[656,256]{1,0:T(8,128)(2,1)S(1)}, u32[]{:S(2)}, u32[]{:S(2)}) collective-permute-start(bf16[656,256]{1,0:T(8,128)(2,1)S(1)} %collective-permute-done.19.refs_0_), channel_id=1, source_target_pairs={{0,32},{1,33},{2,34},{3,35},{4,36},{5,37},{6,38},{7,39},{8,40},{9,... | collective-permute-start | bytes 1007624 | tf_op jit(solution)/shard_map/ppermute | solution.py:29
  109.3 2.1 %collective-permute-start.26 = (bf16[400,256]{1,0:T(8,128)(2,1)S(1)}, bf16[400,256]{1,0:T(8,128)(2,1)S(1)}, u32[]{:S(2)}, u32[]{:S(2)}) collective-permute-start(bf16[400,256]{1,0:T(8,128)(2,1)S(1)} %collective-permute-done.21.refs_2_), channel_id=1, source_target_pairs={{0,32},{1,33},{2,34},{3,35},{4,36},{5,37},{6,38},{7,39},{8,40},{9,... | collective-permute-start | bytes 614408 | tf_op jit(solution)/shard_map/ppermute | solution.py:29
  109.3 2.0 %collective-permute-start.25 = (bf16[272,256]{1,0:T(8,128)(2,1)S(1)}, bf16[272,256]{1,0:T(8,128)(2,1)S(1)}, u32[]{:S(2)}, u32[]{:S(2)}) collective-permute-start(bf16[272,256]{1,0:T(8,128)(2,1)S(1)} %collective-permute-done.20.refs_1_), channel_id=1, source_target_pairs={{0,32},{1,33},{2,34},{3,35},{4,36},{5,37},{6,38},{7,39},{8,40},{9,... | collective-permute-start | bytes 417800 | tf_op jit(solution)/shard_map/ppermute | solution.py:29
  109.8 1.6 %collective-permute-start.27 = (bf16[272,256]{1,0:T(8,128)(2,1)S(1)}, bf16[272,256]{1,0:T(8,128)(2,1)S(1)}, u32[]{:S(2)}, u32[]{:S(2)}) collective-permute-start(bf16[272,256]{1,0:T(8,128)(2,1)S(1)} %collective-permute-done.22.refs_3_), channel_id=1, source_target_pairs={{0,32},{1,33},{2,34},{3,35},{4,36},{5,37},{6,38},{7,39},{8,40},{9,... | collective-permute-start | bytes 417800 | tf_op jit(solution)/shard_map/ppermute | solution.py:29
  109.9 1.5 %collective-permute-start.28 = (bf16[144,256]{1,0:T(8,128)(2,1)S(1)}, bf16[144,256]{1,0:T(8,128)(2,1)S(1)}, u32[]{:S(2)}, u32[]{:S(2)}) collective-permute-start(bf16[144,256]{1,0:T(8,128)(2,1)S(1)} %collective-permute-done.23.refs_4_), channel_id=1, source_target_pairs={{0,32},{1,33},{2,34},{3,35},{4,36},{5,37},{6,38},{7,39},{8,40},{9,... | collective-permute-start | bytes 221192 | tf_op jit(solution)/shard_map/ppermute | solution.py:29

commit v6 on v5

--- a/solution.py
+++ b/solution.py
@@ -45,9 +45,9 @@
     return where
 
 
-def to_owner(m1):
+def to_owner(m1, m2=0):
     def where(x, z, yh, yl, c):
-        return x, z, c, yl ^ m1, yh
+        return x, z, c, yl ^ m1, yh ^ m2
 
     return where
 
@@ -111,11 +111,17 @@
     )(*args)
 
 
-def tiles_kernel(classes, n_in, n_extra, place, *refs):
+WHOLE = ((1, 0), (0, 0))
+SPLIT = ((1, 0), (1, 1), (0, 0), (0, 1))
+
+
+def tiles_kernel(classes, split, n_in, n_extra, place, *refs):
     ins = refs[:n_in]
-    outs, (held, *accs, sems) = refs[n_in + n_extra : n_in + n_extra + 2], refs[n_in + n_extra + 2 :]
-    yl, c = place[1], place[2]
+    n_out = 4 if split else 2
+    outs, (held, *accs, sems) = refs[n_in + n_extra :][:n_out], refs[n_in + n_extra + n_out :]
+    yh, yl, c = place[0], place[1], place[2]
     rows = outs[0].shape[1]
+    size = rows // 2 if split else rows
     copies = [pltpu.make_async_copy(r, held.at[i], sems.at[i]) for i, r in enumerate(ins)]
     for copy in copies:
         copy.start()
@@ -133,21 +139,22 @@
         acc[1] = product(held[r], held[other])
         coded = bound_of(jnp.max(jnp.abs(acc[...])), rows)
         bounds = jnp.where(row == k, coded, bounds)
-        for m1, out in zip((1, 0), outs):
-            part = acc[jnp.where(yl ^ m1 == c, 0, 1)]
-            out[k * rows : (k + 1) * rows, :] = encode(part, coded[0:1, :])
+        for (m1, m2), out in zip(SPLIT if split else WHOLE, outs):
+            part = jnp.where(yl ^ m1 == c, 0, 1)
+            start = pl.multiple_of((yh ^ m2) * size, size) if split else 0
+            out[k * size : (k + 1) * size, :] = encode(acc[part, pl.ds(start, size), :], coded[0:1, :])
     for out in outs:
-        out[len(classes) * rows :, :] = bounds.astype(jnp.bfloat16)
-
-
-def partial_tiles(place, arrays, classes, rows, after=()):
+        out[len(classes) * size :, :] = bounds.astype(jnp.bfloat16)
+
+
+def partial_tiles(place, arrays, classes, split, rows, after=()):
     names = list(arrays)
     listed = tuple(tuple((names.index(i), names.index(j)) for i, j in k) for k in classes)
     depth = arrays[names[0]].shape[1]
     return call(
-        functools.partial(tiles_kernel, listed, len(names), len(after)),
+        functools.partial(tiles_kernel, listed, split, len(names), len(after)),
         [place, *arrays.values(), *after],
-        [coded_shape(len(classes), rows, rows)] * 2,
+        [coded_shape(len(classes), rows // 2 if split else rows, rows)] * (4 if split else 2),
         scratch=[
             pltpu.VMEM((len(names), rows, depth), jnp.bfloat16),
             pltpu.VMEM((2, rows, rows), jnp.float32),
@@ -160,31 +167,40 @@
     )
 
 
-def sum_kernel(whole, place, a, b, _, *outs):
+def sum_kernel(members, place, a, b, _, kept, given):
     c = place[2]
     rows = a.shape[1]
     half = rows // 2
-    full, kept, given = outs
-    count = (a.shape[0] - 16) // rows
-    for k in range(count):
-        if k < whole:
-            full[k, :, :] = part_of(a, k, rows) + part_of(b, k, rows)
-        else:
-            for out, h in ((kept, c), (given, 1 - c)):
-                start = pl.multiple_of(h * half, half)
-                out[k - whole, :, :] = part_of(a, k, rows, start) + part_of(b, k, rows, start)
-
-
-def group_kernel(classes, groups, place, *refs):
-    ins, outs = refs[: len(refs) - len(groups)], refs[len(refs) - len(groups) :]
-    width = outs[0].shape[1]
-    half = width // 2
-    start = pl.multiple_of(place[2] * half, half)
+    for i, k in enumerate(members):
+        for out, h in ((kept, c), (given, 1 - c)):
+            start = pl.multiple_of(h * half, half)
+            out[i, :, :] = part_of(a, k, rows, start) + part_of(b, k, rows, start)
+
+
+def whole_sum_kernel(a, b, _, out):
+    rows = a.shape[1]
+    for k in range(out.shape[0]):
+        out[k, :, :] = part_of(a, k, rows) + part_of(b, k, rows)
+
+
+def half_sum_kernel(a, b, c, d, out):
+    half = a.shape[1] // 2
+    for k in range(out.shape[0]):
+        out[k, :, :] = (part_of(a, k, half) + part_of(b, k, half)) + (part_of(c, k, half) + part_of(d, k, half))
+
+
+def group_kernel(early, groups, kept, given, late, *outs):
+    half, width = kept.shape[1:]
     row = lax.broadcasted_iota(jnp.int32, (16, width), 0)
     bounds = [jnp.zeros((16, width), jnp.float32) for _ in groups]
-    for k, (pair, i) in classes.items():
-        rows = pl.ds(start, half) if ins[2 * pair].shape[1] == width else pl.ds(0, half)
-        total = ins[2 * pair][i, rows, :] + ins[2 * pair + 1][i, rows, :]
+    for k in range(len(CLASSES)):
+        if k in early:
+            i = early.index(k)
+            total = kept[i, :, :] + given[i, :, :]
+        elif k >= len(EARLY):
+            total = late[k - len(EARLY), :, :]
+        else:
+            continue
         bound = bound_of(jnp.max(jnp.abs(total)), width)
         code = encode(total, bound[0:1, :])
         for j, (out, members) in enumerate(zip(outs, groups)):
@@ -197,15 +213,14 @@
 
 
 def place_kernel(stay, tiles, n, place, *refs):
-    own, other, sums = refs[:n], refs[n : 2 * n], refs[2 * n : 2 * n + 4]
-    out, result, early, late, in_sems, out_sem = refs[2 * n + 4 :]
-    held = (early, late)
+    own, other, sums = refs[:n], refs[n : 2 * n], refs[2 * n : 2 * n + 2]
+    out, result, held, in_sems, out_sem = refs[2 * n + 2 :]
     c, z, x = place[2], place[3], place[4]
     rows = result.shape[0]
     half = rows // 2
     first = pl.multiple_of(c * half, half)
     second = pl.multiple_of((1 - c) * half, half)
-    arriving = [pltpu.make_async_copy(v, held[i // 2].at[i % 2], in_sems.at[i]) for i, v in enumerate(sums)]
+    arriving = [pltpu.make_async_copy(v, held.at[i], in_sems.at[i]) for i, v in enumerate(sums)]
     for copy in arriving:
         copy.start()
 
@@ -234,26 +249,26 @@
         at(d, write)
     for copy in arriving:
         copy.wait()
-    for stage, i, d in stay:
-
-        def write(start, stage=stage, i=i):
-            result[:, pl.ds(start, rows)] = held[stage][0, i, :, :] + held[stage][1, i, :, :]
+    for i, d in stay:
+
+        def write(start, i=i):
+            result[:, pl.ds(start, rows)] = held[0, i, :, :] + held[1, i, :, :]
 
         at(d, write)
     pltpu.make_async_copy(result, out, out_sem).wait()
 
 
 O, PX, MX, PZ, MZ, PE, ME = (0, 0), (1, 0), (3, 0), (0, 1), (0, 3), (1, 1), (3, 3)
-EARLY = ((O, PX), (O, PZ), (MX, PX), (MZ, PZ), (MZ, PX), (PZ, PX))
-LATE = ((O, O), (ME, PX), (ME, PZ), (ME, PE))
+EARLY = ((O, PX), (O, PZ), (O, O), (MX, PX), (MZ, PZ), (MZ, PX), (PZ, PX))
+LATE = ((ME, PX), (ME, PZ), (ME, PE))
 CLASSES = EARLY + LATE
-STAY = (2, 1)
+STAY = 3
 SENDS = (
-    (PX, True, (0, 2, 4, 5, 7)),
+    (PX, True, (0, 3, 5, 6, 7)),
     (PZ, True, (1, 8)),
     (ME, False, (7, 8, 9)),
-    (MZ, False, (3, 4)),
-    (PZ, False, (5,)),
+    (MZ, False, (4, 5)),
+    (PZ, False, (6,)),
 )
 OWN = {
     O: ("o", "o"),
@@ -291,47 +306,56 @@
     held["me"] = fetch(held["q3"], MX, MZ)
     for name, source in (("s1", "q1"), ("s2", "q2")):
         held[name] = move(held[source], to_core)
+    held["so"] = move(lax.optimization_barrier((held["o"], held["q4"]))[0], to_core)
 
     coded, after = [], ()
     for classes in (EARLY, LATE):
         if after:
-            first, second, _ = lax.optimization_barrier((held["o"], held["pe"], after[0]))
-            held["so"] = move(first, to_core)
-            held["spe"] = move(second, to_core)
+            first, _ = lax.optimization_barrier((held["pe"], after[0]))
+            held["spe"] = move(first, to_core)
         listed = [(OWN[r], OWN[q], OTHER[q]) for r, q in classes]
         used = {i for k in listed for pair in k for i in pair}
         arrays = {name: v for name, v in held.items() if name in used}
-        coded.append(partial_tiles(place, arrays, listed, rows, after))
+        coded.append(partial_tiles(place, arrays, listed, bool(after), rows, after))
         after = (coded[-1][0],)
 
-    sums = []
-    for classes, stage, whole, weight in zip((EARLY, LATE), coded, STAY, (1, 10**11)):
-        halves = jax.ShapeDtypeStruct((len(classes) - whole, rows // 2, rows), jnp.float32)
-        full = jax.ShapeDtypeStruct((whole, rows, rows), jnp.float32)
-        full, kept, given = call(
-            functools.partial(sum_kernel, whole),
-            [place, *(move(v, to_owner(m1)) for m1, v in zip((1, 0), stage)), *after],
-            [full, halves, halves],
-            any_from=3,
-            flops=weight,
-            moved=weight,
-            transcendentals=weight,
+    groups = tuple(members for _, _, members in SENDS)
+    early = tuple(k for k in range(len(EARLY)) if any(k in g for g in groups))
+    arrived = [move(v, to_owner(*m)) for m, v in zip(WHOLE, coded[0])]
+    kept, given = call(
+        functools.partial(sum_kernel, early),
+        [place, *arrived, *after],
+        [jax.ShapeDtypeStruct((len(early), rows // 2, rows), jnp.float32)] * 2,
+        any_from=3,
+        flops=1,
+        moved=1,
+    )
+    weight = 10**11
+    late = call(
+        half_sum_kernel,
+        [move(v, to_owner(*m)) for m, v in zip(SPLIT, coded[1])],
+        jax.ShapeDtypeStruct((len(LATE), rows // 2, rows), jnp.float32),
+        flops=weight,
+        moved=weight,
+        transcendentals=weight,
+    )
+    parts = list(
+        call(
+            functools.partial(group_kernel, early, groups),
+            [kept, move(given, to_core), late],
+            [coded_shape(len(g), rows // 2, rows) for g in groups],
+            moved=4 << 20,
         )
-        sums += [full, move(full, to_core), kept, move(given, to_core)]
-
-    where = {}
-    for stage, (classes, whole) in enumerate(zip((EARLY, LATE), STAY)):
-        for k in range(len(classes)):
-            pair = (2 * stage, k) if k < whole else (2 * stage + 1, k - whole)
-            where[len(where)] = pair
-    sent = {k: where[k] for k in range(len(CLASSES)) if any(k in m for _, _, m in SENDS)}
-    groups = tuple(members for _, _, members in SENDS)
-    parts = call(
-        functools.partial(group_kernel, sent, groups),
-        [place, *sums],
-        [coded_shape(len(g), rows // 2, rows) for g in groups],
-        moved=4 << 20,
-    )
+    )
+    full = call(
+        whole_sum_kernel,
+        [*arrived, parts[0]],
+        jax.ShapeDtypeStruct((STAY, rows, rows), jnp.float32),
+        any_from=2,
+        flops=1,
+        moved=1,
+    )
+    parts[3], other_full = lax.optimization_barrier((parts[3], move(full, to_core)))
     own, tiles = [], []
     for j, (part, (to, turned, members)) in enumerate(zip(parts, SENDS)):
         for i, k in enumerate(members):
@@ -340,17 +364,15 @@
         own.append(move(part, to_position(*to, swap=turned)))
     own = lax.optimization_barrier(own)
     other = [move(v, to_core) for v in own]
-    stay = tuple(
-        (where[k][0] // 2, where[k][1], minus(q, r)) for k, (r, q) in enumerate(CLASSES) if where[k][0] % 2 == 0
-    )
+    stay = tuple((k, minus(q, r)) for k, (r, q) in enumerate(CLASSES[:STAY]))
     return call(
         functools.partial(place_kernel, stay, tuple(tiles), len(own)),
-        [place, *own, *other, *sums[:2], *sums[4:6]],
+        [place, *own, *other, full, other_full],
         jax.ShapeDtypeStruct((rows, 8 * rows), jnp.float32),
         scratch=[
             pltpu.VMEM((rows, 8 * rows), jnp.float32),
-            *(pltpu.VMEM((2, n, rows, rows), jnp.float32) for n in STAY),
-            pltpu.SemaphoreType.DMA((4,)),
+            pltpu.VMEM((2, STAY, rows, rows), jnp.float32),
+            pltpu.SemaphoreType.DMA((2,)),
             pltpu.SemaphoreType.DMA,
         ],
         any_from=1 + 2 * len(own),

time: 114 us -> 114 us (level)
  local copies, waits for them, and re-layouts: 1.58 us -> 3.77 us
  waiting for transfers between devices: 53.3 us -> 51.6 us
    unnamed x1 -> x5, local copies, waits for them, and re-layouts: 1.5 us -> 3.69 us
    ppermute x29, waiting for transfers between devices: 53.3 us -> 51.6 us  [move(): return lax.ppermute(value, ('aux', 'blk'), pairs)]
    pallas_call x6 -> x7, Pallas kernels: 22.5 us -> 22.4 us  [call(): pl.pallas_call(kernel, out_shape=out_shape, in_specs=specs, out_specs=[wh...]
  transfers between devices with their start and end apart: 29 -> 29, of which waited for: 12 -> 11; matrix products, arithmetic and copies ran while one was open for 0% -> 0% of each run, Pallas kernels for 16% -> 15%
where the time goes in v6:
time: 114 us; the launch traced here: 113 us
  waiting for transfers between devices  51.6 us (45%)
  starting transfers between devices  35.2 us (31%)
  Pallas kernels  22.4 us (20%)
  local copies, waits for them, and re-layouts  3.77 us (3%)
    ppermute x29, waiting for transfers between devices, move(): return lax.ppermute(value, ('aux', 'blk'), pairs)  51.6 us
    ppermute x29, starting transfers between devices, move(): return lax.ppermute(value, ('aux', 'blk'), pairs)  35.2 us
    pallas_call x7, Pallas kernels, call(): pl.pallas_call(kernel, out_shape=out_shape, in_specs=specs, out_specs=[wh...  22.4 us
    unnamed x5, local copies, waits for them, and re-layouts  3.69 us
  transfers between devices with their start and end apart: 29, of which 11 were waited for; matrix products, arithmetic and copies ran while one was open for 0% of the time, Pallas kernels for 15%

profile of v6, /device:TPU:9, one launch (start us, length us, event | category | flops | bytes accessed | tf_op | source)
XLA Modules:
  0.0 113.3 jit_solution(3795793427788916233)
XLA Ops:
  0.0 1.5 %copy.4 = bf16[32,8,16,128]{3,1,2,0:T(8,128)(2,1)S(1)} copy(bf16[32,8,16,128]{3,2,1,0:T(8,128)(2,1)} %bitcast.9) | data formatting | bytes 2097152
  1.5 4.5 %collective-permute-start = (bf16[256,2048]{1,0:T(8,128)(2,1)S(1)}, bf16[256,2048]{1,0:T(8,128)(2,1)}, u32[]{:S(2)}, u32[]{:S(2)}) collective-permute-start(bf16[256,2048]{1,0:T(8,128)(2,1)S(1)} %bitcast.10), channel_id=1, source_target_pairs={{0,0},{1,1},{2,2},{3,3},{4,4},{5,5},{6,6},{7,7},{8,8},{9,9},{10,10... | collective-permute-start | bytes 3145736 | tf_op jit(solution)/shard_map/ppermute | solution.py:29
  6.0 13.5 %collective-permute-done.refs_0_ = bf16[256,2048]{1,0:T(8,128)(2,1)} collective-permute-done((bf16[256,2048]{1,0:T(8,128)(2,1)S(1)}, bf16[256,2048]{1,0:T(8,128)(2,1)}, u32[]{:S(2)}, u32[]{:S(2)}) %collective-permute-start) | collective-permute-done | bytes 1048608 | tf_op jit(solution)/shard_map/ppermute | solution.py:29
  19.5 1.5 %collective-permute-start.4 = (bf16[256,2048]{1,0:T(8,128)(2,1)}, bf16[256,2048]{1,0:T(8,128)(2,1)S(1)}, u32[]{:S(2)}, u32[]{:S(2)}) collective-permute-start(bf16[256,2048]{1,0:T(8,128)(2,1)} %collective-permute-done.refs_0_), channel_id=1, source_target_pairs={{0,1},{1,2},{2,3},{3,0},{4,5},{5,6},{6,7},{7,4},{8,9},{9,10},{10,1... | collective-permute-start | bytes 3145736 | tf_op jit(solution)/shard_map/ppermute | solution.py:29
  21.1 2.5 %collective-permute-start.1 = (bf16[256,2048]{1,0:T(8,128)(2,1)}, bf16[256,2048]{1,0:T(8,128)(2,1)S(1)}, u32[]{:S(2)}, u32[]{:S(2)}) collective-permute-start(bf16[256,2048]{1,0:T(8,128)(2,1)} %collective-permute-done.refs_0_), channel_id=1, source_target_pairs={{0,12},{1,13},{2,14},{3,15},{4,0},{5,1},{6,2},{7,3},{8,4},{9,5},{1... | collective-permute-start | bytes 3145736 | tf_op jit(solution)/shard_map/ppermute | solution.py:29
  23.5 2.1 %collective-permute-start.2 = (bf16[256,2048]{1,0:T(8,128)(2,1)}, bf16[256,2048]{1,0:T(8,128)(2,1)S(1)}, u32[]{:S(2)}, u32[]{:S(2)}) collective-permute-start(bf16[256,2048]{1,0:T(8,128)(2,1)} %collective-permute-done.refs_0_), channel_id=1, source_target_pairs={{0,3},{1,0},{2,1},{3,2},{4,7},{5,4},{6,5},{7,6},{8,11},{9,8},{10,9... | collective-permute-start | bytes 3145736 | tf_op jit(solution)/shard_map/ppermute | solution.py:29
  25.7 0.0 collective-permute-start.3
  25.7 12.2 %collective-permute-done.4.refs_4_ = bf16[256,2048]{1,0:T(8,128)(2,1)S(1)} collective-permute-done((bf16[256,2048]{1,0:T(8,128)(2,1)}, bf16[256,2048]{1,0:T(8,128)(2,1)S(1)}, u32[]{:S(2)}, u32[]{:S(2)}) %collective-permute-start.4) | collective-permute-done | bytes 1048608 | tf_op jit(solution)/shard_map/ppermute | solution.py:29
  37.8 1.0 copy-done
  38.8 0.5 collective-permute-start.5
  39.3 0.1 collective-permute-start.6
  39.4 1.3 %collective-permute-start.10 = (bf16[256,2048]{1,0:T(8,128)(2,1)S(1)}, bf16[256,2048]{1,0:T(8,128)(2,1)}, u32[]{:S(2)}, u32[]{:S(2)}) collective-permute-start(bf16[256,2048]{1,0:T(8,128)(2,1)S(1)} %collective-permute-done.1.refs_1_.refs_0_), channel_id=1, source_target_pairs={{0,3},{1,0},{2,1},{3,2},{4,7},{5,4},{6,5},{7,6},{8,11},{9,8},{10,9... | collective-permute-start | bytes 3145736 | tf_op jit(solution)/shard_map/ppermute | solution.py:29
  40.7 0.1 stack.23.place
  40.8 0.0 collective-permute-done.3.refs_3_
  40.8 0.1 collective-permute-start.11
  41.0 2.3 %collective-permute-done.7.refs_7_ = bf16[256,2048]{1,0:T(8,128)(2,1)} collective-permute-done((bf16[256,2048]{1,0:T(8,128)(2,1)}, bf16[256,2048]{1,0:T(8,128)(2,1)}, u32[]{:S(2)}, u32[]{:S(2)}) %collective-permute-start.7) | collective-permute-done | bytes 1048608 | tf_op jit(solution)/shard_map/ppermute | solution.py:29
  43.2 0.9 collective-permute-done.5.refs_5_.refs_4_
  44.1 0.5 collective-permute-done.6.refs_6_.refs_5_
  44.6 1.2 %copy-done.1 = bf16[256,2048]{1,0:T(8,128)(2,1)S(1)} copy-done((bf16[256,2048]{1,0:T(8,128)(2,1)S(1)}, bf16[256,2048]{1,0:T(8,128)(2,1)}, u32[]{:S(2)}) %copy-start.1) | copy-done | bytes 1048600
  45.8 8.7 %shard_map.17 = (bf16[1808,256]{1,0:T(8,128)(2,1)S(1)}, bf16[1808,256]{1,0:T(8,128)(2,1)S(1)}) custom-call(s32[5]{0:T(128)S(1)} %stack.23.place, bf16[256,2048]{1,0:T(8,128)(2,1)} %collective-permute-done.refs_0_, bf16[256,2048]{1,0:T(8,128)(2,1)S(1)} %collective-permute-done.1.refs_1_.refs_0_, bf16[256,2048]{1,0:T(8,128)(2,1)S(1)} %collective-permute-done.2.refs_2_.refs_1_, ...), custom_call_target="tpu_custom_call" | custom-call | flops 3758096384 | bytes 8388608 | tf_op jit(solution)/shard_map/pallas_call | solution.py:103
  54.6 0.2 collective-permute-start.12
  54.8 2.1 %collective-permute-start.8 = (bf16[1808,256]{1,0:T(8,128)(2,1)S(1)}, bf16[1808,256]{1,0:T(8,128)(2,1)S(1)}, u32[]{:S(2)}, u32[]{:S(2)}) collective-permute-start(bf16[1808,256]{1,0:T(8,128)(2,1)S(1)} %get-tuple-element.28.refs_7_), channel_id=1, source_target_pairs={{0,64},{1,65},{2,66},{3,67},{4,68},{5,69},{6,70},{7,71},{8,72},{9,... | collective-permute-start | bytes 2777096 | tf_op jit(solution)/shard_map/ppermute | solution.py:29
  56.9 2.6 %collective-permute-start.9 = (bf16[1808,256]{1,0:T(8,128)(2,1)S(1)}, bf16[1808,256]{1,0:T(8,128)(2,1)S(1)}, u32[]{:S(2)}, u32[]{:S(2)}) collective-permute-start(bf16[1808,256]{1,0:T(8,128)(2,1)S(1)} %get-tuple-element.29), channel_id=1, source_target_pairs={{0,0},{1,1},{2,2},{3,3},{4,4},{5,5},{6,6},{7,7},{8,8},{9,9},{10,10... | collective-permute-start | bytes 2777096 | tf_op jit(solution)/shard_map/ppermute | solution.py:29
  59.6 5.4 %shard_map.18 = (bf16[400,256]{1,0:T(8,128)(2,1)S(1)}, bf16[400,256]{1,0:T(8,128)(2,1)S(1)}, bf16[400,256]{1,0:T(8,128)(2,1)S(1)}, bf16[400,256]{1,0:T(8,128)(2,1)S(1)}) custom-call(s32[5]{0:T(128)S(1)} %stack.23.place, bf16[256,2048]{1,0:T(8,128)(2,1)S(1)} %collective-permute-done.1.refs_1_.refs_0_, ...), custom_call_target="tpu_custom_call" | custom-call | flops 1610612736 | bytes 7340032 | tf_op jit(solution)/shard_map/pallas_call | solution.py:103
  64.9 2.6 %collective-permute-start.14 = (bf16[400,256]{1,0:T(8,128)(2,1)S(1)}, bf16[400,256]{1,0:T(8,128)(2,1)S(1)}, u32[]{:S(2)}, u32[]{:S(2)}) collective-permute-start(bf16[400,256]{1,0:T(8,128)(2,1)S(1)} %get-tuple-element.31._), channel_id=1, source_target_pairs={{0,64},{1,65},{2,66},{3,67},{4,68},{5,69},{6,70},{7,71},{8,72},{9,... | collective-permute-start | bytes 614408 | tf_op jit(solution)/shard_map/ppermute | solution.py:29
  67.6 2.7 %collective-permute-start.16 = (bf16[400,256]{1,0:T(8,128)(2,1)S(1)}, bf16[400,256]{1,0:T(8,128)(2,1)S(1)}, u32[]{:S(2)}, u32[]{:S(2)}) collective-permute-start(bf16[400,256]{1,0:T(8,128)(2,1)S(1)} %get-tuple-element.35), channel_id=1, source_target_pairs={{0,0},{1,1},{2,2},{3,3},{4,4},{5,5},{6,6},{7,7},{8,8},{9,9},{10,10... | collective-permute-start | bytes 614408 | tf_op jit(solution)/shard_map/ppermute | solution.py:29
  70.2 3.4 %collective-permute-done.8.a = bf16[1808,256]{1,0:T(8,128)(2,1)S(1)} collective-permute-done((bf16[1808,256]{1,0:T(8,128)(2,1)S(1)}, bf16[1808,256]{1,0:T(8,128)(2,1)S(1)}, u32[]{:S(2)}, u32[]{:S(2)}) %collective-permute-start.8) | collective-permute-done | bytes 925728 | tf_op jit(solution)/shard_map/ppermute | solution.py:29
  73.6 2.4 %collective-permute-start.17 = (bf16[400,256]{1,0:T(8,128)(2,1)S(1)}, bf16[400,256]{1,0:T(8,128)(2,1)S(1)}, u32[]{:S(2)}, u32[]{:S(2)}) collective-permute-start(bf16[400,256]{1,0:T(8,128)(2,1)S(1)} %get-tuple-element.36), channel_id=1, source_target_pairs={{0,32},{1,33},{2,34},{3,35},{4,36},{5,37},{6,38},{7,39},{8,40},{9,... | collective-permute-start | bytes 614408 | tf_op jit(solution)/shard_map/ppermute | solution.py:29
  76.1 7.1 %collective-permute-done.9.b = bf16[1808,256]{1,0:T(8,128)(2,1)S(1)} collective-permute-done((bf16[1808,256]{1,0:T(8,128)(2,1)S(1)}, bf16[1808,256]{1,0:T(8,128)(2,1)S(1)}, u32[]{:S(2)}, u32[]{:S(2)}) %collective-permute-start.9) | collective-permute-done | bytes 925728 | tf_op jit(solution)/shard_map/ppermute | solution.py:29
  83.2 2.6 %shard_map.19 = (f32[6,128,256]{2,1,0:T(8,128)S(1)}, f32[6,128,256]{2,1,0:T(8,128)}) custom-call(s32[5]{0:T(128)S(1)} %stack.23.place, bf16[1808,256]{1,0:T(8,128)(2,1)S(1)} %collective-permute-done.8.a, bf16[1808,256]{1,0:T(8,128)(2,1)S(1)} %collective-permute-done.9.b, bf16[400,256]{1,0:T(8,128)(2,1)S(1)} %get-tuple-element.31._), custom_call_target="tpu_custom_call" | custom-call | flops 1 | bytes 1 | tf_op jit(solution)/shard_map/pallas_call | solution.py:103
  85.8 0.7 shard_map.20.late
  86.5 1.9 %collective-permute-done.13.given = f32[6,128,256]{2,1,0:T(8,128)} collective-permute-done((f32[6,128,256]{2,1,0:T(8,128)}, f32[6,128,256]{2,1,0:T(8,128)}, u32[]{:S(2)}, u32[]{:S(2)}) %collective-permute-start.13) | collective-permute-done | bytes 786464 | tf_op jit(solution)/shard_map/ppermute | solution.py:29
  88.4 1.8 %shard_map.21 = (bf16[656,256]{1,0:T(8,128)(2,1)S(1)}, bf16[272,256]{1,0:T(8,128)(2,1)S(1)}, bf16[400,256]{1,0:T(8,128)(2,1)S(1)}, bf16[272,256]{1,0:T(8,128)(2,1)S(1)}, bf16[144,256]{1,0:T(8,128)(2,1)S(1)}) custom-call(f32[6,128,256]{2,1,0:T(8,128)S(1)} %get-tuple-element.32.kept, f32[6,128,256]{2,1,0:T(8,128)} %collective-permute-done.13.given, ...), custom_call_target="tpu_custom_call" | custom-call | bytes 4194304 | tf_op jit(solution)/shard_map/pallas_call | solution.py:103
  90.2 0.6 shard_map.22.refs_10_
  90.9 0.8 collective-permute-start.21
  91.7 0.1 collective-permute-start.18
  91.8 3.3 %collective-permute-start.20 = (bf16[400,256]{1,0:T(8,128)(2,1)S(1)}, bf16[400,256]{1,0:T(8,128)(2,1)S(1)}, u32[]{:S(2)}, u32[]{:S(2)}) collective-permute-start(bf16[400,256]{1,0:T(8,128)(2,1)S(1)} %get-tuple-element.39), channel_id=1, source_target_pairs={{0,15},{1,12},{2,13},{3,14},{4,3},{5,0},{6,1},{7,2},{8,7},{9,4},{1... | collective-permute-start | bytes 614408 | tf_op jit(solution)/shard_map/ppermute | solution.py:29
  95.2 1.3 %collective-permute-start.19 = (bf16[272,256]{1,0:T(8,128)(2,1)S(1)}, bf16[272,256]{1,0:T(8,128)(2,1)S(1)}, u32[]{:S(2)}, u32[]{:S(2)}) collective-permute-start(bf16[272,256]{1,0:T(8,128)(2,1)S(1)} %get-tuple-element.38), channel_id=1, source_target_pairs={{0,4},{1,5},{2,6},{3,7},{4,8},{5,9},{6,10},{7,11},{8,12},{9,13},{1... | collective-permute-start | bytes 417800 | tf_op jit(solution)/shard_map/ppermute | solution.py:29
  96.5 2.3 %collective-permute-start.22 = (bf16[272,256]{1,0:T(8,128)(2,1)S(1)}, bf16[272,256]{1,0:T(8,128)(2,1)S(1)}, u32[]{:S(2)}, u32[]{:S(2)}) collective-permute-start(bf16[272,256]{1,0:T(8,128)(2,1)S(1)} %get-tuple-element.41), channel_id=1, source_target_pairs={{0,12},{1,13},{2,14},{3,15},{4,0},{5,1},{6,2},{7,3},{8,4},{9,5},{1... | collective-permute-start | bytes 417800 | tf_op jit(solution)/shard_map/ppermute | solution.py:29
  98.8 4.7 %collective-permute-done.23.refs_4_ = bf16[144,256]{1,0:T(8,128)(2,1)S(1)} collective-permute-done((bf16[144,256]{1,0:T(8,128)(2,1)S(1)}, bf16[144,256]{1,0:T(8,128)(2,1)S(1)}, u32[]{:S(2)}, u32[]{:S(2)}) %collective-permute-start.23) | collective-permute-done | bytes 73760 | tf_op jit(solution)/shard_map/ppermute | solution.py:29
  103.5 4.0 %collective-permute-done.19.refs_1_ = bf16[272,256]{1,0:T(8,128)(2,1)S(1)} collective-permute-done((bf16[272,256]{1,0:T(8,128)(2,1)S(1)}, bf16[272,256]{1,0:T(8,128)(2,1)S(1)}, u32[]{:S(2)}, u32[]{:S(2)}) %collective-permute-start.19) | collective-permute-done | bytes 139296 | tf_op jit(solution)/shard_map/ppermute | solution.py:29
  107.5 1.0 collective-permute-start.24
  108.5 0.1 collective-permute-start.26
  108.6 0.4 collective-permute-start.25
  109.0 0.1 collective-permute-start.27
  109.1 0.4 collective-permute-start.28
  109.5 1.0 collective-permute-done.28.refs_9_
  110.6 2.6 %shard_map.23 = f32[256,2048]{1,0:T(8,128)} custom-call(s32[5]{0:T(128)S(1)} %stack.23.place, bf16[656,256]{1,0:T(8,128)(2,1)S(1)} %collective-permute-done.18.refs_0_, bf16[272,256]{1,0:T(8,128)(2,1)S(1)} %collective-permute-done.19.refs_1_, bf16[400,256]{1,0:T(8,128)(2,1)S(1)} %collective-permute-done.20.refs_2_, ...), custom_call_target="tpu_custom_call" | custom-call | bytes 6291456 | tf_op jit(solution)/shard_map/pallas_call | solution.py:103
  (23 shorter events, 0.1 us)
Async XLA Ops:
  1.5 18.0 %collective-permute-start = (bf16[256,2048]{1,0:T(8,128)(2,1)S(1)}, bf16[256,2048]{1,0:T(8,128)(2,1)}, u32[]{:S(2)}, u32[]{:S(2)}) collective-permute-start(bf16[256,2048]{1,0:T(8,128)(2,1)S(1)} %bitcast.10), channel_id=1, source_target_pairs={{0,0},{1,1},{2,2},{3,3},{4,4},{5,5},{6,6},{7,7},{8,8},{9,9},{10,10... | collective-permute-start | bytes 3145736 | tf_op jit(solution)/shard_map/ppermute | solution.py:29
  19.5 18.3 %collective-permute-start.4 = (bf16[256,2048]{1,0:T(8,128)(2,1)}, bf16[256,2048]{1,0:T(8,128)(2,1)S(1)}, u32[]{:S(2)}, u32[]{:S(2)}) collective-permute-start(bf16[256,2048]{1,0:T(8,128)(2,1)} %collective-permute-done.refs_0_), channel_id=1, source_target_pairs={{0,1},{1,2},{2,3},{3,0},{4,5},{5,6},{6,7},{7,4},{8,9},{9,10},{10,1... | collective-permute-start | bytes 3145736 | tf_op jit(solution)/shard_map/ppermute | solution.py:29
  21.1 17.8 %collective-permute-start.1 = (bf16[256,2048]{1,0:T(8,128)(2,1)}, bf16[256,2048]{1,0:T(8,128)(2,1)S(1)}, u32[]{:S(2)}, u32[]{:S(2)}) collective-permute-start(bf16[256,2048]{1,0:T(8,128)(2,1)} %collective-permute-done.refs_0_), channel_id=1, source_target_pairs={{0,12},{1,13},{2,14},{3,15},{4,0},{5,1},{6,2},{7,3},{8,4},{9,5},{1... | collective-permute-start | bytes 3145736 | tf_op jit(solution)/shard_map/ppermute | solution.py:29
  23.5 15.8 %collective-permute-start.2 = (bf16[256,2048]{1,0:T(8,128)(2,1)}, bf16[256,2048]{1,0:T(8,128)(2,1)S(1)}, u32[]{:S(2)}, u32[]{:S(2)}) collective-permute-start(bf16[256,2048]{1,0:T(8,128)(2,1)} %collective-permute-done.refs_0_), channel_id=1, source_target_pairs={{0,3},{1,0},{2,1},{3,2},{4,7},{5,4},{6,5},{7,6},{8,11},{9,8},{10,9... | collective-permute-start | bytes 3145736 | tf_op jit(solution)/shard_map/ppermute | solution.py:29
  25.7 15.2 %collective-permute-start.3 = (bf16[256,2048]{1,0:T(8,128)(2,1)}, bf16[256,2048]{1,0:T(8,128)(2,1)}, u32[]{:S(2)}, u32[]{:S(2)}) collective-permute-start(bf16[256,2048]{1,0:T(8,128)(2,1)} %collective-permute-done.refs_0_), channel_id=1, source_target_pairs={{0,4},{1,5},{2,6},{3,7},{4,8},{5,9},{6,10},{7,11},{8,12},{9,13},{1... | collective-permute-start | bytes 3145736 | tf_op jit(solution)/shard_map/ppermute | solution.py:29
  37.8 1.0 copy-start
  38.8 4.4 %collective-permute-start.7 = (bf16[256,2048]{1,0:T(8,128)(2,1)}, bf16[256,2048]{1,0:T(8,128)(2,1)}, u32[]{:S(2)}, u32[]{:S(2)}) collective-permute-start(bf16[256,2048]{1,0:T(8,128)(2,1)} %collective-permute-done.refs_0_), channel_id=1, source_target_pairs={{0,32},{1,33},{2,34},{3,35},{4,36},{5,37},{6,38},{7,39},{8,40},{9,... | collective-permute-start | bytes 3145736 | tf_op jit(solution)/shard_map/ppermute | solution.py:29
  38.8 5.3 %collective-permute-start.5 = (bf16[256,2048]{1,0:T(8,128)(2,1)S(1)}, bf16[256,2048]{1,0:T(8,128)(2,1)S(1)}, u32[]{:S(2)}, u32[]{:S(2)}) collective-permute-start(bf16[256,2048]{1,0:T(8,128)(2,1)S(1)} %collective-permute-done.1.refs_1_.refs_0_), channel_id=1, source_target_pairs={{0,32},{1,33},{2,34},{3,35},{4,36},{5,37},{6,38},{7,39},{8,40},{9,... | collective-permute-start | bytes 3145736 | tf_op jit(solution)/shard_map/ppermute | solution.py:29
  39.3 5.3 %collective-permute-start.6 = (bf16[256,2048]{1,0:T(8,128)(2,1)S(1)}, bf16[256,2048]{1,0:T(8,128)(2,1)}, u32[]{:S(2)}, u32[]{:S(2)}) collective-permute-start(bf16[256,2048]{1,0:T(8,128)(2,1)S(1)} %collective-permute-done.2.refs_2_.refs_1_), channel_id=1, source_target_pairs={{0,32},{1,33},{2,34},{3,35},{4,36},{5,37},{6,38},{7,39},{8,40},{9,... | collective-permute-start | bytes 3145736 | tf_op jit(solution)/shard_map/ppermute | solution.py:29
  39.4 15.2 %collective-permute-start.10 = (bf16[256,2048]{1,0:T(8,128)(2,1)S(1)}, bf16[256,2048]{1,0:T(8,128)(2,1)}, u32[]{:S(2)}, u32[]{:S(2)}) collective-permute-start(bf16[256,2048]{1,0:T(8,128)(2,1)S(1)} %collective-permute-done.1.refs_1_.refs_0_), channel_id=1, source_target_pairs={{0,3},{1,0},{2,1},{3,2},{4,7},{5,4},{6,5},{7,6},{8,11},{9,8},{10,9... | collective-permute-start | bytes 3145736 | tf_op jit(solution)/shard_map/ppermute | solution.py:29
  40.8 18.7 %collective-permute-start.11 = (bf16[256,2048]{1,0:T(8,128)(2,1)}, bf16[256,2048]{1,0:T(8,128)(2,1)S(1)}, u32[]{:S(2)}, u32[]{:S(2)}) collective-permute-start(bf16[256,2048]{1,0:T(8,128)(2,1)} %collective-permute-done.3.refs_3_), channel_id=1, source_target_pairs={{0,1},{1,2},{2,3},{3,0},{4,5},{5,6},{6,7},{7,4},{8,9},{9,10},{10,1... | collective-permute-start | bytes 3145736 | tf_op jit(solution)/shard_map/ppermute | solution.py:29
  44.6 1.2 %copy-start.1 = (bf16[256,2048]{1,0:T(8,128)(2,1)S(1)}, bf16[256,2048]{1,0:T(8,128)(2,1)}, u32[]{:S(2)}) copy-start(bf16[256,2048]{1,0:T(8,128)(2,1)} %copy-done) | copy-start | bytes 3145732
  54.6 4.9 %collective-permute-start.12 = (bf16[256,2048]{1,0:T(8,128)(2,1)}, bf16[256,2048]{1,0:T(8,128)(2,1)S(1)}, u32[]{:S(2)}, u32[]{:S(2)}) collective-permute-start(bf16[256,2048]{1,0:T(8,128)(2,1)} %collective-permute-done.10.refs_2_), channel_id=1, source_target_pairs={{0,32},{1,33},{2,34},{3,35},{4,36},{5,37},{6,38},{7,39},{8,40},{9,... | collective-permute-start | bytes 3145736 | tf_op jit(solution)/shard_map/ppermute | solution.py:29
  54.8 18.8 %collective-permute-start.8 = (bf16[1808,256]{1,0:T(8,128)(2,1)S(1)}, bf16[1808,256]{1,0:T(8,128)(2,1)S(1)}, u32[]{:S(2)}, u32[]{:S(2)}) collective-permute-start(bf16[1808,256]{1,0:T(8,128)(2,1)S(1)} %get-tuple-element.28.refs_7_), channel_id=1, source_target_pairs={{0,64},{1,65},{2,66},{3,67},{4,68},{5,69},{6,70},{7,71},{8,72},{9,... | collective-permute-start | bytes 2777096 | tf_op jit(solution)/shard_map/ppermute | solution.py:29
  56.9 26.3 %collective-permute-start.9 = (bf16[1808,256]{1,0:T(8,128)(2,1)S(1)}, bf16[1808,256]{1,0:T(8,128)(2,1)S(1)}, u32[]{:S(2)}, u32[]{:S(2)}) collective-permute-start(bf16[1808,256]{1,0:T(8,128)(2,1)S(1)} %get-tuple-element.29), channel_id=1, source_target_pairs={{0,0},{1,1},{2,2},{3,3},{4,4},{5,5},{6,6},{7,7},{8,8},{9,9},{10,10... | collective-permute-start | bytes 2777096 | tf_op jit(solution)/shard_map/ppermute | solution.py:29
  64.9 20.8 %collective-permute-start.14 = (bf16[400,256]{1,0:T(8,128)(2,1)S(1)}, bf16[400,256]{1,0:T(8,128)(2,1)S(1)}, u32[]{:S(2)}, u32[]{:S(2)}) collective-permute-start(bf16[400,256]{1,0:T(8,128)(2,1)S(1)} %get-tuple-element.31._), channel_id=1, source_target_pairs={{0,64},{1,65},{2,66},{3,67},{4,68},{5,69},{6,70},{7,71},{8,72},{9,... | collective-permute-start | bytes 614408 | tf_op jit(solution)/shard_map/ppermute | solution.py:29
  67.5 18.2 %collective-permute-start.15 = (bf16[400,256]{1,0:T(8,128)(2,1)S(1)}, bf16[400,256]{1,0:T(8,128)(2,1)S(1)}, u32[]{:S(2)}, u32[]{:S(2)}) collective-permute-start(bf16[400,256]{1,0:T(8,128)(2,1)S(1)} %get-tuple-element.34), channel_id=1, source_target_pairs={{0,96},{1,97},{2,98},{3,99},{4,100},{5,101},{6,102},{7,103},{8,104... | collective-permute-start | bytes 614408 | tf_op jit(solution)/shard_map/ppermute | solution.py:29
  67.6 18.2 %collective-permute-start.16 = (bf16[400,256]{1,0:T(8,128)(2,1)S(1)}, bf16[400,256]{1,0:T(8,128)(2,1)S(1)}, u32[]{:S(2)}, u32[]{:S(2)}) collective-permute-start(bf16[400,256]{1,0:T(8,128)(2,1)S(1)} %get-tuple-element.35), channel_id=1, source_target_pairs={{0,0},{1,1},{2,2},{3,3},{4,4},{5,5},{6,6},{7,7},{8,8},{9,9},{10,10... | collective-permute-start | bytes 614408 | tf_op jit(solution)/shard_map/ppermute | solution.py:29
  73.6 12.2 %collective-permute-start.17 = (bf16[400,256]{1,0:T(8,128)(2,1)S(1)}, bf16[400,256]{1,0:T(8,128)(2,1)S(1)}, u32[]{:S(2)}, u32[]{:S(2)}) collective-permute-start(bf16[400,256]{1,0:T(8,128)(2,1)S(1)} %get-tuple-element.36), channel_id=1, source_target_pairs={{0,32},{1,33},{2,34},{3,35},{4,36},{5,37},{6,38},{7,39},{8,40},{9,... | collective-permute-start | bytes 614408 | tf_op jit(solution)/shard_map/ppermute | solution.py:29
  85.8 2.6 %collective-permute-start.13 = (f32[6,128,256]{2,1,0:T(8,128)}, f32[6,128,256]{2,1,0:T(8,128)}, u32[]{:S(2)}, u32[]{:S(2)}) collective-permute-start(f32[6,128,256]{2,1,0:T(8,128)} %get-tuple-element.33), channel_id=1, source_target_pairs={{0,32},{1,33},{2,34},{3,35},{4,36},{5,37},{6,38},{7,39},{8,40},{9,... | collective-permute-start | bytes 2359304 | tf_op jit(solution)/shard_map/ppermute | solution.py:29
  90.9 5.6 %collective-permute-start.21 = (f32[3,256,256]{2,1,0:T(8,128)S(1)}, f32[3,256,256]{2,1,0:T(8,128)S(1)}, u32[]{:S(2)}, u32[]{:S(2)}) collective-permute-start(f32[3,256,256]{2,1,0:T(8,128)S(1)} %shard_map.22.refs_10_), channel_id=1, source_target_pairs={{0,32},{1,33},{2,34},{3,35},{4,36},{5,37},{6,38},{7,39},{8,40},{9,... | collective-permute-start | bytes 2359304 | tf_op jit(solution)/shard_map/ppermute | solution.py:29
  91.7 15.8 %collective-permute-start.18 = (bf16[656,256]{1,0:T(8,128)(2,1)S(1)}, bf16[656,256]{1,0:T(8,128)(2,1)S(1)}, u32[]{:S(2)}, u32[]{:S(2)}) collective-permute-start(bf16[656,256]{1,0:T(8,128)(2,1)S(1)} %get-tuple-element.37._), channel_id=1, source_target_pairs={{0,1},{1,2},{2,3},{3,0},{4,5},{5,6},{6,7},{7,4},{8,9},{9,10},{10,1... | collective-permute-start | bytes 1007624 | tf_op jit(solution)/shard_map/ppermute | solution.py:29
  91.8 15.6 %collective-permute-start.20 = (bf16[400,256]{1,0:T(8,128)(2,1)S(1)}, bf16[400,256]{1,0:T(8,128)(2,1)S(1)}, u32[]{:S(2)}, u32[]{:S(2)}) collective-permute-start(bf16[400,256]{1,0:T(8,128)(2,1)S(1)} %get-tuple-element.39), channel_id=1, source_target_pairs={{0,15},{1,12},{2,13},{3,14},{4,3},{5,0},{6,1},{7,2},{8,7},{9,4},{1... | collective-permute-start | bytes 614408 | tf_op jit(solution)/shard_map/ppermute | solution.py:29
  95.2 12.3 %collective-permute-start.19 = (bf16[272,256]{1,0:T(8,128)(2,1)S(1)}, bf16[272,256]{1,0:T(8,128)(2,1)S(1)}, u32[]{:S(2)}, u32[]{:S(2)}) collective-permute-start(bf16[272,256]{1,0:T(8,128)(2,1)S(1)} %get-tuple-element.38), channel_id=1, source_target_pairs={{0,4},{1,5},{2,6},{3,7},{4,8},{5,9},{6,10},{7,11},{8,12},{9,13},{1... | collective-permute-start | bytes 417800 | tf_op jit(solution)/shard_map/ppermute | solution.py:29
  96.5 11.0 %collective-permute-start.22 = (bf16[272,256]{1,0:T(8,128)(2,1)S(1)}, bf16[272,256]{1,0:T(8,128)(2,1)S(1)}, u32[]{:S(2)}, u32[]{:S(2)}) collective-permute-start(bf16[272,256]{1,0:T(8,128)(2,1)S(1)} %get-tuple-element.41), channel_id=1, source_target_pairs={{0,12},{1,13},{2,14},{3,15},{4,0},{5,1},{6,2},{7,3},{8,4},{9,5},{1... | collective-permute-start | bytes 417800 | tf_op jit(solution)/shard_map/ppermute | solution.py:29
  98.8 4.7 %collective-permute-start.23 = (bf16[144,256]{1,0:T(8,128)(2,1)S(1)}, bf16[144,256]{1,0:T(8,128)(2,1)S(1)}, u32[]{:S(2)}, u32[]{:S(2)}) collective-permute-start(bf16[144,256]{1,0:T(8,128)(2,1)S(1)} %get-tuple-element.42), channel_id=1, source_target_pairs={{0,4},{1,5},{2,6},{3,7},{4,8},{5,9},{6,10},{7,11},{8,12},{9,13},{1... | collective-permute-start | bytes 221192 | tf_op jit(solution)/shard_map/ppermute | solution.py:29
  107.5 3.1 %collective-permute-start.24 = (bf16[656,256]{1,0:T(8,128)(2,1)S(1)}, bf16[656,256]{1,0:T(8,128)(2,1)S(1)}, u32[]{:S(2)}, u32[]{:S(2)}) collective-permute-start(bf16[656,256]{1,0:T(8,128)(2,1)S(1)} %collective-permute-done.18.refs_0_), channel_id=1, source_target_pairs={{0,32},{1,33},{2,34},{3,35},{4,36},{5,37},{6,38},{7,39},{8,40},{9,... | collective-permute-start | bytes 1007624 | tf_op jit(solution)/shard_map/ppermute | solution.py:29
  108.5 2.1 %collective-permute-start.26 = (bf16[400,256]{1,0:T(8,128)(2,1)S(1)}, bf16[400,256]{1,0:T(8,128)(2,1)S(1)}, u32[]{:S(2)}, u32[]{:S(2)}) collective-permute-start(bf16[400,256]{1,0:T(8,128)(2,1)S(1)} %collective-permute-done.20.refs_2_), channel_id=1, source_target_pairs={{0,32},{1,33},{2,34},{3,35},{4,36},{5,37},{6,38},{7,39},{8,40},{9,... | collective-permute-start | bytes 614408 | tf_op jit(solution)/shard_map/ppermute | solution.py:29
  108.6 2.0 %collective-permute-start.25 = (bf16[272,256]{1,0:T(8,128)(2,1)S(1)}, bf16[272,256]{1,0:T(8,128)(2,1)S(1)}, u32[]{:S(2)}, u32[]{:S(2)}) collective-permute-start(bf16[272,256]{1,0:T(8,128)(2,1)S(1)} %collective-permute-done.19.refs_1_), channel_id=1, source_target_pairs={{0,32},{1,33},{2,34},{3,35},{4,36},{5,37},{6,38},{7,39},{8,40},{9,... | collective-permute-start | bytes 417800 | tf_op jit(solution)/shard_map/ppermute | solution.py:29
  109.0 1.6 %collective-permute-start.27 = (bf16[272,256]{1,0:T(8,128)(2,1)S(1)}, bf16[272,256]{1,0:T(8,128)(2,1)S(1)}, u32[]{:S(2)}, u32[]{:S(2)}) collective-permute-start(bf16[272,256]{1,0:T(8,128)(2,1)S(1)} %collective-permute-done.22.refs_3_), channel_id=1, source_target_pairs={{0,32},{1,33},{2,34},{3,35},{4,36},{5,37},{6,38},{7,39},{8,40},{9,... | collective-permute-start | bytes 417800 | tf_op jit(solution)/shard_map/ppermute | solution.py:29
  109.1 1.5 %collective-permute-start.28 = (bf16[144,256]{1,0:T(8,128)(2,1)S(1)}, bf16[144,256]{1,0:T(8,128)(2,1)S(1)}, u32[]{:S(2)}, u32[]{:S(2)}) collective-permute-start(bf16[144,256]{1,0:T(8,128)(2,1)S(1)} %collective-permute-done.23.refs_4_), channel_id=1, source_target_pairs={{0,32},{1,33},{2,34},{3,35},{4,36},{5,37},{6,38},{7,39},{8,40},{9,... | collective-permute-start | bytes 221192 | tf_op jit(solution)/shard_map/ppermute | solution.py:29

commit v7 on v6

--- a/solution.py
+++ b/solution.py
@@ -115,23 +115,35 @@
 SPLIT = ((1, 0), (1, 1), (0, 0), (0, 1))
 
 
-def tiles_kernel(classes, split, n_in, n_extra, place, *refs):
+def tiles_kernel(classes, split, pieces, n_extra, place, *refs):
+    n_in = sum(pieces)
     ins = refs[:n_in]
     n_out = 4 if split else 2
     outs, (held, *accs, sems) = refs[n_in + n_extra :][:n_out], refs[n_in + n_extra + n_out :]
     yh, yl, c = place[0], place[1], place[2]
     rows = outs[0].shape[1]
     size = rows // 2 if split else rows
-    copies = [pltpu.make_async_copy(r, held.at[i], sems.at[i]) for i, r in enumerate(ins)]
-    for copy in copies:
-        copy.start()
+    copies, at = [], 0
+    for i, n in enumerate(pieces):
+        part = rows // n
+        copies.append(
+            [
+                pltpu.make_async_copy(ins[at + j], held.at[i, j * part : (j + 1) * part], sems.at[at + j])
+                for j in range(n)
+            ]
+        )
+        at += n
+    for group in copies:
+        for copy in group:
+            copy.start()
     ready = set()
     row = lax.broadcasted_iota(jnp.int32, (16, rows), 0)
     bounds = jnp.zeros((16, rows), jnp.float32)
     for k, names in enumerate(classes):
         for i in (i for pair in names for i in pair):
             if i not in ready:
-                copies[i].wait()
+                for copy in copies[i]:
+                    copy.wait()
                 ready.add(i)
         acc = accs[k % 2]
         r, own, other = (i if i == j else jnp.where(c == 0, i, j) for i, j in names)
@@ -150,16 +162,18 @@
 def partial_tiles(place, arrays, classes, split, rows, after=()):
     names = list(arrays)
     listed = tuple(tuple((names.index(i), names.index(j)) for i, j in k) for k in classes)
-    depth = arrays[names[0]].shape[1]
+    pieces = tuple(len(v) for v in arrays.values())
+    blocks = [v for p in arrays.values() for v in p]
+    depth = blocks[0].shape[1]
     return call(
-        functools.partial(tiles_kernel, listed, split, len(names), len(after)),
-        [place, *arrays.values(), *after],
+        functools.partial(tiles_kernel, listed, split, pieces, len(after)),
+        [place, *blocks, *after],
         [coded_shape(len(classes), rows // 2 if split else rows, rows)] * (4 if split else 2),
         scratch=[
             pltpu.VMEM((len(names), rows, depth), jnp.bfloat16),
             pltpu.VMEM((2, rows, rows), jnp.float32),
             pltpu.VMEM((2, rows, rows), jnp.float32),
-            pltpu.SemaphoreType.DMA((len(names),)),
+            pltpu.SemaphoreType.DMA((len(blocks),)),
         ],
         any_from=1,
         flops=len(classes) * 4 * rows * rows * depth,
@@ -306,16 +320,17 @@
     held["me"] = fetch(held["q3"], MX, MZ)
     for name, source in (("s1", "q1"), ("s2", "q2")):
         held[name] = move(held[source], to_core)
-    held["so"] = move(lax.optimization_barrier((held["o"], held["q4"]))[0], to_core)
+    held["so"] = move(lax.optimization_barrier((held["o"], held["q1"]))[0], to_core)
 
     coded, after = [], ()
     for classes in (EARLY, LATE):
         if after:
             first, _ = lax.optimization_barrier((held["pe"], after[0]))
-            held["spe"] = move(first, to_core)
+            half = rows // 2
+            held["spe"] = (move(first[:half], to_core), move(first[half:], to_core))
         listed = [(OWN[r], OWN[q], OTHER[q]) for r, q in classes]
         used = {i for k in listed for pair in k for i in pair}
-        arrays = {name: v for name, v in held.items() if name in used}
+        arrays = {name: v if isinstance(v, tuple) else (v,) for name, v in held.items() if name in used}
         coded.append(partial_tiles(place, arrays, listed, bool(after), rows, after))
         after = (coded[-1][0],)
 

time: 114 us -> 112 us (0.982)
  waiting for transfers between devices: 51.6 us -> 46.6 us
  starting transfers between devices: 35.2 us -> 39.5 us
  local copies, waits for them, and re-layouts: 3.77 us -> 1.65 us
    ppermute x29 -> x30, waiting for transfers between devices: 51.6 us -> 46.6 us  [move(): return lax.ppermute(value, ('aux', 'blk'), pairs)]
    ppermute x29 -> x30, starting transfers between devices: 35.2 us -> 39.5 us  [move(): return lax.ppermute(value, ('aux', 'blk'), pairs)]
    unnamed x5 -> x1, local copies, waits for them, and re-layouts: 3.69 us -> 1.5 us
  transfers between devices with their start and end apart: 29 -> 30, of which waited for: 11 -> 13; matrix products, arithmetic and copies ran while one was open for 0% -> 0% of each run, Pallas kernels for 15% -> 16%
where the time goes in v7:
time: 112 us; the launch traced here: 111 us
  waiting for transfers between devices  46.6 us (42%)
  starting transfers between devices  39.5 us (35%)
  Pallas kernels  23.2 us (21%)
  local copies, waits for them, and re-layouts  1.65 us (1%)
    ppermute x30, waiting for transfers between devices, move(): return lax.ppermute(value, ('aux', 'blk'), pairs)  46.6 us
    ppermute x30, starting transfers between devices, move(): return lax.ppermute(value, ('aux', 'blk'), pairs)  39.5 us
    pallas_call x7, Pallas kernels, call(): pl.pallas_call(kernel, out_shape=out_shape, in_specs=specs, out_specs=[wh...  23.2 us
  transfers between devices with their start and end apart: 30, of which 13 were waited for; matrix products, arithmetic and copies ran while one was open for 0% of the time, Pallas kernels for 16%

profile of v7, /device:TPU:9, one launch (start us, length us, event | category | flops | bytes accessed | tf_op | source)
XLA Modules:
  0.0 111.3 jit_solution(8379412646159846411)
XLA Ops:
  0.0 1.5 %copy.4 = bf16[32,8,16,128]{3,1,2,0:T(8,128)(2,1)S(1)} copy(bf16[32,8,16,128]{3,2,1,0:T(8,128)(2,1)} %bitcast.9) | data formatting | bytes 2097152
  1.5 4.5 %collective-permute-start = (bf16[256,2048]{1,0:T(8,128)(2,1)S(1)}, bf16[256,2048]{1,0:T(8,128)(2,1)}, u32[]{:S(2)}, u32[]{:S(2)}) collective-permute-start(bf16[256,2048]{1,0:T(8,128)(2,1)S(1)} %bitcast.10), channel_id=1, source_target_pairs={{0,0},{1,1},{2,2},{3,3},{4,4},{5,5},{6,6},{7,7},{8,8},{9,9},{10,10... | collective-permute-start | bytes 3145736 | tf_op jit(solution)/shard_map/ppermute | solution.py:29
  6.0 13.5 %collective-permute-done.refs_0_ = bf16[256,2048]{1,0:T(8,128)(2,1)} collective-permute-done((bf16[256,2048]{1,0:T(8,128)(2,1)S(1)}, bf16[256,2048]{1,0:T(8,128)(2,1)}, u32[]{:S(2)}, u32[]{:S(2)}) %collective-permute-start) | collective-permute-done | bytes 1048608 | tf_op jit(solution)/shard_map/ppermute | solution.py:29
  19.5 2.5 %collective-permute-start.1 = (bf16[256,2048]{1,0:T(8,128)(2,1)}, bf16[256,2048]{1,0:T(8,128)(2,1)S(1)}, u32[]{:S(2)}, u32[]{:S(2)}) collective-permute-start(bf16[256,2048]{1,0:T(8,128)(2,1)} %collective-permute-done.refs_0_), channel_id=1, source_target_pairs={{0,12},{1,13},{2,14},{3,15},{4,0},{5,1},{6,2},{7,3},{8,4},{9,5},{1... | collective-permute-start | bytes 3145736 | tf_op jit(solution)/shard_map/ppermute | solution.py:29
  22.0 3.7 %collective-permute-start.2 = (bf16[256,2048]{1,0:T(8,128)(2,1)}, bf16[256,2048]{1,0:T(8,128)(2,1)S(1)}, u32[]{:S(2)}, u32[]{:S(2)}) collective-permute-start(bf16[256,2048]{1,0:T(8,128)(2,1)} %collective-permute-done.refs_0_), channel_id=1, source_target_pairs={{0,3},{1,0},{2,1},{3,2},{4,7},{5,4},{6,5},{7,6},{8,11},{9,8},{10,9... | collective-permute-start | bytes 3145736 | tf_op jit(solution)/shard_map/ppermute | solution.py:29
  25.7 0.0 collective-permute-start.3
  25.7 8.4 %collective-permute-done.1.refs_1_.refs_0_ = bf16[256,2048]{1,0:T(8,128)(2,1)S(1)} collective-permute-done((bf16[256,2048]{1,0:T(8,128)(2,1)}, bf16[256,2048]{1,0:T(8,128)(2,1)S(1)}, u32[]{:S(2)}, u32[]{:S(2)}) %collective-permute-start.1) | collective-permute-done | bytes 1048608 | tf_op jit(solution)/shard_map/ppermute | solution.py:29
  34.1 0.0 collective-permute-start.7
  34.1 0.5 collective-permute-start.5
  34.6 3.1 %collective-permute-done.2.refs_2_.refs_1_ = bf16[256,2048]{1,0:T(8,128)(2,1)S(1)} collective-permute-done((bf16[256,2048]{1,0:T(8,128)(2,1)}, bf16[256,2048]{1,0:T(8,128)(2,1)S(1)}, u32[]{:S(2)}, u32[]{:S(2)}) %collective-permute-start.2) | collective-permute-done | bytes 1048608 | tf_op jit(solution)/shard_map/ppermute | solution.py:29
  37.7 3.1 %collective-permute-done.3.refs_3_ = bf16[256,2048]{1,0:T(8,128)(2,1)} collective-permute-done((bf16[256,2048]{1,0:T(8,128)(2,1)}, bf16[256,2048]{1,0:T(8,128)(2,1)}, u32[]{:S(2)}, u32[]{:S(2)}) %collective-permute-start.3) | collective-permute-done | bytes 1048608 | tf_op jit(solution)/shard_map/ppermute | solution.py:29
  40.8 0.1 collective-permute-start.10
  41.0 0.1 stack.23.place
  41.0 1.3 %collective-permute-start.11 = (bf16[256,2048]{1,0:T(8,128)(2,1)}, bf16[256,2048]{1,0:T(8,128)(2,1)S(1)}, u32[]{:S(2)}, u32[]{:S(2)}) collective-permute-start(bf16[256,2048]{1,0:T(8,128)(2,1)} %collective-permute-done.3.refs_3_), channel_id=1, source_target_pairs={{0,1},{1,2},{2,3},{3,0},{4,5},{5,6},{6,7},{7,4},{8,9},{9,10},{10,1... | collective-permute-start | bytes 3145736 | tf_op jit(solution)/shard_map/ppermute | solution.py:29
  42.4 9.3 %shard_map.17 = (bf16[1808,256]{1,0:T(8,128)(2,1)S(1)}, bf16[1808,256]{1,0:T(8,128)(2,1)S(1)}) custom-call(s32[5]{0:T(128)S(1)} %stack.23.place, bf16[256,2048]{1,0:T(8,128)(2,1)} %collective-permute-done.refs_0_, bf16[256,2048]{1,0:T(8,128)(2,1)S(1)} %collective-permute-done.1.refs_1_.refs_0_, bf16[256,2048]{1,0:T(8,128)(2,1)S(1)} %collective-permute-done.2.refs_2_.refs_1_, ...), custom_call_target="tpu_custom_call" | custom-call | flops 3758096384 | bytes 8388608 | tf_op jit(solution)/shard_map/pallas_call | solution.py:103
  51.8 4.0 %collective-permute-start.8 = (bf16[1808,256]{1,0:T(8,128)(2,1)S(1)}, bf16[1808,256]{1,0:T(8,128)(2,1)S(1)}, u32[]{:S(2)}, u32[]{:S(2)}) collective-permute-start(bf16[1808,256]{1,0:T(8,128)(2,1)S(1)} %get-tuple-element.28.refs_8_), channel_id=1, source_target_pairs={{0,64},{1,65},{2,66},{3,67},{4,68},{5,69},{6,70},{7,71},{8,72},{9,... | collective-permute-start | bytes 2777096 | tf_op jit(solution)/shard_map/ppermute | solution.py:29
  55.8 5.8 %collective-permute-start.9 = (bf16[1808,256]{1,0:T(8,128)(2,1)S(1)}, bf16[1808,256]{1,0:T(8,128)(2,1)S(1)}, u32[]{:S(2)}, u32[]{:S(2)}) collective-permute-start(bf16[1808,256]{1,0:T(8,128)(2,1)S(1)} %get-tuple-element.29), channel_id=1, source_target_pairs={{0,0},{1,1},{2,2},{3,3},{4,4},{5,5},{6,6},{7,7},{8,8},{9,9},{10,10... | collective-permute-start | bytes 2777096 | tf_op jit(solution)/shard_map/ppermute | solution.py:29
  61.6 0.1 fusion
  61.7 0.1 collective-permute-start.12
  61.8 0.5 collective-permute-start.13
  62.3 1.4 %collective-permute-done.12.refs_6_ = bf16[128,2048]{1,0:T(8,128)(2,1)S(1)} collective-permute-done((bf16[128,2048]{1,0:T(8,128)(2,1)S(1)}, bf16[128,2048]{1,0:T(8,128)(2,1)S(1)}, u32[]{:S(2)}, u32[]{:S(2)}) %collective-permute-start.12) | collective-permute-done | bytes 524320 | tf_op jit(solution)/shard_map/ppermute | solution.py:29
  63.7 0.7 collective-permute-done.13.refs_7_
  64.4 5.5 %shard_map.18 = (bf16[400,256]{1,0:T(8,128)(2,1)S(1)}, bf16[400,256]{1,0:T(8,128)(2,1)S(1)}, bf16[400,256]{1,0:T(8,128)(2,1)S(1)}, bf16[400,256]{1,0:T(8,128)(2,1)S(1)}) custom-call(s32[5]{0:T(128)S(1)} %stack.23.place, bf16[256,2048]{1,0:T(8,128)(2,1)S(1)} %collective-permute-done.1.refs_1_.refs_0_, ...), custom_call_target="tpu_custom_call" | custom-call | flops 1610612736 | bytes 7340032 | tf_op jit(solution)/shard_map/pallas_call | solution.py:103
  70.0 0.1 collective-permute-start.15
  70.0 0.1 collective-permute-start.16
  70.1 5.6 %collective-permute-start.17 = (bf16[400,256]{1,0:T(8,128)(2,1)S(1)}, bf16[400,256]{1,0:T(8,128)(2,1)S(1)}, u32[]{:S(2)}, u32[]{:S(2)}) collective-permute-start(bf16[400,256]{1,0:T(8,128)(2,1)S(1)} %get-tuple-element.35), channel_id=1, source_target_pairs={{0,0},{1,1},{2,2},{3,3},{4,4},{5,5},{6,6},{7,7},{8,8},{9,9},{10,10... | collective-permute-start | bytes 614408 | tf_op jit(solution)/shard_map/ppermute | solution.py:29
  75.8 0.4 collective-permute-done.8.a
  76.1 2.1 %collective-permute-done.9.b = bf16[1808,256]{1,0:T(8,128)(2,1)S(1)} collective-permute-done((bf16[1808,256]{1,0:T(8,128)(2,1)S(1)}, bf16[1808,256]{1,0:T(8,128)(2,1)S(1)}, u32[]{:S(2)}, u32[]{:S(2)}) %collective-permute-start.9) | collective-permute-done | bytes 925728 | tf_op jit(solution)/shard_map/ppermute | solution.py:29
  78.2 2.6 %shard_map.19 = (f32[6,128,256]{2,1,0:T(8,128)S(1)}, f32[6,128,256]{2,1,0:T(8,128)}) custom-call(s32[5]{0:T(128)S(1)} %stack.23.place, bf16[1808,256]{1,0:T(8,128)(2,1)S(1)} %collective-permute-done.8.a, bf16[1808,256]{1,0:T(8,128)(2,1)S(1)} %collective-permute-done.9.b, bf16[400,256]{1,0:T(8,128)(2,1)S(1)} %get-tuple-element.31._), custom_call_target="tpu_custom_call" | custom-call | flops 1 | bytes 1 | tf_op jit(solution)/shard_map/pallas_call | solution.py:103
  80.8 1.9 %collective-permute-done.15.a = bf16[400,256]{1,0:T(8,128)(2,1)S(1)} collective-permute-done((bf16[400,256]{1,0:T(8,128)(2,1)S(1)}, bf16[400,256]{1,0:T(8,128)(2,1)S(1)}, u32[]{:S(2)}, u32[]{:S(2)}) %collective-permute-start.15) | collective-permute-done | bytes 204832 | tf_op jit(solution)/shard_map/ppermute | solution.py:29
  82.7 2.2 %collective-permute-done.16.b = bf16[400,256]{1,0:T(8,128)(2,1)S(1)} collective-permute-done((bf16[400,256]{1,0:T(8,128)(2,1)S(1)}, bf16[400,256]{1,0:T(8,128)(2,1)S(1)}, u32[]{:S(2)}, u32[]{:S(2)}) %collective-permute-start.16) | collective-permute-done | bytes 204832 | tf_op jit(solution)/shard_map/ppermute | solution.py:29
  84.9 0.7 shard_map.20.late
  85.6 1.8 %shard_map.21 = (bf16[656,256]{1,0:T(8,128)(2,1)S(1)}, bf16[272,256]{1,0:T(8,128)(2,1)S(1)}, bf16[400,256]{1,0:T(8,128)(2,1)S(1)}, bf16[272,256]{1,0:T(8,128)(2,1)S(1)}, bf16[144,256]{1,0:T(8,128)(2,1)S(1)}) custom-call(f32[6,128,256]{2,1,0:T(8,128)S(1)} %get-tuple-element.32.kept, f32[6,128,256]{2,1,0:T(8,128)} %collective-permute-done.14.given, ...), custom_call_target="tpu_custom_call" | custom-call | bytes 4194304 | tf_op jit(solution)/shard_map/pallas_call | solution.py:103
  87.4 0.6 shard_map.22.refs_10_
  88.1 1.5 %collective-permute-start.22 = (f32[3,256,256]{2,1,0:T(8,128)S(1)}, f32[3,256,256]{2,1,0:T(8,128)S(1)}, u32[]{:S(2)}, u32[]{:S(2)}) collective-permute-start(f32[3,256,256]{2,1,0:T(8,128)S(1)} %shard_map.22.refs_10_), channel_id=1, source_target_pairs={{0,32},{1,33},{2,34},{3,35},{4,36},{5,37},{6,38},{7,39},{8,40},{9,... | collective-permute-start | bytes 2359304 | tf_op jit(solution)/shard_map/ppermute | solution.py:29
  89.6 0.0 collective-permute-start.19
  89.6 3.5 %collective-permute-start.21 = (bf16[400,256]{1,0:T(8,128)(2,1)S(1)}, bf16[400,256]{1,0:T(8,128)(2,1)S(1)}, u32[]{:S(2)}, u32[]{:S(2)}) collective-permute-start(bf16[400,256]{1,0:T(8,128)(2,1)S(1)} %get-tuple-element.39), channel_id=1, source_target_pairs={{0,15},{1,12},{2,13},{3,14},{4,3},{5,0},{6,1},{7,2},{8,7},{9,4},{1... | collective-permute-start | bytes 614408 | tf_op jit(solution)/shard_map/ppermute | solution.py:29
  93.1 1.3 %collective-permute-start.20 = (bf16[272,256]{1,0:T(8,128)(2,1)S(1)}, bf16[272,256]{1,0:T(8,128)(2,1)S(1)}, u32[]{:S(2)}, u32[]{:S(2)}) collective-permute-start(bf16[272,256]{1,0:T(8,128)(2,1)S(1)} %get-tuple-element.38), channel_id=1, source_target_pairs={{0,4},{1,5},{2,6},{3,7},{4,8},{5,9},{6,10},{7,11},{8,12},{9,13},{1... | collective-permute-start | bytes 417800 | tf_op jit(solution)/shard_map/ppermute | solution.py:29
  94.4 2.3 %collective-permute-start.23 = (bf16[272,256]{1,0:T(8,128)(2,1)S(1)}, bf16[272,256]{1,0:T(8,128)(2,1)S(1)}, u32[]{:S(2)}, u32[]{:S(2)}) collective-permute-start(bf16[272,256]{1,0:T(8,128)(2,1)S(1)} %get-tuple-element.41), channel_id=1, source_target_pairs={{0,12},{1,13},{2,14},{3,15},{4,0},{5,1},{6,2},{7,3},{8,4},{9,5},{1... | collective-permute-start | bytes 417800 | tf_op jit(solution)/shard_map/ppermute | solution.py:29
  96.7 4.7 %collective-permute-done.24.refs_4_ = bf16[144,256]{1,0:T(8,128)(2,1)S(1)} collective-permute-done((bf16[144,256]{1,0:T(8,128)(2,1)S(1)}, bf16[144,256]{1,0:T(8,128)(2,1)S(1)}, u32[]{:S(2)}, u32[]{:S(2)}) %collective-permute-start.24) | collective-permute-done | bytes 73760 | tf_op jit(solution)/shard_map/ppermute | solution.py:29
  101.4 4.0 %collective-permute-done.20.refs_1_ = bf16[272,256]{1,0:T(8,128)(2,1)S(1)} collective-permute-done((bf16[272,256]{1,0:T(8,128)(2,1)S(1)}, bf16[272,256]{1,0:T(8,128)(2,1)S(1)}, u32[]{:S(2)}, u32[]{:S(2)}) %collective-permute-start.20) | collective-permute-done | bytes 139296 | tf_op jit(solution)/shard_map/ppermute | solution.py:29
  105.4 1.0 collective-permute-start.25
  106.4 0.1 collective-permute-start.27
  106.5 0.4 collective-permute-start.26
  107.0 0.1 collective-permute-start.28
  107.0 0.4 collective-permute-start.29
  107.5 1.0 collective-permute-done.29.refs_9_
  108.5 2.6 %shard_map.23 = f32[256,2048]{1,0:T(8,128)} custom-call(s32[5]{0:T(128)S(1)} %stack.23.place, bf16[656,256]{1,0:T(8,128)(2,1)S(1)} %collective-permute-done.19.refs_0_, bf16[272,256]{1,0:T(8,128)(2,1)S(1)} %collective-permute-done.20.refs_1_, bf16[400,256]{1,0:T(8,128)(2,1)S(1)} %collective-permute-done.21.refs_2_, ...), custom_call_target="tpu_custom_call" | custom-call | bytes 6291456 | tf_op jit(solution)/shard_map/pallas_call | solution.py:103
  (22 shorter events, 0.1 us)
Async XLA Ops:
  1.5 18.0 %collective-permute-start = (bf16[256,2048]{1,0:T(8,128)(2,1)S(1)}, bf16[256,2048]{1,0:T(8,128)(2,1)}, u32[]{:S(2)}, u32[]{:S(2)}) collective-permute-start(bf16[256,2048]{1,0:T(8,128)(2,1)S(1)} %bitcast.10), channel_id=1, source_target_pairs={{0,0},{1,1},{2,2},{3,3},{4,4},{5,5},{6,6},{7,7},{8,8},{9,9},{10,10... | collective-permute-start | bytes 3145736 | tf_op jit(solution)/shard_map/ppermute | solution.py:29
  19.5 14.6 %collective-permute-start.1 = (bf16[256,2048]{1,0:T(8,128)(2,1)}, bf16[256,2048]{1,0:T(8,128)(2,1)S(1)}, u32[]{:S(2)}, u32[]{:S(2)}) collective-permute-start(bf16[256,2048]{1,0:T(8,128)(2,1)} %collective-permute-done.refs_0_), channel_id=1, source_target_pairs={{0,12},{1,13},{2,14},{3,15},{4,0},{5,1},{6,2},{7,3},{8,4},{9,5},{1... | collective-permute-start | bytes 3145736 | tf_op jit(solution)/shard_map/ppermute | solution.py:29
  22.0 15.7 %collective-permute-start.2 = (bf16[256,2048]{1,0:T(8,128)(2,1)}, bf16[256,2048]{1,0:T(8,128)(2,1)S(1)}, u32[]{:S(2)}, u32[]{:S(2)}) collective-permute-start(bf16[256,2048]{1,0:T(8,128)(2,1)} %collective-permute-done.refs_0_), channel_id=1, source_target_pairs={{0,3},{1,0},{2,1},{3,2},{4,7},{5,4},{6,5},{7,6},{8,11},{9,8},{10,9... | collective-permute-start | bytes 3145736 | tf_op jit(solution)/shard_map/ppermute | solution.py:29
  25.7 15.2 %collective-permute-start.3 = (bf16[256,2048]{1,0:T(8,128)(2,1)}, bf16[256,2048]{1,0:T(8,128)(2,1)}, u32[]{:S(2)}, u32[]{:S(2)}) collective-permute-start(bf16[256,2048]{1,0:T(8,128)(2,1)} %collective-permute-done.refs_0_), channel_id=1, source_target_pairs={{0,4},{1,5},{2,6},{3,7},{4,8},{5,9},{6,10},{7,11},{8,12},{9,13},{1... | collective-permute-start | bytes 3145736 | tf_op jit(solution)/shard_map/ppermute | solution.py:29
  25.7 15.4 %collective-permute-start.4 = (bf16[256,2048]{1,0:T(8,128)(2,1)}, bf16[256,2048]{1,0:T(8,128)(2,1)}, u32[]{:S(2)}, u32[]{:S(2)}) collective-permute-start(bf16[256,2048]{1,0:T(8,128)(2,1)} %collective-permute-done.refs_0_), channel_id=1, source_target_pairs={{0,1},{1,2},{2,3},{3,0},{4,5},{5,6},{6,7},{7,4},{8,9},{9,10},{10,1... | collective-permute-start | bytes 3145736 | tf_op jit(solution)/shard_map/ppermute | solution.py:29
  34.1 8.3 %collective-permute-start.7 = (bf16[256,2048]{1,0:T(8,128)(2,1)}, bf16[256,2048]{1,0:T(8,128)(2,1)}, u32[]{:S(2)}, u32[]{:S(2)}) collective-permute-start(bf16[256,2048]{1,0:T(8,128)(2,1)} %collective-permute-done.refs_0_), channel_id=1, source_target_pairs={{0,32},{1,33},{2,34},{3,35},{4,36},{5,37},{6,38},{7,39},{8,40},{9,... | collective-permute-start | bytes 3145736 | tf_op jit(solution)/shard_map/ppermute | solution.py:29
  34.1 8.3 %collective-permute-start.5 = (bf16[256,2048]{1,0:T(8,128)(2,1)S(1)}, bf16[256,2048]{1,0:T(8,128)(2,1)}, u32[]{:S(2)}, u32[]{:S(2)}) collective-permute-start(bf16[256,2048]{1,0:T(8,128)(2,1)S(1)} %collective-permute-done.1.refs_1_.refs_0_), channel_id=1, source_target_pairs={{0,32},{1,33},{2,34},{3,35},{4,36},{5,37},{6,38},{7,39},{8,40},{9,... | collective-permute-start | bytes 3145736 | tf_op jit(solution)/shard_map/ppermute | solution.py:29
  37.7 4.7 %collective-permute-start.6 = (bf16[256,2048]{1,0:T(8,128)(2,1)S(1)}, bf16[256,2048]{1,0:T(8,128)(2,1)}, u32[]{:S(2)}, u32[]{:S(2)}) collective-permute-start(bf16[256,2048]{1,0:T(8,128)(2,1)S(1)} %collective-permute-done.2.refs_2_.refs_1_), channel_id=1, source_target_pairs={{0,32},{1,33},{2,34},{3,35},{4,36},{5,37},{6,38},{7,39},{8,40},{9,... | collective-permute-start | bytes 3145736 | tf_op jit(solution)/shard_map/ppermute | solution.py:29
  40.8 14.9 %collective-permute-start.10 = (bf16[256,2048]{1,0:T(8,128)(2,1)S(1)}, bf16[256,2048]{1,0:T(8,128)(2,1)S(1)}, u32[]{:S(2)}, u32[]{:S(2)}) collective-permute-start(bf16[256,2048]{1,0:T(8,128)(2,1)S(1)} %collective-permute-done.1.refs_1_.refs_0_), channel_id=1, source_target_pairs={{0,3},{1,0},{2,1},{3,2},{4,7},{5,4},{6,5},{7,6},{8,11},{9,8},{10,9... | collective-permute-start | bytes 3145736 | tf_op jit(solution)/shard_map/ppermute | solution.py:29
  41.0 21.3 %collective-permute-start.11 = (bf16[256,2048]{1,0:T(8,128)(2,1)}, bf16[256,2048]{1,0:T(8,128)(2,1)S(1)}, u32[]{:S(2)}, u32[]{:S(2)}) collective-permute-start(bf16[256,2048]{1,0:T(8,128)(2,1)} %collective-permute-done.3.refs_3_), channel_id=1, source_target_pairs={{0,1},{1,2},{2,3},{3,0},{4,5},{5,6},{6,7},{7,4},{8,9},{9,10},{10,1... | collective-permute-start | bytes 3145736 | tf_op jit(solution)/shard_map/ppermute | solution.py:29
  51.8 24.4 %collective-permute-start.8 = (bf16[1808,256]{1,0:T(8,128)(2,1)S(1)}, bf16[1808,256]{1,0:T(8,128)(2,1)S(1)}, u32[]{:S(2)}, u32[]{:S(2)}) collective-permute-start(bf16[1808,256]{1,0:T(8,128)(2,1)S(1)} %get-tuple-element.28.refs_8_), channel_id=1, source_target_pairs={{0,64},{1,65},{2,66},{3,67},{4,68},{5,69},{6,70},{7,71},{8,72},{9,... | collective-permute-start | bytes 2777096 | tf_op jit(solution)/shard_map/ppermute | solution.py:29
  55.8 22.4 %collective-permute-start.9 = (bf16[1808,256]{1,0:T(8,128)(2,1)S(1)}, bf16[1808,256]{1,0:T(8,128)(2,1)S(1)}, u32[]{:S(2)}, u32[]{:S(2)}) collective-permute-start(bf16[1808,256]{1,0:T(8,128)(2,1)S(1)} %get-tuple-element.29), channel_id=1, source_target_pairs={{0,0},{1,1},{2,2},{3,3},{4,4},{5,5},{6,6},{7,7},{8,8},{9,9},{10,10... | collective-permute-start | bytes 2777096 | tf_op jit(solution)/shard_map/ppermute | solution.py:29
  61.7 2.0 %collective-permute-start.12 = (bf16[128,2048]{1,0:T(8,128)(2,1)S(1)}, bf16[128,2048]{1,0:T(8,128)(2,1)S(1)}, u32[]{:S(2)}, u32[]{:S(2)}) collective-permute-start(bf16[128,2048]{1,0:T(8,128)(2,1)S(1)} %get-tuple-element.50), channel_id=1, source_target_pairs={{0,32},{1,33},{2,34},{3,35},{4,36},{5,37},{6,38},{7,39},{8,40},{9,... | collective-permute-start | bytes 1572872 | tf_op jit(solution)/shard_map/ppermute | solution.py:29
  61.8 2.6 %collective-permute-start.13 = (bf16[128,2048]{1,0:T(8,128)(2,1)S(1)}, bf16[128,2048]{1,0:T(8,128)(2,1)S(1)}, u32[]{:S(2)}, u32[]{:S(2)}) collective-permute-start(bf16[128,2048]{1,0:T(8,128)(2,1)S(1)} %get-tuple-element.49), channel_id=1, source_target_pairs={{0,32},{1,33},{2,34},{3,35},{4,36},{5,37},{6,38},{7,39},{8,40},{9,... | collective-permute-start | bytes 1572872 | tf_op jit(solution)/shard_map/ppermute | solution.py:29
  70.0 12.8 %collective-permute-start.15 = (bf16[400,256]{1,0:T(8,128)(2,1)S(1)}, bf16[400,256]{1,0:T(8,128)(2,1)S(1)}, u32[]{:S(2)}, u32[]{:S(2)}) collective-permute-start(bf16[400,256]{1,0:T(8,128)(2,1)S(1)} %get-tuple-element.31._), channel_id=1, source_target_pairs={{0,64},{1,65},{2,66},{3,67},{4,68},{5,69},{6,70},{7,71},{8,72},{9,... | collective-permute-start | bytes 614408 | tf_op jit(solution)/shard_map/ppermute | solution.py:29
  70.0 14.9 %collective-permute-start.16 = (bf16[400,256]{1,0:T(8,128)(2,1)S(1)}, bf16[400,256]{1,0:T(8,128)(2,1)S(1)}, u32[]{:S(2)}, u32[]{:S(2)}) collective-permute-start(bf16[400,256]{1,0:T(8,128)(2,1)S(1)} %get-tuple-element.34), channel_id=1, source_target_pairs={{0,96},{1,97},{2,98},{3,99},{4,100},{5,101},{6,102},{7,103},{8,104... | collective-permute-start | bytes 614408 | tf_op jit(solution)/shard_map/ppermute | solution.py:29
  70.1 14.8 %collective-permute-start.17 = (bf16[400,256]{1,0:T(8,128)(2,1)S(1)}, bf16[400,256]{1,0:T(8,128)(2,1)S(1)}, u32[]{:S(2)}, u32[]{:S(2)}) collective-permute-start(bf16[400,256]{1,0:T(8,128)(2,1)S(1)} %get-tuple-element.35), channel_id=1, source_target_pairs={{0,0},{1,1},{2,2},{3,3},{4,4},{5,5},{6,6},{7,7},{8,8},{9,9},{10,10... | collective-permute-start | bytes 614408 | tf_op jit(solution)/shard_map/ppermute | solution.py:29
  76.1 8.8 %collective-permute-start.18 = (bf16[400,256]{1,0:T(8,128)(2,1)S(1)}, bf16[400,256]{1,0:T(8,128)(2,1)S(1)}, u32[]{:S(2)}, u32[]{:S(2)}) collective-permute-start(bf16[400,256]{1,0:T(8,128)(2,1)S(1)} %get-tuple-element.36), channel_id=1, source_target_pairs={{0,32},{1,33},{2,34},{3,35},{4,36},{5,37},{6,38},{7,39},{8,40},{9,... | collective-permute-start | bytes 614408 | tf_op jit(solution)/shard_map/ppermute | solution.py:29
  80.8 4.8 %collective-permute-start.14 = (f32[6,128,256]{2,1,0:T(8,128)}, f32[6,128,256]{2,1,0:T(8,128)}, u32[]{:S(2)}, u32[]{:S(2)}) collective-permute-start(f32[6,128,256]{2,1,0:T(8,128)} %get-tuple-element.33), channel_id=1, source_target_pairs={{0,32},{1,33},{2,34},{3,35},{4,36},{5,37},{6,38},{7,39},{8,40},{9,... | collective-permute-start | bytes 2359304 | tf_op jit(solution)/shard_map/ppermute | solution.py:29
  88.1 6.3 %collective-permute-start.22 = (f32[3,256,256]{2,1,0:T(8,128)S(1)}, f32[3,256,256]{2,1,0:T(8,128)S(1)}, u32[]{:S(2)}, u32[]{:S(2)}) collective-permute-start(f32[3,256,256]{2,1,0:T(8,128)S(1)} %shard_map.22.refs_10_), channel_id=1, source_target_pairs={{0,32},{1,33},{2,34},{3,35},{4,36},{5,37},{6,38},{7,39},{8,40},{9,... | collective-permute-start | bytes 2359304 | tf_op jit(solution)/shard_map/ppermute | solution.py:29
  89.6 15.8 %collective-permute-start.19 = (bf16[656,256]{1,0:T(8,128)(2,1)S(1)}, bf16[656,256]{1,0:T(8,128)(2,1)S(1)}, u32[]{:S(2)}, u32[]{:S(2)}) collective-permute-start(bf16[656,256]{1,0:T(8,128)(2,1)S(1)} %get-tuple-element.37._), channel_id=1, source_target_pairs={{0,1},{1,2},{2,3},{3,0},{4,5},{5,6},{6,7},{7,4},{8,9},{9,10},{10,1... | collective-permute-start | bytes 1007624 | tf_op jit(solution)/shard_map/ppermute | solution.py:29
  89.6 15.8 %collective-permute-start.21 = (bf16[400,256]{1,0:T(8,128)(2,1)S(1)}, bf16[400,256]{1,0:T(8,128)(2,1)S(1)}, u32[]{:S(2)}, u32[]{:S(2)}) collective-permute-start(bf16[400,256]{1,0:T(8,128)(2,1)S(1)} %get-tuple-element.39), channel_id=1, source_target_pairs={{0,15},{1,12},{2,13},{3,14},{4,3},{5,0},{6,1},{7,2},{8,7},{9,4},{1... | collective-permute-start | bytes 614408 | tf_op jit(solution)/shard_map/ppermute | solution.py:29
  93.1 12.3 %collective-permute-start.20 = (bf16[272,256]{1,0:T(8,128)(2,1)S(1)}, bf16[272,256]{1,0:T(8,128)(2,1)S(1)}, u32[]{:S(2)}, u32[]{:S(2)}) collective-permute-start(bf16[272,256]{1,0:T(8,128)(2,1)S(1)} %get-tuple-element.38), channel_id=1, source_target_pairs={{0,4},{1,5},{2,6},{3,7},{4,8},{5,9},{6,10},{7,11},{8,12},{9,13},{1... | collective-permute-start | bytes 417800 | tf_op jit(solution)/shard_map/ppermute | solution.py:29
  94.4 11.0 %collective-permute-start.23 = (bf16[272,256]{1,0:T(8,128)(2,1)S(1)}, bf16[272,256]{1,0:T(8,128)(2,1)S(1)}, u32[]{:S(2)}, u32[]{:S(2)}) collective-permute-start(bf16[272,256]{1,0:T(8,128)(2,1)S(1)} %get-tuple-element.41), channel_id=1, source_target_pairs={{0,12},{1,13},{2,14},{3,15},{4,0},{5,1},{6,2},{7,3},{8,4},{9,5},{1... | collective-permute-start | bytes 417800 | tf_op jit(solution)/shard_map/ppermute | solution.py:29
  96.7 4.7 %collective-permute-start.24 = (bf16[144,256]{1,0:T(8,128)(2,1)S(1)}, bf16[144,256]{1,0:T(8,128)(2,1)S(1)}, u32[]{:S(2)}, u32[]{:S(2)}) collective-permute-start(bf16[144,256]{1,0:T(8,128)(2,1)S(1)} %get-tuple-element.42), channel_id=1, source_target_pairs={{0,4},{1,5},{2,6},{3,7},{4,8},{5,9},{6,10},{7,11},{8,12},{9,13},{1... | collective-permute-start | bytes 221192 | tf_op jit(solution)/shard_map/ppermute | solution.py:29
  105.4 3.1 %collective-permute-start.25 = (bf16[656,256]{1,0:T(8,128)(2,1)S(1)}, bf16[656,256]{1,0:T(8,128)(2,1)S(1)}, u32[]{:S(2)}, u32[]{:S(2)}) collective-permute-start(bf16[656,256]{1,0:T(8,128)(2,1)S(1)} %collective-permute-done.19.refs_0_), channel_id=1, source_target_pairs={{0,32},{1,33},{2,34},{3,35},{4,36},{5,37},{6,38},{7,39},{8,40},{9,... | collective-permute-start | bytes 1007624 | tf_op jit(solution)/shard_map/ppermute | solution.py:29
  106.4 2.1 %collective-permute-start.27 = (bf16[400,256]{1,0:T(8,128)(2,1)S(1)}, bf16[400,256]{1,0:T(8,128)(2,1)S(1)}, u32[]{:S(2)}, u32[]{:S(2)}) collective-permute-start(bf16[400,256]{1,0:T(8,128)(2,1)S(1)} %collective-permute-done.21.refs_2_), channel_id=1, source_target_pairs={{0,32},{1,33},{2,34},{3,35},{4,36},{5,37},{6,38},{7,39},{8,40},{9,... | collective-permute-start | bytes 614408 | tf_op jit(solution)/shard_map/ppermute | solution.py:29
  106.5 2.0 %collective-permute-start.26 = (bf16[272,256]{1,0:T(8,128)(2,1)S(1)}, bf16[272,256]{1,0:T(8,128)(2,1)S(1)}, u32[]{:S(2)}, u32[]{:S(2)}) collective-permute-start(bf16[272,256]{1,0:T(8,128)(2,1)S(1)} %collective-permute-done.20.refs_1_), channel_id=1, source_target_pairs={{0,32},{1,33},{2,34},{3,35},{4,36},{5,37},{6,38},{7,39},{8,40},{9,... | collective-permute-start | bytes 417800 | tf_op jit(solution)/shard_map/ppermute | solution.py:29
  107.0 1.6 %collective-permute-start.28 = (bf16[272,256]{1,0:T(8,128)(2,1)S(1)}, bf16[272,256]{1,0:T(8,128)(2,1)S(1)}, u32[]{:S(2)}, u32[]{:S(2)}) collective-permute-start(bf16[272,256]{1,0:T(8,128)(2,1)S(1)} %collective-permute-done.23.refs_3_), channel_id=1, source_target_pairs={{0,32},{1,33},{2,34},{3,35},{4,36},{5,37},{6,38},{7,39},{8,40},{9,... | collective-permute-start | bytes 417800 | tf_op jit(solution)/shard_map/ppermute | solution.py:29
  107.0 1.5 %collective-permute-start.29 = (bf16[144,256]{1,0:T(8,128)(2,1)S(1)}, bf16[144,256]{1,0:T(8,128)(2,1)S(1)}, u32[]{:S(2)}, u32[]{:S(2)}) collective-permute-start(bf16[144,256]{1,0:T(8,128)(2,1)S(1)} %collective-permute-done.24.refs_4_), channel_id=1, source_target_pairs={{0,32},{1,33},{2,34},{3,35},{4,36},{5,37},{6,38},{7,39},{8,40},{9,... | collective-permute-start | bytes 221192 | tf_op jit(solution)/shard_map/ppermute | solution.py:29

commit v8 on v7

--- a/solution.py
+++ b/solution.py
@@ -197,7 +197,7 @@
         out[k, :, :] = part_of(a, k, rows) + part_of(b, k, rows)
 
 
-def half_sum_kernel(a, b, c, d, out):
+def half_sum_kernel(a, b, c, d, _, out):
     half = a.shape[1] // 2
     for k in range(out.shape[0]):
         out[k, :, :] = (part_of(a, k, half) + part_of(b, k, half)) + (part_of(c, k, half) + part_of(d, k, half))
@@ -345,11 +345,20 @@
         flops=1,
         moved=1,
     )
+    full = call(
+        whole_sum_kernel,
+        [*arrived, kept],
+        jax.ShapeDtypeStruct((STAY, rows, rows), jnp.float32),
+        any_from=2,
+        flops=1,
+        moved=1,
+    )
     weight = 10**11
     late = call(
         half_sum_kernel,
-        [move(v, to_owner(*m)) for m, v in zip(SPLIT, coded[1])],
+        [*(move(v, to_owner(*m)) for m, v in zip(SPLIT, coded[1])), full],
         jax.ShapeDtypeStruct((len(LATE), rows // 2, rows), jnp.float32),
+        any_from=4,
         flops=weight,
         moved=weight,
         transcendentals=weight,
@@ -361,14 +370,6 @@
             [coded_shape(len(g), rows // 2, rows) for g in groups],
             moved=4 << 20,
         )
-    )
-    full = call(
-        whole_sum_kernel,
-        [*arrived, parts[0]],
-        jax.ShapeDtypeStruct((STAY, rows, rows), jnp.float32),
-        any_from=2,
-        flops=1,
-        moved=1,
     )
     parts[3], other_full = lax.optimization_barrier((parts[3], move(full, to_core)))
     own, tiles = [], []

time: 112 us -> 110 us (0.982)
  starting transfers between devices: 39.5 us -> 37.6 us
    ppermute x30, starting transfers between devices: 39.5 us -> 37.6 us  [move(): return lax.ppermute(value, ('aux', 'blk'), pairs)]
  transfers between devices with their start and end apart: 30 -> 30, of which waited for: 13 -> 14; matrix products, arithmetic and copies ran while one was open for 0% -> 0% of each run, Pallas kernels for 16% -> 20%
where the time goes in v8:
time: 110 us
  waiting for transfers between devices  46 us (42%)
  starting transfers between devices  37.6 us (34%)
  Pallas kernels  24 us (22%)
  local copies, waits for them, and re-layouts  1.65 us (2%)
    ppermute x30, waiting for transfers between devices, move(): return lax.ppermute(value, ('aux', 'blk'), pairs)  46 us
    ppermute x30, starting transfers between devices, move(): return lax.ppermute(value, ('aux', 'blk'), pairs)  37.6 us
    pallas_call x7, Pallas kernels, call(): pl.pallas_call(kernel, out_shape=out_shape, in_specs=specs, out_specs=[wh...  24 us
  transfers between devices with their start and end apart: 30, of which 14 were waited for; matrix products, arithmetic and copies ran while one was open for 0% of the time, Pallas kernels for 20%

profile of v8, /device:TPU:9, one launch (start us, length us, event | category | flops | bytes accessed | tf_op | source)
XLA Modules:
  0.0 109.5 jit_solution(4335507525224491207)
XLA Ops:
  0.0 1.5 %copy.4 = bf16[32,8,16,128]{3,1,2,0:T(8,128)(2,1)S(1)} copy(bf16[32,8,16,128]{3,2,1,0:T(8,128)(2,1)} %bitcast.9) | data formatting | bytes 2097152
  1.5 4.5 %collective-permute-start = (bf16[256,2048]{1,0:T(8,128)(2,1)S(1)}, bf16[256,2048]{1,0:T(8,128)(2,1)}, u32[]{:S(2)}, u32[]{:S(2)}) collective-permute-start(bf16[256,2048]{1,0:T(8,128)(2,1)S(1)} %bitcast.10), channel_id=1, source_target_pairs={{0,0},{1,1},{2,2},{3,3},{4,4},{5,5},{6,6},{7,7},{8,8},{9,9},{10,10... | collective-permute-start | bytes 3145736 | tf_op jit(solution)/shard_map/ppermute | solution.py:29
  6.0 13.5 %collective-permute-done.refs_0_ = bf16[256,2048]{1,0:T(8,128)(2,1)} collective-permute-done((bf16[256,2048]{1,0:T(8,128)(2,1)S(1)}, bf16[256,2048]{1,0:T(8,128)(2,1)}, u32[]{:S(2)}, u32[]{:S(2)}) %collective-permute-start) | collective-permute-done | bytes 1048608 | tf_op jit(solution)/shard_map/ppermute | solution.py:29
  19.5 2.5 %collective-permute-start.1 = (bf16[256,2048]{1,0:T(8,128)(2,1)}, bf16[256,2048]{1,0:T(8,128)(2,1)S(1)}, u32[]{:S(2)}, u32[]{:S(2)}) collective-permute-start(bf16[256,2048]{1,0:T(8,128)(2,1)} %collective-permute-done.refs_0_), channel_id=1, source_target_pairs={{0,12},{1,13},{2,14},{3,15},{4,0},{5,1},{6,2},{7,3},{8,4},{9,5},{1... | collective-permute-start | bytes 3145736 | tf_op jit(solution)/shard_map/ppermute | solution.py:29
  22.0 3.7 %collective-permute-start.2 = (bf16[256,2048]{1,0:T(8,128)(2,1)}, bf16[256,2048]{1,0:T(8,128)(2,1)S(1)}, u32[]{:S(2)}, u32[]{:S(2)}) collective-permute-start(bf16[256,2048]{1,0:T(8,128)(2,1)} %collective-permute-done.refs_0_), channel_id=1, source_target_pairs={{0,3},{1,0},{2,1},{3,2},{4,7},{5,4},{6,5},{7,6},{8,11},{9,8},{10,9... | collective-permute-start | bytes 3145736 | tf_op jit(solution)/shard_map/ppermute | solution.py:29
  25.7 8.4 %collective-permute-done.1.refs_1_.refs_0_ = bf16[256,2048]{1,0:T(8,128)(2,1)S(1)} collective-permute-done((bf16[256,2048]{1,0:T(8,128)(2,1)}, bf16[256,2048]{1,0:T(8,128)(2,1)S(1)}, u32[]{:S(2)}, u32[]{:S(2)}) %collective-permute-start.1) | collective-permute-done | bytes 1048608 | tf_op jit(solution)/shard_map/ppermute | solution.py:29
  34.1 0.5 collective-permute-start.5
  34.6 3.1 %collective-permute-done.2.refs_2_.refs_1_ = bf16[256,2048]{1,0:T(8,128)(2,1)S(1)} collective-permute-done((bf16[256,2048]{1,0:T(8,128)(2,1)}, bf16[256,2048]{1,0:T(8,128)(2,1)S(1)}, u32[]{:S(2)}, u32[]{:S(2)}) %collective-permute-start.2) | collective-permute-done | bytes 1048608 | tf_op jit(solution)/shard_map/ppermute | solution.py:29
  37.7 3.1 %collective-permute-done.3.refs_3_ = bf16[256,2048]{1,0:T(8,128)(2,1)} collective-permute-done((bf16[256,2048]{1,0:T(8,128)(2,1)}, bf16[256,2048]{1,0:T(8,128)(2,1)}, u32[]{:S(2)}, u32[]{:S(2)}) %collective-permute-start.3) | collective-permute-done | bytes 1048608 | tf_op jit(solution)/shard_map/ppermute | solution.py:29
  40.8 0.1 collective-permute-start.10
  41.0 0.1 stack.23.place
  41.0 1.3 %collective-permute-start.11 = (bf16[256,2048]{1,0:T(8,128)(2,1)}, bf16[256,2048]{1,0:T(8,128)(2,1)S(1)}, u32[]{:S(2)}, u32[]{:S(2)}) collective-permute-start(bf16[256,2048]{1,0:T(8,128)(2,1)} %collective-permute-done.3.refs_3_), channel_id=1, source_target_pairs={{0,1},{1,2},{2,3},{3,0},{4,5},{5,6},{6,7},{7,4},{8,9},{9,10},{10,1... | collective-permute-start | bytes 3145736 | tf_op jit(solution)/shard_map/ppermute | solution.py:29
  42.4 0.0 collective-permute-done.7.refs_7_
  42.4 0.0 collective-permute-done.5.refs_5_.refs_4_
  42.4 9.3 %shard_map.17 = (bf16[1808,256]{1,0:T(8,128)(2,1)S(1)}, bf16[1808,256]{1,0:T(8,128)(2,1)S(1)}) custom-call(s32[5]{0:T(128)S(1)} %stack.23.place, bf16[256,2048]{1,0:T(8,128)(2,1)} %collective-permute-done.refs_0_, bf16[256,2048]{1,0:T(8,128)(2,1)S(1)} %collective-permute-done.1.refs_1_.refs_0_, bf16[256,2048]{1,0:T(8,128)(2,1)S(1)} %collective-permute-done.2.refs_2_.refs_1_, ...), custom_call_target="tpu_custom_call" | custom-call | flops 3758096384 | bytes 8388608 | tf_op jit(solution)/shard_map/pallas_call | solution.py:103
  51.8 4.0 %collective-permute-start.8 = (bf16[1808,256]{1,0:T(8,128)(2,1)S(1)}, bf16[1808,256]{1,0:T(8,128)(2,1)S(1)}, u32[]{:S(2)}, u32[]{:S(2)}) collective-permute-start(bf16[1808,256]{1,0:T(8,128)(2,1)S(1)} %get-tuple-element.28.refs_8_), channel_id=1, source_target_pairs={{0,64},{1,65},{2,66},{3,67},{4,68},{5,69},{6,70},{7,71},{8,72},{9,... | collective-permute-start | bytes 2777096 | tf_op jit(solution)/shard_map/ppermute | solution.py:29
  55.8 5.8 %collective-permute-start.9 = (bf16[1808,256]{1,0:T(8,128)(2,1)S(1)}, bf16[1808,256]{1,0:T(8,128)(2,1)S(1)}, u32[]{:S(2)}, u32[]{:S(2)}) collective-permute-start(bf16[1808,256]{1,0:T(8,128)(2,1)S(1)} %get-tuple-element.29), channel_id=1, source_target_pairs={{0,0},{1,1},{2,2},{3,3},{4,4},{5,5},{6,6},{7,7},{8,8},{9,9},{10,10... | collective-permute-start | bytes 2777096 | tf_op jit(solution)/shard_map/ppermute | solution.py:29
  61.6 0.1 fusion
  61.7 0.1 collective-permute-start.12
  61.8 0.5 collective-permute-start.13
  62.3 1.4 %collective-permute-done.12.refs_6_ = bf16[128,2048]{1,0:T(8,128)(2,1)S(1)} collective-permute-done((bf16[128,2048]{1,0:T(8,128)(2,1)S(1)}, bf16[128,2048]{1,0:T(8,128)(2,1)S(1)}, u32[]{:S(2)}, u32[]{:S(2)}) %collective-permute-start.12) | collective-permute-done | bytes 524320 | tf_op jit(solution)/shard_map/ppermute | solution.py:29
  63.7 0.7 collective-permute-done.13.refs_7_
  64.4 5.5 %shard_map.18 = (bf16[400,256]{1,0:T(8,128)(2,1)S(1)}, bf16[400,256]{1,0:T(8,128)(2,1)S(1)}, bf16[400,256]{1,0:T(8,128)(2,1)S(1)}, bf16[400,256]{1,0:T(8,128)(2,1)S(1)}) custom-call(s32[5]{0:T(128)S(1)} %stack.23.place, bf16[256,2048]{1,0:T(8,128)(2,1)S(1)} %collective-permute-done.1.refs_1_.refs_0_, ...), custom_call_target="tpu_custom_call" | custom-call | flops 1610612736 | bytes 7340032 | tf_op jit(solution)/shard_map/pallas_call | solution.py:103
  70.0 0.1 collective-permute-start.15
  70.0 0.1 collective-permute-start.16
  70.1 5.6 %collective-permute-start.17 = (bf16[400,256]{1,0:T(8,128)(2,1)S(1)}, bf16[400,256]{1,0:T(8,128)(2,1)S(1)}, u32[]{:S(2)}, u32[]{:S(2)}) collective-permute-start(bf16[400,256]{1,0:T(8,128)(2,1)S(1)} %get-tuple-element.35), channel_id=1, source_target_pairs={{0,0},{1,1},{2,2},{3,3},{4,4},{5,5},{6,6},{7,7},{8,8},{9,9},{10,10... | collective-permute-start | bytes 614408 | tf_op jit(solution)/shard_map/ppermute | solution.py:29
  75.8 0.4 collective-permute-done.8.a
  76.1 2.1 %collective-permute-done.9.b = bf16[1808,256]{1,0:T(8,128)(2,1)S(1)} collective-permute-done((bf16[1808,256]{1,0:T(8,128)(2,1)S(1)}, bf16[1808,256]{1,0:T(8,128)(2,1)S(1)}, u32[]{:S(2)}, u32[]{:S(2)}) %collective-permute-start.9) | collective-permute-done | bytes 925728 | tf_op jit(solution)/shard_map/ppermute | solution.py:29
  78.2 2.6 %shard_map.19 = (f32[6,128,256]{2,1,0:T(8,128)S(1)}, f32[6,128,256]{2,1,0:T(8,128)}) custom-call(s32[5]{0:T(128)S(1)} %stack.23.place, bf16[1808,256]{1,0:T(8,128)(2,1)S(1)} %collective-permute-done.8.a, bf16[1808,256]{1,0:T(8,128)(2,1)S(1)} %collective-permute-done.9.b, bf16[400,256]{1,0:T(8,128)(2,1)S(1)} %get-tuple-element.31._), custom_call_target="tpu_custom_call" | custom-call | flops 1 | bytes 1 | tf_op jit(solution)/shard_map/pallas_call | solution.py:103
  80.8 1.6 %shard_map.20._.refs_10_ = f32[3,256,256]{2,1,0:T(8,128)} custom-call(bf16[1808,256]{1,0:T(8,128)(2,1)S(1)} %collective-permute-done.8.a, bf16[1808,256]{1,0:T(8,128)(2,1)S(1)} %collective-permute-done.9.b, f32[6,128,256]{2,1,0:T(8,128)S(1)} %get-tuple-element.32._.kept), custom_call_target="tpu_custom_call" | custom-call | flops 1 | bytes 1 | tf_op jit(solution)/shard_map/pallas_call | solution.py:103
  82.4 0.3 collective-permute-done.15.a
  82.7 0.2 collective-permute-start.22
  82.9 2.0 %collective-permute-done.16.b = bf16[400,256]{1,0:T(8,128)(2,1)S(1)} collective-permute-done((bf16[400,256]{1,0:T(8,128)(2,1)S(1)}, bf16[400,256]{1,0:T(8,128)(2,1)S(1)}, u32[]{:S(2)}, u32[]{:S(2)}) %collective-permute-start.16) | collective-permute-done | bytes 204832 | tf_op jit(solution)/shard_map/ppermute | solution.py:29
  84.9 0.7 shard_map.21.late
  85.6 1.8 %shard_map.22 = (bf16[656,256]{1,0:T(8,128)(2,1)S(1)}, bf16[272,256]{1,0:T(8,128)(2,1)S(1)}, bf16[400,256]{1,0:T(8,128)(2,1)S(1)}, bf16[272,256]{1,0:T(8,128)(2,1)S(1)}, bf16[144,256]{1,0:T(8,128)(2,1)S(1)}) custom-call(f32[6,128,256]{2,1,0:T(8,128)S(1)} %get-tuple-element.32._.kept, f32[6,128,256]{2,1,0:T(8,128)} %collective-permute-done.14.given, ...), custom_call_target="tpu_custom_call" | custom-call | bytes 4194304 | tf_op jit(solution)/shard_map/pallas_call | solution.py:103
  87.4 1.4 %collective-permute-start.19 = (bf16[656,256]{1,0:T(8,128)(2,1)S(1)}, bf16[656,256]{1,0:T(8,128)(2,1)S(1)}, u32[]{:S(2)}, u32[]{:S(2)}) collective-permute-start(bf16[656,256]{1,0:T(8,128)(2,1)S(1)} %get-tuple-element.37), channel_id=1, source_target_pairs={{0,1},{1,2},{2,3},{3,0},{4,5},{5,6},{6,7},{7,4},{8,9},{9,10},{10,1... | collective-permute-start | bytes 1007624 | tf_op jit(solution)/shard_map/ppermute | solution.py:29
  88.9 3.5 %collective-permute-start.21 = (bf16[400,256]{1,0:T(8,128)(2,1)S(1)}, bf16[400,256]{1,0:T(8,128)(2,1)S(1)}, u32[]{:S(2)}, u32[]{:S(2)}) collective-permute-start(bf16[400,256]{1,0:T(8,128)(2,1)S(1)} %get-tuple-element.39), channel_id=1, source_target_pairs={{0,15},{1,12},{2,13},{3,14},{4,3},{5,0},{6,1},{7,2},{8,7},{9,4},{1... | collective-permute-start | bytes 614408 | tf_op jit(solution)/shard_map/ppermute | solution.py:29
  92.4 2.1 %collective-permute-start.20 = (bf16[272,256]{1,0:T(8,128)(2,1)S(1)}, bf16[272,256]{1,0:T(8,128)(2,1)S(1)}, u32[]{:S(2)}, u32[]{:S(2)}) collective-permute-start(bf16[272,256]{1,0:T(8,128)(2,1)S(1)} %get-tuple-element.38), channel_id=1, source_target_pairs={{0,4},{1,5},{2,6},{3,7},{4,8},{5,9},{6,10},{7,11},{8,12},{9,13},{1... | collective-permute-start | bytes 417800 | tf_op jit(solution)/shard_map/ppermute | solution.py:29
  94.4 4.7 %collective-permute-done.24.refs_4_ = bf16[144,256]{1,0:T(8,128)(2,1)S(1)} collective-permute-done((bf16[144,256]{1,0:T(8,128)(2,1)S(1)}, bf16[144,256]{1,0:T(8,128)(2,1)S(1)}, u32[]{:S(2)}, u32[]{:S(2)}) %collective-permute-start.24) | collective-permute-done | bytes 73760 | tf_op jit(solution)/shard_map/ppermute | solution.py:29
  99.1 0.6 collective-permute-done.23.refs_3_
  99.8 4.5 %collective-permute-done.20.refs_1_ = bf16[272,256]{1,0:T(8,128)(2,1)S(1)} collective-permute-done((bf16[272,256]{1,0:T(8,128)(2,1)S(1)}, bf16[272,256]{1,0:T(8,128)(2,1)S(1)}, u32[]{:S(2)}, u32[]{:S(2)}) %collective-permute-start.20) | collective-permute-done | bytes 139296 | tf_op jit(solution)/shard_map/ppermute | solution.py:29
  104.3 0.5 collective-permute-start.25
  104.8 0.1 collective-permute-start.27
  104.9 0.4 collective-permute-start.26
  105.3 0.1 collective-permute-start.28
  105.4 0.4 collective-permute-start.29
  105.8 1.0 collective-permute-done.29.refs_9_
  106.9 2.5 %shard_map.23 = f32[256,2048]{1,0:T(8,128)} custom-call(s32[5]{0:T(128)S(1)} %stack.23.place, bf16[656,256]{1,0:T(8,128)(2,1)S(1)} %collective-permute-done.19.refs_0_, bf16[272,256]{1,0:T(8,128)(2,1)S(1)} %collective-permute-done.20.refs_1_, bf16[400,256]{1,0:T(8,128)(2,1)S(1)} %collective-permute-done.21.refs_2_, ...), custom_call_target="tpu_custom_call" | custom-call | bytes 6291456 | tf_op jit(solution)/shard_map/pallas_call | solution.py:103
  (22 shorter events, 0.1 us)
Async XLA Ops:
  1.5 18.0 %collective-permute-start = (bf16[256,2048]{1,0:T(8,128)(2,1)S(1)}, bf16[256,2048]{1,0:T(8,128)(2,1)}, u32[]{:S(2)}, u32[]{:S(2)}) collective-permute-start(bf16[256,2048]{1,0:T(8,128)(2,1)S(1)} %bitcast.10), channel_id=1, source_target_pairs={{0,0},{1,1},{2,2},{3,3},{4,4},{5,5},{6,6},{7,7},{8,8},{9,9},{10,10... | collective-permute-start | bytes 3145736 | tf_op jit(solution)/shard_map/ppermute | solution.py:29
  19.5 14.6 %collective-permute-start.1 = (bf16[256,2048]{1,0:T(8,128)(2,1)}, bf16[256,2048]{1,0:T(8,128)(2,1)S(1)}, u32[]{:S(2)}, u32[]{:S(2)}) collective-permute-start(bf16[256,2048]{1,0:T(8,128)(2,1)} %collective-permute-done.refs_0_), channel_id=1, source_target_pairs={{0,12},{1,13},{2,14},{3,15},{4,0},{5,1},{6,2},{7,3},{8,4},{9,5},{1... | collective-permute-start | bytes 3145736 | tf_op jit(solution)/shard_map/ppermute | solution.py:29
  22.0 15.7 %collective-permute-start.2 = (bf16[256,2048]{1,0:T(8,128)(2,1)}, bf16[256,2048]{1,0:T(8,128)(2,1)S(1)}, u32[]{:S(2)}, u32[]{:S(2)}) collective-permute-start(bf16[256,2048]{1,0:T(8,128)(2,1)} %collective-permute-done.refs_0_), channel_id=1, source_target_pairs={{0,3},{1,0},{2,1},{3,2},{4,7},{5,4},{6,5},{7,6},{8,11},{9,8},{10,9... | collective-permute-start | bytes 3145736 | tf_op jit(solution)/shard_map/ppermute | solution.py:29
  25.7 15.2 %collective-permute-start.3 = (bf16[256,2048]{1,0:T(8,128)(2,1)}, bf16[256,2048]{1,0:T(8,128)(2,1)}, u32[]{:S(2)}, u32[]{:S(2)}) collective-permute-start(bf16[256,2048]{1,0:T(8,128)(2,1)} %collective-permute-done.refs_0_), channel_id=1, source_target_pairs={{0,4},{1,5},{2,6},{3,7},{4,8},{5,9},{6,10},{7,11},{8,12},{9,13},{1... | collective-permute-start | bytes 3145736 | tf_op jit(solution)/shard_map/ppermute | solution.py:29
  25.7 15.4 %collective-permute-start.4 = (bf16[256,2048]{1,0:T(8,128)(2,1)}, bf16[256,2048]{1,0:T(8,128)(2,1)}, u32[]{:S(2)}, u32[]{:S(2)}) collective-permute-start(bf16[256,2048]{1,0:T(8,128)(2,1)} %collective-permute-done.refs_0_), channel_id=1, source_target_pairs={{0,1},{1,2},{2,3},{3,0},{4,5},{5,6},{6,7},{7,4},{8,9},{9,10},{10,1... | collective-permute-start | bytes 3145736 | tf_op jit(solution)/shard_map/ppermute | solution.py:29
  34.1 8.3 %collective-permute-start.7 = (bf16[256,2048]{1,0:T(8,128)(2,1)}, bf16[256,2048]{1,0:T(8,128)(2,1)}, u32[]{:S(2)}, u32[]{:S(2)}) collective-permute-start(bf16[256,2048]{1,0:T(8,128)(2,1)} %collective-permute-done.refs_0_), channel_id=1, source_target_pairs={{0,32},{1,33},{2,34},{3,35},{4,36},{5,37},{6,38},{7,39},{8,40},{9,... | collective-permute-start | bytes 3145736 | tf_op jit(solution)/shard_map/ppermute | solution.py:29
  34.1 8.3 %collective-permute-start.5 = (bf16[256,2048]{1,0:T(8,128)(2,1)S(1)}, bf16[256,2048]{1,0:T(8,128)(2,1)}, u32[]{:S(2)}, u32[]{:S(2)}) collective-permute-start(bf16[256,2048]{1,0:T(8,128)(2,1)S(1)} %collective-permute-done.1.refs_1_.refs_0_), channel_id=1, source_target_pairs={{0,32},{1,33},{2,34},{3,35},{4,36},{5,37},{6,38},{7,39},{8,40},{9,... | collective-permute-start | bytes 3145736 | tf_op jit(solution)/shard_map/ppermute | solution.py:29
  37.7 4.7 %collective-permute-start.6 = (bf16[256,2048]{1,0:T(8,128)(2,1)S(1)}, bf16[256,2048]{1,0:T(8,128)(2,1)}, u32[]{:S(2)}, u32[]{:S(2)}) collective-permute-start(bf16[256,2048]{1,0:T(8,128)(2,1)S(1)} %collective-permute-done.2.refs_2_.refs_1_), channel_id=1, source_target_pairs={{0,32},{1,33},{2,34},{3,35},{4,36},{5,37},{6,38},{7,39},{8,40},{9,... | collective-permute-start | bytes 3145736 | tf_op jit(solution)/shard_map/ppermute | solution.py:29
  40.8 14.9 %collective-permute-start.10 = (bf16[256,2048]{1,0:T(8,128)(2,1)S(1)}, bf16[256,2048]{1,0:T(8,128)(2,1)S(1)}, u32[]{:S(2)}, u32[]{:S(2)}) collective-permute-start(bf16[256,2048]{1,0:T(8,128)(2,1)S(1)} %collective-permute-done.1.refs_1_.refs_0_), channel_id=1, source_target_pairs={{0,3},{1,0},{2,1},{3,2},{4,7},{5,4},{6,5},{7,6},{8,11},{9,8},{10,9... | collective-permute-start | bytes 3145736 | tf_op jit(solution)/shard_map/ppermute | solution.py:29
  41.0 21.3 %collective-permute-start.11 = (bf16[256,2048]{1,0:T(8,128)(2,1)}, bf16[256,2048]{1,0:T(8,128)(2,1)S(1)}, u32[]{:S(2)}, u32[]{:S(2)}) collective-permute-start(bf16[256,2048]{1,0:T(8,128)(2,1)} %collective-permute-done.3.refs_3_), channel_id=1, source_target_pairs={{0,1},{1,2},{2,3},{3,0},{4,5},{5,6},{6,7},{7,4},{8,9},{9,10},{10,1... | collective-permute-start | bytes 3145736 | tf_op jit(solution)/shard_map/ppermute | solution.py:29
  51.8 24.4 %collective-permute-start.8 = (bf16[1808,256]{1,0:T(8,128)(2,1)S(1)}, bf16[1808,256]{1,0:T(8,128)(2,1)S(1)}, u32[]{:S(2)}, u32[]{:S(2)}) collective-permute-start(bf16[1808,256]{1,0:T(8,128)(2,1)S(1)} %get-tuple-element.28.refs_8_), channel_id=1, source_target_pairs={{0,64},{1,65},{2,66},{3,67},{4,68},{5,69},{6,70},{7,71},{8,72},{9,... | collective-permute-start | bytes 2777096 | tf_op jit(solution)/shard_map/ppermute | solution.py:29
  55.8 22.4 %collective-permute-start.9 = (bf16[1808,256]{1,0:T(8,128)(2,1)S(1)}, bf16[1808,256]{1,0:T(8,128)(2,1)S(1)}, u32[]{:S(2)}, u32[]{:S(2)}) collective-permute-start(bf16[1808,256]{1,0:T(8,128)(2,1)S(1)} %get-tuple-element.29), channel_id=1, source_target_pairs={{0,0},{1,1},{2,2},{3,3},{4,4},{5,5},{6,6},{7,7},{8,8},{9,9},{10,10... | collective-permute-start | bytes 2777096 | tf_op jit(solution)/shard_map/ppermute | solution.py:29
  61.7 2.0 %collective-permute-start.12 = (bf16[128,2048]{1,0:T(8,128)(2,1)S(1)}, bf16[128,2048]{1,0:T(8,128)(2,1)S(1)}, u32[]{:S(2)}, u32[]{:S(2)}) collective-permute-start(bf16[128,2048]{1,0:T(8,128)(2,1)S(1)} %get-tuple-element.50), channel_id=1, source_target_pairs={{0,32},{1,33},{2,34},{3,35},{4,36},{5,37},{6,38},{7,39},{8,40},{9,... | collective-permute-start | bytes 1572872 | tf_op jit(solution)/shard_map/ppermute | solution.py:29
  61.8 2.6 %collective-permute-start.13 = (bf16[128,2048]{1,0:T(8,128)(2,1)S(1)}, bf16[128,2048]{1,0:T(8,128)(2,1)S(1)}, u32[]{:S(2)}, u32[]{:S(2)}) collective-permute-start(bf16[128,2048]{1,0:T(8,128)(2,1)S(1)} %get-tuple-element.49), channel_id=1, source_target_pairs={{0,32},{1,33},{2,34},{3,35},{4,36},{5,37},{6,38},{7,39},{8,40},{9,... | collective-permute-start | bytes 1572872 | tf_op jit(solution)/shard_map/ppermute | solution.py:29
  70.0 12.8 %collective-permute-start.15 = (bf16[400,256]{1,0:T(8,128)(2,1)S(1)}, bf16[400,256]{1,0:T(8,128)(2,1)S(1)}, u32[]{:S(2)}, u32[]{:S(2)}) collective-permute-start(bf16[400,256]{1,0:T(8,128)(2,1)S(1)} %get-tuple-element.31._), channel_id=1, source_target_pairs={{0,64},{1,65},{2,66},{3,67},{4,68},{5,69},{6,70},{7,71},{8,72},{9,... | collective-permute-start | bytes 614408 | tf_op jit(solution)/shard_map/ppermute | solution.py:29
  70.0 14.9 %collective-permute-start.16 = (bf16[400,256]{1,0:T(8,128)(2,1)S(1)}, bf16[400,256]{1,0:T(8,128)(2,1)S(1)}, u32[]{:S(2)}, u32[]{:S(2)}) collective-permute-start(bf16[400,256]{1,0:T(8,128)(2,1)S(1)} %get-tuple-element.34), channel_id=1, source_target_pairs={{0,96},{1,97},{2,98},{3,99},{4,100},{5,101},{6,102},{7,103},{8,104... | collective-permute-start | bytes 614408 | tf_op jit(solution)/shard_map/ppermute | solution.py:29
  70.1 14.8 %collective-permute-start.17 = (bf16[400,256]{1,0:T(8,128)(2,1)S(1)}, bf16[400,256]{1,0:T(8,128)(2,1)S(1)}, u32[]{:S(2)}, u32[]{:S(2)}) collective-permute-start(bf16[400,256]{1,0:T(8,128)(2,1)S(1)} %get-tuple-element.35), channel_id=1, source_target_pairs={{0,0},{1,1},{2,2},{3,3},{4,4},{5,5},{6,6},{7,7},{8,8},{9,9},{10,10... | collective-permute-start | bytes 614408 | tf_op jit(solution)/shard_map/ppermute | solution.py:29
  76.1 8.8 %collective-permute-start.18 = (bf16[400,256]{1,0:T(8,128)(2,1)S(1)}, bf16[400,256]{1,0:T(8,128)(2,1)S(1)}, u32[]{:S(2)}, u32[]{:S(2)}) collective-permute-start(bf16[400,256]{1,0:T(8,128)(2,1)S(1)} %get-tuple-element.36), channel_id=1, source_target_pairs={{0,32},{1,33},{2,34},{3,35},{4,36},{5,37},{6,38},{7,39},{8,40},{9,... | collective-permute-start | bytes 614408 | tf_op jit(solution)/shard_map/ppermute | solution.py:29
  80.8 4.8 %collective-permute-start.14 = (f32[6,128,256]{2,1,0:T(8,128)}, f32[6,128,256]{2,1,0:T(8,128)}, u32[]{:S(2)}, u32[]{:S(2)}) collective-permute-start(f32[6,128,256]{2,1,0:T(8,128)} %get-tuple-element.33), channel_id=1, source_target_pairs={{0,32},{1,33},{2,34},{3,35},{4,36},{5,37},{6,38},{7,39},{8,40},{9,... | collective-permute-start | bytes 2359304 | tf_op jit(solution)/shard_map/ppermute | solution.py:29
  82.7 9.6 %collective-permute-start.22 = (f32[3,256,256]{2,1,0:T(8,128)}, f32[3,256,256]{2,1,0:T(8,128)}, u32[]{:S(2)}, u32[]{:S(2)}) collective-permute-start(f32[3,256,256]{2,1,0:T(8,128)} %shard_map.20._.refs_10_), channel_id=1, source_target_pairs={{0,32},{1,33},{2,34},{3,35},{4,36},{5,37},{6,38},{7,39},{8,40},{9,... | collective-permute-start | bytes 2359304 | tf_op jit(solution)/shard_map/ppermute | solution.py:29
  87.4 16.9 %collective-permute-start.19 = (bf16[656,256]{1,0:T(8,128)(2,1)S(1)}, bf16[656,256]{1,0:T(8,128)(2,1)S(1)}, u32[]{:S(2)}, u32[]{:S(2)}) collective-permute-start(bf16[656,256]{1,0:T(8,128)(2,1)S(1)} %get-tuple-element.37), channel_id=1, source_target_pairs={{0,1},{1,2},{2,3},{3,0},{4,5},{5,6},{6,7},{7,4},{8,9},{9,10},{10,1... | collective-permute-start | bytes 1007624 | tf_op jit(solution)/shard_map/ppermute | solution.py:29
  88.9 15.4 %collective-permute-start.21 = (bf16[400,256]{1,0:T(8,128)(2,1)S(1)}, bf16[400,256]{1,0:T(8,128)(2,1)S(1)}, u32[]{:S(2)}, u32[]{:S(2)}) collective-permute-start(bf16[400,256]{1,0:T(8,128)(2,1)S(1)} %get-tuple-element.39), channel_id=1, source_target_pairs={{0,15},{1,12},{2,13},{3,14},{4,3},{5,0},{6,1},{7,2},{8,7},{9,4},{1... | collective-permute-start | bytes 614408 | tf_op jit(solution)/shard_map/ppermute | solution.py:29
  92.4 7.4 %collective-permute-start.23 = (bf16[272,256]{1,0:T(8,128)(2,1)S(1)}, bf16[272,256]{1,0:T(8,128)(2,1)S(1)}, u32[]{:S(2)}, u32[]{:S(2)}) collective-permute-start(bf16[272,256]{1,0:T(8,128)(2,1)S(1)} %get-tuple-element.41), channel_id=1, source_target_pairs={{0,12},{1,13},{2,14},{3,15},{4,0},{5,1},{6,2},{7,3},{8,4},{9,5},{1... | collective-permute-start | bytes 417800 | tf_op jit(solution)/shard_map/ppermute | solution.py:29
  92.4 11.9 %collective-permute-start.20 = (bf16[272,256]{1,0:T(8,128)(2,1)S(1)}, bf16[272,256]{1,0:T(8,128)(2,1)S(1)}, u32[]{:S(2)}, u32[]{:S(2)}) collective-permute-start(bf16[272,256]{1,0:T(8,128)(2,1)S(1)} %get-tuple-element.38), channel_id=1, source_target_pairs={{0,4},{1,5},{2,6},{3,7},{4,8},{5,9},{6,10},{7,11},{8,12},{9,13},{1... | collective-permute-start | bytes 417800 | tf_op jit(solution)/shard_map/ppermute | solution.py:29
  94.4 4.7 %collective-permute-start.24 = (bf16[144,256]{1,0:T(8,128)(2,1)S(1)}, bf16[144,256]{1,0:T(8,128)(2,1)S(1)}, u32[]{:S(2)}, u32[]{:S(2)}) collective-permute-start(bf16[144,256]{1,0:T(8,128)(2,1)S(1)} %get-tuple-element.42), channel_id=1, source_target_pairs={{0,4},{1,5},{2,6},{3,7},{4,8},{5,9},{6,10},{7,11},{8,12},{9,13},{1... | collective-permute-start | bytes 221192 | tf_op jit(solution)/shard_map/ppermute | solution.py:29
  104.3 2.6 %collective-permute-start.25 = (bf16[656,256]{1,0:T(8,128)(2,1)S(1)}, bf16[656,256]{1,0:T(8,128)(2,1)S(1)}, u32[]{:S(2)}, u32[]{:S(2)}) collective-permute-start(bf16[656,256]{1,0:T(8,128)(2,1)S(1)} %collective-permute-done.19.refs_0_), channel_id=1, source_target_pairs={{0,32},{1,33},{2,34},{3,35},{4,36},{5,37},{6,38},{7,39},{8,40},{9,... | collective-permute-start | bytes 1007624 | tf_op jit(solution)/shard_map/ppermute | solution.py:29
  104.8 2.1 %collective-permute-start.27 = (bf16[400,256]{1,0:T(8,128)(2,1)S(1)}, bf16[400,256]{1,0:T(8,128)(2,1)S(1)}, u32[]{:S(2)}, u32[]{:S(2)}) collective-permute-start(bf16[400,256]{1,0:T(8,128)(2,1)S(1)} %collective-permute-done.21.refs_2_), channel_id=1, source_target_pairs={{0,32},{1,33},{2,34},{3,35},{4,36},{5,37},{6,38},{7,39},{8,40},{9,... | collective-permute-start | bytes 614408 | tf_op jit(solution)/shard_map/ppermute | solution.py:29
  104.9 2.0 %collective-permute-start.26 = (bf16[272,256]{1,0:T(8,128)(2,1)S(1)}, bf16[272,256]{1,0:T(8,128)(2,1)S(1)}, u32[]{:S(2)}, u32[]{:S(2)}) collective-permute-start(bf16[272,256]{1,0:T(8,128)(2,1)S(1)} %collective-permute-done.20.refs_1_), channel_id=1, source_target_pairs={{0,32},{1,33},{2,34},{3,35},{4,36},{5,37},{6,38},{7,39},{8,40},{9,... | collective-permute-start | bytes 417800 | tf_op jit(solution)/shard_map/ppermute | solution.py:29
  105.3 1.6 %collective-permute-start.28 = (bf16[272,256]{1,0:T(8,128)(2,1)S(1)}, bf16[272,256]{1,0:T(8,128)(2,1)S(1)}, u32[]{:S(2)}, u32[]{:S(2)}) collective-permute-start(bf16[272,256]{1,0:T(8,128)(2,1)S(1)} %collective-permute-done.23.refs_3_), channel_id=1, source_target_pairs={{0,32},{1,33},{2,34},{3,35},{4,36},{5,37},{6,38},{7,39},{8,40},{9,... | collective-permute-start | bytes 417800 | tf_op jit(solution)/shard_map/ppermute | solution.py:29
  105.4 1.5 %collective-permute-start.29 = (bf16[144,256]{1,0:T(8,128)(2,1)S(1)}, bf16[144,256]{1,0:T(8,128)(2,1)S(1)}, u32[]{:S(2)}, u32[]{:S(2)}) collective-permute-start(bf16[144,256]{1,0:T(8,128)(2,1)S(1)} %collective-permute-done.24.refs_4_), channel_id=1, source_target_pairs={{0,32},{1,33},{2,34},{3,35},{4,36},{5,37},{6,38},{7,39},{8,40},{9,... | collective-permute-start | bytes 221192 | tf_op jit(solution)/shard_map/ppermute | solution.py:29

commit v9 on v8

--- a/solution.py
+++ b/solution.py
@@ -317,7 +317,6 @@
     held["q3"] = fetch(held["o"], MZ, MX)
     held["q4"] = fetch(held["o"], MX, MZ)
     held["pe"] = fetch(held["q1"], PX, PZ)
-    held["me"] = fetch(held["q3"], MX, MZ)
     for name, source in (("s1", "q1"), ("s2", "q2")):
         held[name] = move(held[source], to_core)
     held["so"] = move(lax.optimization_barrier((held["o"], held["q1"]))[0], to_core)
@@ -325,7 +324,8 @@
     coded, after = [], ()
     for classes in (EARLY, LATE):
         if after:
-            first, _ = lax.optimization_barrier((held["pe"], after[0]))
+            first, source, _ = lax.optimization_barrier((held["pe"], held["q3"], after[0]))
+            held["me"] = fetch(source, MX, MZ)
             half = rows // 2
             held["spe"] = (move(first[:half], to_core), move(first[half:], to_core))
         listed = [(OWN[r], OWN[q], OTHER[q]) for r, q in classes]

time: 110 us -> 114 us (1.036)
  waiting for transfers between devices: 46 us -> 49.3 us
  local copies, waits for them, and re-layouts: 1.65 us -> 3.87 us
  starting transfers between devices: 37.6 us -> 36.4 us
    ppermute x30, waiting for transfers between devices: 46 us -> 49.3 us  [move(): return lax.ppermute(value, ('aux', 'blk'), pairs)]
    unnamed x1 -> x5, local copies, waits for them, and re-layouts: 1.5 us -> 3.69 us
    ppermute x30, starting transfers between devices: 37.6 us -> 36.4 us  [move(): return lax.ppermute(value, ('aux', 'blk'), pairs)]
  transfers between devices with their start and end apart: 30 -> 30, of which waited for: 14 -> 13; matrix products, arithmetic and copies ran while one was open for 0% -> 0% of each run, Pallas kernels for 20% -> 19%
where the time goes in v9:
time: 114 us; the launch traced here: 113 us
  waiting for transfers between devices  49.3 us (43%)
  starting transfers between devices  36.4 us (32%)
  Pallas kernels  23.6 us (21%)
  local copies, waits for them, and re-layouts  3.87 us (3%)
    ppermute x30, waiting for transfers between devices, move(): return lax.ppermute(value, ('aux', 'blk'), pairs)  49.3 us
    ppermute x30, starting transfers between devices, move(): return lax.ppermute(value, ('aux', 'blk'), pairs)  36.4 us
    pallas_call x7, Pallas kernels, call(): pl.pallas_call(kernel, out_shape=out_shape, in_specs=specs, out_specs=[wh...  23.6 us
    unnamed x5, local copies, waits for them, and re-layouts  3.69 us
  transfers between devices with their start and end apart: 30, of which 13 were waited for; matrix products, arithmetic and copies ran while one was open for 0% of the time, Pallas kernels for 19%

profile of v9, /device:TPU:9, one launch (start us, length us, event | category | flops | bytes accessed | tf_op | source)
XLA Modules:
  0.0 113.4 jit_solution(18410382742214372984)
XLA Ops:
  0.0 1.5 %copy.4 = bf16[32,8,16,128]{3,1,2,0:T(8,128)(2,1)S(1)} copy(bf16[32,8,16,128]{3,2,1,0:T(8,128)(2,1)} %bitcast.9) | data formatting | bytes 2097152
  1.5 4.5 %collective-permute-start = (bf16[256,2048]{1,0:T(8,128)(2,1)S(1)}, bf16[256,2048]{1,0:T(8,128)(2,1)}, u32[]{:S(2)}, u32[]{:S(2)}) collective-permute-start(bf16[256,2048]{1,0:T(8,128)(2,1)S(1)} %bitcast.10), channel_id=1, source_target_pairs={{0,0},{1,1},{2,2},{3,3},{4,4},{5,5},{6,6},{7,7},{8,8},{9,9},{10,10... | collective-permute-start | bytes 3145736 | tf_op jit(solution)/shard_map/ppermute | solution.py:29
  6.0 13.5 %collective-permute-done.refs_0_ = bf16[256,2048]{1,0:T(8,128)(2,1)} collective-permute-done((bf16[256,2048]{1,0:T(8,128)(2,1)S(1)}, bf16[256,2048]{1,0:T(8,128)(2,1)}, u32[]{:S(2)}, u32[]{:S(2)}) %collective-permute-start) | collective-permute-done | bytes 1048608 | tf_op jit(solution)/shard_map/ppermute | solution.py:29
  19.5 2.4 %collective-permute-start.1 = (bf16[256,2048]{1,0:T(8,128)(2,1)}, bf16[256,2048]{1,0:T(8,128)(2,1)S(1)}, u32[]{:S(2)}, u32[]{:S(2)}) collective-permute-start(bf16[256,2048]{1,0:T(8,128)(2,1)} %collective-permute-done.refs_0_), channel_id=1, source_target_pairs={{0,12},{1,13},{2,14},{3,15},{4,0},{5,1},{6,2},{7,3},{8,4},{9,5},{1... | collective-permute-start | bytes 3145736 | tf_op jit(solution)/shard_map/ppermute | solution.py:29
  21.9 3.8 %collective-permute-start.2 = (bf16[256,2048]{1,0:T(8,128)(2,1)}, bf16[256,2048]{1,0:T(8,128)(2,1)S(1)}, u32[]{:S(2)}, u32[]{:S(2)}) collective-permute-start(bf16[256,2048]{1,0:T(8,128)(2,1)} %collective-permute-done.refs_0_), channel_id=1, source_target_pairs={{0,3},{1,0},{2,1},{3,2},{4,7},{5,4},{6,5},{7,6},{8,11},{9,8},{10,9... | collective-permute-start | bytes 3145736 | tf_op jit(solution)/shard_map/ppermute | solution.py:29
  25.7 8.4 %collective-permute-done.1.refs_1_.refs_0_ = bf16[256,2048]{1,0:T(8,128)(2,1)S(1)} collective-permute-done((bf16[256,2048]{1,0:T(8,128)(2,1)}, bf16[256,2048]{1,0:T(8,128)(2,1)S(1)}, u32[]{:S(2)}, u32[]{:S(2)}) %collective-permute-start.1) | collective-permute-done | bytes 1048608 | tf_op jit(solution)/shard_map/ppermute | solution.py:29
  34.1 0.5 collective-permute-start.5
  34.6 3.1 %collective-permute-done.2.refs_2_.refs_1_ = bf16[256,2048]{1,0:T(8,128)(2,1)S(1)} collective-permute-done((bf16[256,2048]{1,0:T(8,128)(2,1)}, bf16[256,2048]{1,0:T(8,128)(2,1)S(1)}, u32[]{:S(2)}, u32[]{:S(2)}) %collective-permute-start.2) | collective-permute-done | bytes 1048608 | tf_op jit(solution)/shard_map/ppermute | solution.py:29
  37.7 3.0 %collective-permute-done.3.refs_3_ = bf16[256,2048]{1,0:T(8,128)(2,1)S(1)} collective-permute-done((bf16[256,2048]{1,0:T(8,128)(2,1)}, bf16[256,2048]{1,0:T(8,128)(2,1)S(1)}, u32[]{:S(2)}, u32[]{:S(2)}) %collective-permute-start.3) | collective-permute-done | bytes 1048608 | tf_op jit(solution)/shard_map/ppermute | solution.py:29
  40.7 1.0 copy-done
  41.7 0.1 collective-permute-start.10
  41.8 0.1 stack.23.place
  41.9 1.2 %copy-done.1 = bf16[256,2048]{1,0:T(8,128)(2,1)S(1)} copy-done((bf16[256,2048]{1,0:T(8,128)(2,1)S(1)}, bf16[256,2048]{1,0:T(8,128)(2,1)}, u32[]{:S(2)}) %copy-start.1) | copy-done | bytes 1048600
  43.2 9.0 %shard_map.17 = (bf16[1808,256]{1,0:T(8,128)(2,1)S(1)}, bf16[1808,256]{1,0:T(8,128)(2,1)S(1)}) custom-call(s32[5]{0:T(128)S(1)} %stack.23.place, bf16[256,2048]{1,0:T(8,128)(2,1)} %collective-permute-done.refs_0_, bf16[256,2048]{1,0:T(8,128)(2,1)S(1)} %collective-permute-done.1.refs_1_.refs_0_, bf16[256,2048]{1,0:T(8,128)(2,1)S(1)} %collective-permute-done.2.refs_2_.refs_1_, ...), custom_call_target="tpu_custom_call" | custom-call | flops 3758096384 | bytes 8388608 | tf_op jit(solution)/shard_map/pallas_call | solution.py:103
  52.2 3.1 %collective-permute-done.10.refs_2_ = bf16[256,2048]{1,0:T(8,128)(2,1)S(1)} collective-permute-done((bf16[256,2048]{1,0:T(8,128)(2,1)S(1)}, bf16[256,2048]{1,0:T(8,128)(2,1)S(1)}, u32[]{:S(2)}, u32[]{:S(2)}) %collective-permute-start.10) | collective-permute-done | bytes 1048608 | tf_op jit(solution)/shard_map/ppermute | solution.py:29
  55.3 4.5 %collective-permute-start.8 = (bf16[1808,256]{1,0:T(8,128)(2,1)S(1)}, bf16[1808,256]{1,0:T(8,128)(2,1)S(1)}, u32[]{:S(2)}, u32[]{:S(2)}) collective-permute-start(bf16[1808,256]{1,0:T(8,128)(2,1)S(1)} %get-tuple-element.29.refs_8_), channel_id=1, source_target_pairs={{0,64},{1,65},{2,66},{3,67},{4,68},{5,69},{6,70},{7,71},{8,72},{9,... | collective-permute-start | bytes 2777096 | tf_op jit(solution)/shard_map/ppermute | solution.py:29
  59.9 2.6 %collective-permute-start.9 = (bf16[1808,256]{1,0:T(8,128)(2,1)S(1)}, bf16[1808,256]{1,0:T(8,128)(2,1)S(1)}, u32[]{:S(2)}, u32[]{:S(2)}) collective-permute-start(bf16[1808,256]{1,0:T(8,128)(2,1)S(1)} %get-tuple-element.30), channel_id=1, source_target_pairs={{0,0},{1,1},{2,2},{3,3},{4,4},{5,5},{6,6},{7,7},{8,8},{9,9},{10,10... | collective-permute-start | bytes 2777096 | tf_op jit(solution)/shard_map/ppermute | solution.py:29
  62.5 0.1 fusion
  62.6 0.1 collective-permute-start.12
  62.7 0.5 collective-permute-start.13
  63.2 1.4 %collective-permute-done.12.refs_6_ = bf16[128,2048]{1,0:T(8,128)(2,1)S(1)} collective-permute-done((bf16[128,2048]{1,0:T(8,128)(2,1)S(1)}, bf16[128,2048]{1,0:T(8,128)(2,1)S(1)}, u32[]{:S(2)}, u32[]{:S(2)}) %collective-permute-start.12) | collective-permute-done | bytes 524320 | tf_op jit(solution)/shard_map/ppermute | solution.py:29
  64.6 0.7 collective-permute-done.13.refs_7_
  65.4 4.9 %collective-permute-done.11.refs_5_ = bf16[256,2048]{1,0:T(8,128)(2,1)S(1)} collective-permute-done((bf16[256,2048]{1,0:T(8,128)(2,1)S(1)}, bf16[256,2048]{1,0:T(8,128)(2,1)S(1)}, u32[]{:S(2)}, u32[]{:S(2)}) %collective-permute-start.11) | collective-permute-done | bytes 1048608 | tf_op jit(solution)/shard_map/ppermute | solution.py:29
  70.2 5.4 %shard_map.18 = (bf16[400,256]{1,0:T(8,128)(2,1)S(1)}, bf16[400,256]{1,0:T(8,128)(2,1)S(1)}, bf16[400,256]{1,0:T(8,128)(2,1)S(1)}, bf16[400,256]{1,0:T(8,128)(2,1)S(1)}) custom-call(s32[5]{0:T(128)S(1)} %stack.23.place, bf16[256,2048]{1,0:T(8,128)(2,1)S(1)} %collective-permute-done.1.refs_1_.refs_0_, ...), custom_call_target="tpu_custom_call" | custom-call | flops 1610612736 | bytes 7340032 | tf_op jit(solution)/shard_map/pallas_call | solution.py:103
  75.6 5.8 %collective-permute-start.15 = (bf16[400,256]{1,0:T(8,128)(2,1)S(1)}, bf16[400,256]{1,0:T(8,128)(2,1)S(1)}, u32[]{:S(2)}, u32[]{:S(2)}) collective-permute-start(bf16[400,256]{1,0:T(8,128)(2,1)S(1)} %get-tuple-element.33._), channel_id=1, source_target_pairs={{0,64},{1,65},{2,66},{3,67},{4,68},{5,69},{6,70},{7,71},{8,72},{9,... | collective-permute-start | bytes 614408 | tf_op jit(solution)/shard_map/ppermute | solution.py:29
  81.4 2.7 %collective-permute-start.17 = (bf16[400,256]{1,0:T(8,128)(2,1)S(1)}, bf16[400,256]{1,0:T(8,128)(2,1)S(1)}, u32[]{:S(2)}, u32[]{:S(2)}) collective-permute-start(bf16[400,256]{1,0:T(8,128)(2,1)S(1)} %get-tuple-element.37), channel_id=1, source_target_pairs={{0,0},{1,1},{2,2},{3,3},{4,4},{5,5},{6,6},{7,7},{8,8},{9,9},{10,10... | collective-permute-start | bytes 614408 | tf_op jit(solution)/shard_map/ppermute | solution.py:29
  84.1 0.1 collective-permute-start.18
  84.2 2.6 %shard_map.19 = (f32[6,128,256]{2,1,0:T(8,128)S(1)}, f32[6,128,256]{2,1,0:T(8,128)}) custom-call(s32[5]{0:T(128)S(1)} %stack.23.place, bf16[1808,256]{1,0:T(8,128)(2,1)S(1)} %collective-permute-done.8.a, bf16[1808,256]{1,0:T(8,128)(2,1)S(1)} %collective-permute-done.9.b, bf16[400,256]{1,0:T(8,128)(2,1)S(1)} %get-tuple-element.33._), custom_call_target="tpu_custom_call" | custom-call | flops 1 | bytes 1 | tf_op jit(solution)/shard_map/pallas_call | solution.py:103
  86.8 0.5 collective-permute-start.14
  87.3 1.5 %shard_map.20._.refs_10_ = f32[3,256,256]{2,1,0:T(8,128)} custom-call(bf16[1808,256]{1,0:T(8,128)(2,1)S(1)} %collective-permute-done.8.a, bf16[1808,256]{1,0:T(8,128)(2,1)S(1)} %collective-permute-done.9.b, f32[6,128,256]{2,1,0:T(8,128)S(1)} %get-tuple-element.34._.kept), custom_call_target="tpu_custom_call" | custom-call | flops 1 | bytes 1 | tf_op jit(solution)/shard_map/pallas_call | solution.py:103
  88.9 0.0 collective-permute-start.22
  88.9 1.8 %collective-permute-done.16.b = bf16[400,256]{1,0:T(8,128)(2,1)S(1)} collective-permute-done((bf16[400,256]{1,0:T(8,128)(2,1)S(1)}, bf16[400,256]{1,0:T(8,128)(2,1)S(1)}, u32[]{:S(2)}, u32[]{:S(2)}) %collective-permute-start.16) | collective-permute-done | bytes 204832 | tf_op jit(solution)/shard_map/ppermute | solution.py:29
  90.7 0.7 shard_map.21.late
  91.4 1.8 %shard_map.22 = (bf16[656,256]{1,0:T(8,128)(2,1)S(1)}, bf16[272,256]{1,0:T(8,128)(2,1)S(1)}, bf16[400,256]{1,0:T(8,128)(2,1)S(1)}, bf16[272,256]{1,0:T(8,128)(2,1)S(1)}, bf16[144,256]{1,0:T(8,128)(2,1)S(1)}) custom-call(f32[6,128,256]{2,1,0:T(8,128)S(1)} %get-tuple-element.34._.kept, f32[6,128,256]{2,1,0:T(8,128)} %collective-permute-done.14.given, ...), custom_call_target="tpu_custom_call" | custom-call | bytes 4194304 | tf_op jit(solution)/shard_map/pallas_call | solution.py:103
  93.2 0.5 collective-permute-start.19
  93.7 3.0 %collective-permute-start.21 = (bf16[400,256]{1,0:T(8,128)(2,1)S(1)}, bf16[400,256]{1,0:T(8,128)(2,1)S(1)}, u32[]{:S(2)}, u32[]{:S(2)}) collective-permute-start(bf16[400,256]{1,0:T(8,128)(2,1)S(1)} %get-tuple-element.41), channel_id=1, source_target_pairs={{0,15},{1,12},{2,13},{3,14},{4,3},{5,0},{6,1},{7,2},{8,7},{9,4},{1... | collective-permute-start | bytes 614408 | tf_op jit(solution)/shard_map/ppermute | solution.py:29
  96.7 1.4 %collective-permute-start.20 = (bf16[272,256]{1,0:T(8,128)(2,1)S(1)}, bf16[272,256]{1,0:T(8,128)(2,1)S(1)}, u32[]{:S(2)}, u32[]{:S(2)}) collective-permute-start(bf16[272,256]{1,0:T(8,128)(2,1)S(1)} %get-tuple-element.40), channel_id=1, source_target_pairs={{0,4},{1,5},{2,6},{3,7},{4,8},{5,9},{6,10},{7,11},{8,12},{9,13},{1... | collective-permute-start | bytes 417800 | tf_op jit(solution)/shard_map/ppermute | solution.py:29
  98.0 1.5 %collective-permute-start.24 = (bf16[144,256]{1,0:T(8,128)(2,1)S(1)}, bf16[144,256]{1,0:T(8,128)(2,1)S(1)}, u32[]{:S(2)}, u32[]{:S(2)}) collective-permute-start(bf16[144,256]{1,0:T(8,128)(2,1)S(1)} %get-tuple-element.44), channel_id=1, source_target_pairs={{0,4},{1,5},{2,6},{3,7},{4,8},{5,9},{6,10},{7,11},{8,12},{9,13},{1... | collective-permute-start | bytes 221192 | tf_op jit(solution)/shard_map/ppermute | solution.py:29
  99.5 3.3 %collective-permute-done.24.refs_4_ = bf16[144,256]{1,0:T(8,128)(2,1)S(1)} collective-permute-done((bf16[144,256]{1,0:T(8,128)(2,1)S(1)}, bf16[144,256]{1,0:T(8,128)(2,1)S(1)}, u32[]{:S(2)}, u32[]{:S(2)}) %collective-permute-start.24) | collective-permute-done | bytes 73760 | tf_op jit(solution)/shard_map/ppermute | solution.py:29
  102.8 2.0 %collective-permute-done.23.refs_3_ = bf16[272,256]{1,0:T(8,128)(2,1)S(1)} collective-permute-done((bf16[272,256]{1,0:T(8,128)(2,1)S(1)}, bf16[272,256]{1,0:T(8,128)(2,1)S(1)}, u32[]{:S(2)}, u32[]{:S(2)}) %collective-permute-start.23) | collective-permute-done | bytes 139296 | tf_op jit(solution)/shard_map/ppermute | solution.py:29
  104.8 2.9 %collective-permute-done.20.refs_1_ = bf16[272,256]{1,0:T(8,128)(2,1)S(1)} collective-permute-done((bf16[272,256]{1,0:T(8,128)(2,1)S(1)}, bf16[272,256]{1,0:T(8,128)(2,1)S(1)}, u32[]{:S(2)}, u32[]{:S(2)}) %collective-permute-start.20) | collective-permute-done | bytes 139296 | tf_op jit(solution)/shard_map/ppermute | solution.py:29
  107.7 1.0 collective-permute-start.25
  108.7 0.1 collective-permute-start.27
  108.8 0.4 collective-permute-start.26
  109.2 0.1 collective-permute-start.28
  109.3 0.4 collective-permute-start.29
  109.7 1.0 collective-permute-done.29.refs_9_
  110.8 2.5 %shard_map.23 = f32[256,2048]{1,0:T(8,128)} custom-call(s32[5]{0:T(128)S(1)} %stack.23.place, bf16[656,256]{1,0:T(8,128)(2,1)S(1)} %collective-permute-done.19.refs_0_, bf16[272,256]{1,0:T(8,128)(2,1)S(1)} %collective-permute-done.20.refs_1_, bf16[400,256]{1,0:T(8,128)(2,1)S(1)} %collective-permute-done.21.refs_2_, ...), custom_call_target="tpu_custom_call" | custom-call | bytes 6291456 | tf_op jit(solution)/shard_map/pallas_call | solution.py:103
  (26 shorter events, 0.1 us)
Async XLA Ops:
  1.5 18.0 %collective-permute-start = (bf16[256,2048]{1,0:T(8,128)(2,1)S(1)}, bf16[256,2048]{1,0:T(8,128)(2,1)}, u32[]{:S(2)}, u32[]{:S(2)}) collective-permute-start(bf16[256,2048]{1,0:T(8,128)(2,1)S(1)} %bitcast.10), channel_id=1, source_target_pairs={{0,0},{1,1},{2,2},{3,3},{4,4},{5,5},{6,6},{7,7},{8,8},{9,9},{10,10... | collective-permute-start | bytes 3145736 | tf_op jit(solution)/shard_map/ppermute | solution.py:29
  19.5 14.6 %collective-permute-start.1 = (bf16[256,2048]{1,0:T(8,128)(2,1)}, bf16[256,2048]{1,0:T(8,128)(2,1)S(1)}, u32[]{:S(2)}, u32[]{:S(2)}) collective-permute-start(bf16[256,2048]{1,0:T(8,128)(2,1)} %collective-permute-done.refs_0_), channel_id=1, source_target_pairs={{0,12},{1,13},{2,14},{3,15},{4,0},{5,1},{6,2},{7,3},{8,4},{9,5},{1... | collective-permute-start | bytes 3145736 | tf_op jit(solution)/shard_map/ppermute | solution.py:29
  21.9 15.8 %collective-permute-start.2 = (bf16[256,2048]{1,0:T(8,128)(2,1)}, bf16[256,2048]{1,0:T(8,128)(2,1)S(1)}, u32[]{:S(2)}, u32[]{:S(2)}) collective-permute-start(bf16[256,2048]{1,0:T(8,128)(2,1)} %collective-permute-done.refs_0_), channel_id=1, source_target_pairs={{0,3},{1,0},{2,1},{3,2},{4,7},{5,4},{6,5},{7,6},{8,11},{9,8},{10,9... | collective-permute-start | bytes 3145736 | tf_op jit(solution)/shard_map/ppermute | solution.py:29
  25.7 15.1 %collective-permute-start.3 = (bf16[256,2048]{1,0:T(8,128)(2,1)}, bf16[256,2048]{1,0:T(8,128)(2,1)S(1)}, u32[]{:S(2)}, u32[]{:S(2)}) collective-permute-start(bf16[256,2048]{1,0:T(8,128)(2,1)} %collective-permute-done.refs_0_), channel_id=1, source_target_pairs={{0,4},{1,5},{2,6},{3,7},{4,8},{5,9},{6,10},{7,11},{8,12},{9,13},{1... | collective-permute-start | bytes 3145736 | tf_op jit(solution)/shard_map/ppermute | solution.py:29
  25.7 16.2 %collective-permute-start.4 = (bf16[256,2048]{1,0:T(8,128)(2,1)}, bf16[256,2048]{1,0:T(8,128)(2,1)}, u32[]{:S(2)}, u32[]{:S(2)}) collective-permute-start(bf16[256,2048]{1,0:T(8,128)(2,1)} %collective-permute-done.refs_0_), channel_id=1, source_target_pairs={{0,1},{1,2},{2,3},{3,0},{4,5},{5,6},{6,7},{7,4},{8,9},{9,10},{10,1... | collective-permute-start | bytes 3145736 | tf_op jit(solution)/shard_map/ppermute | solution.py:29
  34.1 7.8 %collective-permute-start.7 = (bf16[256,2048]{1,0:T(8,128)(2,1)}, bf16[256,2048]{1,0:T(8,128)(2,1)}, u32[]{:S(2)}, u32[]{:S(2)}) collective-permute-start(bf16[256,2048]{1,0:T(8,128)(2,1)} %collective-permute-done.refs_0_), channel_id=1, source_target_pairs={{0,32},{1,33},{2,34},{3,35},{4,36},{5,37},{6,38},{7,39},{8,40},{9,... | collective-permute-start | bytes 3145736 | tf_op jit(solution)/shard_map/ppermute | solution.py:29
  34.1 7.8 %collective-permute-start.5 = (bf16[256,2048]{1,0:T(8,128)(2,1)S(1)}, bf16[256,2048]{1,0:T(8,128)(2,1)}, u32[]{:S(2)}, u32[]{:S(2)}) collective-permute-start(bf16[256,2048]{1,0:T(8,128)(2,1)S(1)} %collective-permute-done.1.refs_1_.refs_0_), channel_id=1, source_target_pairs={{0,32},{1,33},{2,34},{3,35},{4,36},{5,37},{6,38},{7,39},{8,40},{9,... | collective-permute-start | bytes 3145736 | tf_op jit(solution)/shard_map/ppermute | solution.py:29
  37.7 4.2 %collective-permute-start.6 = (bf16[256,2048]{1,0:T(8,128)(2,1)S(1)}, bf16[256,2048]{1,0:T(8,128)(2,1)}, u32[]{:S(2)}, u32[]{:S(2)}) collective-permute-start(bf16[256,2048]{1,0:T(8,128)(2,1)S(1)} %collective-permute-done.2.refs_2_.refs_1_), channel_id=1, source_target_pairs={{0,32},{1,33},{2,34},{3,35},{4,36},{5,37},{6,38},{7,39},{8,40},{9,... | collective-permute-start | bytes 3145736 | tf_op jit(solution)/shard_map/ppermute | solution.py:29
  40.7 1.0 copy-start
  41.7 13.6 %collective-permute-start.10 = (bf16[256,2048]{1,0:T(8,128)(2,1)S(1)}, bf16[256,2048]{1,0:T(8,128)(2,1)S(1)}, u32[]{:S(2)}, u32[]{:S(2)}) collective-permute-start(bf16[256,2048]{1,0:T(8,128)(2,1)S(1)} %collective-permute-done.1.refs_1_.refs_0_), channel_id=1, source_target_pairs={{0,3},{1,0},{2,1},{3,2},{4,7},{5,4},{6,5},{7,6},{8,11},{9,8},{10,9... | collective-permute-start | bytes 3145736 | tf_op jit(solution)/shard_map/ppermute | solution.py:29
  41.9 1.2 %copy-start.1 = (bf16[256,2048]{1,0:T(8,128)(2,1)S(1)}, bf16[256,2048]{1,0:T(8,128)(2,1)}, u32[]{:S(2)}) copy-start(bf16[256,2048]{1,0:T(8,128)(2,1)} %copy-done) | copy-start | bytes 3145732
  55.3 14.9 %collective-permute-start.11 = (bf16[256,2048]{1,0:T(8,128)(2,1)S(1)}, bf16[256,2048]{1,0:T(8,128)(2,1)S(1)}, u32[]{:S(2)}, u32[]{:S(2)}) collective-permute-start(bf16[256,2048]{1,0:T(8,128)(2,1)S(1)} %copy-done.1), channel_id=1, source_target_pairs={{0,1},{1,2},{2,3},{3,0},{4,5},{5,6},{6,7},{7,4},{8,9},{9,10},{10,1... | collective-permute-start | bytes 3145736 | tf_op jit(solution)/shard_map/ppermute | solution.py:29
  55.3 28.8 %collective-permute-start.8 = (bf16[1808,256]{1,0:T(8,128)(2,1)S(1)}, bf16[1808,256]{1,0:T(8,128)(2,1)S(1)}, u32[]{:S(2)}, u32[]{:S(2)}) collective-permute-start(bf16[1808,256]{1,0:T(8,128)(2,1)S(1)} %get-tuple-element.29.refs_8_), channel_id=1, source_target_pairs={{0,64},{1,65},{2,66},{3,67},{4,68},{5,69},{6,70},{7,71},{8,72},{9,... | collective-permute-start | bytes 2777096 | tf_op jit(solution)/shard_map/ppermute | solution.py:29
  59.9 24.4 %collective-permute-start.9 = (bf16[1808,256]{1,0:T(8,128)(2,1)S(1)}, bf16[1808,256]{1,0:T(8,128)(2,1)S(1)}, u32[]{:S(2)}, u32[]{:S(2)}) collective-permute-start(bf16[1808,256]{1,0:T(8,128)(2,1)S(1)} %get-tuple-element.30), channel_id=1, source_target_pairs={{0,0},{1,1},{2,2},{3,3},{4,4},{5,5},{6,6},{7,7},{8,8},{9,9},{10,10... | collective-permute-start | bytes 2777096 | tf_op jit(solution)/shard_map/ppermute | solution.py:29
  62.6 2.0 %collective-permute-start.12 = (bf16[128,2048]{1,0:T(8,128)(2,1)S(1)}, bf16[128,2048]{1,0:T(8,128)(2,1)S(1)}, u32[]{:S(2)}, u32[]{:S(2)}) collective-permute-start(bf16[128,2048]{1,0:T(8,128)(2,1)S(1)} %get-tuple-element.52), channel_id=1, source_target_pairs={{0,32},{1,33},{2,34},{3,35},{4,36},{5,37},{6,38},{7,39},{8,40},{9,... | collective-permute-start | bytes 1572872 | tf_op jit(solution)/shard_map/ppermute | solution.py:29
  62.7 2.6 %collective-permute-start.13 = (bf16[128,2048]{1,0:T(8,128)(2,1)S(1)}, bf16[128,2048]{1,0:T(8,128)(2,1)S(1)}, u32[]{:S(2)}, u32[]{:S(2)}) collective-permute-start(bf16[128,2048]{1,0:T(8,128)(2,1)S(1)} %get-tuple-element.51), channel_id=1, source_target_pairs={{0,32},{1,33},{2,34},{3,35},{4,36},{5,37},{6,38},{7,39},{8,40},{9,... | collective-permute-start | bytes 1572872 | tf_op jit(solution)/shard_map/ppermute | solution.py:29
  75.6 13.2 %collective-permute-start.15 = (bf16[400,256]{1,0:T(8,128)(2,1)S(1)}, bf16[400,256]{1,0:T(8,128)(2,1)S(1)}, u32[]{:S(2)}, u32[]{:S(2)}) collective-permute-start(bf16[400,256]{1,0:T(8,128)(2,1)S(1)} %get-tuple-element.33._), channel_id=1, source_target_pairs={{0,64},{1,65},{2,66},{3,67},{4,68},{5,69},{6,70},{7,71},{8,72},{9,... | collective-permute-start | bytes 614408 | tf_op jit(solution)/shard_map/ppermute | solution.py:29
  81.4 9.3 %collective-permute-start.16 = (bf16[400,256]{1,0:T(8,128)(2,1)S(1)}, bf16[400,256]{1,0:T(8,128)(2,1)S(1)}, u32[]{:S(2)}, u32[]{:S(2)}) collective-permute-start(bf16[400,256]{1,0:T(8,128)(2,1)S(1)} %get-tuple-element.36), channel_id=1, source_target_pairs={{0,96},{1,97},{2,98},{3,99},{4,100},{5,101},{6,102},{7,103},{8,104... | collective-permute-start | bytes 614408 | tf_op jit(solution)/shard_map/ppermute | solution.py:29
  81.4 9.3 %collective-permute-start.17 = (bf16[400,256]{1,0:T(8,128)(2,1)S(1)}, bf16[400,256]{1,0:T(8,128)(2,1)S(1)}, u32[]{:S(2)}, u32[]{:S(2)}) collective-permute-start(bf16[400,256]{1,0:T(8,128)(2,1)S(1)} %get-tuple-element.37), channel_id=1, source_target_pairs={{0,0},{1,1},{2,2},{3,3},{4,4},{5,5},{6,6},{7,7},{8,8},{9,9},{10,10... | collective-permute-start | bytes 614408 | tf_op jit(solution)/shard_map/ppermute | solution.py:29
  84.1 6.5 %collective-permute-start.18 = (bf16[400,256]{1,0:T(8,128)(2,1)S(1)}, bf16[400,256]{1,0:T(8,128)(2,1)S(1)}, u32[]{:S(2)}, u32[]{:S(2)}) collective-permute-start(bf16[400,256]{1,0:T(8,128)(2,1)S(1)} %get-tuple-element.38), channel_id=1, source_target_pairs={{0,32},{1,33},{2,34},{3,35},{4,36},{5,37},{6,38},{7,39},{8,40},{9,... | collective-permute-start | bytes 614408 | tf_op jit(solution)/shard_map/ppermute | solution.py:29
  86.8 4.5 %collective-permute-start.14 = (f32[6,128,256]{2,1,0:T(8,128)}, f32[6,128,256]{2,1,0:T(8,128)}, u32[]{:S(2)}, u32[]{:S(2)}) collective-permute-start(f32[6,128,256]{2,1,0:T(8,128)} %get-tuple-element.35), channel_id=1, source_target_pairs={{0,32},{1,33},{2,34},{3,35},{4,36},{5,37},{6,38},{7,39},{8,40},{9,... | collective-permute-start | bytes 2359304 | tf_op jit(solution)/shard_map/ppermute | solution.py:29
  88.9 7.8 %collective-permute-start.22 = (f32[3,256,256]{2,1,0:T(8,128)}, f32[3,256,256]{2,1,0:T(8,128)}, u32[]{:S(2)}, u32[]{:S(2)}) collective-permute-start(f32[3,256,256]{2,1,0:T(8,128)} %shard_map.20._.refs_10_), channel_id=1, source_target_pairs={{0,32},{1,33},{2,34},{3,35},{4,36},{5,37},{6,38},{7,39},{8,40},{9,... | collective-permute-start | bytes 2359304 | tf_op jit(solution)/shard_map/ppermute | solution.py:29
  93.2 14.5 %collective-permute-start.19 = (bf16[656,256]{1,0:T(8,128)(2,1)S(1)}, bf16[656,256]{1,0:T(8,128)(2,1)S(1)}, u32[]{:S(2)}, u32[]{:S(2)}) collective-permute-start(bf16[656,256]{1,0:T(8,128)(2,1)S(1)} %get-tuple-element.39), channel_id=1, source_target_pairs={{0,1},{1,2},{2,3},{3,0},{4,5},{5,6},{6,7},{7,4},{8,9},{9,10},{10,1... | collective-permute-start | bytes 1007624 | tf_op jit(solution)/shard_map/ppermute | solution.py:29
  93.7 14.0 %collective-permute-start.21 = (bf16[400,256]{1,0:T(8,128)(2,1)S(1)}, bf16[400,256]{1,0:T(8,128)(2,1)S(1)}, u32[]{:S(2)}, u32[]{:S(2)}) collective-permute-start(bf16[400,256]{1,0:T(8,128)(2,1)S(1)} %get-tuple-element.41), channel_id=1, source_target_pairs={{0,15},{1,12},{2,13},{3,14},{4,3},{5,0},{6,1},{7,2},{8,7},{9,4},{1... | collective-permute-start | bytes 614408 | tf_op jit(solution)/shard_map/ppermute | solution.py:29
  96.7 8.1 %collective-permute-start.23 = (bf16[272,256]{1,0:T(8,128)(2,1)S(1)}, bf16[272,256]{1,0:T(8,128)(2,1)S(1)}, u32[]{:S(2)}, u32[]{:S(2)}) collective-permute-start(bf16[272,256]{1,0:T(8,128)(2,1)S(1)} %get-tuple-element.43), channel_id=1, source_target_pairs={{0,12},{1,13},{2,14},{3,15},{4,0},{5,1},{6,2},{7,3},{8,4},{9,5},{1... | collective-permute-start | bytes 417800 | tf_op jit(solution)/shard_map/ppermute | solution.py:29
  96.7 11.0 %collective-permute-start.20 = (bf16[272,256]{1,0:T(8,128)(2,1)S(1)}, bf16[272,256]{1,0:T(8,128)(2,1)S(1)}, u32[]{:S(2)}, u32[]{:S(2)}) collective-permute-start(bf16[272,256]{1,0:T(8,128)(2,1)S(1)} %get-tuple-element.40), channel_id=1, source_target_pairs={{0,4},{1,5},{2,6},{3,7},{4,8},{5,9},{6,10},{7,11},{8,12},{9,13},{1... | collective-permute-start | bytes 417800 | tf_op jit(solution)/shard_map/ppermute | solution.py:29
  98.0 4.8 %collective-permute-start.24 = (bf16[144,256]{1,0:T(8,128)(2,1)S(1)}, bf16[144,256]{1,0:T(8,128)(2,1)S(1)}, u32[]{:S(2)}, u32[]{:S(2)}) collective-permute-start(bf16[144,256]{1,0:T(8,128)(2,1)S(1)} %get-tuple-element.44), channel_id=1, source_target_pairs={{0,4},{1,5},{2,6},{3,7},{4,8},{5,9},{6,10},{7,11},{8,12},{9,13},{1... | collective-permute-start | bytes 221192 | tf_op jit(solution)/shard_map/ppermute | solution.py:29
  107.7 3.1 %collective-permute-start.25 = (bf16[656,256]{1,0:T(8,128)(2,1)S(1)}, bf16[656,256]{1,0:T(8,128)(2,1)S(1)}, u32[]{:S(2)}, u32[]{:S(2)}) collective-permute-start(bf16[656,256]{1,0:T(8,128)(2,1)S(1)} %collective-permute-done.19.refs_0_), channel_id=1, source_target_pairs={{0,32},{1,33},{2,34},{3,35},{4,36},{5,37},{6,38},{7,39},{8,40},{9,... | collective-permute-start | bytes 1007624 | tf_op jit(solution)/shard_map/ppermute | solution.py:29
  108.7 2.1 %collective-permute-start.27 = (bf16[400,256]{1,0:T(8,128)(2,1)S(1)}, bf16[400,256]{1,0:T(8,128)(2,1)S(1)}, u32[]{:S(2)}, u32[]{:S(2)}) collective-permute-start(bf16[400,256]{1,0:T(8,128)(2,1)S(1)} %collective-permute-done.21.refs_2_), channel_id=1, source_target_pairs={{0,32},{1,33},{2,34},{3,35},{4,36},{5,37},{6,38},{7,39},{8,40},{9,... | collective-permute-start | bytes 614408 | tf_op jit(solution)/shard_map/ppermute | solution.py:29
  108.8 2.0 %collective-permute-start.26 = (bf16[272,256]{1,0:T(8,128)(2,1)S(1)}, bf16[272,256]{1,0:T(8,128)(2,1)S(1)}, u32[]{:S(2)}, u32[]{:S(2)}) collective-permute-start(bf16[272,256]{1,0:T(8,128)(2,1)S(1)} %collective-permute-done.20.refs_1_), channel_id=1, source_target_pairs={{0,32},{1,33},{2,34},{3,35},{4,36},{5,37},{6,38},{7,39},{8,40},{9,... | collective-permute-start | bytes 417800 | tf_op jit(solution)/shard_map/ppermute | solution.py:29
  109.2 1.6 %collective-permute-start.28 = (bf16[272,256]{1,0:T(8,128)(2,1)S(1)}, bf16[272,256]{1,0:T(8,128)(2,1)S(1)}, u32[]{:S(2)}, u32[]{:S(2)}) collective-permute-start(bf16[272,256]{1,0:T(8,128)(2,1)S(1)} %collective-permute-done.23.refs_3_), channel_id=1, source_target_pairs={{0,32},{1,33},{2,34},{3,35},{4,36},{5,37},{6,38},{7,39},{8,40},{9,... | collective-permute-start | bytes 417800 | tf_op jit(solution)/shard_map/ppermute | solution.py:29
  109.3 1.5 %collective-permute-start.29 = (bf16[144,256]{1,0:T(8,128)(2,1)S(1)}, bf16[144,256]{1,0:T(8,128)(2,1)S(1)}, u32[]{:S(2)}, u32[]{:S(2)}) collective-permute-start(bf16[144,256]{1,0:T(8,128)(2,1)S(1)} %collective-permute-done.24.refs_4_), channel_id=1, source_target_pairs={{0,32},{1,33},{2,34},{3,35},{4,36},{5,37},{6,38},{7,39},{8,40},{9,... | collective-permute-start | bytes 221192 | tf_op jit(solution)/shard_map/ppermute | solution.py:29
